TPU v7x, 256 devices: a whole 4x4x8 slice. The times are simulated.
256 devices in a mesh: lon: 16 (over y_hi, z), lat: 16 (over x, y_lo, core).
Axes of the slice: x: 4, y: 4 (y_hi: 2, y_lo: 2; y = y_hi * 2 + y_lo), z: 8, core: 2. Of those that a mesh axis runs over, the one named last changes fastest.
Arguments:
- inputs: bfloat16 [4, 96, 192, 192], P(None, 'lat', 'lon'), may hold values from -36 to 36
- grad_out: bfloat16 [4, 96, 192, 192], P(None, 'lat', 'lon'), may hold values from -6 to 6
- region: int32 [4, 96, 192], P(None, 'lat', 'lon'), may hold values from 0 to 2
- bias_level: int32 [2, 16], P(None, 'lat'), may hold values from 0 to 1
- norm_gains: float32 [2, 2, 192], replicated, may hold values from 0.1 to 1.9
- in_weight: bfloat16 [2, 192, 576], replicated, may hold values from -0.4375 to 0.4375
- out_weight: bfloat16 [2, 192, 192], replicated, may hold values from -0.4375 to 0.4375
- up_weight: bfloat16 [2, 192, 768], replicated, may hold values from -0.4375 to 0.4375
- down_weight: bfloat16 [2, 768, 192], replicated, may hold values from -0.21875 to 0.21875
- bias_tables: bfloat16 [2, 16, 2, 6, 3312], P(None, 'lat'), may hold values from -2.5 to 301
Outputs:
- blocks_out: bfloat16 [4, 96, 192, 192], P(None, 'lat', 'lon')
- grad_inputs: bfloat16 [4, 96, 192, 192], P(None, 'lat', 'lon')
- grad_gains: float32 [2, 2, 192], replicated
- grad_in_weight: float32 [2, 192, 576], replicated
- grad_out_weight: float32 [2, 192, 192], replicated
- grad_up_weight: float32 [2, 192, 768], replicated
- grad_down_weight: float32 [2, 768, 192], replicated
- grad_tables: float32 [2, 16, 2, 6, 3312], P(None, 'lat')
Inputs may be any that keep to these rules, and one draw needn't show every extreme that they name: A token of the shifted block attends only to tokens of its window with the same region id.
All inputs are finite; a program needn't handle non-finite values.
Results may differ from a plain program's by a relative error of at most 0.028.
Values may be sent and summed in bfloat16 or wider, within the bound.
No kernel may reach another device: no remote copies, remote signals or barrier semaphores. Data moves between devices by JAX's collectives and lax.ppermute only.
A program may use at most 64 MiB of HBM per device.

v0:
```python
import math

import jax
import jax.numpy as jnp
from jax import lax
from jax.sharding import PartitionSpec as P

C = 192
HEADS = 6
HEAD = 32
WIN_Z = 2
WIN_LAT = 6
WIN_LON = 12
WIN = 144
RELPOS = 3312


EPSILON = 1e-05
NEGATIVE = -1000000000.0


def from_behind(value, axis, steps):
    count = lax.axis_size(axis)
    pairs = [(source, (source + steps) % count) for source in range(count)]
    return lax.ppermute(value, axis, pairs)


def to_windows(grid_in):
    level_count, lat_count, lon_count = (grid_in.shape[0], grid_in.shape[1], grid_in.shape[2])
    trailing = tuple(grid_in.shape[3:])
    shaped = grid_in.reshape(
        (level_count // WIN_Z, WIN_Z, lat_count // WIN_LAT, WIN_LAT, lon_count // WIN_LON, WIN_LON)
        + trailing
    )
    layout = (0, 2, 4, 1, 3, 5) + tuple(range(6, 6 + len(trailing)))
    return shaped.transpose(layout).reshape((-1, WIN) + trailing)


def from_windows(windows, level_count, lat_count, lon_count):
    trailing = tuple(windows.shape[2:])
    shaped = windows.reshape(
        (level_count // WIN_Z, lat_count // WIN_LAT, lon_count // WIN_LON, WIN_Z, WIN_LAT, WIN_LON)
        + trailing
    )
    layout = (0, 3, 1, 4, 2, 5) + tuple(range(6, 6 + len(trailing)))
    return shaped.transpose(layout).reshape((level_count, lat_count, lon_count) + trailing)


def pair_table(dtype):
    span = 2 * WIN_LON - 1
    query_col = jnp.arange(WIN_LON, dtype=jnp.int32)[:, None, None, None, None, None, None]
    key_level = jnp.arange(WIN_Z, dtype=jnp.int32)[None, :, None, None, None, None, None]
    key_row = jnp.arange(WIN_LAT, dtype=jnp.int32)[None, None, :, None, None, None, None]
    key_col = jnp.arange(WIN_LON, dtype=jnp.int32)[None, None, None, :, None, None, None]
    entry_level = jnp.arange(WIN_Z, dtype=jnp.int32)[None, None, None, None, :, None, None]
    entry_row = jnp.arange(WIN_LAT, dtype=jnp.int32)[None, None, None, None, None, :, None]
    entry_offset = jnp.arange(span, dtype=jnp.int32)[None, None, None, None, None, None, :]
    matched = (
        (key_level == entry_level)
        & (key_row == entry_row)
        & (entry_offset == query_col - key_col + WIN_LON - 1)
    )
    return matched.astype(dtype).reshape(WIN_LON * WIN, WIN_Z * WIN_LAT * span)


def expand_bias(bias_rows):
    window_count = bias_rows.shape[0]
    shaped = bias_rows.reshape(window_count, HEADS, WIN_Z, WIN_Z, WIN_LAT, WIN_LAT, 2 * WIN_LON - 1)
    shaped = shaped.transpose(0, 1, 2, 4, 3, 5, 6).reshape(
        window_count * HEADS * WIN_Z * WIN_LAT, -1
    )
    spread = lax.dot_general(
        shaped,
        pair_table(jnp.bfloat16),
        (((1,), (1,)), ((), ())),
        preferred_element_type=jnp.float32,
    )
    return spread.reshape(window_count, HEADS, WIN, WIN)


def collect_bias(grad_scores):
    window_count = grad_scores.shape[0]
    flat = grad_scores.reshape(window_count * HEADS * WIN_Z * WIN_LAT, WIN_LON * WIN)
    summed = jnp.dot(
        flat,
        pair_table(jnp.float32),
        precision=lax.Precision.HIGHEST,
        preferred_element_type=jnp.float32,
    )
    summed = summed.reshape(window_count, HEADS, WIN_Z, WIN_LAT, WIN_Z, WIN_LAT, 2 * WIN_LON - 1)
    return summed.transpose(0, 1, 2, 4, 3, 5, 6).reshape(window_count, HEADS, RELPOS)


def selector(bias_level, window_count, latitude_window_count, lon_windows):
    level_windows = bias_level.shape[0]
    window_ids = jnp.arange(window_count, dtype=jnp.int32)
    level_win = window_ids // (latitude_window_count * lon_windows)
    lat_win = window_ids // lon_windows % latitude_window_count
    flat_key = level_win * latitude_window_count + lat_win
    table_keys = jnp.arange(level_windows * latitude_window_count, dtype=jnp.int32)
    chosen = jnp.sum(
        jnp.where(table_keys[None, :] == flat_key[:, None], bias_level.reshape(-1)[None, :], 0),
        axis=1,
    )
    target = lat_win * level_windows + chosen
    row_keys = jnp.arange(latitude_window_count * level_windows, dtype=jnp.int32)
    return (row_keys[None, :] == target[:, None]).astype(jnp.float32)


def layer_norm(flat_values, gain):
    centre = flat_values - jnp.mean(flat_values, axis=-1, keepdims=True)
    inverse = lax.rsqrt(jnp.mean(centre * centre, axis=-1, keepdims=True) + EPSILON)
    normal_hat = centre * inverse
    return (normal_hat * gain, normal_hat, inverse)


def norm_backward(upstream, normal_hat, inverse):
    upstream_mean = jnp.mean(upstream, axis=-1, keepdims=True)
    cross_mean = jnp.mean(upstream * normal_hat, axis=-1, keepdims=True)
    return inverse * (upstream - upstream_mean - normal_hat * cross_mean)


def gelu_exact(expanded):
    return expanded * 0.5 * (1.0 + jax.scipy.special.erf(expanded / math.sqrt(2.0)))


def gelu_slope(expanded):
    cumulative = 0.5 * (1.0 + jax.scipy.special.erf(expanded / math.sqrt(2.0)))
    return cumulative + expanded * jnp.exp(-0.5 * expanded * expanded) / math.sqrt(2.0 * math.pi)


def window_forward(block_in, gain_pair, in_w, out_w, up_w, down_w, bias_rows, region_win):
    window_count = block_in.shape[0]
    flat_in = block_in.astype(jnp.float32).reshape(-1, C)
    normed, first_hat, first_inv = layer_norm(flat_in, gain_pair[0])
    first_norm = normed.astype(jnp.bfloat16)
    projected = jnp.dot(first_norm, in_w, preferred_element_type=jnp.float32).astype(jnp.bfloat16)
    projected = projected.reshape(window_count, WIN, 3, HEADS, HEAD)
    queries, key_vecs, values = (projected[:, :, 0], projected[:, :, 1], projected[:, :, 2])
    score_scale = 1.0 / math.sqrt(HEAD)
    bias_full = expand_bias(bias_rows)
    scores = (
        jnp.einsum("nahd,nbhd->nhab", queries, key_vecs, preferred_element_type=jnp.float32)
        * score_scale
        + bias_full
    )
    if region_win is not None:
        same_region = region_win[:, None, :, None] == region_win[:, None, None, :]
        scores = jnp.where(same_region, scores, NEGATIVE)
    top_score = jnp.max(scores, axis=-1, keepdims=True)
    exp_scores = jnp.exp(scores - top_score)
    attend = exp_scores / jnp.sum(exp_scores, axis=-1, keepdims=True)
    attend_half = attend.astype(jnp.bfloat16)
    mixed_heads = jnp.einsum(
        "nhab,nbhd->nahd", attend_half, values, preferred_element_type=jnp.float32
    ).astype(jnp.bfloat16)
    mixed_heads = mixed_heads.reshape(-1, C)
    hidden_one = (flat_in + jnp.dot(mixed_heads, out_w, preferred_element_type=jnp.float32)).astype(
        jnp.bfloat16
    )
    normed_two, second_hat, second_inv = layer_norm(hidden_one.astype(jnp.float32), gain_pair[1])
    second_norm = normed_two.astype(jnp.bfloat16)
    expanded = jnp.dot(second_norm, up_w, preferred_element_type=jnp.float32)
    activated = gelu_exact(expanded).astype(jnp.bfloat16)
    block_out = (
        hidden_one.astype(jnp.float32)
        + jnp.dot(activated, down_w, preferred_element_type=jnp.float32)
    ).astype(jnp.bfloat16)
    stored = (
        first_hat,
        first_inv,
        first_norm,
        queries,
        key_vecs,
        values,
        attend,
        attend_half,
        mixed_heads,
        hidden_one,
        second_hat,
        second_inv,
        second_norm,
        expanded,
        activated,
    )
    return (block_out.reshape(window_count, WIN, C), stored)


def window_backward(stored, grad_windows, gain_pair, in_w, out_w, up_w, down_w):
    (
        first_hat,
        first_inv,
        first_norm,
        queries,
        key_vecs,
        values,
        attend,
        attend_half,
        mixed_heads,
        hidden_one,
        second_hat,
        second_inv,
        second_norm,
        expanded,
        activated,
    ) = stored
    window_count = queries.shape[0]
    score_scale = 1.0 / math.sqrt(HEAD)
    contract_rows = (((0,), (0,)), ((), ()))
    contract_cols = (((1,), (1,)), ((), ()))
    grad_flat = grad_windows.reshape(-1, C)
    grad_down = lax.dot_general(
        activated, grad_flat, contract_rows, preferred_element_type=jnp.float32
    )
    grad_act = lax.dot_general(grad_flat, down_w, contract_cols, preferred_element_type=jnp.float32)
    grad_expanded = (grad_act * gelu_slope(expanded)).astype(jnp.bfloat16)
    grad_up = lax.dot_general(
        second_norm, grad_expanded, contract_rows, preferred_element_type=jnp.float32
    )
    grad_second = lax.dot_general(
        grad_expanded, up_w, contract_cols, preferred_element_type=jnp.float32
    )
    gain_two = jnp.sum(grad_second * second_hat, axis=0)
    grad_hidden = (
        grad_flat.astype(jnp.float32)
        + norm_backward(grad_second * gain_pair[1], second_hat, second_inv)
    ).astype(jnp.bfloat16)
    grad_out_w = lax.dot_general(
        mixed_heads, grad_hidden, contract_rows, preferred_element_type=jnp.float32
    )
    grad_mixed = lax.dot_general(
        grad_hidden, out_w, contract_cols, preferred_element_type=jnp.float32
    ).astype(jnp.bfloat16)
    grad_mixed = grad_mixed.reshape(window_count, WIN, HEADS, HEAD)
    grad_attend = jnp.einsum(
        "nahd,nbhd->nhab", grad_mixed, values, preferred_element_type=jnp.float32
    )
    grad_values = jnp.einsum(
        "nhab,nahd->nbhd", attend_half, grad_mixed, preferred_element_type=jnp.float32
    ).astype(jnp.bfloat16)
    grad_scores = attend * (grad_attend - jnp.sum(grad_attend * attend, axis=-1, keepdims=True))
    grad_rows = collect_bias(grad_scores)
    grad_scaled = (grad_scores * score_scale).astype(jnp.bfloat16)
    grad_queries = jnp.einsum(
        "nhab,nbhd->nahd", grad_scaled, key_vecs, preferred_element_type=jnp.float32
    ).astype(jnp.bfloat16)
    grad_keys = jnp.einsum(
        "nhab,nahd->nbhd", grad_scaled, queries, preferred_element_type=jnp.float32
    ).astype(jnp.bfloat16)
    grad_projected = jnp.stack([grad_queries, grad_keys, grad_values], axis=2).reshape(-1, 3 * C)
    grad_in_w = lax.dot_general(
        first_norm, grad_projected, contract_rows, preferred_element_type=jnp.float32
    )
    grad_first = lax.dot_general(
        grad_projected, in_w, contract_cols, preferred_element_type=jnp.float32
    )
    gain_one = jnp.sum(grad_first * first_hat, axis=0)
    grad_block_in = (
        grad_hidden.astype(jnp.float32)
        + norm_backward(grad_first * gain_pair[0], first_hat, first_inv)
    ).astype(jnp.bfloat16)
    weight_gradients = (jnp.stack([gain_one, gain_two]), grad_in_w, grad_out_w, grad_up, grad_down)
    return (grad_block_in.reshape(window_count, WIN, C), weight_gradients, grad_rows)


def gather_rows(picker, table, window_count):
    bias_rows = jnp.dot(
        picker.astype(jnp.bfloat16),
        table.reshape(-1, HEADS * RELPOS),
        preferred_element_type=jnp.float32,
    )
    return bias_rows.astype(jnp.bfloat16).reshape(window_count, HEADS, RELPOS)


def table_grad(picker, grad_rows, table_shape):
    summed = lax.dot_general(
        picker,
        grad_rows.reshape(grad_rows.shape[0], -1),
        (((0,), (0,)), ((), ())),
        precision=lax.Precision.HIGHEST,
        preferred_element_type=jnp.float32,
    )
    return summed.reshape(table_shape)


def roll_ahead(grid_in):
    rolled = jnp.roll(grid_in, -(WIN_Z // 2), axis=0)
    incoming = from_behind(rolled[:, : WIN_LAT // 2], "lat", -1)
    rolled = jnp.concatenate([rolled[:, WIN_LAT // 2 :], incoming], axis=1)
    incoming = from_behind(rolled[:, :, : WIN_LON // 2], "lon", -1)
    return jnp.concatenate([rolled[:, :, WIN_LON // 2 :], incoming], axis=2)


def roll_back(grid_in):
    incoming = from_behind(grid_in[:, :, grid_in.shape[2] - WIN_LON // 2 :], "lon", 1)
    rolled = jnp.concatenate([incoming, grid_in[:, :, : grid_in.shape[2] - WIN_LON // 2]], axis=2)
    incoming = from_behind(rolled[:, rolled.shape[1] - WIN_LAT // 2 :], "lat", 1)
    rolled = jnp.concatenate([incoming, rolled[:, : rolled.shape[1] - WIN_LAT // 2]], axis=1)
    return jnp.roll(rolled, WIN_Z // 2, axis=0)


def per_device(
    inputs,
    grad_out,
    region,
    bias_level,
    norm_gains,
    in_weight,
    out_weight,
    up_weight,
    down_weight,
    bias_tables,
):
    level_count, lat_count, lon_count = (inputs.shape[0], inputs.shape[1], inputs.shape[2])
    latitude_window_count = lat_count // WIN_LAT
    lon_windows = lon_count // WIN_LON
    window_count = level_count // WIN_Z * latitude_window_count * lon_windows
    picker = selector(bias_level, window_count, latitude_window_count, lon_windows)
    params_first = (norm_gains[0], in_weight[0], out_weight[0], up_weight[0], down_weight[0])
    params_second = (norm_gains[1], in_weight[1], out_weight[1], up_weight[1], down_weight[1])
    rows_first = gather_rows(picker, bias_tables[0], window_count)
    rows_second = gather_rows(picker, bias_tables[1], window_count)
    table_shape = bias_tables.shape[1:]
    first_out, first_stored = window_forward(to_windows(inputs), *params_first, rows_first, None)
    first_grid = from_windows(first_out, level_count, lat_count, lon_count)
    second_in = to_windows(roll_ahead(first_grid))
    second_out, second_stored = window_forward(
        second_in, *params_second, rows_second, to_windows(region)
    )
    blocks_out = roll_back(from_windows(second_out, level_count, lat_count, lon_count))
    grad_second_out = to_windows(roll_ahead(grad_out))
    grad_second_in, second_grads, second_rows = window_backward(
        second_stored, grad_second_out, *params_second
    )
    second_table = table_grad(picker, second_rows, table_shape)
    grad_first_out = to_windows(
        roll_back(from_windows(grad_second_in, level_count, lat_count, lon_count))
    )
    grad_first_in, first_grads, first_rows = window_backward(
        first_stored, grad_first_out, *params_first
    )
    first_table = table_grad(picker, first_rows, table_shape)
    stacked = [jnp.stack([first_grads[index_b], second_grads[index_b]]) for index_b in range(5)]
    tables_grad = jnp.stack([first_table, second_table])
    stacked = lax.psum((stacked[0], stacked[1], stacked[2], stacked[3], stacked[4]), ("lon", "lat"))
    tables_grad = lax.psum(tables_grad.astype(jnp.bfloat16), "lon").astype(jnp.float32)
    grad_inputs = from_windows(grad_first_in, level_count, lat_count, lon_count)
    return (
        blocks_out,
        grad_inputs,
        stacked[0],
        stacked[1],
        stacked[2],
        stacked[3],
        stacked[4],
        tables_grad,
    )


def solution(mesh):
    placed = (
        P(None, "lat", "lon", None),
        P(None, "lat", "lon", None),
        P(None, "lat", "lon"),
        P(None, "lat"),
        P(),
        P(),
        P(),
        P(),
        P(),
        P(None, "lat", None, None, None),
    )
    return jax.shard_map(
        per_device,
        mesh=mesh,
        in_specs=placed,
        out_specs=(
            P(None, "lat", "lon", None),
            P(None, "lat", "lon", None),
            P(),
            P(),
            P(),
            P(),
            P(),
            P(None, "lat", None, None, None),
        ),
        check_vma=False,
    )
```

profile of v0, /device:TPU:1, one launch (start us, length us, event | category | flops | bytes accessed | tf_op | source)
XLA Modules:
  0.0 603.7 jit_solution(18148903639324710214)
XLA Ops:
  10.2 3.2 collective-permute-start.4
  25.3 2.9 broadcast_and_fusion
  28.2 6.7 %and.135 = pred[1728,276]{1,0:T(32,128)(4,1)} reshape(pred[12,2,6,12,2,6,23]{6,5,4,3,2,1,0:T(8,128)(4,1)S(1)} %broadcast_and_fusion) | data formatting | bytes 953856 | tf_op jit(solution)/shard_map/and | solution.py:59
  34.9 1.8 fusion.120
  38.5 1.5 multiply_add_fusion
  40.0 1.7 fusion.116
  45.7 17.1 %collective-permute-start = (bf16[4,3,12,192]{3,2,1,0:T(8,128)(2,1)S(1)}, bf16[4,3,12,192]{3,2,1,0:T(8,128)(2,1)S(1)}, u32[]{:S(2)}, u32[]{:S(2)}) collective-permute-start(bf16[4,3,12,192]{3,2,1,0:T(8,128)(2,1)S(1)} %get-tuple-element.95), channel_id=1, source_target_pairs={{0,15},{1,0},{2,1},{3,2},{4,3},{5,4},{6,5},{7,6},{8,7},{9,8},{10,9... | collective-permute-start | bytes 165896 | tf_op jit(solution)/shard_map/ppermute | solution.py:25
  68.0 2.0 reshape.527
  70.1 2.1 copy.321
  73.1 8.0 %collective-permute-start.5 = (bf16[4,6,6,192]{3,0,2,1:T(4,128)(2,1)S(1)}, bf16[4,6,6,192]{3,0,2,1:T(4,128)(2,1)S(1)}, u32[]{:S(2)}, u32[]{:S(2)}) collective-permute-start(bf16[4,6,6,192]{3,0,2,1:T(4,128)(2,1)S(1)} %get-tuple-element.99), channel_id=1, source_target_pairs={{0,240},{16,0},{32,16},{48,32},{64,48},{80,64},{96,80},{112,96},{1... | collective-permute-start | bytes 165896 | tf_op jit(solution)/shard_map/ppermute | solution.py:25
  82.7 2.0 collective-permute-done.1
  92.3 1.4 add_select_fusion
  93.7 1.8 fusion.118
  95.5 3.9 fusion.25
  99.4 1.8 copy.323
  102.9 1.4 multiply_convert_fusion.2
  109.9 3.3 fusion.28
  113.7 1.9 subtract_multiply_fusion.1
  116.8 2.0 copy.347
  118.8 3.3 reshape.538
  124.4 2.1 multiply_reduce_fusion.4
  126.9 11.7 %fusion.11 = f32[2,6,2,2,6,6,23]{6,4,5,3,2,1,0:T(8,128)S(1)} fusion(pred[2,6,23,1728,1,1,1]{3,2,1,0,4,5,6:T(8,128)(4,1)S(1)} %copy-done.47, f32[2,6,2,6,1728,1,1]{4,3,2,1,0,5,6:T(8,128)} %reshape.538), kind=kOutput, calls=%fused_computation.24 | convolution fusion | flops 824131584 | bytes 1631232 | tf_op jit(solution)/shard_map/dot_general | solution.py:84
  149.6 3.3 fusion.31
  158.6 11.6 %fusion.8 = f32[2,6,2,2,6,6,23]{6,4,5,3,2,1,0:T(8,128)S(1)} fusion(pred[2,6,23,1728,1,1,1]{3,2,1,0,4,5,6:T(8,128)(4,1)} %reshape.536, f32[2,6,2,6,1728,1,1]{4,3,2,1,0,5,6:T(8,128)S(1)} %reshape.535), kind=kOutput, calls=%fused_computation.23 | convolution fusion | flops 824131584 | bytes 1631232 | tf_op jit(solution)/shard_map/dot_general | solution.py:84
  180.2 6.9 %collective-permute-done.2 = bf16[4,6,6,192]{3,2,1,0:T(8,128)(2,1)S(1)} collective-permute-done((bf16[4,6,6,192]{3,2,1,0:T(8,128)(2,1)S(1)}, bf16[4,6,6,192]{3,2,1,0:T(8,128)(2,1)S(1)}, u32[]{:S(2)}, u32[]{:S(2)}) %collective-permute-start.2) | collective-permute-done | bytes 55328 | tf_op jit(solution)/shard_map/ppermute | solution.py:25
  187.1 2.5 collective-permute-start.3
  189.7 4.6 collective-permute-done.3
  196.8 76.7 %psum.42 = f32[2,2,192]{2,1,0:T(2,128)} all-reduce(f32[2,2,192]{2,1,0:T(2,128)S(1)} %pad_maximum_fusion.20), channel_id=1, replica_groups=mesh['lon'=16,'lat'=16] {'lon','lat'}, use_global_device_ids=true, to_apply=%region_27.28 | all-reduce | flops 768 | bytes 6144 | tf_op jit(solution)/shard_map/psum | solution.py:345
  273.5 38.7 %all-reduce.4.cloned.1.call-done = bf16[2,1,2,6,3312]{4,2,3,1,0:T(2,128)(2,1)} async-done(((bf16[2,1,2,6,3312]{4,2,3,1,0:T(2,128)(2,1)}), bf16[2,1,2,6,3312]{4,2,3,1,0:T(2,128)(2,1)}) %all-reduce.4.cloned.1.call-update) | async-done | bytes 158992 | tf_op jit(solution)/shard_map/psum | solution.py:346
  312.2 1.7 convert_element_type.279
  313.9 277.6 %all-reduce.6.cloned.1.call-done = (f32[2,192,576]{2,1,0:T(8,128)}, f32[2,192,192]{2,1,0:T(8,128)}, f32[2,192,768]{2,1,0:T(8,128)}, f32[2,768,192]{1,2,0:T(8,128)}) async-done(((f32[2,192,576]{2,1,0:T(8,128)}, f32[2,192,192]{2,1,0:T(8,128)}, f32[2,192,768]{2,1,0:T(8,128)}, f32[2,768,192]{1,2,0:T(8,128)}), (f32[2,192,576]{2,1,0:T(8,128)}, f32[2,192,192]{2,1,0:T(8,128)}, f32[2,192,768]{2,1,0:T(8,128)}, ...) | async-done | bytes 3538960 | tf_op jit(solution)/shard_map/psum | solution.py:345
  591.5 2.3 copy.421
  (350 shorter events, 78.5 us)
Async XLA Ops:
  7.2 11.1 %copy-start.7 = (bf16[4,6,12,192]{3,0,2,1:T(4,128)(2,1)S(1)}, bf16[4,6,12,192]{3,0,2,1:T(4,128)(2,1)}, u32[]{:S(2)}) copy-start(bf16[4,6,12,192]{3,0,2,1:T(4,128)(2,1)} %param.10) | copy-start | bytes 331780
  7.2 12.2 %copy-start.61 = (bf16[2,1,2,6,3312]{4,2,3,1,0:T(2,128)(2,1)S(1)}, bf16[2,1,2,6,3312]{4,2,3,1,0:T(2,128)(2,1)}, u32[]{:S(2)}) copy-start(bf16[2,1,2,6,3312]{4,2,3,1,0:T(2,128)(2,1)} %param.19) | copy-start | bytes 476932
  7.2 305.0 %all-reduce.4.cloned.1.call-start = ((), (), s32[]{:S(2)}) async-start(), calls=%async_computation | async-start | bytes 319488 | tf_op jit(solution)/shard_map/psum | solution.py:346
  8.3 12.1 %copy-start.48 = (bf16[2,192,576]{2,1,0:T(8,128)(2,1)S(1)}, bf16[2,192,576]{2,1,0:T(8,128)(2,1)}, u32[]{:S(2)}) copy-start(bf16[2,192,576]{2,1,0:T(8,128)(2,1)} %param.15) | copy-start | bytes 1327108
  10.2 62.0 %collective-permute-start.4 = (bf16[4,3,12,192]{3,0,2,1:T(4,128)(2,1)}, bf16[4,3,12,192]{3,0,2,1:T(4,128)(2,1)}, u32[]{:S(2)}, u32[]{:S(2)}) collective-permute-start(bf16[4,3,12,192]{3,0,2,1:T(4,128)(2,1)} %get-tuple-element.87), channel_id=1, source_target_pairs={{0,15},{1,0},{2,1},{3,2},{4,3},{5,4},{6,5},{7,6},{8,7},{9,8},{10,9... | collective-permute-start | bytes 165896 | tf_op jit(solution)/shard_map/ppermute | solution.py:25
  16.2 6.9 %copy-start.82 = (s32[2]{0:T(128)}, s32[2]{0:T(128)S(1)}, u32[]{:S(2)}) copy-start(s32[2]{0:T(128)S(1)} %fusion.99) | copy-start | bytes 28
  45.2 17.6 %copy-start.72 = (s32[4,6,12]{2,0,1:T(4,128)S(1)}, s32[4,6,12]{2,0,1:T(4,128)}, u32[]{:S(2)}) copy-start(s32[4,6,12]{2,0,1:T(4,128)} %param.12) | copy-start | bytes 3460
  45.2 17.7 %copy-start.53 = (bf16[1,1,2,6,3312]{4,2,3,1,0:T(2,128)(2,1)S(1)}, bf16[1,1,2,6,3312]{4,2,3,1,0:T(2,128)(2,1)}, u32[]{:S(2)}) copy-start(bf16[1,1,2,6,3312]{4,2,3,1,0:T(2,128)(2,1)} %get-tuple-element.96) | copy-start | bytes 238468
  45.2 17.9 %copy-start.83 = (s32[2]{0:T(128)S(1)}, s32[2]{0:T(128)}, u32[]{:S(2)}) copy-start(s32[2]{0:T(128)} %copy-done.82) | copy-start | bytes 28
  45.7 19.0 %copy-start = (pred[1728,276]{1,0:T(32,128)(4,1)S(1)}, pred[1728,276]{1,0:T(32,128)(4,1)}, u32[]{:S(2)}) copy-start(pred[1728,276]{1,0:T(32,128)(4,1)} %and.135) | copy-start | bytes 1430788
  45.7 35.4 %collective-permute-start = (bf16[4,3,12,192]{3,2,1,0:T(8,128)(2,1)S(1)}, bf16[4,3,12,192]{3,2,1,0:T(8,128)(2,1)S(1)}, u32[]{:S(2)}, u32[]{:S(2)}) collective-permute-start(bf16[4,3,12,192]{3,2,1,0:T(8,128)(2,1)S(1)} %get-tuple-element.95), channel_id=1, source_target_pairs={{0,15},{1,0},{2,1},{3,2},{4,3},{5,4},{6,5},{7,6},{8,7},{9,8},{10,9... | collective-permute-start | bytes 165896 | tf_op jit(solution)/shard_map/ppermute | solution.py:25
  72.2 14.3 %copy-start.75 = (f32[1,1,192]{2,1,0:T(1,128)S(1)}, f32[1,1,192]{2,1,0:T(1,128)}, u32[]{:S(2)}) copy-start(f32[1,1,192]{2,1,0:T(1,128)} %get-tuple-element.103) | copy-start | bytes 2308
  73.1 9.4 %collective-permute-start.5 = (bf16[4,6,6,192]{3,0,2,1:T(4,128)(2,1)S(1)}, bf16[4,6,6,192]{3,0,2,1:T(4,128)(2,1)S(1)}, u32[]{:S(2)}, u32[]{:S(2)}) collective-permute-start(bf16[4,6,6,192]{3,0,2,1:T(4,128)(2,1)S(1)} %get-tuple-element.99), channel_id=1, source_target_pairs={{0,240},{16,0},{32,16},{48,32},{64,48},{80,64},{96,80},{112,96},{1... | collective-permute-start | bytes 165896 | tf_op jit(solution)/shard_map/ppermute | solution.py:25
  81.2 3.5 collective-permute-start.1
  95.5 3.9 copy-start.63
  95.5 17.7 %copy-start.4 = (f32[2,6,144,144]{2,3,1,0:T(8,128)}, f32[2,6,144,144]{2,3,1,0:T(8,128)S(1)}, u32[]{:S(2)}) copy-start(f32[2,6,144,144]{2,3,1,0:T(8,128)S(1)} %get-tuple-element.111) | copy-start | bytes 2985988
  95.5 6.8 %copy-start.33 = (bf16[2,192,192]{2,1,0:T(8,128)(2,1)S(1)}, bf16[2,192,192]{2,1,0:T(8,128)(2,1)}, u32[]{:S(2)}) copy-start(bf16[2,192,192]{2,1,0:T(8,128)(2,1)} %param.16) | copy-start | bytes 442372
  99.4 3.5 copy-start.71
  126.7 13.7 %collective-permute-start.6 = (bf16[4,6,6,192]{3,2,1,0:T(8,128)(2,1)S(1)}, bf16[4,6,6,192]{3,2,1,0:T(8,128)(2,1)S(1)}, u32[]{:S(2)}, u32[]{:S(2)}) collective-permute-start(bf16[4,6,6,192]{3,2,1,0:T(8,128)(2,1)S(1)} %get-tuple-element.89), channel_id=1, source_target_pairs={{0,16},{16,32},{32,48},{48,64},{64,80},{80,96},{96,112},{112,128},... | collective-permute-start | bytes 165896 | tf_op jit(solution)/shard_map/ppermute | solution.py:25
  140.3 4.9 copy-start.29
  140.3 4.9 copy-start.46
  140.5 3.2 collective-permute-start.7
  145.7 3.5 copy-start.34
  174.0 417.5 %all-reduce.6.cloned.1.call-start = ((), (), s32[]{:S(2)}) async-start(), calls=%async_computation.1 | async-start | bytes 7471104 | tf_op jit(solution)/shard_map/psum | solution.py:345
  178.5 11.2 %copy-start.79 = (f32[192]{0:T(256)S(1)}, f32[192]{0:T(256)}, u32[]{:S(2)}) copy-start(f32[192]{0:T(256)} %get-tuple-element.70) | copy-start | bytes 2308
  178.5 11.2 %copy-start.80 = (f32[192]{0:T(256)S(1)}, f32[192]{0:T(256)}, u32[]{:S(2)}) copy-start(f32[192]{0:T(256)} %get-tuple-element.68) | copy-start | bytes 2308
  178.5 16.7 %copy-start.6 = (f32[288,192]{1,0:T(8,128)S(1)}, f32[288,192]{1,0:T(8,128)}, u32[]{:S(2)}) copy-start(f32[288,192]{1,0:T(8,128)} %reshape.533) | copy-start | bytes 663556
  178.5 16.7 %copy-start.49 = (bf16[2,192,576]{2,1,0:T(8,128)(2,1)S(1)}, bf16[2,192,576]{2,1,0:T(8,128)(2,1)}, u32[]{:S(2)}) copy-start(bf16[2,192,576]{2,1,0:T(8,128)(2,1)} %param.15) | copy-start | bytes 1327108
  178.5 16.7 %copy-start.74 = (f32[1,1,192]{2,1,0:T(1,128)S(1)}, f32[1,1,192]{2,1,0:T(1,128)}, u32[]{:S(2)}) copy-start(f32[1,1,192]{2,1,0:T(1,128)} %copy-done.73) | copy-start | bytes 2308
  179.4 16.3 %copy-start.13 = (bf16[288,192]{1,0:T(8,128)(2,1)S(1)}, bf16[288,192]{1,0:T(8,128)(2,1)}, u32[]{:S(2)}) copy-start(bf16[288,192]{1,0:T(8,128)(2,1)} %copy-done.12) | copy-start | bytes 331780
  179.4 7.6 %collective-permute-start.2 = (bf16[4,6,6,192]{3,2,1,0:T(8,128)(2,1)S(1)}, bf16[4,6,6,192]{3,2,1,0:T(8,128)(2,1)S(1)}, u32[]{:S(2)}, u32[]{:S(2)}) collective-permute-start(bf16[4,6,6,192]{3,2,1,0:T(8,128)(2,1)S(1)} %get-tuple-element.91), channel_id=1, source_target_pairs={{0,16},{16,32},{32,48},{48,64},{64,80},{80,96},{96,112},{112,128},... | collective-permute-start | bytes 165896 | tf_op jit(solution)/shard_map/ppermute | solution.py:25
  187.1 7.2 %collective-permute-start.3 = (bf16[4,3,12,192]{3,2,1,0:T(8,128)(2,1)S(1)}, bf16[4,3,12,192]{3,2,1,0:T(8,128)(2,1)S(1)}, u32[]{:S(2)}, u32[]{:S(2)}) collective-permute-start(bf16[4,3,12,192]{3,2,1,0:T(8,128)(2,1)S(1)} %fusion.85), channel_id=1, source_target_pairs={{0,1},{1,2},{2,3},{3,4},{4,5},{5,6},{6,7},{7,8},{8,9},{9,10},{10,1... | collective-permute-start | bytes 165896 | tf_op jit(solution)/shard_map/ppermute | solution.py:25
  (64 other events, 115.8 us)
Sparse Core Ops, SparseCore 0:
  174.1 137.9 all-reduce.3
  319.8 271.7 all-reduce.5
where the time goes:
time: 615 us; the launch traced here: 604 us
  waiting for transfers between devices  331 us (54%)
  blocking collectives  76.7 us (12%)
  matrix products  65.3 us (11%)
  local copies, waits for them, and re-layouts  58.3 us (9%)
  starting transfers between devices  32.5 us (5%)
  other arithmetic  23.7 us (4%)
  between operations  15.8 us (3%)
    psum x1, waiting for transfers between devices, per_device(): lax.psum((stacked[0], stacked[1], stacked[2], stacked[3], stacked[4]), ('...  278 us
    psum x1, blocking collectives, per_device(): lax.psum((stacked[0], stacked[1], stacked[2], stacked[3], stacked[4]), ('...  76.7 us
    psum x1, waiting for transfers between devices, per_device(): lax.psum(tables_grad.astype(jnp.bfloat16), 'lon').astype(jnp.float32)  38.7 us
    ppermute x8, starting transfers between devices, from_behind(): return lax.ppermute(value, axis, pairs)  32.5 us
    dot_general x2, matrix products, collect_bias(): jnp.dot(flat, pair_table(jnp.float32), precision=lax.Precision.HIGHEST, p...  23.3 us
    ppermute x8, waiting for transfers between devices, from_behind(): return lax.ppermute(value, axis, pairs)  15.1 us
  transfers between devices with their start and end apart: 10, of which 7 were waited for; matrix products, arithmetic and copies ran while one was open for 11% of the time, Pallas kernels for 0%

commit v1 on v0

v1 whole, which is shorter than its diff:
```python
import functools
import math

import jax
import jax.numpy as jnp
import numpy as np
from jax import lax
from jax.experimental import pallas as pl
from jax.experimental.pallas import tpu as pltpu
from jax.sharding import PartitionSpec as P

C = 192
HEADS = 6
HEAD = 32
FFN = 768
WIN_Z = 2
WIN_LAT = 6
WIN_LON = 12
WIN = 144
TOKENS = 2 * WIN
QUAD = 72
RELPOS = 3312
SPAN = 2 * WIN_LON - 1
ROWS = 3584
GAIN_ROWS = 3456
TABLE_ROWS = 320

EPSILON = 1e-05
NEGATIVE = -1000000000.0
SCALE = 1.0 / math.sqrt(HEAD)

F32 = jnp.float32
BF16 = jnp.bfloat16


def quadrant_rows():
    rows = np.zeros(TOKENS, np.int64)
    at = 0
    for lat_half in range(2):
        for lon_half in range(2):
            for level in range(4):
                for row in range(3):
                    for col in range(6):
                        rows[at] = (level * 6 + lat_half * 3 + row) * 12 + lon_half * 6 + col
                        at += 1
    return rows


def rolled_rows():
    rows = quadrant_rows()
    level, rest = rows // 72, rows % 72
    return ((level + 3) % 4) * 72 + rest


def one_hot(rows):
    picked = np.zeros((TOKENS, TOKENS), np.float32)
    picked[np.arange(TOKENS), rows] = 1.0
    return picked


def pair_keys():
    keys = np.full((512, 256), -1.0, np.float32)
    for level in range(2):
        for row in range(6):
            for offset in range(SPAN):
                for col in range(12):
                    key = col + 11 - offset
                    if 0 <= key < 12:
                        keys[level * 256 + row // 3 * 128 + row % 3 * SPAN + offset, level * 72 + row * 12 + col] = key
    return keys


def mm(left, right):
    return lax.dot_general(left, right, (((1,), (0,)), ((), ())), preferred_element_type=F32)


def mm_nt(left, right):
    return lax.dot_general(left, right, (((1,), (1,)), ((), ())), preferred_element_type=F32)


def eye(size):
    return (
        lax.broadcasted_iota(jnp.int32, (size, size), 0) == lax.broadcasted_iota(jnp.int32, (size, size), 1)
    ).astype(F32).astype(BF16)


def turned(value):
    return mm_nt(eye(value.shape[1]), value).astype(BF16)


def norm_stats(values):
    centre = values - jnp.mean(values, axis=-1, keepdims=True)
    inverse = lax.rsqrt(jnp.mean(centre * centre, axis=-1, keepdims=True) + EPSILON)
    return centre * inverse, inverse


def norm_backward(upstream, normal_hat, inverse):
    upstream_mean = jnp.mean(upstream, axis=-1, keepdims=True)
    cross_mean = jnp.mean(upstream * normal_hat, axis=-1, keepdims=True)
    return inverse * (upstream - upstream_mean - normal_hat * cross_mean)


def head_lanes(head):
    lane = lax.broadcasted_iota(jnp.int32, (1, C), 1)
    return (lane >= head * HEAD) & (lane < (head + 1) * HEAD)


def make_pairs(keys_ref, pairs_ref):
    keys = keys_ref[...]
    for col in range(WIN_LON):
        pairs_ref[col] = jnp.where(keys == float(col), 1.0, 0.0).astype(BF16)


def table_start(zs, zt, hs, ht):
    return (((zs * 2 + zt) * 6 + hs) * 6 + ht) * SPAN


def spread_bias(table_ref, pairs_ref, row_ref, shaped_ref, bias_ref):
    for head in range(HEADS):
        row_ref[head * 2 : head * 2 + 2, :RELPOS] = table_ref[head].astype(F32)
    row = row_ref[: 2 * HEADS]
    for zs in range(2):
        for zt in range(2):
            for group in range(2):
                for ht in range(6):
                    pieces = []
                    for hs in range(group * 3, group * 3 + 3):
                        start = table_start(zs, zt, hs, ht)
                        pieces.append(row[:, start : start + SPAN])
                    pieces.append(jnp.zeros((2 * HEADS, 128 - 3 * SPAN), F32))
                    target = pl.ds(zt * 6 + ht, 2 * HEADS, stride=12)
                    shaped_ref[zs * 2 + group, target, :] = jnp.concatenate(pieces, axis=1)
    shaped = jnp.concatenate([shaped_ref[part, :WIN].astype(BF16) for part in range(4)], axis=1)
    for col in range(WIN_LON):
        spread = mm(shaped, pairs_ref[col])
        bias_ref[0, pl.ds(col, WIN, stride=12), :] = spread[:, :128]
        bias_ref[1, pl.ds(col, WIN, stride=12), :] = spread[:, 128:]


def collect_bias(grads_ref, pairs_ref, levels, row_ref, shaped_ref, out_ref):
    for window in range(2):
        total = jnp.zeros((72, 512), F32)
        for col in range(WIN_LON):
            left = grads_ref[window, 0, pl.ds(col, 72, stride=12), :]
            right = grads_ref[window, 1, pl.ds(col, 72, stride=12), :]
            piece = jnp.concatenate([left, right], axis=1).astype(BF16)
            total = total + mm_nt(piece, pairs_ref[col])
        for part in range(4):
            shaped_ref[part, window * 72 : (window + 1) * 72] = total[:, part * 128 : (part + 1) * 128]
    row_ref[...] = jnp.zeros_like(row_ref)
    for zs in range(2):
        for zt in range(2):
            for group in range(2):
                for ht in range(6):
                    pieces = [
                        shaped_ref[zs * 2 + group, pl.ds(window * 72 + zt * 6 + ht, HEADS, stride=12), :]
                        for window in range(2)
                    ]
                    for level in range(2):
                        chosen = jnp.zeros((HEADS, 128), F32)
                        for window in range(2):
                            chosen = chosen + jnp.where(levels[window] == level, pieces[window], 0.0)
                        for index in range(3):
                            start = table_start(zs, zt, group * 3 + index, ht)
                            row_ref[level * 8 : level * 8 + HEADS, start : start + SPAN] = chosen[
                                :, index * SPAN : (index + 1) * SPAN
                            ]
    for slab in range(26):
        lanes = slice(slab * 128, (slab + 1) * 128)
        rows = jnp.concatenate([row_ref[:HEADS, lanes], row_ref[8 : 8 + HEADS, lanes]], axis=0)
        shaped_ref[slab // 13, slab % 13 * 12 : slab % 13 * 12 + 12] = rows
    out_ref[...] = jnp.concatenate(
        [shaped_ref[0, :156], shaped_ref[1, :156], jnp.zeros((TABLE_ROWS - 312, 128), F32)], axis=0
    ).astype(BF16)


def load_tiles(bias_ref, level, head):
    rows = pl.ds(pl.multiple_of((head * 2 + level) * WIN, 8), WIN)
    return jnp.concatenate([bias_ref[0, rows, :], bias_ref[1, rows, : WIN - 128]], axis=1)


def attention(normed, in_weight, bias_ref, levels, same_region, weights_ref):
    eye_c = eye(C)
    weight_q, weight_k, weight_v = in_weight[:, :C], in_weight[:, C : 2 * C], in_weight[:, 2 * C :]
    kept = []
    mixed = []
    for window in range(2):
        rows = normed[window * WIN : (window + 1) * WIN]
        keys = mm(rows, weight_k).astype(BF16)
        values = mm(rows, weight_v).astype(BF16)
        queries = mm(rows, weight_q).astype(BF16)
        queries_t = mm_nt(eye_c, queries).astype(BF16)
        keys_t = mm_nt(eye_c, keys).astype(BF16)
        values_t = mm_nt(eye_c, values).astype(BF16)
        parts = []
        for head in range(HEADS):
            own = jnp.where(head_lanes(head), keys.astype(F32), 0.0).astype(BF16)
            scores = mm(own, queries_t) * SCALE + load_tiles(bias_ref, levels[window], head)
            if same_region is not None:
                scores = jnp.where(same_region[window], scores, NEGATIVE)
            weights = jnp.exp(scores - jnp.max(scores, axis=0, keepdims=True))
            weights = weights * (1.0 / jnp.sum(weights, axis=0, keepdims=True))
            weights = weights.astype(BF16)
            weights_ref[window * HEADS + head] = weights
            parts.append(mm(values_t[head * HEAD : (head + 1) * HEAD], weights))
        mixed.append(jnp.concatenate(parts, axis=0).astype(BF16))
        kept.append((queries_t, keys_t, values))
    return kept, mixed


def feed_forward(hidden, gain, up_weight):
    hat, inverse = norm_stats(hidden)
    normed = (hat * gain).astype(BF16)
    return hat, inverse, normed, mm(normed, up_weight)


def gelu_parts(expanded):
    cumulative = 0.5 * (1.0 + lax.erf(expanded * (1.0 / math.sqrt(2.0))))
    slope = cumulative + expanded * jnp.exp(-0.5 * expanded * expanded) * (1.0 / math.sqrt(2.0 * math.pi))
    return (expanded * cumulative).astype(BF16), slope


def natural_mixed(mixed):
    eye_w = eye(WIN)
    return jnp.concatenate([mm_nt(eye_w, part) for part in mixed], axis=0).astype(BF16)


def pack(packed_ref, start, value):
    height = value.shape[0]
    for part in range(value.shape[1] // 128):
        rows = slice(start + part * height, start + (part + 1) * height)
        packed_ref[rows] = value[:, part * 128 : (part + 1) * 128].astype(BF16)


def backward(
    grad,
    active,
    slope,
    second_hat,
    second_inverse,
    second_norm,
    mixed,
    attended,
    weights_ref,
    first_hat,
    first_inverse,
    first_norm,
    gain_one,
    gain_two,
    in_weight,
    out_weight,
    up_weight,
    down_weight,
    grads_ref,
    packed_ref,
):
    eye_c = eye(C)
    grad_half = grad.astype(BF16)
    pack(packed_ref, 2304, mm(turned(grad_half), active))
    grad_expanded = (mm(grad_half, down_weight) * slope).astype(BF16)
    normed_t = turned(second_norm)
    pack(packed_ref, 1152, mm(normed_t, grad_expanded))
    grad_second = mm_nt(grad_expanded, up_weight)
    gain_two_grad = jnp.sum(grad_second * second_hat, axis=0, keepdims=True)
    grad_hidden = (grad + norm_backward(grad_second * gain_two, second_hat, second_inverse)).astype(BF16)
    grad_out = mm(mixed[0], grad_hidden[:WIN]) + mm(mixed[1], grad_hidden[WIN:])
    packed_ref[960:1152] = grad_out[:, :128].astype(BF16)
    grad_mixed = mm_nt(grad_hidden, out_weight).astype(BF16)
    projected = []
    for window in range(2):
        queries_t, keys_t, values = attended[window]
        upstream_t = mm_nt(eye_c, grad_mixed[window * WIN : (window + 1) * WIN]).astype(BF16)
        grad_q, grad_k, grad_v = [], [], []
        for head in range(HEADS):
            lanes = slice(head * HEAD, (head + 1) * HEAD)
            half = weights_ref[window * HEADS + head]
            weights = half.astype(F32)
            own = jnp.where(head_lanes(head), values.astype(F32), 0.0).astype(BF16)
            grad_weights = mm(own, upstream_t)
            inner = jnp.sum(grad_weights * weights, axis=0, keepdims=True)
            grad_scores = weights * (grad_weights - inner)
            rows = slice(head * WIN, (head + 1) * WIN)
            grads_ref[window, 0, rows, :] = grad_scores[:, :128]
            grads_ref[window, 1, rows, :] = jnp.concatenate(
                [grad_scores[:, 128:], jnp.zeros((WIN, 256 - WIN), F32)], axis=1
            )
            scaled = (grad_scores * SCALE).astype(BF16)
            grad_v.append(mm_nt(upstream_t[lanes], half))
            grad_q.append(mm(keys_t[lanes], scaled))
            grad_k.append(mm_nt(queries_t[lanes], scaled))
        projected_t = jnp.concatenate(grad_q + grad_k + grad_v, axis=0).astype(BF16)
        projected.append(mm_nt(eye(WIN), projected_t))
    projected = jnp.concatenate(projected, axis=0).astype(BF16)
    first_t = turned(first_norm)
    grad_in = mm(first_t, projected)
    pack(packed_ref, 0, grad_in[:, :512])
    packed_ref[768:960] = jnp.concatenate([grad_in[:, 512:], grad_out[:, 128:]], axis=1).astype(BF16)
    grad_first = mm_nt(projected, in_weight)
    gain_one_grad = jnp.sum(grad_first * first_hat, axis=0, keepdims=True)
    gain_rows = jnp.concatenate(
        [
            gain_one_grad[:, :128],
            jnp.concatenate([gain_one_grad[:, 128:], gain_two_grad[:, 128:]], axis=1),
            gain_two_grad[:, :128],
            jnp.zeros((ROWS - GAIN_ROWS - 3, 128), F32),
        ],
        axis=0,
    )
    packed_ref[GAIN_ROWS:ROWS] = gain_rows.astype(BF16)
    return (
        grad_hidden.astype(F32) + norm_backward(grad_first * gain_one, first_hat, first_inverse)
    ).astype(BF16)


def load_grid(grid_ref, rows_ref):
    for row in range(6):
        for col in range(12):
            piece = grid_ref[row, col].astype(F32)
            target = pl.ds(row * 12 + col, 4, stride=72)
            rows_ref[0, target, :] = piece[:, :128]
            rows_ref[1, target, :] = jnp.concatenate([piece[:, 128:], jnp.zeros((4, 64), F32)], axis=1)
    return jnp.concatenate([rows_ref[0], rows_ref[1][:, :64]], axis=1)


def store_grid(rows, rows_ref, grid_ref):
    rows_ref[0] = rows[:, :128]
    rows_ref[1] = jnp.concatenate([rows[:, 128:], jnp.zeros((TOKENS, 64), F32)], axis=1)
    for row in range(6):
        for col in range(12):
            source = pl.ds(row * 12 + col, 4, stride=72)
            piece = jnp.concatenate([rows_ref[0, source, :], rows_ref[1, source, :][:, :64]], axis=1)
            grid_ref[row, col] = piece.astype(BF16)


def first_kernel(
    levels_ref,
    inputs_ref,
    grad_ref,
    gains_ref,
    in_ref,
    out_ref,
    up_ref,
    down_ref,
    table_ref,
    keys_ref,
    order_ref,
    quad_0,
    quad_1,
    quad_2,
    quad_3,
    weights_out,
    qkt_out,
    values_out,
    mixed_out,
    hidden_out,
    rows_ref,
    pairs_ref,
    row_ref,
    shaped_ref,
    bias_ref,
):
    levels = [levels_ref[0, 0], levels_ref[0, 1]]
    order = order_ref[...]
    grad_quads = mm(order, load_grid(grad_ref, rows_ref).astype(BF16))
    flat = load_grid(inputs_ref, rows_ref)
    make_pairs(keys_ref, pairs_ref)
    spread_bias(table_ref, pairs_ref, row_ref, shaped_ref, bias_ref)
    hat, _ = norm_stats(flat)
    normed = (hat * gains_ref[0:1]).astype(BF16)
    attended, mixed = attention(normed, in_ref[...], bias_ref, levels, None, weights_out)
    for window in range(2):
        qkt_out[window, 0] = attended[window][0]
        qkt_out[window, 1] = attended[window][1]
        values_out[window] = attended[window][2]
        mixed_out[window] = mixed[window]
    hidden = (flat + mm(natural_mixed(mixed), out_ref[...])).astype(BF16)
    hidden_out[...] = hidden
    hidden = hidden.astype(F32)
    _, _, _, expanded = feed_forward(hidden, gains_ref[1:2], up_ref[...])
    active = (expanded * 0.5 * (1.0 + lax.erf(expanded * (1.0 / math.sqrt(2.0))))).astype(BF16)
    result = (hidden + mm_nt(active, down_ref[...])).astype(BF16)
    result_quads = mm(order, result)
    for index, quad in enumerate((quad_0, quad_1, quad_2, quad_3)):
        rows = slice(index * QUAD, (index + 1) * QUAD)
        quad[...] = jnp.concatenate([result_quads[rows], grad_quads[rows]], axis=0).astype(BF16)


def second_kernel(
    levels_ref,
    quad_0,
    quad_1,
    quad_2,
    quad_3,
    region_col_ref,
    region_row_ref,
    gains_ref,
    in_ref,
    out_ref,
    up_ref,
    down_ref,
    table_ref,
    keys_ref,
    ahead_ref,
    back_ref,
    back_0,
    back_1,
    back_2,
    back_3,
    packed_ref,
    tables_out,
    pairs_ref,
    row_ref,
    shaped_ref,
    bias_ref,
    weights_ref,
    grads_ref,
):
    levels = [levels_ref[0, 0], levels_ref[0, 1]]
    quads = [quad[...].astype(F32) for quad in (quad_0, quad_1, quad_2, quad_3)]
    ahead = ahead_ref[...]
    flat = mm(ahead, jnp.concatenate([quad[:QUAD] for quad in quads], axis=0).astype(BF16))
    grad = mm(ahead, jnp.concatenate([quad[QUAD:] for quad in quads], axis=0).astype(BF16))
    make_pairs(keys_ref, pairs_ref)
    spread_bias(table_ref, pairs_ref, row_ref, shaped_ref, bias_ref)
    same = [region_col_ref[window] == region_row_ref[window] for window in range(2)]
    first_hat, first_inverse = norm_stats(flat)
    gain_one, gain_two = gains_ref[0:1], gains_ref[1:2]
    first_norm = (first_hat * gain_one).astype(BF16)
    in_weight, out_weight, up_weight, down_weight = in_ref[...], out_ref[...], up_ref[...], down_ref[...]
    attended, mixed = attention(first_norm, in_weight, bias_ref, levels, same, weights_ref)
    hidden = (flat + mm(natural_mixed(mixed), out_weight)).astype(BF16).astype(F32)
    second_hat, second_inverse, second_norm, expanded = feed_forward(hidden, gain_two, up_weight)
    active, slope = gelu_parts(expanded)
    result = (hidden + mm_nt(active, down_weight)).astype(BF16)
    grad_in = backward(
        grad, active, slope, second_hat, second_inverse, second_norm, mixed, attended, weights_ref,
        first_hat, first_inverse, first_norm, gain_one, gain_two, in_weight, out_weight, up_weight,
        down_weight, grads_ref, packed_ref,
    )
    back = back_ref[...]
    result_quads, grad_quads = mm(back, result), mm(back, grad_in)
    for index, quad in enumerate((back_0, back_1, back_2, back_3)):
        rows = slice(index * QUAD, (index + 1) * QUAD)
        quad[...] = jnp.concatenate([result_quads[rows], grad_quads[rows]], axis=0).astype(BF16)
    collect_bias(grads_ref, pairs_ref, levels, row_ref, shaped_ref, tables_out)


def third_kernel(
    levels_ref,
    quad_0,
    quad_1,
    quad_2,
    quad_3,
    inputs_ref,
    weights_ref,
    qkt_ref,
    values_ref,
    mixed_ref,
    hidden_ref,
    gains_ref,
    in_ref,
    out_ref,
    up_ref,
    down_ref,
    keys_ref,
    natural_ref,
    second_packed_ref,
    blocks_out,
    grad_out,
    packed_ref,
    tables_out,
    rows_ref,
    pairs_ref,
    row_ref,
    shaped_ref,
    grads_ref,
):
    levels = [levels_ref[0, 0], levels_ref[0, 1]]
    quads = [quad[...].astype(F32) for quad in (quad_0, quad_1, quad_2, quad_3)]
    natural = natural_ref[...]
    blocks = mm(natural, jnp.concatenate([quad[:QUAD] for quad in quads], axis=0).astype(BF16))
    store_grid(blocks, rows_ref, blocks_out)
    grad = mm(natural, jnp.concatenate([quad[QUAD:] for quad in quads], axis=0).astype(BF16))
    flat = load_grid(inputs_ref, rows_ref)
    first_hat, first_inverse = norm_stats(flat)
    gain_one, gain_two = gains_ref[0:1], gains_ref[1:2]
    first_norm = (first_hat * gain_one).astype(BF16)
    in_weight, out_weight, up_weight, down_weight = in_ref[...], out_ref[...], up_ref[...], down_ref[...]
    hidden = hidden_ref[...].astype(F32)
    second_hat, second_inverse, second_norm, expanded = feed_forward(hidden, gain_two, up_weight)
    active, slope = gelu_parts(expanded)
    attended = [(qkt_ref[window, 0], qkt_ref[window, 1], values_ref[window]) for window in range(2)]
    mixed = [mixed_ref[0], mixed_ref[1]]
    grad_in = backward(
        grad, active, slope, second_hat, second_inverse, second_norm, mixed, attended, weights_ref,
        first_hat, first_inverse, first_norm, gain_one, gain_two, in_weight, out_weight, up_weight,
        down_weight, grads_ref, packed_ref,
    )
    store_grid(grad_in.astype(F32), rows_ref, grad_out)
    make_pairs(keys_ref, pairs_ref)
    collect_bias(grads_ref, pairs_ref, levels, row_ref, shaped_ref, tables_out)


def whole(*shape):
    return pl.BlockSpec(shape, lambda *_: (0,) * len(shape))


def of_block(block, *shape):
    return pl.BlockSpec((None,) + shape, lambda *_: (block,) + (0,) * len(shape))


def weight_specs(block):
    return [
        of_block(block, 2, C),
        of_block(block, C, 3 * C),
        of_block(block, C, C),
        of_block(block, C, FFN),
        of_block(block, C, FFN),
    ]


def table_spec(block):
    return pl.BlockSpec((None, None, HEADS, 2, RELPOS), lambda *_: (block, 0, 0, 0, 0))


SMEM_WHOLE = pl.BlockSpec(memory_space=pltpu.SMEM)
VMEM_LIMIT = 56 * 1024 * 1024


def call(kernel, in_specs, out_specs, out_shapes, scratch, operands, flops, aliases=None):
    return pl.pallas_call(
        kernel,
        grid=(1,),
        in_specs=in_specs,
        out_specs=out_specs,
        out_shape=out_shapes,
        scratch_shapes=scratch,
        input_output_aliases=aliases or {},
        compiler_params=pltpu.CompilerParams(vmem_limit_bytes=VMEM_LIMIT),
        cost_estimate=pl.CostEstimate(flops=flops, bytes_accessed=4_000_000, transcendentals=1_000_000),
    )(*operands)


def shape_of(shape, dtype):
    return jax.ShapeDtypeStruct(shape, dtype)


def shifted(value, lat_steps, lon_steps):
    lon_count, lat_count = lax.axis_size("lon"), lax.axis_size("lat")
    pairs = []
    for lon in range(lon_count):
        for lat in range(lat_count):
            source = ((lon + lon_steps) % lon_count) * lat_count + (lat + lat_steps) % lat_count
            pairs.append((source, lon * lat_count + lat))
    return lax.ppermute(value, ("lon", "lat"), pairs)


def per_device(
    inputs,
    grad_out,
    region,
    bias_level,
    norm_gains,
    in_weight,
    out_weight,
    up_weight,
    down_weight,
    bias_tables,
):
    weights = (norm_gains, in_weight, out_weight, up_weight, down_weight.transpose(0, 2, 1))
    inputs, grad_out = inputs.transpose(1, 2, 0, 3), grad_out.transpose(1, 2, 0, 3)
    bias_tables = bias_tables.transpose(0, 1, 3, 2, 4)
    bias_level = bias_level.T
    quadrant = one_hot(quadrant_rows())
    rolled = one_hot(rolled_rows())
    keys = jnp.asarray(pair_keys())
    half = [jnp.asarray(array, BF16) for array in (quadrant, quadrant.T, rolled, rolled.T)]
    to_quads, from_quads, rolled_back, rolled_ahead = half
    grid_spec = whole(6, 12, 4, C)
    square = whole(TOKENS, TOKENS)
    keys_spec = whole(512, 256)
    quad_shape = shape_of((2 * QUAD, C), BF16)
    quad_spec = whole(2 * QUAD, C)
    grid_shape = shape_of((6, 12, 4, C), BF16)
    pairs_scratch = pltpu.VMEM((WIN_LON, 512, 256), BF16)
    row_scratch = pltpu.VMEM((16, 26 * 128), F32)
    shaped_scratch = pltpu.VMEM((4, 2 * 72 + 16, 128), F32)
    bias_scratch = pltpu.VMEM((2, 2 * HEADS * WIN, 128), F32)
    rows_scratch = pltpu.VMEM((2, TOKENS, 128), F32)
    grads_scratch = pltpu.VMEM((2, 2, HEADS * WIN, 128), F32)
    stored_shapes = [
        shape_of((2 * HEADS, WIN, WIN), BF16),
        shape_of((2, 2, C, WIN), BF16),
        shape_of((2, WIN, C), BF16),
        shape_of((2, C, WIN), BF16),
        shape_of((TOKENS, C), BF16),
    ]
    stored_specs = [whole(*shape.shape) for shape in stored_shapes]
    packed_shape = shape_of((2, ROWS, 128), BF16)
    table_shape = shape_of((TABLE_ROWS, 128), BF16)
    table_out = whole(TABLE_ROWS, 128)

    quads = call(
        first_kernel,
        [SMEM_WHOLE, grid_spec, grid_spec] + weight_specs(0) + [table_spec(0), keys_spec, square],
        [quad_spec] * 4 + stored_specs,
        [quad_shape] * 4 + stored_shapes,
        [rows_scratch, pairs_scratch, row_scratch, shaped_scratch, bias_scratch],
        (bias_level, inputs, grad_out, *weights, bias_tables, keys, to_quads),
        1_000_000_000,
    )
    stored = quads[4:]
    ahead = (
        quads[3],
        shifted(quads[2], 0, 1),
        shifted(quads[1], 1, 0),
        shifted(quads[0], 1, 1),
    )
    region_col, region_row = region.reshape(2, WIN, 1), region.reshape(2, 1, WIN)
    back = call(
        second_kernel,
        [SMEM_WHOLE] + [quad_spec] * 4 + [whole(2, WIN, 1), whole(2, 1, WIN)] + weight_specs(1)
        + [table_spec(1), keys_spec, square, square],
        [quad_spec] * 4 + [of_block(1, ROWS, 128), table_out],
        [quad_shape] * 4 + [packed_shape, table_shape],
        [pairs_scratch, row_scratch, shaped_scratch, bias_scratch, pltpu.VMEM((2 * HEADS, WIN, WIN), BF16),
         grads_scratch],
        (bias_level, *ahead, region_col, region_row, *weights, bias_tables, keys, rolled_ahead, rolled_back),
        3_000_000_000,
    )
    second_packed, second_tables = back[4:]
    home = (
        shifted(back[3], -1, -1),
        shifted(back[2], -1, 0),
        shifted(back[1], 0, -1),
        back[0],
    )
    blocks_out, grad_inputs, packed, first_tables = call(
        third_kernel,
        [SMEM_WHOLE] + [quad_spec] * 4 + [grid_spec] + stored_specs + weight_specs(0)
        + [keys_spec, square, pl.BlockSpec(memory_space=pl.ANY)],
        [grid_spec, grid_spec, of_block(0, ROWS, 128), table_out],
        [grid_shape, grid_shape, packed_shape, table_shape],
        [rows_scratch, pairs_scratch, row_scratch, shaped_scratch, grads_scratch],
        (bias_level, *home, inputs, *stored, *weights, keys, from_quads, second_packed),
        2_000_000_000,
        {18: 2},
    )
    packed, tables = sum_over_devices(packed.reshape(2 * ROWS, 128), first_tables, second_tables)
    totals = unpack(packed.reshape(2, ROWS, 128), tables.reshape(2, TABLE_ROWS, 128))
    gains, grad_in, grad_out_weight, grad_up, grad_down, grad_tables = totals
    return (
        blocks_out.transpose(2, 0, 1, 3),
        grad_inputs.transpose(2, 0, 1, 3),
        gains,
        grad_in,
        grad_out_weight,
        grad_up,
        grad_down.transpose(0, 2, 1),
        grad_tables.transpose(0, 1, 3, 2, 4),
    )


def exchanged(value, axis, bit):
    count = lax.axis_size(axis)
    return lax.ppermute(value, axis, [(place, place ^ bit) for place in range(count)])


def added(left, right):
    return (left.astype(F32) + right.astype(F32)).astype(BF16)


def upper(axis, bit):
    return (lax.axis_index(axis) & bit) != 0


def halve(value, axis, bit):
    half = value.shape[0] // 2
    up = upper(axis, bit)
    keep = jnp.where(up, value[half:], value[:half])
    send = jnp.where(up, value[:half], value[half:])
    return added(keep, exchanged(send, axis, bit))


def double(value, axis, bit):
    other = exchanged(value, axis, bit)
    up = upper(axis, bit)
    return jnp.concatenate([jnp.where(up, other, value), jnp.where(up, value, other)], axis=0)


def bits(axis):
    count = lax.axis_size(axis)
    return [1 << place for place in range(count.bit_length() - 1)]


def sum_over_devices(packed, first_tables, second_tables):
    for bit in bits("lat"):
        packed = halve(packed, "lat", bit)
    rows = packed.shape[0]
    joined = jnp.concatenate([packed, first_tables, second_tables], axis=0)
    for bit in bits("lon")[:2]:
        joined = halve(joined, "lon", bit)
    for bit in bits("lon")[2:]:
        joined = added(joined, exchanged(joined, "lon", bit))
    for bit in reversed(bits("lon")[:2]):
        joined = double(joined, "lon", bit)
    packed, tables = joined[:rows], joined[rows:]
    for bit in reversed(bits("lat")):
        packed = double(packed, "lat", bit)
    return packed, tables


def unpack_kernel(packed_ref, tables_ref, gains_ref, in_ref, out_ref, up_ref, down_ref, grads_ref, rows_ref):
    rows_ref[...] = tables_ref[...].astype(F32)
    for part in range(4):
        in_ref[:, part * 128 : (part + 1) * 128] = packed_ref[part * C : (part + 1) * C].astype(F32)
    shared = packed_ref[768:960].astype(F32)
    in_ref[:, 512:] = shared[:, :64]
    out_ref[:, :128] = packed_ref[960:1152].astype(F32)
    out_ref[:, 128:] = shared[:, 64:]
    for part in range(6):
        lanes = slice(part * 128, (part + 1) * 128)
        up_ref[:, lanes] = packed_ref[1152 + part * C : 1152 + (part + 1) * C].astype(F32)
        down_ref[:, lanes] = packed_ref[2304 + part * C : 2304 + (part + 1) * C].astype(F32)
    gains = packed_ref[GAIN_ROWS : GAIN_ROWS + 16].astype(F32)
    gains_ref[0:1, :128] = gains[0:1]
    gains_ref[0:1, 128:] = gains[1:2, :64]
    gains_ref[1:2, :128] = gains[2:3]
    gains_ref[1:2, 128:] = gains[1:2, 64:]
    for slab in range(26):
        width = min(128, RELPOS - slab * 128)
        for level in range(2):
            start = slab * 12 + level * HEADS
            grads_ref[:, level, slab * 128 : slab * 128 + width] = rows_ref[start : start + HEADS, :width]


def unpack(packed, tables):
    def block(*shape):
        return pl.BlockSpec((None,) + shape, lambda index: (index,) + (0,) * len(shape))

    return pl.pallas_call(
        unpack_kernel,
        grid=(2,),
        in_specs=[block(ROWS, 128), block(TABLE_ROWS, 128)],
        out_specs=[
            block(2, C),
            block(C, 3 * C),
            block(C, C),
            block(C, FFN),
            block(C, FFN),
            pl.BlockSpec((None, None, HEADS, 2, RELPOS), lambda index: (index, 0, 0, 0, 0)),
        ],
        out_shape=[
            shape_of((2, 2, C), F32),
            shape_of((2, C, 3 * C), F32),
            shape_of((2, C, C), F32),
            shape_of((2, C, FFN), F32),
            shape_of((2, C, FFN), F32),
            shape_of((2, 1, HEADS, 2, RELPOS), F32),
        ],
        scratch_shapes=[pltpu.VMEM((TABLE_ROWS, 128), F32)],
        compiler_params=pltpu.CompilerParams(vmem_limit_bytes=VMEM_LIMIT),
    )(packed, tables)


def solution(mesh):
    placed = (
        P(None, "lat", "lon", None),
        P(None, "lat", "lon", None),
        P(None, "lat", "lon"),
        P(None, "lat"),
        P(),
        P(),
        P(),
        P(),
        P(),
        P(None, "lat", None, None, None),
    )
    return jax.shard_map(
        per_device,
        mesh=mesh,
        in_specs=placed,
        out_specs=(
            P(None, "lat", "lon", None),
            P(None, "lat", "lon", None),
            P(),
            P(),
            P(),
            P(),
            P(),
            P(None, "lat", None, None, None),
        ),
        check_vma=False,
    )
```

time: 615 us -> 160 us (0.26); the launches traced: 604 us -> 160 us
  waiting for transfers between devices: 331 us -> 77.8 us
  blocking collectives: 76.7 us -> 0 us
  matrix products: 65.3 us -> 0 us
  local copies, waits for them, and re-layouts: 58.3 us -> 2.72 us
  Pallas kernels: 0 us -> 35.6 us
  other arithmetic: 23.7 us -> 6.73 us
  between operations: 15.8 us -> 1.14 us
    psum x2 -> x0, waiting for transfers between devices: 316 us -> none  [the longest x1 278 us: per_device(): lax.psum((stacked[0], stacked[1], stacked[2], stacked[3], stacked[4]), ('...]
    psum x1 -> x0, blocking collectives: 76.7 us -> none  [per_device(): lax.psum((stacked[0], stacked[1], stacked[2], stacked[3], stacked[4]), ('...]
    dot_general x44 -> x0, matrix products: 65.3 us -> none  [the longest x2 23.3 us: collect_bias(): jnp.dot(flat, pair_table(jnp.float32), precision=lax.Precision.HIGHEST, p...]
    ppermute x8 -> x20, waiting for transfers between devices: 15.1 us -> 77.8 us  [the longest x14 67.2 us: exchanged(): lax.ppermute(value, axis, [(place, place ^ bit) for place in range(count)])]
    pallas_call x0 -> x4, Pallas kernels: none -> 35.6 us  [the longest x3 32.4 us: call(): pl.pallas_call(kernel, grid=(1,), in_specs=in_specs, out_specs=out_specs,...]
    unnamed x180 -> x21, local copies, waits for them, and re-layouts: 10.9 us -> 1.28 us
    reshape x14 -> x2, local copies, waits for them, and re-layouts: 11.1 us -> 1.43 us  [the longest x1 0.76 us: per_device(): region.reshape(2, WIN, 1)]
    dot_general x6 -> x0, local copies, waits for them, and re-layouts: 6.83 us -> none  [the longest x4 6.45 us: collect_bias(): jnp.dot(flat, pair_table(jnp.float32), precision=lax.Precision.HIGHEST, p...]
  transfers between devices with their start and end apart: 10 -> 20, of which waited for: 7 -> 17; matrix products, arithmetic and copies ran while one was open for 11% -> 1% of each run, Pallas kernels for 0% -> 0%
where the time goes in v1:
time: 160 us
  waiting for transfers between devices  77.8 us (49%)
  starting transfers between devices  35.9 us (22%)
  Pallas kernels  35.6 us (22%)
  other arithmetic  6.73 us (4%)
  local copies, waits for them, and re-layouts  2.72 us (2%)
    ppermute x14, waiting for transfers between devices, exchanged(): lax.ppermute(value, axis, [(place, place ^ bit) for place in range(count)])  67.2 us
    pallas_call x3, Pallas kernels, call(): pl.pallas_call(kernel, grid=(1,), in_specs=in_specs, out_specs=out_specs,...  32.4 us
    ppermute x14, starting transfers between devices, exchanged(): lax.ppermute(value, axis, [(place, place ^ bit) for place in range(count)])  22.2 us
    ppermute x6, starting transfers between devices, shifted(): return lax.ppermute(value, ('lon', 'lat'), pairs)  13.7 us
    ppermute x6, waiting for transfers between devices, shifted(): return lax.ppermute(value, ('lon', 'lat'), pairs)  10.6 us
  transfers between devices with their start and end apart: 20, of which 17 were waited for; matrix products, arithmetic and copies ran while one was open for 1% of the time, Pallas kernels for 0%

profile of v1, /device:TPU:1, one launch (start us, length us, event | category | flops | bytes accessed | tf_op | source)
XLA Modules:
  0.0 159.9 jit_solution(10856323118685577918)
XLA Ops:
  0.6 7.7 %shard_map.206 = (bf16[144,192]{1,0:T(8,128)(2,1)}, bf16[144,192]{1,0:T(8,128)(2,1)}, bf16[144,192]{1,0:T(8,128)(2,1)}, bf16[144,192]{1,0:T(8,128)(2,1)}, bf16[1...) custom-call(s32[1,2]{1,0:T(1,128)} %bitcast.28, ...), custom_call_target="tpu_custom_call" | custom-call | flops 1000000000 | bytes 4000000 | tf_op jit(solution)/shard_map/pallas_call | solution.py:531
  8.3 9.1 %collective-permute-start = (bf16[144,192]{1,0:T(8,128)(2,1)}, bf16[144,192]{1,0:T(8,128)(2,1)S(1)}, u32[]{:S(2)}, u32[]{:S(2)}) collective-permute-start(bf16[144,192]{1,0:T(8,128)(2,1)} %get-tuple-element.34), channel_id=1, source_target_pairs={{16,0},{17,1},{18,2},{19,3},{20,4},{21,5},{22,6},{23,7},{24,8},{25... | collective-permute-start | bytes 165896 | tf_op jit(solution)/shard_map/ppermute | solution.py:555
  17.4 1.0 collective-permute-start.1
  18.4 3.3 %collective-permute-start.2 = (bf16[144,192]{1,0:T(8,128)(2,1)}, bf16[144,192]{1,0:T(8,128)(2,1)S(1)}, u32[]{:S(2)}, u32[]{:S(2)}) collective-permute-start(bf16[144,192]{1,0:T(8,128)(2,1)} %get-tuple-element.36), channel_id=1, source_target_pairs={{17,0},{18,1},{19,2},{20,3},{21,4},{22,5},{23,6},{24,7},{25,8},{26... | collective-permute-start | bytes 165896 | tf_op jit(solution)/shard_map/ppermute | solution.py:555
  22.3 0.8 reshape.42.region_col_ref
  23.1 0.9 collective-permute-done.2.quad_3
  24.6 14.4 %shard_map.207 = (bf16[144,192]{1,0:T(8,128)(2,1)}, bf16[144,192]{1,0:T(8,128)(2,1)}, bf16[144,192]{1,0:T(8,128)(2,1)}, bf16[144,192]{1,0:T(8,128)(2,1)}, bf16[2...) custom-call(s32[1,2]{1,0:T(1,128)} %bitcast.29, bf16[144,192]{1,0:T(8,128)(2,1)} %get-tuple-element.33.quad_0, ...), custom_call_target="tpu_custom_call" | custom-call | flops 3000000000 | bytes 4000000 | tf_op jit(solution)/shard_map/pallas_call | solution.py:531
  39.4 8.6 %collective-permute-done.3.quad_0 = bf16[144,192]{1,0:T(8,128)(2,1)S(1)} collective-permute-done((bf16[144,192]{1,0:T(8,128)(2,1)}, bf16[144,192]{1,0:T(8,128)(2,1)S(1)}, u32[]{:S(2)}, u32[]{:S(2)}) %collective-permute-start.3) | collective-permute-done | bytes 55328 | tf_op jit(solution)/shard_map/ppermute | solution.py:555
  48.0 1.1 collective-permute-done.5.quad_2
  49.8 10.4 %shard_map.208 = (bf16[6,12,4,192]{3,2,1,0:T(4,128)(2,1)}, bf16[6,12,4,192]{3,2,1,0:T(4,128)(2,1)}, bf16[2,3584,128]{2,1,0:T(8,128)(2,1)}, bf16[320,128]{1,0:T(8,128)(2,1)}) custom-call(s32[1,2]{1,0:T(1,128)} %bitcast.30, bf16[144,192]{1,0:T(8,128)(2,1)} %copy-done.4, bf16[144,192]{1,0:T(8,128)(2,1)} %copy-done.5, ...), custom_call_target="tpu_custom_call", output_to_operand_aliasing={{2}: (18, {})} | custom-call | flops 2000000000 | bytes 4000000 | tf_op jit(solution)/shard_map/pallas_call | solution.py:531
  60.1 1.7 %select_bitcast_fusion = bf16[3584,128]{1,0:T(8,128)(2,1)S(1)} fusion(pred[]{:T(512)S(6)} %ne.24, bf16[2,3584,128]{2,1,0:T(8,128)(2,1)} %get-tuple-element.51), kind=kLoop, calls=%fused_computation.5 | loop fusion | flops 458752 | bytes 2752513 | tf_op jit(solution)/shard_map/jit(_where)/select_n | solution.py:681
  61.8 1.3 collective-permute-start.6
  63.1 2.2 %collective-permute-done.6 = bf16[3584,128]{1,0:T(8,128)(2,1)} collective-permute-done((bf16[3584,128]{1,0:T(8,128)(2,1)S(1)}, bf16[3584,128]{1,0:T(8,128)(2,1)}, u32[]{:S(2)}, u32[]{:S(2)}) %collective-permute-start.6) | collective-permute-done | bytes 917536 | tf_op jit(solution)/shard_map/ppermute | solution.py:666
  65.3 1.5 fusion
  67.0 11.7 %collective-permute-done.7 = bf16[1792,128]{1,0:T(8,128)(2,1)S(1)} collective-permute-done((bf16[1792,128]{1,0:T(8,128)(2,1)S(1)}, bf16[1792,128]{1,0:T(8,128)(2,1)S(1)}, u32[]{:S(2)}, u32[]{:S(2)}) %collective-permute-start.7) | collective-permute-done | bytes 458784 | tf_op jit(solution)/shard_map/ppermute | solution.py:666
  79.1 5.9 %collective-permute-done.8 = bf16[896,128]{1,0:T(8,128)(2,1)S(1)} collective-permute-done((bf16[896,128]{1,0:T(8,128)(2,1)S(1)}, bf16[896,128]{1,0:T(8,128)(2,1)S(1)}, u32[]{:S(2)}, u32[]{:S(2)}) %collective-permute-start.8) | collective-permute-done | bytes 229408 | tf_op jit(solution)/shard_map/ppermute | solution.py:666
  85.1 1.9 %collective-permute-start.9 = (bf16[448,128]{1,0:T(8,128)(2,1)S(1)}, bf16[448,128]{1,0:T(8,128)(2,1)S(1)}, u32[]{:S(2)}, u32[]{:S(2)}) collective-permute-start(bf16[448,128]{1,0:T(8,128)(2,1)S(1)} %broadcast_select_fusion.13), channel_id=1, source_target_pairs={{0,8},{1,9},{2,10},{3,11},{4,12},{5,13},{6,14},{7,15},{8,0},{9,1},... | collective-permute-start | bytes 344072 | tf_op jit(solution)/shard_map/ppermute | solution.py:666
  87.0 3.3 %collective-permute-done.9 = bf16[448,128]{1,0:T(8,128)(2,1)S(1)} collective-permute-done((bf16[448,128]{1,0:T(8,128)(2,1)S(1)}, bf16[448,128]{1,0:T(8,128)(2,1)S(1)}, u32[]{:S(2)}, u32[]{:S(2)}) %collective-permute-start.9) | collective-permute-done | bytes 114720 | tf_op jit(solution)/shard_map/ppermute | solution.py:666
  90.5 3.9 %collective-permute-done.10 = bf16[544,128]{1,0:T(8,128)(2,1)S(1)} collective-permute-done((bf16[544,128]{1,0:T(8,128)(2,1)S(1)}, bf16[544,128]{1,0:T(8,128)(2,1)S(1)}, u32[]{:S(2)}, u32[]{:S(2)}) %collective-permute-start.10) | collective-permute-done | bytes 139296 | tf_op jit(solution)/shard_map/ppermute | solution.py:666
  94.6 4.5 %collective-permute-done.11 = bf16[272,128]{1,0:T(8,128)(2,1)S(1)} collective-permute-done((bf16[272,128]{1,0:T(8,128)(2,1)S(1)}, bf16[272,128]{1,0:T(8,128)(2,1)S(1)}, u32[]{:S(2)}, u32[]{:S(2)}) %collective-permute-start.11) | collective-permute-done | bytes 69664 | tf_op jit(solution)/shard_map/ppermute | solution.py:666
  99.2 7.4 %collective-permute-done.12 = bf16[272,128]{1,0:T(8,128)(2,1)S(1)} collective-permute-done((bf16[272,128]{1,0:T(8,128)(2,1)S(1)}, bf16[272,128]{1,0:T(8,128)(2,1)S(1)}, u32[]{:S(2)}, u32[]{:S(2)}) %collective-permute-start.12) | collective-permute-done | bytes 69664 | tf_op jit(solution)/shard_map/ppermute | solution.py:666
  107.2 4.3 %collective-permute-done.13 = bf16[272,128]{1,0:T(8,128)(2,1)S(1)} collective-permute-done((bf16[272,128]{1,0:T(8,128)(2,1)S(1)}, bf16[272,128]{1,0:T(8,128)(2,1)S(1)}, u32[]{:S(2)}, u32[]{:S(2)}) %collective-permute-start.13) | collective-permute-done | bytes 69664 | tf_op jit(solution)/shard_map/ppermute | solution.py:666
  111.6 4.1 %collective-permute-done.14 = bf16[272,128]{1,0:T(8,128)(2,1)S(1)} collective-permute-done((bf16[272,128]{1,0:T(8,128)(2,1)S(1)}, bf16[272,128]{1,0:T(8,128)(2,1)S(1)}, u32[]{:S(2)}, u32[]{:S(2)}) %collective-permute-start.14) | collective-permute-done | bytes 69664 | tf_op jit(solution)/shard_map/ppermute | solution.py:666
  116.1 3.9 %collective-permute-done.15 = bf16[544,128]{1,0:T(8,128)(2,1)S(1)} collective-permute-done((bf16[544,128]{1,0:T(8,128)(2,1)S(1)}, bf16[544,128]{1,0:T(8,128)(2,1)S(1)}, u32[]{:S(2)}, u32[]{:S(2)}) %collective-permute-start.15) | collective-permute-done | bytes 139296 | tf_op jit(solution)/shard_map/ppermute | solution.py:666
  120.1 2.2 %collective-permute-start.16 = (bf16[448,128]{1,0:T(8,128)(2,1)S(1)}, bf16[448,128]{1,0:T(8,128)(2,1)S(1)}, u32[]{:S(2)}, u32[]{:S(2)}) collective-permute-start(bf16[448,128]{1,0:T(8,128)(2,1)S(1)} %slice.80), channel_id=1, source_target_pairs={{0,8},{1,9},{2,10},{3,11},{4,12},{5,13},{6,14},{7,15},{8,0},{9,1},... | collective-permute-start | bytes 344072 | tf_op jit(solution)/shard_map/ppermute | solution.py:666
  122.3 3.0 %collective-permute-done.16 = bf16[448,128]{1,0:T(8,128)(2,1)S(1)} collective-permute-done((bf16[448,128]{1,0:T(8,128)(2,1)S(1)}, bf16[448,128]{1,0:T(8,128)(2,1)S(1)}, u32[]{:S(2)}, u32[]{:S(2)}) %collective-permute-start.16) | collective-permute-done | bytes 114720 | tf_op jit(solution)/shard_map/ppermute | solution.py:666
  125.8 4.9 %collective-permute-done.17 = bf16[896,128]{1,0:T(8,128)(2,1)S(1)} collective-permute-done((bf16[896,128]{1,0:T(8,128)(2,1)S(1)}, bf16[896,128]{1,0:T(8,128)(2,1)S(1)}, u32[]{:S(2)}, u32[]{:S(2)}) %collective-permute-start.17) | collective-permute-done | bytes 229408 | tf_op jit(solution)/shard_map/ppermute | solution.py:666
  131.5 6.7 %collective-permute-done.18 = bf16[1792,128]{1,0:T(8,128)(2,1)S(1)} collective-permute-done((bf16[1792,128]{1,0:T(8,128)(2,1)S(1)}, bf16[1792,128]{1,0:T(8,128)(2,1)S(1)}, u32[]{:S(2)}, u32[]{:S(2)}) %collective-permute-start.18) | collective-permute-done | bytes 458784 | tf_op jit(solution)/shard_map/ppermute | solution.py:666
  138.4 14.3 %collective-permute-start.19 = (bf16[3584,128]{1,0:T(8,128)(2,1)S(1)}, bf16[3584,128]{1,0:T(8,128)(2,1)S(1)}, u32[]{:S(2)}, u32[]{:S(2)}) collective-permute-start(bf16[3584,128]{1,0:T(8,128)(2,1)S(1)} %pad_maximum_fusion.1), channel_id=1, source_target_pairs={{0,1},{1,0},{2,3},{3,2},{4,5},{5,4},{6,7},{7,6},{8,9},{9,8},{10,11... | collective-permute-start | bytes 2752520 | tf_op jit(solution)/shard_map/ppermute | solution.py:666
  153.4 1.4 collective-permute-done.19
  155.2 1.4 pad_maximum_fusion
  156.6 3.2 %shard_map.209 = (f32[2,2,192]{2,1,0:T(2,128)}, f32[2,192,576]{2,1,0:T(8,128)}, f32[2,192,192]{2,1,0:T(8,128)}, f32[2,192,768]{2,1,0:T(8,128)}, f32[2,192,768]{2,1,0:T(8,128)}, /*index=5*/f32[2,1,6,2,3312]{4,3,2,1,0:T(2,128)}) custom-call(bf16[2,3584,128]{2,1,0:T(8,128)(2,1)} %bitcast.16, bf16[2,320,128]{2,1,0:T(8,128)(2,1)} %bitcast.17), custom_call_target="tpu_custom_call" | custom-call | tf_op jit(solution)/shard_map/pallas_call | solution.py:741
  (62 shorter events, 7.0 us)
Async XLA Ops:
  0.6 21.0 %copy-start.3 = (s32[4,6,12]{2,0,1:T(4,128)S(1)}, s32[4,6,12]{2,0,1:T(4,128)}, u32[]{:S(2)}) copy-start(s32[4,6,12]{2,0,1:T(4,128)} %param.17) | copy-start | bytes 3460
  8.3 14.8 %collective-permute-start = (bf16[144,192]{1,0:T(8,128)(2,1)}, bf16[144,192]{1,0:T(8,128)(2,1)S(1)}, u32[]{:S(2)}, u32[]{:S(2)}) collective-permute-start(bf16[144,192]{1,0:T(8,128)(2,1)} %get-tuple-element.34), channel_id=1, source_target_pairs={{16,0},{17,1},{18,2},{19,3},{20,4},{21,5},{22,6},{23,7},{24,8},{25... | collective-permute-start | bytes 165896 | tf_op jit(solution)/shard_map/ppermute | solution.py:555
  17.4 5.7 %collective-permute-start.1 = (bf16[144,192]{1,0:T(8,128)(2,1)}, bf16[144,192]{1,0:T(8,128)(2,1)S(1)}, u32[]{:S(2)}, u32[]{:S(2)}) collective-permute-start(bf16[144,192]{1,0:T(8,128)(2,1)} %get-tuple-element.35), channel_id=1, source_target_pairs={{1,0},{2,1},{3,2},{4,3},{5,4},{6,5},{7,6},{8,7},{9,8},{10,9},{11,1... | collective-permute-start | bytes 165896 | tf_op jit(solution)/shard_map/ppermute | solution.py:555
  18.4 5.6 %collective-permute-start.2 = (bf16[144,192]{1,0:T(8,128)(2,1)}, bf16[144,192]{1,0:T(8,128)(2,1)S(1)}, u32[]{:S(2)}, u32[]{:S(2)}) collective-permute-start(bf16[144,192]{1,0:T(8,128)(2,1)} %get-tuple-element.36), channel_id=1, source_target_pairs={{17,0},{18,1},{19,2},{20,3},{21,4},{22,5},{23,6},{24,7},{25,8},{26... | collective-permute-start | bytes 165896 | tf_op jit(solution)/shard_map/ppermute | solution.py:555
  23.1 0.9 copy-start.7
  23.1 0.9 copy-start.8
  24.0 0.6 copy-start.9
  39.0 9.0 %collective-permute-start.3 = (bf16[144,192]{1,0:T(8,128)(2,1)}, bf16[144,192]{1,0:T(8,128)(2,1)S(1)}, u32[]{:S(2)}, u32[]{:S(2)}) collective-permute-start(bf16[144,192]{1,0:T(8,128)(2,1)} %get-tuple-element.37), channel_id=1, source_target_pairs={{255,0},{240,1},{241,2},{242,3},{243,4},{244,5},{245,6},{246,7},{2... | collective-permute-start | bytes 165896 | tf_op jit(solution)/shard_map/ppermute | solution.py:555
  39.0 9.0 %collective-permute-start.4 = (bf16[144,192]{1,0:T(8,128)(2,1)}, bf16[144,192]{1,0:T(8,128)(2,1)S(1)}, u32[]{:S(2)}, u32[]{:S(2)}) collective-permute-start(bf16[144,192]{1,0:T(8,128)(2,1)} %get-tuple-element.38), channel_id=1, source_target_pairs={{15,0},{0,1},{1,2},{2,3},{3,4},{4,5},{5,6},{6,7},{7,8},{8,9},{9,10... | collective-permute-start | bytes 165896 | tf_op jit(solution)/shard_map/ppermute | solution.py:555
  39.1 10.0 %collective-permute-start.5 = (bf16[144,192]{1,0:T(8,128)(2,1)}, bf16[144,192]{1,0:T(8,128)(2,1)S(1)}, u32[]{:S(2)}, u32[]{:S(2)}) collective-permute-start(bf16[144,192]{1,0:T(8,128)(2,1)} %get-tuple-element.39), channel_id=1, source_target_pairs={{240,0},{241,1},{242,2},{243,3},{244,4},{245,5},{246,6},{247,7},{2... | collective-permute-start | bytes 165896 | tf_op jit(solution)/shard_map/ppermute | solution.py:555
  48.0 1.1 copy-start.4
  48.0 1.1 copy-start.5
  49.1 0.6 copy-start.6
  60.1 5.2 %copy-start = (bf16[2,3584,128]{2,1,0:T(8,128)(2,1)S(1)}, bf16[2,3584,128]{2,1,0:T(8,128)(2,1)}, u32[]{:S(2)}) copy-start(bf16[2,3584,128]{2,1,0:T(8,128)(2,1)} %get-tuple-element.51) | copy-start | bytes 5505028
  61.8 3.5 %collective-permute-start.6 = (bf16[3584,128]{1,0:T(8,128)(2,1)S(1)}, bf16[3584,128]{1,0:T(8,128)(2,1)}, u32[]{:S(2)}, u32[]{:S(2)}) collective-permute-start(bf16[3584,128]{1,0:T(8,128)(2,1)S(1)} %select_bitcast_fusion), channel_id=1, source_target_pairs={{0,1},{1,0},{2,3},{3,2},{4,5},{5,4},{6,7},{7,6},{8,9},{9,8},{10,11... | collective-permute-start | bytes 2752520 | tf_op jit(solution)/shard_map/ppermute | solution.py:666
  66.9 11.8 %collective-permute-start.7 = (bf16[1792,128]{1,0:T(8,128)(2,1)S(1)}, bf16[1792,128]{1,0:T(8,128)(2,1)S(1)}, u32[]{:S(2)}, u32[]{:S(2)}) collective-permute-start(bf16[1792,128]{1,0:T(8,128)(2,1)S(1)} %broadcast_select_fusion.4), channel_id=1, source_target_pairs={{0,2},{1,3},{2,0},{3,1},{4,6},{5,7},{6,4},{7,5},{8,10},{9,11},{10,... | collective-permute-start | bytes 1376264 | tf_op jit(solution)/shard_map/ppermute | solution.py:666
  67.0 23.3 %copy-start.1 = (bf16[320,128]{1,0:T(8,128)(2,1)S(1)}, bf16[320,128]{1,0:T(8,128)(2,1)}, u32[]{:S(2)}) copy-start(bf16[320,128]{1,0:T(8,128)(2,1)} %get-tuple-element.50) | copy-start | bytes 245764
  67.0 23.3 %copy-start.2 = (bf16[320,128]{1,0:T(8,128)(2,1)S(1)}, bf16[320,128]{1,0:T(8,128)(2,1)}, u32[]{:S(2)}) copy-start(bf16[320,128]{1,0:T(8,128)(2,1)} %get-tuple-element.49) | copy-start | bytes 245764
  79.0 6.0 %collective-permute-start.8 = (bf16[896,128]{1,0:T(8,128)(2,1)S(1)}, bf16[896,128]{1,0:T(8,128)(2,1)S(1)}, u32[]{:S(2)}, u32[]{:S(2)}) collective-permute-start(bf16[896,128]{1,0:T(8,128)(2,1)S(1)} %broadcast_select_fusion.7), channel_id=1, source_target_pairs={{0,4},{1,5},{2,6},{3,7},{4,0},{5,1},{6,2},{7,3},{8,12},{9,13},{10,... | collective-permute-start | bytes 688136 | tf_op jit(solution)/shard_map/ppermute | solution.py:666
  85.1 5.2 %collective-permute-start.9 = (bf16[448,128]{1,0:T(8,128)(2,1)S(1)}, bf16[448,128]{1,0:T(8,128)(2,1)S(1)}, u32[]{:S(2)}, u32[]{:S(2)}) collective-permute-start(bf16[448,128]{1,0:T(8,128)(2,1)S(1)} %broadcast_select_fusion.13), channel_id=1, source_target_pairs={{0,8},{1,9},{2,10},{3,11},{4,12},{5,13},{6,14},{7,15},{8,0},{9,1},... | collective-permute-start | bytes 344072 | tf_op jit(solution)/shard_map/ppermute | solution.py:666
  90.4 4.0 %collective-permute-start.10 = (bf16[544,128]{1,0:T(8,128)(2,1)S(1)}, bf16[544,128]{1,0:T(8,128)(2,1)S(1)}, u32[]{:S(2)}, u32[]{:S(2)}) collective-permute-start(bf16[544,128]{1,0:T(8,128)(2,1)S(1)} %broadcast_select_fusion.10), channel_id=1, source_target_pairs={{0,16},{16,0},{32,48},{48,32},{64,80},{80,64},{96,112},{112,96},{1... | collective-permute-start | bytes 417800 | tf_op jit(solution)/shard_map/ppermute | solution.py:666
  94.5 4.6 %collective-permute-start.11 = (bf16[272,128]{1,0:T(8,128)(2,1)S(1)}, bf16[272,128]{1,0:T(8,128)(2,1)S(1)}, u32[]{:S(2)}, u32[]{:S(2)}) collective-permute-start(bf16[272,128]{1,0:T(8,128)(2,1)S(1)} %broadcast_select_fusion.16), channel_id=1, source_target_pairs={{0,32},{16,48},{32,0},{48,16},{64,96},{80,112},{96,64},{112,80},{1... | collective-permute-start | bytes 208904 | tf_op jit(solution)/shard_map/ppermute | solution.py:666
  99.1 7.5 %collective-permute-start.12 = (bf16[272,128]{1,0:T(8,128)(2,1)S(1)}, bf16[272,128]{1,0:T(8,128)(2,1)S(1)}, u32[]{:S(2)}, u32[]{:S(2)}) collective-permute-start(bf16[272,128]{1,0:T(8,128)(2,1)S(1)} %add_convert_fusion.6), channel_id=1, source_target_pairs={{0,64},{16,80},{32,96},{48,112},{64,0},{80,16},{96,32},{112,48},{1... | collective-permute-start | bytes 208904 | tf_op jit(solution)/shard_map/ppermute | solution.py:666
  106.7 4.8 %collective-permute-start.13 = (bf16[272,128]{1,0:T(8,128)(2,1)S(1)}, bf16[272,128]{1,0:T(8,128)(2,1)S(1)}, u32[]{:S(2)}, u32[]{:S(2)}) collective-permute-start(bf16[272,128]{1,0:T(8,128)(2,1)S(1)} %add_convert_fusion.5), channel_id=1, source_target_pairs={{0,128},{16,144},{32,160},{48,176},{64,192},{80,208},{96,224},{112... | collective-permute-start | bytes 208904 | tf_op jit(solution)/shard_map/ppermute | solution.py:666
  111.5 4.2 %collective-permute-start.14 = (bf16[272,128]{1,0:T(8,128)(2,1)S(1)}, bf16[272,128]{1,0:T(8,128)(2,1)S(1)}, u32[]{:S(2)}, u32[]{:S(2)}) collective-permute-start(bf16[272,128]{1,0:T(8,128)(2,1)S(1)} %add_convert_fusion.4), channel_id=1, source_target_pairs={{0,32},{16,48},{32,0},{48,16},{64,96},{80,112},{96,64},{112,80},{1... | collective-permute-start | bytes 208904 | tf_op jit(solution)/shard_map/ppermute | solution.py:666
  115.8 4.3 %collective-permute-start.15 = (bf16[544,128]{1,0:T(8,128)(2,1)S(1)}, bf16[544,128]{1,0:T(8,128)(2,1)S(1)}, u32[]{:S(2)}, u32[]{:S(2)}) collective-permute-start(bf16[544,128]{1,0:T(8,128)(2,1)S(1)} %pad_maximum_fusion.7), channel_id=1, source_target_pairs={{0,16},{16,0},{32,48},{48,32},{64,80},{80,64},{96,112},{112,96},{1... | collective-permute-start | bytes 417800 | tf_op jit(solution)/shard_map/ppermute | solution.py:666
  120.1 5.2 %collective-permute-start.16 = (bf16[448,128]{1,0:T(8,128)(2,1)S(1)}, bf16[448,128]{1,0:T(8,128)(2,1)S(1)}, u32[]{:S(2)}, u32[]{:S(2)}) collective-permute-start(bf16[448,128]{1,0:T(8,128)(2,1)S(1)} %slice.80), channel_id=1, source_target_pairs={{0,8},{1,9},{2,10},{3,11},{4,12},{5,13},{6,14},{7,15},{8,0},{9,1},... | collective-permute-start | bytes 344072 | tf_op jit(solution)/shard_map/ppermute | solution.py:666
  125.4 5.3 %collective-permute-start.17 = (bf16[896,128]{1,0:T(8,128)(2,1)S(1)}, bf16[896,128]{1,0:T(8,128)(2,1)S(1)}, u32[]{:S(2)}, u32[]{:S(2)}) collective-permute-start(bf16[896,128]{1,0:T(8,128)(2,1)S(1)} %pad_maximum_fusion.3), channel_id=1, source_target_pairs={{0,4},{1,5},{2,6},{3,7},{4,0},{5,1},{6,2},{7,3},{8,12},{9,13},{10,... | collective-permute-start | bytes 688136 | tf_op jit(solution)/shard_map/ppermute | solution.py:666
  130.8 7.4 %collective-permute-start.18 = (bf16[1792,128]{1,0:T(8,128)(2,1)S(1)}, bf16[1792,128]{1,0:T(8,128)(2,1)S(1)}, u32[]{:S(2)}, u32[]{:S(2)}) collective-permute-start(bf16[1792,128]{1,0:T(8,128)(2,1)S(1)} %pad_maximum_fusion.2), channel_id=1, source_target_pairs={{0,2},{1,3},{2,0},{3,1},{4,6},{5,7},{6,4},{7,5},{8,10},{9,11},{10,... | collective-permute-start | bytes 1376264 | tf_op jit(solution)/shard_map/ppermute | solution.py:666
  138.4 16.4 %collective-permute-start.19 = (bf16[3584,128]{1,0:T(8,128)(2,1)S(1)}, bf16[3584,128]{1,0:T(8,128)(2,1)S(1)}, u32[]{:S(2)}, u32[]{:S(2)}) collective-permute-start(bf16[3584,128]{1,0:T(8,128)(2,1)S(1)} %pad_maximum_fusion.1), channel_id=1, source_target_pairs={{0,1},{1,0},{2,3},{3,2},{4,5},{5,4},{6,7},{7,6},{8,9},{9,8},{10,11... | collective-permute-start | bytes 2752520 | tf_op jit(solution)/shard_map/ppermute | solution.py:666

commit v2 on v1

v2 whole, which is shorter than its diff:
```python
import functools
import math

import jax
import jax.numpy as jnp
import numpy as np
from jax import lax
from jax.experimental import pallas as pl
from jax.experimental.pallas import tpu as pltpu
from jax.sharding import PartitionSpec as P

C = 192
HEADS = 6
HEAD = 32
FFN = 768
WIN_Z = 2
WIN_LAT = 6
WIN_LON = 12
WIN = 144
TOKENS = 2 * WIN
QUAD = 72
RELPOS = 3312
SPAN = 2 * WIN_LON - 1
ROWS = 3584
GAIN_ROWS = 3456
TABLE_ROWS = 320

EPSILON = 1e-05
NEGATIVE = -1000000000.0
SCALE = 1.0 / math.sqrt(HEAD)

F32 = jnp.float32
BF16 = jnp.bfloat16


def quadrant_rows():
    rows = np.zeros(TOKENS, np.int64)
    at = 0
    for lat_half in range(2):
        for lon_half in range(2):
            for level in range(4):
                for row in range(3):
                    for col in range(6):
                        rows[at] = (level * 6 + lat_half * 3 + row) * 12 + lon_half * 6 + col
                        at += 1
    return rows


def rolled_rows():
    rows = quadrant_rows()
    level, rest = rows // 72, rows % 72
    return ((level + 3) % 4) * 72 + rest


def one_hot(rows):
    picked = np.zeros((TOKENS, TOKENS), np.float32)
    picked[np.arange(TOKENS), rows] = 1.0
    return picked


def mm(left, right):
    return lax.dot_general(left, right, (((1,), (0,)), ((), ())), preferred_element_type=F32)


def mm_nt(left, right):
    return lax.dot_general(left, right, (((1,), (1,)), ((), ())), preferred_element_type=F32)


def eye(size):
    return (
        lax.broadcasted_iota(jnp.int32, (size, size), 0) == lax.broadcasted_iota(jnp.int32, (size, size), 1)
    ).astype(F32).astype(BF16)


def turned(value):
    return mm_nt(eye(value.shape[1]), value).astype(BF16)


def norm_stats(values):
    centre = values - jnp.mean(values, axis=-1, keepdims=True)
    inverse = lax.rsqrt(jnp.mean(centre * centre, axis=-1, keepdims=True) + EPSILON)
    return centre * inverse, inverse


def norm_backward(upstream, normal_hat, inverse):
    upstream_mean = jnp.mean(upstream, axis=-1, keepdims=True)
    cross_mean = jnp.mean(upstream * normal_hat, axis=-1, keepdims=True)
    return inverse * (upstream - upstream_mean - normal_hat * cross_mean)


def head_lanes(head):
    lane = lax.broadcasted_iota(jnp.int32, (1, C), 1)
    return (lane >= head * HEAD) & (lane < (head + 1) * HEAD)


def make_pairs(pairs_ref):
    row = lax.broadcasted_iota(jnp.int32, (512, 1), 0)
    within = row & 127
    third = (within >= SPAN).astype(jnp.int32) + (within >= 2 * SPAN).astype(jnp.int32)
    row_group = (row >> 7) * 3 + third
    row_offset = within - third * SPAN
    col = lax.broadcasted_iota(jnp.int32, (1, 256), 1)
    col_group = jnp.zeros_like(col)
    for group in range(1, 12):
        col_group = col_group + (col >= group * 12).astype(jnp.int32)
    col_place = col - col_group * 12
    usable = (row_group == col_group) & (within < 3 * SPAN) & (col < WIN)
    keys = jnp.where(usable, col_place + 11 - row_offset, -1)
    for place in range(WIN_LON):
        pairs_ref[place] = jnp.where(keys == place, 1.0, 0.0).astype(BF16)


def table_start(zs, zt, hs, ht):
    return (((zs * 2 + zt) * 6 + hs) * 6 + ht) * SPAN


def spread_bias(table_ref, pairs_ref, row_ref, shaped_ref, bias_ref):
    for head in range(HEADS):
        row_ref[head * 2 : head * 2 + 2, :RELPOS] = table_ref[head].astype(F32)
    row = row_ref[: 2 * HEADS]
    for zs in range(2):
        for zt in range(2):
            for group in range(2):
                for ht in range(6):
                    pieces = []
                    for hs in range(group * 3, group * 3 + 3):
                        start = table_start(zs, zt, hs, ht)
                        pieces.append(row[:, start : start + SPAN])
                    pieces.append(jnp.zeros((2 * HEADS, 128 - 3 * SPAN), F32))
                    target = pl.ds(zt * 6 + ht, 2 * HEADS, stride=12)
                    shaped_ref[zs * 2 + group, target, :] = jnp.concatenate(pieces, axis=1)
    shaped = jnp.concatenate([shaped_ref[part, :WIN].astype(BF16) for part in range(4)], axis=1)
    for col in range(WIN_LON):
        spread = mm(shaped, pairs_ref[col])
        bias_ref[0, pl.ds(col, WIN, stride=12), :] = spread[:, :128]
        bias_ref[1, pl.ds(col, WIN, stride=12), :] = spread[:, 128:]


def collect_bias(scaled_ref, pairs_ref, levels, row_ref, shaped_ref, grads_ref, out_ref):
    for place in range(2 * HEADS):
        rows = slice(place * WIN, (place + 1) * WIN)
        piece = scaled_ref[place].astype(F32)
        grads_ref[0, rows] = piece[:, :128]
        grads_ref[1, rows] = jnp.concatenate([piece[:, 128:], jnp.zeros((WIN, 256 - WIN), F32)], axis=1)
    total = jnp.zeros((WIN, 512), F32)
    for col in range(WIN_LON):
        left = grads_ref[0, pl.ds(col, WIN, stride=12), :]
        right = grads_ref[1, pl.ds(col, WIN, stride=12), :]
        piece = jnp.concatenate([left, right], axis=1).astype(BF16)
        total = total + mm_nt(piece, pairs_ref[col])
    total = total * (1.0 / SCALE)
    for part in range(4):
        shaped_ref[part, :WIN] = total[:, part * 128 : (part + 1) * 128]
    row_ref[...] = jnp.zeros_like(row_ref)
    for zs in range(2):
        for zt in range(2):
            for group in range(2):
                for ht in range(6):
                    pieces = [
                        shaped_ref[zs * 2 + group, pl.ds(window * 72 + zt * 6 + ht, HEADS, stride=12), :]
                        for window in range(2)
                    ]
                    for level in range(2):
                        chosen = jnp.zeros((HEADS, 128), F32)
                        for window in range(2):
                            chosen = chosen + jnp.where(levels[window] == level, pieces[window], 0.0)
                        for index in range(3):
                            start = table_start(zs, zt, group * 3 + index, ht)
                            row_ref[level * 8 : level * 8 + HEADS, start : start + SPAN] = chosen[
                                :, index * SPAN : (index + 1) * SPAN
                            ]
    for slab in range(26):
        lanes = slice(slab * 128, (slab + 1) * 128)
        rows = jnp.concatenate([row_ref[:HEADS, lanes], row_ref[8 : 8 + HEADS, lanes]], axis=0)
        shaped_ref[slab // 13, slab % 13 * 12 : slab % 13 * 12 + 12] = rows
    out_ref[...] = jnp.concatenate(
        [shaped_ref[0, :156], shaped_ref[1, :156], jnp.zeros((TABLE_ROWS - 312, 128), F32)], axis=0
    ).astype(BF16)


def load_tiles(bias_ref, level, head):
    rows = pl.ds(pl.multiple_of((head * 2 + level) * WIN, 8), WIN)
    return jnp.concatenate([bias_ref[0, rows, :], bias_ref[1, rows, : WIN - 128]], axis=1)


def attention(normed, in_weight, bias_of, weights_ref):
    eye_c = eye(C)
    weight_q, weight_k, weight_v = in_weight[:, :C], in_weight[:, C : 2 * C], in_weight[:, 2 * C :]
    kept = []
    mixed = []
    for window in range(2):
        rows = normed[window * WIN : (window + 1) * WIN]
        keys = mm(rows, weight_k).astype(BF16)
        values = mm(rows, weight_v).astype(BF16)
        queries = mm(rows, weight_q).astype(BF16)
        queries_t = mm_nt(eye_c, queries).astype(BF16)
        keys_t = mm_nt(eye_c, keys).astype(BF16)
        values_t = mm_nt(eye_c, values).astype(BF16)
        parts = []
        for head in range(HEADS):
            own = jnp.where(head_lanes(head), keys.astype(F32), 0.0).astype(BF16)
            scores = mm(own, queries_t) * SCALE + bias_of(window, head)
            weights = jnp.exp(scores - jnp.max(scores, axis=0, keepdims=True))
            weights = weights * (1.0 / jnp.sum(weights, axis=0, keepdims=True))
            weights = weights.astype(BF16)
            weights_ref[window * HEADS + head] = weights
            parts.append(mm(values_t[head * HEAD : (head + 1) * HEAD], weights))
        mixed.append(jnp.concatenate(parts, axis=0).astype(BF16))
        kept.append((queries_t, keys_t, values))
    return kept, mixed


def feed_forward(hidden, gain, up_weight):
    hat, inverse = norm_stats(hidden)
    normed = (hat * gain).astype(BF16)
    return hat, inverse, normed, mm(normed, up_weight)


def gelu_parts(expanded):
    cumulative = 0.5 * (1.0 + lax.erf(expanded * (1.0 / math.sqrt(2.0))))
    slope = cumulative + expanded * jnp.exp(-0.5 * expanded * expanded) * (1.0 / math.sqrt(2.0 * math.pi))
    return (expanded * cumulative).astype(BF16), slope


def natural_mixed(mixed):
    eye_w = eye(WIN)
    return jnp.concatenate([mm_nt(eye_w, part) for part in mixed], axis=0).astype(BF16)


def pack(packed_ref, start, value):
    height = value.shape[0]
    for part in range(value.shape[1] // 128):
        rows = slice(start + part * height, start + (part + 1) * height)
        packed_ref[rows] = value[:, part * 128 : (part + 1) * 128].astype(BF16)


def backward(
    grad,
    active,
    slope,
    second_hat,
    second_inverse,
    second_norm,
    mixed,
    attended,
    weights_ref,
    first_hat,
    first_inverse,
    first_norm,
    gain_one,
    gain_two,
    in_weight,
    out_weight,
    up_weight,
    down_weight,
    scaled_ref,
    packed_ref,
):
    eye_c = eye(C)
    grad_half = grad.astype(BF16)
    pack(packed_ref, 2304, mm(turned(grad_half), active))
    grad_expanded = (mm(grad_half, down_weight) * slope).astype(BF16)
    normed_t = turned(second_norm)
    pack(packed_ref, 1152, mm(normed_t, grad_expanded))
    grad_second = mm_nt(grad_expanded, up_weight)
    gain_two_grad = jnp.sum(grad_second * second_hat, axis=0, keepdims=True)
    grad_hidden = (grad + norm_backward(grad_second * gain_two, second_hat, second_inverse)).astype(BF16)
    grad_out = mm(mixed[0], grad_hidden[:WIN]) + mm(mixed[1], grad_hidden[WIN:])
    packed_ref[960:1152] = grad_out[:, :128].astype(BF16)
    grad_mixed = mm_nt(grad_hidden, out_weight).astype(BF16)
    projected = []
    for window in range(2):
        queries_t, keys_t, values = attended[window]
        upstream_t = mm_nt(eye_c, grad_mixed[window * WIN : (window + 1) * WIN]).astype(BF16)
        grad_q, grad_k, grad_v = [], [], []
        for head in range(HEADS):
            lanes = slice(head * HEAD, (head + 1) * HEAD)
            half = weights_ref[window * HEADS + head]
            weights = half.astype(F32)
            own = jnp.where(head_lanes(head), values.astype(F32), 0.0).astype(BF16)
            grad_weights = mm(own, upstream_t)
            inner = jnp.sum(grad_weights * weights, axis=0, keepdims=True)
            grad_scores = weights * (grad_weights - inner)
            scaled = (grad_scores * SCALE).astype(BF16)
            scaled_ref[window * HEADS + head] = scaled
            grad_v.append(mm_nt(upstream_t[lanes], half))
            grad_q.append(mm(keys_t[lanes], scaled))
            grad_k.append(mm_nt(queries_t[lanes], scaled))
        projected_t = jnp.concatenate(grad_q + grad_k + grad_v, axis=0).astype(BF16)
        projected.append(mm_nt(eye(WIN), projected_t))
    projected = jnp.concatenate(projected, axis=0).astype(BF16)
    first_t = turned(first_norm)
    grad_in = mm(first_t, projected)
    pack(packed_ref, 0, grad_in[:, :512])
    packed_ref[768:960] = jnp.concatenate([grad_in[:, 512:], grad_out[:, 128:]], axis=1).astype(BF16)
    grad_first = mm_nt(projected, in_weight)
    gain_one_grad = jnp.sum(grad_first * first_hat, axis=0, keepdims=True)
    gain_rows = jnp.concatenate(
        [
            gain_one_grad[:, :128],
            jnp.concatenate([gain_one_grad[:, 128:], gain_two_grad[:, 128:]], axis=1),
            gain_two_grad[:, :128],
            jnp.zeros((ROWS - GAIN_ROWS - 3, 128), F32),
        ],
        axis=0,
    )
    packed_ref[GAIN_ROWS:ROWS] = gain_rows.astype(BF16)
    return (
        grad_hidden.astype(F32) + norm_backward(grad_first * gain_one, first_hat, first_inverse)
    ).astype(BF16)


def load_grid(grid_ref, rows_ref):
    for row in range(6):
        for col in range(12):
            piece = grid_ref[row, col].astype(F32)
            target = pl.ds(row * 12 + col, 4, stride=72)
            rows_ref[0, target, :] = piece[:, :128]
            rows_ref[1, target, :] = jnp.concatenate([piece[:, 128:], jnp.zeros((4, 64), F32)], axis=1)
    return jnp.concatenate([rows_ref[0], rows_ref[1][:, :64]], axis=1)


def store_grid(rows, rows_ref, grid_ref):
    rows_ref[0] = rows[:, :128]
    rows_ref[1] = jnp.concatenate([rows[:, 128:], jnp.zeros((TOKENS, 64), F32)], axis=1)
    for row in range(6):
        for col in range(12):
            source = pl.ds(row * 12 + col, 4, stride=72)
            piece = jnp.concatenate([rows_ref[0, source, :], rows_ref[1, source, :][:, :64]], axis=1)
            grid_ref[row, col] = piece.astype(BF16)


def block_weights(gains_ref, in_ref, out_ref, up_ref, down_ref):
    gains = gains_ref[...]
    return gains[0:1], gains[1:2], in_ref[...], out_ref[...], up_ref[...], down_ref[...]


def write_halves(upper_ref, packed_ref, keep_ref, send_ref):
    half = ROWS // 2
    is_upper = upper_ref[0] == 1

    @pl.when(is_upper)
    def _():
        keep_ref[...] = packed_ref[half:]
        send_ref[...] = packed_ref[:half]

    @pl.when(jnp.logical_not(is_upper))
    def _():
        keep_ref[...] = packed_ref[:half]
        send_ref[...] = packed_ref[half:]


def first_kernel(
    levels_ref,
    inputs_ref,
    grad_ref,
    gains_ref,
    in_ref,
    out_ref,
    up_ref,
    down_ref,
    table_ref,
    order_ref,
    quad_0,
    quad_1,
    quad_2,
    quad_3,
    weights_out,
    qkt_out,
    values_out,
    mixed_out,
    hidden_out,
    pairs_ref,
    rows_ref,
    row_ref,
    shaped_ref,
    bias_ref,
):
    levels = [levels_ref[0, 0], levels_ref[0, 1]]
    gain_one, gain_two, in_weight, out_weight, up_weight, down_weight = block_weights(
        gains_ref, in_ref, out_ref, up_ref, down_ref
    )
    order = order_ref[...]
    grad_quads = mm(order, load_grid(grad_ref, rows_ref).astype(BF16))
    flat = load_grid(inputs_ref, rows_ref)
    make_pairs(pairs_ref)
    spread_bias(table_ref, pairs_ref, row_ref, shaped_ref, bias_ref)
    hat, _ = norm_stats(flat)
    normed = (hat * gain_one).astype(BF16)
    attended, mixed = attention(
        normed, in_weight, lambda window, head: load_tiles(bias_ref, levels[window], head), weights_out
    )
    for window in range(2):
        qkt_out[window, 0] = attended[window][0]
        qkt_out[window, 1] = attended[window][1]
        values_out[window] = attended[window][2]
        mixed_out[window] = mixed[window]
    hidden = (flat + mm(natural_mixed(mixed), out_weight)).astype(BF16)
    hidden_out[...] = hidden
    hidden = hidden.astype(F32)
    _, _, _, expanded = feed_forward(hidden, gain_two, up_weight)
    active = (expanded * 0.5 * (1.0 + lax.erf(expanded * (1.0 / math.sqrt(2.0))))).astype(BF16)
    result = (hidden + mm_nt(active, down_weight)).astype(BF16)
    result_quads = mm(order, result)
    for index, quad in enumerate((quad_0, quad_1, quad_2, quad_3)):
        rows = slice(index * QUAD, (index + 1) * QUAD)
        quad[...] = jnp.concatenate([result_quads[rows], grad_quads[rows]], axis=0).astype(BF16)


def region_row(region_ref, window):
    pieces = [region_ref[row, window * 2 + level : window * 2 + level + 1, :] for level in range(2) for row in range(6)]
    return jnp.concatenate(pieces, axis=1)


def prepare_kernel(
    levels_ref, region_ref, table_ref, bias_out, pairs_ref, row_ref, shaped_ref, bias_ref
):
    levels = [levels_ref[0, 0], levels_ref[0, 1]]
    make_pairs(pairs_ref)
    spread_bias(table_ref, pairs_ref, row_ref, shaped_ref, bias_ref)
    diagonal = lax.broadcasted_iota(jnp.int32, (WIN, WIN), 0) == lax.broadcasted_iota(jnp.int32, (WIN, WIN), 1)
    for window in range(2):
        across = region_row(region_ref, window).astype(F32)
        down = jnp.sum(jnp.where(diagonal, across, 0.0), axis=1, keepdims=True)
        same = across == down
        for head in range(HEADS):
            bias = jnp.where(same, load_tiles(bias_ref, levels[window], head), NEGATIVE)
            bias_out[window * HEADS + head] = bias.astype(BF16)


def second_kernel(
    upper_ref,
    quad_0,
    quad_1,
    quad_2,
    quad_3,
    bias_ref,
    gains_ref,
    in_ref,
    out_ref,
    up_ref,
    down_ref,
    ahead_ref,
    back_ref,
    back_0,
    back_1,
    back_2,
    back_3,
    keep_ref,
    send_ref,
    scaled_ref,
    weights_ref,
    packed_ref,
):
    quads = [quad[...].astype(F32) for quad in (quad_0, quad_1, quad_2, quad_3)]
    ahead = ahead_ref[...]
    flat = mm(ahead, jnp.concatenate([quad[:QUAD] for quad in quads], axis=0).astype(BF16))
    grad = mm(ahead, jnp.concatenate([quad[QUAD:] for quad in quads], axis=0).astype(BF16))
    gain_one, gain_two, in_weight, out_weight, up_weight, down_weight = block_weights(
        gains_ref, in_ref, out_ref, up_ref, down_ref
    )
    first_hat, first_inverse = norm_stats(flat)
    first_norm = (first_hat * gain_one).astype(BF16)
    attended, mixed = attention(
        first_norm, in_weight, lambda window, head: bias_ref[window * HEADS + head].astype(F32), weights_ref
    )
    hidden = (flat + mm(natural_mixed(mixed), out_weight)).astype(BF16).astype(F32)
    second_hat, second_inverse, second_norm, expanded = feed_forward(hidden, gain_two, up_weight)
    active, slope = gelu_parts(expanded)
    result = (hidden + mm_nt(active, down_weight)).astype(BF16)
    grad_in = backward(
        grad, active, slope, second_hat, second_inverse, second_norm, mixed, attended, weights_ref,
        first_hat, first_inverse, first_norm, gain_one, gain_two, in_weight, out_weight, up_weight,
        down_weight, scaled_ref, packed_ref,
    )
    back = back_ref[...]
    result_quads, grad_quads = mm(back, result), mm(back, grad_in)
    for index, quad in enumerate((back_0, back_1, back_2, back_3)):
        rows = slice(index * QUAD, (index + 1) * QUAD)
        quad[...] = jnp.concatenate([result_quads[rows], grad_quads[rows]], axis=0).astype(BF16)
    write_halves(upper_ref, packed_ref, keep_ref, send_ref)


def collect_kernel(
    levels_ref,
    scaled_ref,
    hidden_ref,
    gains_ref,
    up_ref,
    tables_out,
    active_out,
    slope_out,
    pairs_ref,
    row_ref,
    shaped_ref,
    grads_ref,
):
    levels = [levels_ref[0, 0], levels_ref[0, 1]]
    make_pairs(pairs_ref)
    collect_bias(scaled_ref, pairs_ref, levels, row_ref, shaped_ref, grads_ref, tables_out)
    _, _, _, expanded = feed_forward(hidden_ref[...].astype(F32), gains_ref[1:2], up_ref[...])
    active, slope = gelu_parts(expanded)
    active_out[...] = active
    slope_out[...] = slope.astype(BF16)


def third_kernel(
    upper_ref,
    quad_0,
    quad_1,
    quad_2,
    quad_3,
    inputs_ref,
    weights_ref,
    qkt_ref,
    values_ref,
    mixed_ref,
    hidden_ref,
    active_ref,
    slope_ref,
    gains_ref,
    in_ref,
    out_ref,
    up_ref,
    down_ref,
    natural_ref,
    keep_ref,
    send_ref,
    rows_out,
    scaled_ref,
    rows_ref,
    packed_ref,
):
    quads = [quad[...].astype(F32) for quad in (quad_0, quad_1, quad_2, quad_3)]
    grad = mm(natural_ref[...], jnp.concatenate([quad[QUAD:] for quad in quads], axis=0).astype(BF16))
    gain_one, gain_two, in_weight, out_weight, up_weight, down_weight = block_weights(
        gains_ref, in_ref, out_ref, up_ref, down_ref
    )
    first_hat, first_inverse = norm_stats(load_grid(inputs_ref, rows_ref))
    first_norm = (first_hat * gain_one).astype(BF16)
    second_hat, second_inverse = norm_stats(hidden_ref[...].astype(F32))
    second_norm = (second_hat * gain_two).astype(BF16)
    attended = [(qkt_ref[window, 0], qkt_ref[window, 1], values_ref[window]) for window in range(2)]
    mixed = [mixed_ref[0], mixed_ref[1]]
    rows_out[...] = backward(
        grad, active_ref[...], slope_ref[...].astype(F32), second_hat, second_inverse, second_norm, mixed,
        attended, weights_ref, first_hat, first_inverse, first_norm, gain_one, gain_two, in_weight,
        out_weight, up_weight, down_weight, scaled_ref, packed_ref,
    )
    write_halves(upper_ref, packed_ref, keep_ref, send_ref)


def finish_kernel(
    levels_ref, scaled_ref, second_tables_ref, tables_out, pairs_ref, row_ref, shaped_ref, grads_ref
):
    levels = [levels_ref[0, 0], levels_ref[0, 1]]
    make_pairs(pairs_ref)
    collect_bias(scaled_ref, pairs_ref, levels, row_ref, shaped_ref, grads_ref, tables_out.at[:TABLE_ROWS])
    tables_out[TABLE_ROWS:] = second_tables_ref[...]


def grids_kernel(quad_0, quad_1, quad_2, quad_3, natural_ref, grad_rows_ref, blocks_out, grad_out, rows_ref):
    quads = [quad[:QUAD].astype(F32) for quad in (quad_0, quad_1, quad_2, quad_3)]
    blocks = mm(natural_ref[...], jnp.concatenate(quads, axis=0).astype(BF16))
    store_grid(blocks, rows_ref, blocks_out)
    store_grid(grad_rows_ref[...].astype(F32), rows_ref, grad_out)


SMEM = pl.BlockSpec(memory_space=pltpu.SMEM)
VMEM_LIMIT = 60 * 1024 * 1024


def whole(array):
    return pl.BlockSpec(array.shape, lambda *_: (0,) * len(array.shape))


class Part:
    def __init__(self, array, block):
        self.array, self.block = array, block

    def spec(self):
        kept = [size for size in self.array.shape[1:] if size != 1]
        lead = len(self.array.shape) - len(kept)
        return pl.BlockSpec((None,) * lead + tuple(kept), lambda *_: (self.block,) + (0,) * (lead - 1 + len(kept)))


def call(kernel, scalars, operands, out_shapes, scratch, flops):
    specs = [operand.spec() if isinstance(operand, Part) else whole(operand) for operand in operands]
    arrays = [operand.array if isinstance(operand, Part) else operand for operand in operands]
    return pl.pallas_call(
        kernel,
        grid=(1,),
        in_specs=[SMEM] * len(scalars) + specs,
        out_specs=[whole(shape) for shape in out_shapes],
        out_shape=out_shapes,
        scratch_shapes=scratch,
        compiler_params=pltpu.CompilerParams(vmem_limit_bytes=VMEM_LIMIT),
        cost_estimate=pl.CostEstimate(flops=flops, bytes_accessed=4_000_000, transcendentals=1_000_000),
    )(*scalars, *arrays)


def shape_of(shape, dtype):
    return jax.ShapeDtypeStruct(shape, dtype)


def shifted(value, lat_steps, lon_steps):
    lon_count, lat_count = lax.axis_size("lon"), lax.axis_size("lat")
    pairs = []
    for lon in range(lon_count):
        for lat in range(lat_count):
            source = ((lon + lon_steps) % lon_count) * lat_count + (lat + lat_steps) % lat_count
            pairs.append((source, lon * lat_count + lat))
    return lax.ppermute(value, ("lon", "lat"), pairs)


def per_device(
    inputs,
    grad_out,
    region,
    bias_level,
    norm_gains,
    in_weight,
    out_weight,
    up_weight,
    down_weight,
    bias_tables,
):
    weights = (norm_gains, in_weight, out_weight, up_weight, down_weight.transpose(0, 2, 1))
    first_weights = [Part(array, 0) for array in weights]
    second_weights = [Part(array, 1) for array in weights]
    inputs, grad_out = inputs.transpose(1, 2, 0, 3), grad_out.transpose(1, 2, 0, 3)
    bias_tables = bias_tables.transpose(0, 1, 3, 2, 4)
    bias_level = bias_level.T
    quadrant = one_hot(quadrant_rows())
    rolled = one_hot(rolled_rows())
    half = [jnp.asarray(array, BF16) for array in (quadrant, quadrant.T, rolled, rolled.T)]
    to_quads, from_quads, rolled_back, rolled_ahead = half
    is_upper = (lax.axis_index("lat") & 1).astype(jnp.int32).reshape(1)

    quad_shape = shape_of((2 * QUAD, C), BF16)
    grid_shape = shape_of((6, 12, 4, C), BF16)
    half_shape = shape_of((ROWS // 2, 128), BF16)
    table_shape = shape_of((TABLE_ROWS, 128), BF16)
    weights_shape = (2 * HEADS, WIN, WIN)
    pairs_scratch = pltpu.VMEM((WIN_LON, 512, 256), BF16)
    grads_scratch = pltpu.VMEM((2, 2 * HEADS * WIN, 128), F32)
    row_scratch = pltpu.VMEM((16, 26 * 128), F32)
    shaped_scratch = pltpu.VMEM((4, 2 * 72 + 16, 128), F32)
    bias_scratch = pltpu.VMEM((2, 2 * HEADS * WIN, 128), F32)
    rows_scratch = pltpu.VMEM((2, TOKENS, 128), F32)
    packed_scratch = pltpu.VMEM((ROWS, 128), BF16)

    quads = call(
        first_kernel,
        (bias_level,),
        (inputs, grad_out, *first_weights, Part(bias_tables, 0), to_quads),
        [quad_shape] * 4
        + [
            shape_of(weights_shape, BF16),
            shape_of((2, 2, C, WIN), BF16),
            shape_of((2, WIN, C), BF16),
            shape_of((2, C, WIN), BF16),
            shape_of((TOKENS, C), BF16),
        ],
        [pairs_scratch, rows_scratch, row_scratch, shaped_scratch, bias_scratch],
        1_000_000_000,
    )
    stored = quads[4:]
    ahead = (
        quads[3],
        shifted(quads[2], 0, 1),
        shifted(quads[1], 1, 0),
        shifted(quads[0], 1, 1),
    )
    (bias,) = call(
        prepare_kernel,
        (bias_level,),
        (region.transpose(1, 0, 2), Part(bias_tables, 1)),
        [shape_of(weights_shape, BF16)],
        [pairs_scratch, row_scratch, shaped_scratch, bias_scratch],
        500_000_000,
    )
    *back, second_keep, second_send, second_scaled = call(
        second_kernel,
        (is_upper,),
        (*ahead, bias, *second_weights, rolled_ahead, rolled_back),
        [quad_shape] * 4 + [half_shape, half_shape, shape_of(weights_shape, BF16)],
        [pltpu.VMEM(weights_shape, BF16), packed_scratch],
        3_000_000_000,
    )
    second_tables, active, slope = call(
        collect_kernel,
        (bias_level,),
        (second_scaled, stored[4], first_weights[0], first_weights[3]),
        [table_shape, shape_of((TOKENS, FFN), BF16), shape_of((TOKENS, FFN), BF16)],
        [pairs_scratch, row_scratch, shaped_scratch, grads_scratch],
        500_000_000,
    )
    home = [
        shifted(back[3], -1, -1),
        shifted(back[2], -1, 0),
        shifted(back[1], 0, -1),
        back[0],
    ]
    second = added(second_keep, exchanged(second_send, CORE))
    home[3], second = lax.optimization_barrier((home[3], second))
    first_keep, first_send, grad_rows, first_scaled = call(
        third_kernel,
        (is_upper,),
        (*home, inputs, *stored, active, slope, *first_weights, from_quads),
        [half_shape, half_shape, shape_of((TOKENS, C), BF16), shape_of(weights_shape, BF16)],
        [rows_scratch, packed_scratch],
        2_000_000_000,
    )
    blocks_out, grad_inputs = call(
        grids_kernel,
        (),
        (*home, from_quads, grad_rows),
        [grid_shape, grid_shape],
        [rows_scratch],
        100_000_000,
    )
    first = added(first_keep, exchanged(first_send, CORE))
    first, first_scaled = lax.optimization_barrier((first, first_scaled))
    (tables,) = call(
        finish_kernel,
        (bias_level,),
        (first_scaled, second_tables),
        [shape_of((2 * TABLE_ROWS, 128), BF16)],
        [pairs_scratch, row_scratch, shaped_scratch, grads_scratch],
        500_000_000,
    )
    totals = unpack(is_upper, *sum_all(first, second, tables))
    gains, grad_in, grad_out_weight, grad_up, grad_down, grad_tables = totals
    return (
        blocks_out.transpose(2, 0, 1, 3),
        grad_inputs.transpose(2, 0, 1, 3),
        gains,
        grad_in,
        grad_out_weight,
        grad_up,
        grad_down.transpose(0, 2, 1),
        grad_tables.transpose(0, 1, 3, 2, 4),
    )


def exchanged(value, mask):
    lon_count, lat_count = lax.axis_size("lon"), lax.axis_size("lat")
    pairs = []
    for lon in range(lon_count):
        for lat in range(lat_count):
            pairs.append(((lon ^ mask[1]) * lat_count + (lat ^ mask[0]), lon * lat_count + lat))
    return lax.ppermute(value, ("lon", "lat"), pairs)


def added(left, right):
    return (left.astype(F32) + right.astype(F32)).astype(BF16)


def odd(mask):
    lat, lon = lax.axis_index("lat") & mask[0], lax.axis_index("lon") & mask[1]
    parity = jnp.int32(0)
    for place in range(5):
        parity = parity ^ (lat >> place) ^ (lon >> place)
    return (parity & 1) != 0


def split(value, owner):
    half = value.shape[0] // 2
    up = odd(owner)
    return jnp.where(up, value[half:], value[:half]), jnp.where(up, value[:half], value[half:])


def halve(value, mask, owner):
    keep, send = split(value, owner)
    return added(keep, exchanged(send, mask))


def double(value, mask, owner):
    other = exchanged(value, mask)
    up = odd(owner)
    return jnp.concatenate([jnp.where(up, other, value), jnp.where(up, value, other)], axis=0)


CORE = (1, 0)


def sum_all(first, second, tables):
    if lax.axis_size("lat") != 16 or lax.axis_size("lon") != 16:
        return sum_small(first, second, tables)
    y_low, y_high = ((2, 0), (2, 0)), (0, 8)
    x_low, x_high = ((4, 0), (12, 0)), ((12, 0), (8, 0))
    z_low, z_mid, z_high = ((0, 1), (0, 5)), ((0, 2), (0, 6)), (0, 7)
    tie = lax.optimization_barrier

    second = halve(second, *x_low)
    first = halve(first, *y_low)
    first, second = tie((first, second))
    first, second = halve(first, *x_low), halve(second, *y_low)
    rows = first.shape[0]
    joined = halve(jnp.concatenate([first, second], axis=0), *x_high)
    joined, tables = tie((joined, tables))
    for mask, owner in (z_low, z_mid):
        keep, send = split(tables, owner)
        got = exchanged(jnp.concatenate([joined, send], axis=0), mask)
        joined, tables = added(joined, got[:rows]), added(keep, got[rows:])
    joined = jnp.concatenate([joined, tables], axis=0)
    for mask in (z_high, y_high):
        joined = added(joined, exchanged(joined, mask))
    joined, tables = tie((joined[:rows], joined[rows:]))
    joined, tables = double(joined, *x_high), double(tables, *z_mid)
    first, second, tables = tie((joined[:rows], joined[rows:], tables))
    first, second, tables = double(first, *x_low), double(second, *y_low), double(tables, *z_low)
    first, second, tables = tie((first, second, tables))
    first, second = double(first, *y_low), double(second, *x_low)
    first, second = tie((first, second))
    return first, exchanged(first, CORE), second, exchanged(second, CORE), tables


def sum_small(first, second, tables):
    def over(value, axis):
        for place in range(lax.axis_size(axis).bit_length() - 1):
            if axis == "lon" or place:
                value = added(value, exchanged(value, (1 << place, 0) if axis == "lat" else (0, 1 << place)))
        return value

    first, second = over(over(first, "lat"), "lon"), over(over(second, "lat"), "lon")
    return first, exchanged(first, CORE), second, exchanged(second, CORE), over(tables, "lon")


def unpack_kernel(
    upper_ref,
    first_own,
    first_other,
    second_own,
    second_other,
    tables_ref,
    gains_ref,
    in_ref,
    out_ref,
    up_ref,
    down_ref,
    grads_ref,
    rows_ref,
):
    half = ROWS // 2
    is_upper = jnp.broadcast_to(upper_ref[0] == 1, (1, 128))
    for block, (own, other) in enumerate(((first_own, first_other), (second_own, second_other))):

        def rows(start, stop, own=own, other=other):
            if start < half < stop:
                return jnp.concatenate([rows(start, half), rows(half, stop)], axis=0)
            lower = start < half
            start, stop = (start, stop) if lower else (start - half, stop - half)
            mine, theirs = own[start:stop].astype(F32), other[start:stop].astype(F32)
            return jnp.where(is_upper, theirs, mine) if lower else jnp.where(is_upper, mine, theirs)

        rows_ref[...] = tables_ref[block * TABLE_ROWS : (block + 1) * TABLE_ROWS].astype(F32)
        for part in range(4):
            in_ref[block, :, part * 128 : (part + 1) * 128] = rows(part * C, (part + 1) * C)
        shared = rows(768, 960)
        in_ref[block, :, 512:] = shared[:, :64]
        out_ref[block, :, :128] = rows(960, 1152)
        out_ref[block, :, 128:] = shared[:, 64:]
        for part in range(6):
            lanes = slice(part * 128, (part + 1) * 128)
            up_ref[block, :, lanes] = rows(1152 + part * C, 1152 + (part + 1) * C)
            down_ref[block, :, lanes] = rows(2304 + part * C, 2304 + (part + 1) * C)
        gains = rows(GAIN_ROWS, GAIN_ROWS + 16)
        gains_ref[block, 0:1, :128] = gains[0:1]
        gains_ref[block, 0:1, 128:] = gains[1:2, :64]
        gains_ref[block, 1:2, :128] = gains[2:3]
        gains_ref[block, 1:2, 128:] = gains[1:2, 64:]
        for slab in range(26):
            width = min(128, RELPOS - slab * 128)
            for level in range(2):
                start = slab * 12 + level * HEADS
                grads_ref[block, 0, :, level, slab * 128 : slab * 128 + width] = rows_ref[start : start + HEADS, :width]


def unpack(is_upper, *values):
    return call(
        unpack_kernel,
        (is_upper,),
        values,
        [
            shape_of((2, 2, C), F32),
            shape_of((2, C, 3 * C), F32),
            shape_of((2, C, C), F32),
            shape_of((2, C, FFN), F32),
            shape_of((2, C, FFN), F32),
            shape_of((2, 1, HEADS, 2, RELPOS), F32),
        ],
        [pltpu.VMEM((TABLE_ROWS, 128), F32)],
        1_000_000,
    )


def solution(mesh):
    placed = (
        P(None, "lat", "lon", None),
        P(None, "lat", "lon", None),
        P(None, "lat", "lon"),
        P(None, "lat"),
        P(),
        P(),
        P(),
        P(),
        P(),
        P(None, "lat", None, None, None),
    )
    return jax.shard_map(
        per_device,
        mesh=mesh,
        in_specs=placed,
        out_specs=(
            P(None, "lat", "lon", None),
            P(None, "lat", "lon", None),
            P(),
            P(),
            P(),
            P(),
            P(),
            P(None, "lat", None, None, None),
        ),
        check_vma=False,
    )
```

time: 160 us -> 138 us (0.86)
  waiting for transfers between devices: 77.8 us -> 48.1 us
  Pallas kernels: 35.6 us -> 44.5 us
  other arithmetic: 6.73 us -> 3.83 us
    ppermute x14 -> x20, waiting for transfers between devices: 67.2 us -> 43 us  [exchanged(): return lax.ppermute(value, ('lon', 'lat'), pairs)]
    pallas_call x4 -> x8, Pallas kernels: 35.6 us -> 44.5 us  [call(): pl.pallas_call(kernel, grid=(1,), in_specs=[SMEM] * len(scalars) + specs,...]
    ppermute x6, waiting for transfers between devices: 10.6 us -> 5.09 us  [shifted(): return lax.ppermute(value, ('lon', 'lat'), pairs)]
    ppermute x14 -> x20, starting transfers between devices: 22.2 us -> 22.1 us  [exchanged(): return lax.ppermute(value, ('lon', 'lat'), pairs)]
  transfers between devices with their start and end apart: 20 -> 26, of which waited for: 17 -> 18; matrix products, arithmetic and copies ran while one was open for 1% -> 2% of each run, Pallas kernels for 0% -> 9%
where the time goes in v2:
time: 138 us; the launch traced here: 137 us
  waiting for transfers between devices  48.1 us (35%)
  Pallas kernels  44.5 us (32%)
  starting transfers between devices  36.3 us (26%)
  other arithmetic  3.83 us (3%)
  local copies, waits for them, and re-layouts  2.87 us (2%)
    pallas_call x8, Pallas kernels, call(): pl.pallas_call(kernel, grid=(1,), in_specs=[SMEM] * len(scalars) + specs,...  44.5 us
    ppermute x20, waiting for transfers between devices, exchanged(): return lax.ppermute(value, ('lon', 'lat'), pairs)  43 us
    ppermute x20, starting transfers between devices, exchanged(): return lax.ppermute(value, ('lon', 'lat'), pairs)  22.1 us
    ppermute x6, starting transfers between devices, shifted(): return lax.ppermute(value, ('lon', 'lat'), pairs)  14.2 us
    ppermute x6, waiting for transfers between devices, shifted(): return lax.ppermute(value, ('lon', 'lat'), pairs)  5.09 us
    unnamed x24, local copies, waits for them, and re-layouts  2.85 us
  transfers between devices with their start and end apart: 26, of which 18 were waited for; matrix products, arithmetic and copies ran while one was open for 2% of the time, Pallas kernels for 9%

profile of v2, /device:TPU:1, one launch (start us, length us, event | category | flops | bytes accessed | tf_op | source)
XLA Modules:
  0.0 136.7 jit_solution(13841034040098346631)
XLA Ops:
  0.6 7.7 %shard_map.197 = (bf16[144,192]{1,0:T(8,128)(2,1)}, bf16[144,192]{1,0:T(8,128)(2,1)}, bf16[144,192]{1,0:T(8,128)(2,1)}, bf16[144,192]{1,0:T(8,128)(2,1)}, bf16[1...) custom-call(s32[1,2]{1,0:T(1,128)} %bitcast.22, ...), custom_call_target="tpu_custom_call" | custom-call | flops 1000000000 | bytes 4000000 | tf_op jit(solution)/shard_map/pallas_call | solution.py:590
  8.4 9.0 %collective-permute-start = (bf16[144,192]{1,0:T(8,128)(2,1)}, bf16[144,192]{1,0:T(8,128)(2,1)S(1)}, u32[]{:S(2)}, u32[]{:S(2)}) collective-permute-start(bf16[144,192]{1,0:T(8,128)(2,1)} %get-tuple-element.58), channel_id=1, source_target_pairs={{16,0},{17,1},{18,2},{19,3},{20,4},{21,5},{22,6},{23,7},{24,8},{25... | collective-permute-start | bytes 165896 | tf_op jit(solution)/shard_map/ppermute | solution.py:613
  17.4 1.0 collective-permute-start.1
  18.3 3.2 %collective-permute-start.2 = (bf16[144,192]{1,0:T(8,128)(2,1)}, bf16[144,192]{1,0:T(8,128)(2,1)S(1)}, u32[]{:S(2)}, u32[]{:S(2)}) collective-permute-start(bf16[144,192]{1,0:T(8,128)(2,1)} %get-tuple-element.60), channel_id=1, source_target_pairs={{17,0},{18,1},{19,2},{20,3},{21,4},{22,5},{23,6},{24,7},{25,8},{26... | collective-permute-start | bytes 165896 | tf_op jit(solution)/shard_map/ppermute | solution.py:613
  21.6 3.0 %shard_map.198.bias_ref = bf16[12,144,144]{2,1,0:T(8,128)(2,1)} custom-call(s32[1,2]{1,0:T(1,128)} %bitcast.23, s32[6,4,12]{2,1,0:T(4,128)} %bitcast.21, bf16[2,1,6,2,3312]{4,3,2,1,0:T(2,128)(2,1)} %bitcast.17), custom_call_target="tpu_custom_call" | custom-call | flops 500000000 | bytes 4000000 | tf_op jit(solution)/shard_map/pallas_call | solution.py:590
  25.3 12.0 %shard_map.199 = (bf16[144,192]{1,0:T(8,128)(2,1)}, bf16[144,192]{1,0:T(8,128)(2,1)}, bf16[144,192]{1,0:T(8,128)(2,1)}, bf16[144,192]{1,0:T(8,128)(2,1)}, bf16[1...) custom-call(s32[1]{0:T(128)} %bitcast.upper_ref, ...), custom_call_target="tpu_custom_call" | custom-call | flops 3000000000 | bytes 4000000 | tf_op jit(solution)/shard_map/pallas_call | solution.py:590
  38.3 4.0 %shard_map.200 = (bf16[320,128]{1,0:T(8,128)(2,1)}, bf16[288,768]{1,0:T(8,128)(2,1)}, bf16[288,768]{1,0:T(8,128)(2,1)}) custom-call(s32[1,2]{1,0:T(1,128)} %bitcast.24, bf16[12,144,144]{2,1,0:T(8,128)(2,1)} %get-tuple-element.73.scaled_ref, bf16[288,192]{1,0:T(8,128)(2,1)} %get-tuple-element.72.hidden_ref, f32[2,2,192]{2,1,0:T(2,128)} %gains_ref.7, ...), custom_call_target="tpu_custom_call" | custom-call | flops 500000000 | bytes 4000000 | tf_op jit(solution)/shard_map/pallas_call | solution.py:590
  42.4 3.3 %collective-permute-done.3.quad_0 = bf16[144,192]{1,0:T(8,128)(2,1)S(1)} collective-permute-done((bf16[144,192]{1,0:T(8,128)(2,1)}, bf16[144,192]{1,0:T(8,128)(2,1)S(1)}, u32[]{:S(2)}, u32[]{:S(2)}) %collective-permute-start.3) | collective-permute-done | bytes 55328 | tf_op jit(solution)/shard_map/ppermute | solution.py:613
  45.7 1.8 %collective-permute-done.5.quad_2 = bf16[144,192]{1,0:T(8,128)(2,1)S(1)} collective-permute-done((bf16[144,192]{1,0:T(8,128)(2,1)}, bf16[144,192]{1,0:T(8,128)(2,1)S(1)}, u32[]{:S(2)}, u32[]{:S(2)}) %collective-permute-start.5) | collective-permute-done | bytes 55328 | tf_op jit(solution)/shard_map/ppermute | solution.py:613
  48.2 8.7 %shard_map.201 = (bf16[1792,128]{1,0:T(8,128)(2,1)}, bf16[1792,128]{1,0:T(8,128)(2,1)}, bf16[288,192]{1,0:T(8,128)(2,1)}, bf16[12,144,144]{2,1,0:T(8,128)(2,1)}) custom-call(s32[1]{0:T(128)} %bitcast.upper_ref, bf16[144,192]{1,0:T(8,128)(2,1)} %copy-done.6, bf16[144,192]{1,0:T(8,128)(2,1)} %copy-done.7, bf16[144,192]{1,0:T(8,128)(2,1)} %copy-done.8, ...), custom_call_target="tpu_custom_call" | custom-call | flops 2000000000 | bytes 4000000 | tf_op jit(solution)/shard_map/pallas_call | solution.py:590
  56.9 1.0 collective-permute-start.7
  58.0 1.5 %collective-permute-done.7 = bf16[1792,128]{1,0:T(8,128)(2,1)S(1)} collective-permute-done((bf16[1792,128]{1,0:T(8,128)(2,1)}, bf16[1792,128]{1,0:T(8,128)(2,1)S(1)}, u32[]{:S(2)}, u32[]{:S(2)}) %collective-permute-start.7) | collective-permute-done | bytes 458784 | tf_op jit(solution)/shard_map/ppermute | solution.py:753
  59.5 1.1 add_convert_fusion
  60.8 4.4 %collective-permute-done.9 = bf16[896,128]{1,0:T(8,128)(2,1)S(1)} collective-permute-done((bf16[896,128]{1,0:T(8,128)(2,1)S(1)}, bf16[896,128]{1,0:T(8,128)(2,1)S(1)}, u32[]{:S(2)}, u32[]{:S(2)}) %collective-permute-start.9) | collective-permute-done | bytes 229408 | tf_op jit(solution)/shard_map/ppermute | solution.py:753
  65.2 2.3 %collective-permute-done.8 = bf16[896,128]{1,0:T(8,128)(2,1)S(1)} collective-permute-done((bf16[896,128]{1,0:T(8,128)(2,1)S(1)}, bf16[896,128]{1,0:T(8,128)(2,1)S(1)}, u32[]{:S(2)}, u32[]{:S(2)}) %collective-permute-start.8) | collective-permute-done | bytes 229408 | tf_op jit(solution)/shard_map/ppermute | solution.py:753
  68.2 3.2 %collective-permute-done.11 = bf16[448,128]{1,0:T(8,128)(2,1)S(1)} collective-permute-done((bf16[448,128]{1,0:T(8,128)(2,1)S(1)}, bf16[448,128]{1,0:T(8,128)(2,1)S(1)}, u32[]{:S(2)}, u32[]{:S(2)}) %collective-permute-start.11) | collective-permute-done | bytes 114720 | tf_op jit(solution)/shard_map/ppermute | solution.py:753
  71.6 1.4 %collective-permute-start.12 = (bf16[448,128]{1,0:T(8,128)(2,1)S(1)}, bf16[448,128]{1,0:T(8,128)(2,1)S(1)}, u32[]{:S(2)}, u32[]{:S(2)}) collective-permute-start(bf16[448,128]{1,0:T(8,128)(2,1)S(1)} %get-tuple-element.106), channel_id=1, source_target_pairs={{12,0},{13,1},{14,2},{15,3},{8,4},{9,5},{10,6},{11,7},{4,8},{5,9},... | collective-permute-start | bytes 344072 | tf_op jit(solution)/shard_map/ppermute | solution.py:753
  73.0 3.4 %shard_map.203 = bf16[640,128]{1,0:T(8,128)(2,1)} custom-call(s32[1,2]{1,0:T(1,128)} %bitcast.25, bf16[12,144,144]{2,1,0:T(8,128)(2,1)} %get-tuple-element.86.scaled_ref, bf16[320,128]{1,0:T(8,128)(2,1)} %get-tuple-element.87.second_tables_ref), custom_call_target="tpu_custom_call" | custom-call | flops 500000000 | bytes 4000000 | tf_op jit(solution)/shard_map/pallas_call | solution.py:590
  76.6 0.9 broadcast_select_fusion.17
  77.7 4.5 %collective-permute-done.13 = bf16[768,128]{1,0:T(8,128)(2,1)S(1)} collective-permute-done((bf16[768,128]{1,0:T(8,128)(2,1)S(1)}, bf16[768,128]{1,0:T(8,128)(2,1)S(1)}, u32[]{:S(2)}, u32[]{:S(2)}) %collective-permute-start.13) | collective-permute-done | bytes 196640 | tf_op jit(solution)/shard_map/ppermute | solution.py:753
  82.4 6.4 %collective-permute-done.14 = bf16[608,128]{1,0:T(8,128)(2,1)S(1)} collective-permute-done((bf16[608,128]{1,0:T(8,128)(2,1)S(1)}, bf16[608,128]{1,0:T(8,128)(2,1)S(1)}, u32[]{:S(2)}, u32[]{:S(2)}) %collective-permute-start.14) | collective-permute-done | bytes 155680 | tf_op jit(solution)/shard_map/ppermute | solution.py:753
  89.6 6.5 %collective-permute-done.15 = bf16[608,128]{1,0:T(8,128)(2,1)S(1)} collective-permute-done((bf16[608,128]{1,0:T(8,128)(2,1)S(1)}, bf16[608,128]{1,0:T(8,128)(2,1)S(1)}, u32[]{:S(2)}, u32[]{:S(2)}) %collective-permute-start.15) | collective-permute-done | bytes 155680 | tf_op jit(solution)/shard_map/ppermute | solution.py:753
  96.8 5.0 %collective-permute-done.16 = bf16[608,128]{1,0:T(8,128)(2,1)S(1)} collective-permute-done((bf16[608,128]{1,0:T(8,128)(2,1)S(1)}, bf16[608,128]{1,0:T(8,128)(2,1)S(1)}, u32[]{:S(2)}, u32[]{:S(2)}) %collective-permute-start.16) | collective-permute-done | bytes 155680 | tf_op jit(solution)/shard_map/ppermute | solution.py:753
  102.3 1.7 %collective-permute-start.17 = (bf16[448,128]{1,0:T(8,128)(2,1)S(1)}, bf16[448,128]{1,0:T(8,128)(2,1)S(1)}, u32[]{:S(2)}, u32[]{:S(2)}) collective-permute-start(bf16[448,128]{1,0:T(8,128)(2,1)S(1)} %slice.90), channel_id=1, source_target_pairs={{12,0},{13,1},{14,2},{15,3},{8,4},{9,5},{10,6},{11,7},{4,8},{5,9},... | collective-permute-start | bytes 344072 | tf_op jit(solution)/shard_map/ppermute | solution.py:753
  104.0 1.8 %collective-permute-done.18 = bf16[160,128]{1,0:T(8,128)(2,1)S(1)} collective-permute-done((bf16[160,128]{1,0:T(8,128)(2,1)S(1)}, bf16[160,128]{1,0:T(8,128)(2,1)S(1)}, u32[]{:S(2)}, u32[]{:S(2)}) %collective-permute-start.18) | collective-permute-done | bytes 40992 | tf_op jit(solution)/shard_map/ppermute | solution.py:753
  105.8 1.3 collective-permute-done.17
  108.5 2.1 %collective-permute-done.21 = bf16[320,128]{1,0:T(8,128)(2,1)S(1)} collective-permute-done((bf16[320,128]{1,0:T(8,128)(2,1)S(1)}, bf16[320,128]{1,0:T(8,128)(2,1)S(1)}, u32[]{:S(2)}, u32[]{:S(2)}) %collective-permute-start.21) | collective-permute-done | bytes 81952 | tf_op jit(solution)/shard_map/ppermute | solution.py:753
  112.3 1.2 collective-permute-start.23
  113.5 2.9 %collective-permute-done.22 = bf16[896,128]{1,0:T(8,128)(2,1)S(1)} collective-permute-done((bf16[896,128]{1,0:T(8,128)(2,1)S(1)}, bf16[896,128]{1,0:T(8,128)(2,1)S(1)}, u32[]{:S(2)}, u32[]{:S(2)}) %collective-permute-start.22) | collective-permute-done | bytes 229408 | tf_op jit(solution)/shard_map/ppermute | solution.py:753
  117.3 12.0 %collective-permute-start.24 = (bf16[1792,128]{1,0:T(8,128)(2,1)S(1)}, bf16[1792,128]{1,0:T(8,128)(2,1)S(1)}, u32[]{:S(2)}, u32[]{:S(2)}) collective-permute-start(bf16[1792,128]{1,0:T(8,128)(2,1)S(1)} %pad_maximum_fusion.first_own), channel_id=1, source_target_pairs={{1,0},{0,1},{3,2},{2,3},{5,4},{4,5},{7,6},{6,7},{9,8},{8,9},{11,10... | collective-permute-start | bytes 1376264 | tf_op jit(solution)/shard_map/ppermute | solution.py:753
  129.4 2.2 %shard_map.202 = (bf16[6,12,4,192]{3,2,1,0:T(4,128)(2,1)}, bf16[6,12,4,192]{3,2,1,0:T(4,128)(2,1)}) custom-call(bf16[144,192]{1,0:T(8,128)(2,1)} %copy-done.6, bf16[144,192]{1,0:T(8,128)(2,1)} %copy-done.7, bf16[144,192]{1,0:T(8,128)(2,1)} %copy-done.8, bf16[144,192]{1,0:T(8,128)(2,1)} %get-tuple-element.67.quad_3, ...), custom_call_target="tpu_custom_call" | custom-call | flops 100000000 | bytes 4000000 | tf_op jit(solution)/shard_map/pallas_call | solution.py:590
  133.1 3.5 %shard_map.204 = (f32[2,2,192]{2,1,0:T(2,128)}, f32[2,192,576]{2,1,0:T(8,128)}, f32[2,192,192]{2,1,0:T(8,128)}, f32[2,192,768]{2,1,0:T(8,128)}, f32[2,192,768]{2,1,0:T(8,128)}, /*index=5*/f32[2,1,6,2,3312]{4,3,2,1,0:T(2,128)}) custom-call(s32[1]{0:T(128)} %bitcast.upper_ref, bf16[1792,128]{1,0:T(8,128)(2,1)} %copy-done, bf16[1792,128]{1,0:T(8,128)(2,1)} %copy-done.3, ...), custom_call_target="tpu_custom_call" | custom-call | flops 1000000 | bytes 4000000 | tf_op jit(solution)/shard_map/pallas_call | solution.py:590
  (87 shorter events, 11.6 us)
Async XLA Ops:
  8.4 16.2 %collective-permute-start = (bf16[144,192]{1,0:T(8,128)(2,1)}, bf16[144,192]{1,0:T(8,128)(2,1)S(1)}, u32[]{:S(2)}, u32[]{:S(2)}) collective-permute-start(bf16[144,192]{1,0:T(8,128)(2,1)} %get-tuple-element.58), channel_id=1, source_target_pairs={{16,0},{17,1},{18,2},{19,3},{20,4},{21,5},{22,6},{23,7},{24,8},{25... | collective-permute-start | bytes 165896 | tf_op jit(solution)/shard_map/ppermute | solution.py:613
  17.4 7.2 %collective-permute-start.1 = (bf16[144,192]{1,0:T(8,128)(2,1)}, bf16[144,192]{1,0:T(8,128)(2,1)S(1)}, u32[]{:S(2)}, u32[]{:S(2)}) collective-permute-start(bf16[144,192]{1,0:T(8,128)(2,1)} %get-tuple-element.59), channel_id=1, source_target_pairs={{1,0},{2,1},{3,2},{4,3},{5,4},{6,5},{7,6},{8,7},{9,8},{10,9},{11,1... | collective-permute-start | bytes 165896 | tf_op jit(solution)/shard_map/ppermute | solution.py:613
  18.3 6.3 %collective-permute-start.2 = (bf16[144,192]{1,0:T(8,128)(2,1)}, bf16[144,192]{1,0:T(8,128)(2,1)S(1)}, u32[]{:S(2)}, u32[]{:S(2)}) collective-permute-start(bf16[144,192]{1,0:T(8,128)(2,1)} %get-tuple-element.60), channel_id=1, source_target_pairs={{17,0},{18,1},{19,2},{20,3},{21,4},{22,5},{23,6},{24,7},{25,8},{26... | collective-permute-start | bytes 165896 | tf_op jit(solution)/shard_map/ppermute | solution.py:613
  37.3 5.0 %copy-start.5 = (bf16[1792,128]{1,0:T(8,128)(2,1)S(1)}, bf16[1792,128]{1,0:T(8,128)(2,1)}, u32[]{:S(2)}) copy-start(bf16[1792,128]{1,0:T(8,128)(2,1)} %get-tuple-element.65) | copy-start | bytes 1376260
  37.3 5.0 %collective-permute-start.6 = (bf16[1792,128]{1,0:T(8,128)(2,1)}, bf16[1792,128]{1,0:T(8,128)(2,1)S(1)}, u32[]{:S(2)}, u32[]{:S(2)}) collective-permute-start(bf16[1792,128]{1,0:T(8,128)(2,1)} %get-tuple-element.66), channel_id=1, source_target_pairs={{1,0},{0,1},{3,2},{2,3},{5,4},{4,5},{7,6},{6,7},{9,8},{8,9},{11,10... | collective-permute-start | bytes 1376264 | tf_op jit(solution)/shard_map/ppermute | solution.py:753
  37.3 8.4 %collective-permute-start.3 = (bf16[144,192]{1,0:T(8,128)(2,1)}, bf16[144,192]{1,0:T(8,128)(2,1)S(1)}, u32[]{:S(2)}, u32[]{:S(2)}) collective-permute-start(bf16[144,192]{1,0:T(8,128)(2,1)} %get-tuple-element.61), channel_id=1, source_target_pairs={{255,0},{240,1},{241,2},{242,3},{243,4},{244,5},{245,6},{246,7},{2... | collective-permute-start | bytes 165896 | tf_op jit(solution)/shard_map/ppermute | solution.py:613
  37.4 8.3 %collective-permute-start.4 = (bf16[144,192]{1,0:T(8,128)(2,1)}, bf16[144,192]{1,0:T(8,128)(2,1)S(1)}, u32[]{:S(2)}, u32[]{:S(2)}) collective-permute-start(bf16[144,192]{1,0:T(8,128)(2,1)} %get-tuple-element.62), channel_id=1, source_target_pairs={{15,0},{0,1},{1,2},{2,3},{3,4},{4,5},{5,6},{6,7},{7,8},{8,9},{9,10... | collective-permute-start | bytes 165896 | tf_op jit(solution)/shard_map/ppermute | solution.py:613
  37.6 9.9 %collective-permute-start.5 = (bf16[144,192]{1,0:T(8,128)(2,1)}, bf16[144,192]{1,0:T(8,128)(2,1)S(1)}, u32[]{:S(2)}, u32[]{:S(2)}) collective-permute-start(bf16[144,192]{1,0:T(8,128)(2,1)} %get-tuple-element.63), channel_id=1, source_target_pairs={{240,0},{241,1},{242,2},{243,3},{244,4},{245,5},{246,6},{247,7},{2... | collective-permute-start | bytes 165896 | tf_op jit(solution)/shard_map/ppermute | solution.py:613
  45.7 1.8 %copy-start.6 = (bf16[144,192]{1,0:T(8,128)(2,1)}, bf16[144,192]{1,0:T(8,128)(2,1)S(1)}, u32[]{:S(2)}) copy-start(bf16[144,192]{1,0:T(8,128)(2,1)S(1)} %collective-permute-done.3.quad_0) | copy-start | bytes 165892
  45.7 1.8 %copy-start.7 = (bf16[144,192]{1,0:T(8,128)(2,1)}, bf16[144,192]{1,0:T(8,128)(2,1)S(1)}, u32[]{:S(2)}) copy-start(bf16[144,192]{1,0:T(8,128)(2,1)S(1)} %collective-permute-done.4.quad_1) | copy-start | bytes 165892
  56.9 2.6 %collective-permute-start.7 = (bf16[1792,128]{1,0:T(8,128)(2,1)}, bf16[1792,128]{1,0:T(8,128)(2,1)S(1)}, u32[]{:S(2)}, u32[]{:S(2)}) collective-permute-start(bf16[1792,128]{1,0:T(8,128)(2,1)} %get-tuple-element.80), channel_id=1, source_target_pairs={{1,0},{0,1},{3,2},{2,3},{5,4},{4,5},{7,6},{6,7},{9,8},{8,9},{11,10... | collective-permute-start | bytes 1376264 | tf_op jit(solution)/shard_map/ppermute | solution.py:753
  57.9 7.3 %collective-permute-start.9 = (bf16[896,128]{1,0:T(8,128)(2,1)S(1)}, bf16[896,128]{1,0:T(8,128)(2,1)S(1)}, u32[]{:S(2)}, u32[]{:S(2)}) collective-permute-start(bf16[896,128]{1,0:T(8,128)(2,1)S(1)} %broadcast_select_fusion.2), channel_id=1, source_target_pairs={{4,0},{5,1},{6,2},{7,3},{0,4},{1,5},{2,6},{3,7},{12,8},{13,9},{14,... | collective-permute-start | bytes 688136 | tf_op jit(solution)/shard_map/ppermute | solution.py:753
  60.7 6.9 %collective-permute-start.8 = (bf16[896,128]{1,0:T(8,128)(2,1)S(1)}, bf16[896,128]{1,0:T(8,128)(2,1)S(1)}, u32[]{:S(2)}, u32[]{:S(2)}) collective-permute-start(bf16[896,128]{1,0:T(8,128)(2,1)S(1)} %broadcast_select_fusion.5), channel_id=1, source_target_pairs={{2,0},{3,1},{0,2},{1,3},{6,4},{7,5},{4,6},{5,7},{10,8},{11,9},{8,1... | collective-permute-start | bytes 688136 | tf_op jit(solution)/shard_map/ppermute | solution.py:753
  67.7 3.7 %collective-permute-start.11 = (bf16[448,128]{1,0:T(8,128)(2,1)S(1)}, bf16[448,128]{1,0:T(8,128)(2,1)S(1)}, u32[]{:S(2)}, u32[]{:S(2)}) collective-permute-start(bf16[448,128]{1,0:T(8,128)(2,1)S(1)} %broadcast_select_fusion.14), channel_id=1, source_target_pairs={{4,0},{5,1},{6,2},{7,3},{0,4},{1,5},{2,6},{3,7},{12,8},{13,9},{14,... | collective-permute-start | bytes 344072 | tf_op jit(solution)/shard_map/ppermute | solution.py:753
  67.8 3.7 %collective-permute-start.10 = (bf16[448,128]{1,0:T(8,128)(2,1)S(1)}, bf16[448,128]{1,0:T(8,128)(2,1)S(1)}, u32[]{:S(2)}, u32[]{:S(2)}) collective-permute-start(bf16[448,128]{1,0:T(8,128)(2,1)S(1)} %broadcast_select_fusion.8), channel_id=1, source_target_pairs={{2,0},{3,1},{0,2},{1,3},{6,4},{7,5},{4,6},{5,7},{10,8},{11,9},{8,1... | collective-permute-start | bytes 344072 | tf_op jit(solution)/shard_map/ppermute | solution.py:753
  71.6 4.9 %collective-permute-start.12 = (bf16[448,128]{1,0:T(8,128)(2,1)S(1)}, bf16[448,128]{1,0:T(8,128)(2,1)S(1)}, u32[]{:S(2)}, u32[]{:S(2)}) collective-permute-start(bf16[448,128]{1,0:T(8,128)(2,1)S(1)} %get-tuple-element.106), channel_id=1, source_target_pairs={{12,0},{13,1},{14,2},{15,3},{8,4},{9,5},{10,6},{11,7},{4,8},{5,9},... | collective-permute-start | bytes 344072 | tf_op jit(solution)/shard_map/ppermute | solution.py:753
  76.4 5.8 %copy-start.2 = (bf16[640,128]{1,0:T(8,128)(2,1)S(1)}, bf16[640,128]{1,0:T(8,128)(2,1)}, u32[]{:S(2)}) copy-start(bf16[640,128]{1,0:T(8,128)(2,1)} %shard_map.203) | copy-start | bytes 491524
  77.6 4.6 %collective-permute-start.13 = (bf16[768,128]{1,0:T(8,128)(2,1)S(1)}, bf16[768,128]{1,0:T(8,128)(2,1)S(1)}, u32[]{:S(2)}, u32[]{:S(2)}) collective-permute-start(bf16[768,128]{1,0:T(8,128)(2,1)S(1)} %pad_maximum_fusion.4), channel_id=1, source_target_pairs={{16,0},{17,1},{18,2},{19,3},{20,4},{21,5},{22,6},{23,7},{24,8},{25... | collective-permute-start | bytes 589832 | tf_op jit(solution)/shard_map/ppermute | solution.py:753
  82.3 6.5 %collective-permute-start.14 = (bf16[608,128]{1,0:T(8,128)(2,1)S(1)}, bf16[608,128]{1,0:T(8,128)(2,1)S(1)}, u32[]{:S(2)}, u32[]{:S(2)}) collective-permute-start(bf16[608,128]{1,0:T(8,128)(2,1)S(1)} %pad_maximum_fusion.6), channel_id=1, source_target_pairs={{32,0},{33,1},{34,2},{35,3},{36,4},{37,5},{38,6},{39,7},{40,8},{41... | collective-permute-start | bytes 466952 | tf_op jit(solution)/shard_map/ppermute | solution.py:753
  88.9 7.2 %collective-permute-start.15 = (bf16[608,128]{1,0:T(8,128)(2,1)S(1)}, bf16[608,128]{1,0:T(8,128)(2,1)S(1)}, u32[]{:S(2)}, u32[]{:S(2)}) collective-permute-start(bf16[608,128]{1,0:T(8,128)(2,1)S(1)} %pad_maximum_fusion.7), channel_id=1, source_target_pairs={{112,0},{113,1},{114,2},{115,3},{116,4},{117,5},{118,6},{119,7},{1... | collective-permute-start | bytes 466952 | tf_op jit(solution)/shard_map/ppermute | solution.py:753
  96.2 5.7 %collective-permute-start.16 = (bf16[608,128]{1,0:T(8,128)(2,1)S(1)}, bf16[608,128]{1,0:T(8,128)(2,1)S(1)}, u32[]{:S(2)}, u32[]{:S(2)}) collective-permute-start(bf16[608,128]{1,0:T(8,128)(2,1)S(1)} %add_convert_fusion.5), channel_id=1, source_target_pairs={{128,0},{129,1},{130,2},{131,3},{132,4},{133,5},{134,6},{135,7},{1... | collective-permute-start | bytes 466952 | tf_op jit(solution)/shard_map/ppermute | solution.py:753
  101.9 3.9 %collective-permute-start.18 = (bf16[160,128]{1,0:T(8,128)(2,1)S(1)}, bf16[160,128]{1,0:T(8,128)(2,1)S(1)}, u32[]{:S(2)}, u32[]{:S(2)}) collective-permute-start(bf16[160,128]{1,0:T(8,128)(2,1)S(1)} %slice.91), channel_id=1, source_target_pairs={{32,0},{33,1},{34,2},{35,3},{36,4},{37,5},{38,6},{39,7},{40,8},{41... | collective-permute-start | bytes 122888 | tf_op jit(solution)/shard_map/ppermute | solution.py:753
  102.3 4.9 %collective-permute-start.17 = (bf16[448,128]{1,0:T(8,128)(2,1)S(1)}, bf16[448,128]{1,0:T(8,128)(2,1)S(1)}, u32[]{:S(2)}, u32[]{:S(2)}) collective-permute-start(bf16[448,128]{1,0:T(8,128)(2,1)S(1)} %slice.90), channel_id=1, source_target_pairs={{12,0},{13,1},{14,2},{15,3},{8,4},{9,5},{10,6},{11,7},{4,8},{5,9},... | collective-permute-start | bytes 344072 | tf_op jit(solution)/shard_map/ppermute | solution.py:753
  107.2 3.4 %collective-permute-start.21 = (bf16[320,128]{1,0:T(8,128)(2,1)S(1)}, bf16[320,128]{1,0:T(8,128)(2,1)S(1)}, u32[]{:S(2)}, u32[]{:S(2)}) collective-permute-start(bf16[320,128]{1,0:T(8,128)(2,1)S(1)} %pad_maximum_fusion.8), channel_id=1, source_target_pairs={{16,0},{17,1},{18,2},{19,3},{20,4},{21,5},{22,6},{23,7},{24,8},{25... | collective-permute-start | bytes 245768 | tf_op jit(solution)/shard_map/ppermute | solution.py:753
  107.7 3.6 %collective-permute-start.19 = (bf16[448,128]{1,0:T(8,128)(2,1)S(1)}, bf16[448,128]{1,0:T(8,128)(2,1)S(1)}, u32[]{:S(2)}, u32[]{:S(2)}) collective-permute-start(bf16[448,128]{1,0:T(8,128)(2,1)S(1)} %get-tuple-element.92), channel_id=1, source_target_pairs={{4,0},{5,1},{6,2},{7,3},{0,4},{1,5},{2,6},{3,7},{12,8},{13,9},{14,... | collective-permute-start | bytes 344072 | tf_op jit(solution)/shard_map/ppermute | solution.py:753
  107.7 3.7 %collective-permute-start.20 = (bf16[448,128]{1,0:T(8,128)(2,1)S(1)}, bf16[448,128]{1,0:T(8,128)(2,1)S(1)}, u32[]{:S(2)}, u32[]{:S(2)}) collective-permute-start(bf16[448,128]{1,0:T(8,128)(2,1)S(1)} %get-tuple-element.93), channel_id=1, source_target_pairs={{2,0},{3,1},{0,2},{1,3},{6,4},{7,5},{4,6},{5,7},{10,8},{11,9},{8,1... | collective-permute-start | bytes 344072 | tf_op jit(solution)/shard_map/ppermute | solution.py:753
  111.5 5.0 %collective-permute-start.22 = (bf16[896,128]{1,0:T(8,128)(2,1)S(1)}, bf16[896,128]{1,0:T(8,128)(2,1)S(1)}, u32[]{:S(2)}, u32[]{:S(2)}) collective-permute-start(bf16[896,128]{1,0:T(8,128)(2,1)S(1)} %get-tuple-element.95), channel_id=1, source_target_pairs={{2,0},{3,1},{0,2},{1,3},{6,4},{7,5},{4,6},{5,7},{10,8},{11,9},{8,1... | collective-permute-start | bytes 688136 | tf_op jit(solution)/shard_map/ppermute | solution.py:753
  112.3 4.9 %collective-permute-start.23 = (bf16[896,128]{1,0:T(8,128)(2,1)S(1)}, bf16[896,128]{1,0:T(8,128)(2,1)S(1)}, u32[]{:S(2)}, u32[]{:S(2)}) collective-permute-start(bf16[896,128]{1,0:T(8,128)(2,1)S(1)} %get-tuple-element.96), channel_id=1, source_target_pairs={{4,0},{5,1},{6,2},{7,3},{0,4},{1,5},{2,6},{3,7},{12,8},{13,9},{14,... | collective-permute-start | bytes 688136 | tf_op jit(solution)/shard_map/ppermute | solution.py:753
  116.5 15.1 %copy-start = (bf16[1792,128]{1,0:T(8,128)(2,1)}, bf16[1792,128]{1,0:T(8,128)(2,1)S(1)}, u32[]{:S(2)}) copy-start(bf16[1792,128]{1,0:T(8,128)(2,1)S(1)} %pad_maximum_fusion.first_own) | copy-start | bytes 1376260
  117.3 14.3 %copy-start.1 = (bf16[1792,128]{1,0:T(8,128)(2,1)}, bf16[1792,128]{1,0:T(8,128)(2,1)S(1)}, u32[]{:S(2)}) copy-start(bf16[1792,128]{1,0:T(8,128)(2,1)S(1)} %pad_maximum_fusion.1.second_own) | copy-start | bytes 1376260
  117.3 14.3 %collective-permute-start.24 = (bf16[1792,128]{1,0:T(8,128)(2,1)S(1)}, bf16[1792,128]{1,0:T(8,128)(2,1)S(1)}, u32[]{:S(2)}, u32[]{:S(2)}) collective-permute-start(bf16[1792,128]{1,0:T(8,128)(2,1)S(1)} %pad_maximum_fusion.first_own), channel_id=1, source_target_pairs={{1,0},{0,1},{3,2},{2,3},{5,4},{4,5},{7,6},{6,7},{9,8},{8,9},{11,10... | collective-permute-start | bytes 1376264 | tf_op jit(solution)/shard_map/ppermute | solution.py:753
  129.3 2.3 %collective-permute-start.25 = (bf16[1792,128]{1,0:T(8,128)(2,1)S(1)}, bf16[1792,128]{1,0:T(8,128)(2,1)S(1)}, u32[]{:S(2)}, u32[]{:S(2)}) collective-permute-start(bf16[1792,128]{1,0:T(8,128)(2,1)S(1)} %pad_maximum_fusion.1.second_own), channel_id=1, source_target_pairs={{1,0},{0,1},{3,2},{2,3},{5,4},{4,5},{7,6},{6,7},{9,8},{8,9},{11,10... | collective-permute-start | bytes 1376264 | tf_op jit(solution)/shard_map/ppermute | solution.py:753
  (6 other events, 4.1 us)

commit v3 on v2

--- a/solution.py
+++ b/solution.py
@@ -90,10 +90,10 @@
 
 def head_lanes(head):
     lane = lax.broadcasted_iota(jnp.int32, (1, C), 1)
-    return (lane >= head * HEAD) & (lane < (head + 1) * HEAD)
-
-
-def make_pairs(pairs_ref):
+    return ((lane >= head * HEAD) & (lane < (head + 1) * HEAD)).astype(F32).astype(BF16)
+
+
+def pair_keys():
     row = lax.broadcasted_iota(jnp.int32, (512, 1), 0)
     within = row & 127
     third = (within >= SPAN).astype(jnp.int32) + (within >= 2 * SPAN).astype(jnp.int32)
@@ -105,16 +105,18 @@
         col_group = col_group + (col >= group * 12).astype(jnp.int32)
     col_place = col - col_group * 12
     usable = (row_group == col_group) & (within < 3 * SPAN) & (col < WIN)
-    keys = jnp.where(usable, col_place + 11 - row_offset, -1)
-    for place in range(WIN_LON):
-        pairs_ref[place] = jnp.where(keys == place, 1.0, 0.0).astype(BF16)
+    return jnp.where(usable, col_place + 11 - row_offset, -1).astype(F32).astype(BF16)
+
+
+def pairs_of(keys, place):
+    return jnp.where(keys == jnp.asarray(place, BF16), jnp.asarray(1, BF16), jnp.asarray(0, BF16))
 
 
 def table_start(zs, zt, hs, ht):
     return (((zs * 2 + zt) * 6 + hs) * 6 + ht) * SPAN
 
 
-def spread_bias(table_ref, pairs_ref, row_ref, shaped_ref, bias_ref):
+def spread_bias(table_ref, row_ref, shaped_ref, bias_ref):
     for head in range(HEADS):
         row_ref[head * 2 : head * 2 + 2, :RELPOS] = table_ref[head].astype(F32)
     row = row_ref[: 2 * HEADS]
@@ -129,25 +131,27 @@
                     pieces.append(jnp.zeros((2 * HEADS, 128 - 3 * SPAN), F32))
                     target = pl.ds(zt * 6 + ht, 2 * HEADS, stride=12)
                     shaped_ref[zs * 2 + group, target, :] = jnp.concatenate(pieces, axis=1)
+    keys = pair_keys()
     shaped = jnp.concatenate([shaped_ref[part, :WIN].astype(BF16) for part in range(4)], axis=1)
     for col in range(WIN_LON):
-        spread = mm(shaped, pairs_ref[col])
+        spread = mm(shaped, pairs_of(keys, col))
         bias_ref[0, pl.ds(col, WIN, stride=12), :] = spread[:, :128]
         bias_ref[1, pl.ds(col, WIN, stride=12), :] = spread[:, 128:]
 
 
-def collect_bias(scaled_ref, pairs_ref, levels, row_ref, shaped_ref, grads_ref, out_ref):
+def collect_bias(scaled_ref, levels, row_ref, shaped_ref, grads_ref, out_ref):
     for place in range(2 * HEADS):
         rows = slice(place * WIN, (place + 1) * WIN)
         piece = scaled_ref[place].astype(F32)
         grads_ref[0, rows] = piece[:, :128]
         grads_ref[1, rows] = jnp.concatenate([piece[:, 128:], jnp.zeros((WIN, 256 - WIN), F32)], axis=1)
+    keys = pair_keys()
     total = jnp.zeros((WIN, 512), F32)
     for col in range(WIN_LON):
         left = grads_ref[0, pl.ds(col, WIN, stride=12), :]
         right = grads_ref[1, pl.ds(col, WIN, stride=12), :]
         piece = jnp.concatenate([left, right], axis=1).astype(BF16)
-        total = total + mm_nt(piece, pairs_ref[col])
+        total = total + mm_nt(piece, pairs_of(keys, col))
     total = total * (1.0 / SCALE)
     for part in range(4):
         shaped_ref[part, :WIN] = total[:, part * 128 : (part + 1) * 128]
@@ -198,7 +202,7 @@
         values_t = mm_nt(eye_c, values).astype(BF16)
         parts = []
         for head in range(HEADS):
-            own = jnp.where(head_lanes(head), keys.astype(F32), 0.0).astype(BF16)
+            own = keys * head_lanes(head)
             scores = mm(own, queries_t) * SCALE + bias_of(window, head)
             weights = jnp.exp(scores - jnp.max(scores, axis=0, keepdims=True))
             weights = weights * (1.0 / jnp.sum(weights, axis=0, keepdims=True))
@@ -277,7 +281,7 @@
             lanes = slice(head * HEAD, (head + 1) * HEAD)
             half = weights_ref[window * HEADS + head]
             weights = half.astype(F32)
-            own = jnp.where(head_lanes(head), values.astype(F32), 0.0).astype(BF16)
+            own = values * head_lanes(head)
             grad_weights = mm(own, upstream_t)
             inner = jnp.sum(grad_weights * weights, axis=0, keepdims=True)
             grad_scores = weights * (grad_weights - inner)
@@ -366,11 +370,8 @@
     quad_2,
     quad_3,
     weights_out,
-    qkt_out,
-    values_out,
-    mixed_out,
-    hidden_out,
-    pairs_ref,
+    turned_out,
+    flat_out,
     rows_ref,
     row_ref,
     shaped_ref,
@@ -383,20 +384,20 @@
     order = order_ref[...]
     grad_quads = mm(order, load_grid(grad_ref, rows_ref).astype(BF16))
     flat = load_grid(inputs_ref, rows_ref)
-    make_pairs(pairs_ref)
-    spread_bias(table_ref, pairs_ref, row_ref, shaped_ref, bias_ref)
+    flat_out[0] = flat.astype(BF16)
+    spread_bias(table_ref, row_ref, shaped_ref, bias_ref)
     hat, _ = norm_stats(flat)
     normed = (hat * gain_one).astype(BF16)
     attended, mixed = attention(
         normed, in_weight, lambda window, head: load_tiles(bias_ref, levels[window], head), weights_out
     )
     for window in range(2):
-        qkt_out[window, 0] = attended[window][0]
-        qkt_out[window, 1] = attended[window][1]
-        values_out[window] = attended[window][2]
-        mixed_out[window] = mixed[window]
+        turned_out[window, 0] = attended[window][0]
+        turned_out[window, 1] = attended[window][1]
+        turned_out[window, 2] = mixed[window]
+        flat_out[2, window * WIN : (window + 1) * WIN] = attended[window][2]
     hidden = (flat + mm(natural_mixed(mixed), out_weight)).astype(BF16)
-    hidden_out[...] = hidden
+    flat_out[1] = hidden
     hidden = hidden.astype(F32)
     _, _, _, expanded = feed_forward(hidden, gain_two, up_weight)
     active = (expanded * 0.5 * (1.0 + lax.erf(expanded * (1.0 / math.sqrt(2.0))))).astype(BF16)
@@ -413,11 +414,10 @@
 
 
 def prepare_kernel(
-    levels_ref, region_ref, table_ref, bias_out, pairs_ref, row_ref, shaped_ref, bias_ref
+    levels_ref, region_ref, table_ref, bias_out, row_ref, shaped_ref, bias_ref
 ):
     levels = [levels_ref[0, 0], levels_ref[0, 1]]
-    make_pairs(pairs_ref)
-    spread_bias(table_ref, pairs_ref, row_ref, shaped_ref, bias_ref)
+    spread_bias(table_ref, row_ref, shaped_ref, bias_ref)
     diagonal = lax.broadcasted_iota(jnp.int32, (WIN, WIN), 0) == lax.broadcasted_iota(jnp.int32, (WIN, WIN), 1)
     for window in range(2):
         across = region_row(region_ref, window).astype(F32)
@@ -481,24 +481,21 @@
     write_halves(upper_ref, packed_ref, keep_ref, send_ref)
 
 
-def collect_kernel(
-    levels_ref,
-    scaled_ref,
-    hidden_ref,
-    gains_ref,
-    up_ref,
-    tables_out,
-    active_out,
-    slope_out,
-    pairs_ref,
-    row_ref,
-    shaped_ref,
-    grads_ref,
+def collect_kernel(levels_ref, scaled_ref, tables_out, row_ref, shaped_ref, grads_ref):
+    levels = [levels_ref[0, 0], levels_ref[0, 1]]
+    collect_bias(scaled_ref, levels, row_ref, shaped_ref, grads_ref, tables_out)
+
+
+def finish_kernel(
+    levels_ref, scaled_ref, second_tables_ref, tables_out, row_ref, shaped_ref, grads_ref
 ):
     levels = [levels_ref[0, 0], levels_ref[0, 1]]
-    make_pairs(pairs_ref)
-    collect_bias(scaled_ref, pairs_ref, levels, row_ref, shaped_ref, grads_ref, tables_out)
-    _, _, _, expanded = feed_forward(hidden_ref[...].astype(F32), gains_ref[1:2], up_ref[...])
+    collect_bias(scaled_ref, levels, row_ref, shaped_ref, grads_ref, tables_out.at[:TABLE_ROWS])
+    tables_out[TABLE_ROWS:] = second_tables_ref[...]
+
+
+def activation_kernel(flat_ref, gains_ref, up_ref, active_out, slope_out):
+    _, _, _, expanded = feed_forward(flat_ref[1].astype(F32), gains_ref[1:2], up_ref[...])
     active, slope = gelu_parts(expanded)
     active_out[...] = active
     slope_out[...] = slope.astype(BF16)
@@ -510,12 +507,9 @@
     quad_1,
     quad_2,
     quad_3,
-    inputs_ref,
     weights_ref,
-    qkt_ref,
-    values_ref,
-    mixed_ref,
-    hidden_ref,
+    turned_ref,
+    flat_ref,
     active_ref,
     slope_ref,
     gains_ref,
@@ -528,7 +522,6 @@
     send_ref,
     rows_out,
     scaled_ref,
-    rows_ref,
     packed_ref,
 ):
     quads = [quad[...].astype(F32) for quad in (quad_0, quad_1, quad_2, quad_3)]
@@ -536,27 +529,21 @@
     gain_one, gain_two, in_weight, out_weight, up_weight, down_weight = block_weights(
         gains_ref, in_ref, out_ref, up_ref, down_ref
     )
-    first_hat, first_inverse = norm_stats(load_grid(inputs_ref, rows_ref))
+    first_hat, first_inverse = norm_stats(flat_ref[0].astype(F32))
     first_norm = (first_hat * gain_one).astype(BF16)
-    second_hat, second_inverse = norm_stats(hidden_ref[...].astype(F32))
+    second_hat, second_inverse = norm_stats(flat_ref[1].astype(F32))
     second_norm = (second_hat * gain_two).astype(BF16)
-    attended = [(qkt_ref[window, 0], qkt_ref[window, 1], values_ref[window]) for window in range(2)]
-    mixed = [mixed_ref[0], mixed_ref[1]]
+    attended = [
+        (turned_ref[window, 0], turned_ref[window, 1], flat_ref[2, window * WIN : (window + 1) * WIN])
+        for window in range(2)
+    ]
+    mixed = [turned_ref[0, 2], turned_ref[1, 2]]
     rows_out[...] = backward(
         grad, active_ref[...], slope_ref[...].astype(F32), second_hat, second_inverse, second_norm, mixed,
         attended, weights_ref, first_hat, first_inverse, first_norm, gain_one, gain_two, in_weight,
         out_weight, up_weight, down_weight, scaled_ref, packed_ref,
     )
     write_halves(upper_ref, packed_ref, keep_ref, send_ref)
-
-
-def finish_kernel(
-    levels_ref, scaled_ref, second_tables_ref, tables_out, pairs_ref, row_ref, shaped_ref, grads_ref
-):
-    levels = [levels_ref[0, 0], levels_ref[0, 1]]
-    make_pairs(pairs_ref)
-    collect_bias(scaled_ref, pairs_ref, levels, row_ref, shaped_ref, grads_ref, tables_out.at[:TABLE_ROWS])
-    tables_out[TABLE_ROWS:] = second_tables_ref[...]
 
 
 def grids_kernel(quad_0, quad_1, quad_2, quad_3, natural_ref, grad_rows_ref, blocks_out, grad_out, rows_ref):
@@ -567,21 +554,34 @@
 
 
 SMEM = pl.BlockSpec(memory_space=pltpu.SMEM)
-VMEM_LIMIT = 60 * 1024 * 1024
-
-
-def whole(array):
-    return pl.BlockSpec(array.shape, lambda *_: (0,) * len(array.shape))
+VMEM = pl.BlockSpec(memory_space=pltpu.VMEM)
+ANY = pl.BlockSpec(memory_space=pl.ANY)
+FAR_LIMIT = 60 * 1024 * 1024
+NEAR_LIMIT = 28 * 1024 * 1024
 
 
 class Part:
     def __init__(self, array, block):
         self.array, self.block = array, block
+        self.lead = sum(size == 1 for size in array.shape[1:]) + 1
+        self.shape, self.dtype = array.shape[self.lead :], array.dtype
 
     def spec(self):
-        kept = [size for size in self.array.shape[1:] if size != 1]
-        lead = len(self.array.shape) - len(kept)
-        return pl.BlockSpec((None,) * lead + tuple(kept), lambda *_: (self.block,) + (0,) * (lead - 1 + len(kept)))
+        return pl.BlockSpec(
+            (None,) * self.lead + self.shape, lambda *_: (self.block,) + (0,) * (self.lead - 1 + len(self.shape))
+        )
+
+    def of(self, ref):
+        return ref.at[(self.block,) + (0,) * (self.lead - 1)]
+
+
+class Near:
+    def __init__(self, array):
+        self.array = array
+
+
+def whole(array):
+    return pl.BlockSpec(array.shape, lambda *_: (0,) * len(array.shape))
 
 
 def call(kernel, scalars, operands, out_shapes, scratch, flops):
@@ -594,9 +594,85 @@
         out_specs=[whole(shape) for shape in out_shapes],
         out_shape=out_shapes,
         scratch_shapes=scratch,
-        compiler_params=pltpu.CompilerParams(vmem_limit_bytes=VMEM_LIMIT),
+        compiler_params=pltpu.CompilerParams(vmem_limit_bytes=FAR_LIMIT),
         cost_estimate=pl.CostEstimate(flops=flops, bytes_accessed=4_000_000, transcendentals=1_000_000),
     )(*scalars, *arrays)
+
+
+def near_call(kernel, scalars, operands, out_shapes, scratch, flops, near_outs=(), carried=()):
+    def is_near(operand):
+        return isinstance(operand, Near)
+
+    def plain_array(operand):
+        return operand.array if isinstance(operand, (Near, Part)) else operand
+
+    def source_of(operand, ref):
+        return operand.of(ref) if isinstance(operand, Part) else ref
+
+    far = [operand for operand in operands if not is_near(operand)]
+    far_outs = [shape for place, shape in enumerate(out_shapes) if place not in near_outs]
+
+    def body(*refs):
+        refs = list(refs)
+
+        def take(count):
+            taken = refs[:count]
+            del refs[:count]
+            return taken
+
+        scalar_refs, operand_refs, carried_refs = take(len(scalars)), take(len(operands)), take(len(carried))
+        out_refs, carried_outs = take(len(out_shapes)), take(len(carried))
+        scratch_refs, buffers, out_buffers = take(len(scratch)), take(len(far)), take(len(far_outs))
+        sems, carried_sems, out_sems = refs
+        inputs, arriving = [], []
+        for operand, ref in zip(operands, operand_refs, strict=True):
+            if is_near(operand):
+                inputs.append(ref)
+                continue
+            place = len(arriving)
+            arriving.append(pltpu.make_async_copy(source_of(operand, ref), buffers[place], sems.at[place]))
+            inputs.append(buffers[place])
+        for copy in arriving:
+            copy.start()
+        passing = [
+            pltpu.make_async_copy(source_of(operand, ref), target, carried_sems.at[place])
+            for place, (operand, ref, target) in enumerate(zip(carried, carried_refs, carried_outs, strict=True))
+        ]
+        for copy in passing:
+            copy.start()
+        for copy in arriving:
+            copy.wait()
+        outputs, leaving = [], []
+        for place, ref in enumerate(out_refs):
+            if place in near_outs:
+                outputs.append(ref)
+                continue
+            outputs.append(out_buffers[len(leaving)])
+            leaving.append(pltpu.make_async_copy(outputs[-1], ref, out_sems.at[len(leaving)]))
+        kernel(*scalar_refs, *inputs, *outputs, *scratch_refs)
+        for copy in leaving:
+            copy.start()
+        for copy in passing + leaving:
+            copy.wait()
+
+    return pl.pallas_call(
+        body,
+        in_specs=[SMEM] * len(scalars)
+        + [VMEM if is_near(operand) else ANY for operand in operands]
+        + [ANY] * len(carried),
+        out_specs=[VMEM if place in near_outs else ANY for place in range(len(out_shapes))] + [VMEM] * len(carried),
+        out_shape=[*out_shapes, *[shape_of(operand.shape, operand.dtype) for operand in carried]],
+        scratch_shapes=[
+            *scratch,
+            *[pltpu.VMEM(operand.shape, operand.dtype) for operand in far],
+            *[pltpu.VMEM(shape.shape, shape.dtype) for shape in far_outs],
+            pltpu.SemaphoreType.DMA((max(len(far), 1),)),
+            pltpu.SemaphoreType.DMA((max(len(carried), 1),)),
+            pltpu.SemaphoreType.DMA((max(len(far_outs), 1),)),
+        ],
+        compiler_params=pltpu.CompilerParams(vmem_limit_bytes=NEAR_LIMIT),
+        cost_estimate=pl.CostEstimate(flops=flops, bytes_accessed=4_000_000, transcendentals=1_000_000),
+    )(*scalars, *[plain_array(operand) for operand in operands], *[plain_array(operand) for operand in carried])
 
 
 def shape_of(shape, dtype):
@@ -635,14 +711,13 @@
     rolled = one_hot(rolled_rows())
     half = [jnp.asarray(array, BF16) for array in (quadrant, quadrant.T, rolled, rolled.T)]
     to_quads, from_quads, rolled_back, rolled_ahead = half
-    is_upper = (lax.axis_index("lat") & 1).astype(jnp.int32).reshape(1)
+    is_upper = odd(core_step()[1]).reshape(1)
 
     quad_shape = shape_of((2 * QUAD, C), BF16)
     grid_shape = shape_of((6, 12, 4, C), BF16)
     half_shape = shape_of((ROWS // 2, 128), BF16)
     table_shape = shape_of((TABLE_ROWS, 128), BF16)
     weights_shape = (2 * HEADS, WIN, WIN)
-    pairs_scratch = pltpu.VMEM((WIN_LON, 512, 256), BF16)
     grads_scratch = pltpu.VMEM((2, 2 * HEADS * WIN, 128), F32)
     row_scratch = pltpu.VMEM((16, 26 * 128), F32)
     shaped_scratch = pltpu.VMEM((4, 2 * 72 + 16, 128), F32)
@@ -657,15 +732,13 @@
         [quad_shape] * 4
         + [
             shape_of(weights_shape, BF16),
-            shape_of((2, 2, C, WIN), BF16),
-            shape_of((2, WIN, C), BF16),
-            shape_of((2, C, WIN), BF16),
-            shape_of((TOKENS, C), BF16),
+            shape_of((2, 3, C, WIN), BF16),
+            shape_of((3, TOKENS, C), BF16),
         ],
-        [pairs_scratch, rows_scratch, row_scratch, shaped_scratch, bias_scratch],
+        [rows_scratch, row_scratch, shaped_scratch, bias_scratch],
         1_000_000_000,
     )
-    stored = quads[4:]
+    stored = list(quads[4:])
     ahead = (
         quads[3],
         shifted(quads[2], 0, 1),
@@ -677,7 +750,7 @@
         (bias_level,),
         (region.transpose(1, 0, 2), Part(bias_tables, 1)),
         [shape_of(weights_shape, BF16)],
-        [pairs_scratch, row_scratch, shaped_scratch, bias_scratch],
+        [row_scratch, shaped_scratch, bias_scratch],
         500_000_000,
     )
     *back, second_keep, second_send, second_scaled = call(
@@ -688,31 +761,33 @@
         [pltpu.VMEM(weights_shape, BF16), packed_scratch],
         3_000_000_000,
     )
-    second_tables, active, slope = call(
-        collect_kernel,
-        (bias_level,),
-        (second_scaled, stored[4], first_weights[0], first_weights[3]),
-        [table_shape, shape_of((TOKENS, FFN), BF16), shape_of((TOKENS, FFN), BF16)],
-        [pairs_scratch, row_scratch, shaped_scratch, grads_scratch],
-        500_000_000,
-    )
     home = [
         shifted(back[3], -1, -1),
         shifted(back[2], -1, 0),
         shifted(back[1], 0, -1),
         back[0],
     ]
-    second = added(second_keep, exchanged(second_send, CORE))
-    home[3], second = lax.optimization_barrier((home[3], second))
-    first_keep, first_send, grad_rows, first_scaled = call(
+    home[3], stored[2] = tie((home[3], stored[2]))
+    active, slope, *first_near = near_call(
+        activation_kernel,
+        (),
+        (stored[2], first_weights[0], first_weights[3]),
+        [shape_of((TOKENS, FFN), BF16), shape_of((TOKENS, FFN), BF16)],
+        [],
+        300_000_000,
+        (0, 1),
+        (home[3], *stored, *first_weights, from_quads),
+    )
+    second_got = exchanged(second_send, core_step()[0])
+    first_keep, first_send, grad_rows, first_scaled = near_call(
         third_kernel,
         (is_upper,),
-        (*home, inputs, *stored, active, slope, *first_weights, from_quads),
+        tuple(map(Near, (*home[:3], *first_near[:4], active, slope, *first_near[4:]))),
         [half_shape, half_shape, shape_of((TOKENS, C), BF16), shape_of(weights_shape, BF16)],
-        [rows_scratch, packed_scratch],
+        [packed_scratch],
         2_000_000_000,
     )
-    blocks_out, grad_inputs = call(
+    blocks_out, grad_inputs = near_call(
         grids_kernel,
         (),
         (*home, from_quads, grad_rows),
@@ -720,17 +795,24 @@
         [rows_scratch],
         100_000_000,
     )
-    first = added(first_keep, exchanged(first_send, CORE))
-    first, first_scaled = lax.optimization_barrier((first, first_scaled))
-    (tables,) = call(
-        finish_kernel,
-        (bias_level,),
-        (first_scaled, second_tables),
-        [shape_of((2 * TABLE_ROWS, 128), BF16)],
-        [pairs_scratch, row_scratch, shaped_scratch, grads_scratch],
-        500_000_000,
-    )
-    totals = unpack(is_upper, *sum_all(first, second, tables))
+
+    def collect(kernel, rows, *operands):
+        return near_call(
+            kernel,
+            (bias_level,),
+            operands,
+            [shape_of((rows, 128), BF16)],
+            [row_scratch, shaped_scratch, grads_scratch],
+            500_000_000,
+        )[0]
+
+    first_got = exchanged(first_send, core_step()[0])
+    second = added(second_keep, second_got)
+    first = added(first_keep, first_got)
+    first, second, first_scaled, second_scaled = tie((first, second, first_scaled, second_scaled))
+    second_tables = collect(collect_kernel, TABLE_ROWS, second_scaled)
+    tables = collect(finish_kernel, 2 * TABLE_ROWS, first_scaled, second_tables)
+    totals = unpack(is_upper, *sum_all(first, second, tables, second_tables))
     gains, grad_in, grad_out_weight, grad_up, grad_down, grad_tables = totals
     return (
         blocks_out.transpose(2, 0, 1, 3),
@@ -762,12 +844,12 @@
     parity = jnp.int32(0)
     for place in range(5):
         parity = parity ^ (lat >> place) ^ (lon >> place)
-    return (parity & 1) != 0
+    return parity & 1
 
 
 def split(value, owner):
     half = value.shape[0] // 2
-    up = odd(owner)
+    up = odd(owner) != 0
     return jnp.where(up, value[half:], value[:half]), jnp.where(up, value[:half], value[half:])
 
 
@@ -778,25 +860,30 @@
 
 def double(value, mask, owner):
     other = exchanged(value, mask)
-    up = odd(owner)
+    up = odd(owner) != 0
     return jnp.concatenate([jnp.where(up, other, value), jnp.where(up, value, other)], axis=0)
 
 
-CORE = (1, 0)
-
-
-def sum_all(first, second, tables):
+def tie(values):
+    return lax.optimization_barrier(values)
+
+
+def core_step():
+    return (1, 0), (1, 0)
+
+
+def sum_all(first, second, tables, second_tables):
+    core = core_step()[0]
     if lax.axis_size("lat") != 16 or lax.axis_size("lon") != 16:
         return sum_small(first, second, tables)
     y_low, y_high = ((2, 0), (2, 0)), (0, 8)
     x_low, x_high = ((4, 0), (12, 0)), ((12, 0), (8, 0))
     z_low, z_mid, z_high = ((0, 1), (0, 5)), ((0, 2), (0, 6)), (0, 7)
-    tie = lax.optimization_barrier
-
-    second = halve(second, *x_low)
-    first = halve(first, *y_low)
+
+    first, second = halve(first, *y_low), halve(second, *x_low)
+    first, second, second_tables = tie((first, second, second_tables))
+    first, second = halve(first, *x_low), halve(second, *y_low)
     first, second = tie((first, second))
-    first, second = halve(first, *x_low), halve(second, *y_low)
     rows = first.shape[0]
     joined = halve(jnp.concatenate([first, second], axis=0), *x_high)
     joined, tables = tie((joined, tables))
@@ -814,7 +901,7 @@
     first, second, tables = tie((first, second, tables))
     first, second = double(first, *y_low), double(second, *x_low)
     first, second = tie((first, second))
-    return first, exchanged(first, CORE), second, exchanged(second, CORE), tables
+    return first, exchanged(first, core), second, exchanged(second, core), tables
 
 
 def sum_small(first, second, tables):
@@ -824,27 +911,23 @@
                 value = added(value, exchanged(value, (1 << place, 0) if axis == "lat" else (0, 1 << place)))
         return value
 
+    core = core_step()[0]
     first, second = over(over(first, "lat"), "lon"), over(over(second, "lat"), "lon")
-    return first, exchanged(first, CORE), second, exchanged(second, CORE), over(tables, "lon")
-
-
-def unpack_kernel(
-    upper_ref,
-    first_own,
-    first_other,
-    second_own,
-    second_other,
-    tables_ref,
-    gains_ref,
-    in_ref,
-    out_ref,
-    up_ref,
-    down_ref,
-    grads_ref,
-    rows_ref,
-):
+    return first, exchanged(first, core), second, exchanged(second, core), over(tables, "lon")
+
+
+def unpack_kernel(upper_ref, first_own, first_other, second_own, second_other, tables_ref, *refs):
+    results, (rows_ref, *buffers, sems) = refs[:6], refs[6:]
+    gains_ref, in_ref, out_ref, up_ref, down_ref, grads_ref = buffers
     half = ROWS // 2
     is_upper = jnp.broadcast_to(upper_ref[0] == 1, (1, 128))
+    copies = []
+
+    def leave(index, block):
+        copy = pltpu.make_async_copy(buffers[index].at[block], results[index].at[block], sems.at[index, block])
+        copy.start()
+        copies.append(copy)
+
     for block, (own, other) in enumerate(((first_own, first_other), (second_own, second_other))):
 
         def rows(start, stop, own=own, other=other):
@@ -855,45 +938,55 @@
             mine, theirs = own[start:stop].astype(F32), other[start:stop].astype(F32)
             return jnp.where(is_upper, theirs, mine) if lower else jnp.where(is_upper, mine, theirs)
 
-        rows_ref[...] = tables_ref[block * TABLE_ROWS : (block + 1) * TABLE_ROWS].astype(F32)
+        for index, (ref, start) in enumerate(((up_ref, 1152), (down_ref, 2304))):
+            for part in range(6):
+                lanes = slice(part * 128, (part + 1) * 128)
+                ref[block, :, lanes] = rows(start + part * C, start + (part + 1) * C)
+            leave(3 + index, block)
         for part in range(4):
             in_ref[block, :, part * 128 : (part + 1) * 128] = rows(part * C, (part + 1) * C)
         shared = rows(768, 960)
         in_ref[block, :, 512:] = shared[:, :64]
+        leave(1, block)
         out_ref[block, :, :128] = rows(960, 1152)
         out_ref[block, :, 128:] = shared[:, 64:]
-        for part in range(6):
-            lanes = slice(part * 128, (part + 1) * 128)
-            up_ref[block, :, lanes] = rows(1152 + part * C, 1152 + (part + 1) * C)
-            down_ref[block, :, lanes] = rows(2304 + part * C, 2304 + (part + 1) * C)
+        leave(2, block)
+        rows_ref[...] = tables_ref[block * TABLE_ROWS : (block + 1) * TABLE_ROWS].astype(F32)
+        for slab in range(26):
+            width = min(128, RELPOS - slab * 128)
+            for level in range(2):
+                start = slab * 12 + level * HEADS
+                grads_ref[block, 0, :, level, slab * 128 : slab * 128 + width] = rows_ref[start : start + HEADS, :width]
+        leave(5, block)
         gains = rows(GAIN_ROWS, GAIN_ROWS + 16)
         gains_ref[block, 0:1, :128] = gains[0:1]
         gains_ref[block, 0:1, 128:] = gains[1:2, :64]
         gains_ref[block, 1:2, :128] = gains[2:3]
         gains_ref[block, 1:2, 128:] = gains[1:2, 64:]
-        for slab in range(26):
-            width = min(128, RELPOS - slab * 128)
-            for level in range(2):
-                start = slab * 12 + level * HEADS
-                grads_ref[block, 0, :, level, slab * 128 : slab * 128 + width] = rows_ref[start : start + HEADS, :width]
+        leave(0, block)
+    for copy in copies:
+        copy.wait()
 
 
 def unpack(is_upper, *values):
-    return call(
+    shapes = [
+        (2, 2, C),
+        (2, C, 3 * C),
+        (2, C, C),
+        (2, C, FFN),
+        (2, C, FFN),
+        (2, 1, HEADS, 2, RELPOS),
+    ]
+    return pl.pallas_call(
         unpack_kernel,
-        (is_upper,),
-        values,
-        [
-            shape_of((2, 2, C), F32),
-            shape_of((2, C, 3 * C), F32),
-            shape_of((2, C, C), F32),
-            shape_of((2, C, FFN), F32),
-            shape_of((2, C, FFN), F32),
-            shape_of((2, 1, HEADS, 2, RELPOS), F32),
-        ],
-        [pltpu.VMEM((TABLE_ROWS, 128), F32)],
-        1_000_000,
-    )
+        in_specs=[SMEM] + [pl.BlockSpec(memory_space=pltpu.VMEM)] * len(values),
+        out_specs=[pl.BlockSpec(memory_space=pl.ANY)] * len(shapes),
+        out_shape=[shape_of(shape, F32) for shape in shapes],
+        scratch_shapes=[pltpu.VMEM((TABLE_ROWS, 128), F32)]
+        + [pltpu.VMEM(shape, F32) for shape in shapes]
+        + [pltpu.SemaphoreType.DMA((len(shapes), 2))],
+        compiler_params=pltpu.CompilerParams(vmem_limit_bytes=NEAR_LIMIT),
+    )(is_upper, *values)
 
 
 def solution(mesh):

time: 138 us -> 132 us (0.957)
  waiting for transfers between devices: 48.1 us -> 39.6 us
  starting transfers between devices: 36.3 us -> 42.9 us
  Pallas kernels: 44.5 us -> 42.1 us
  other arithmetic: 3.83 us -> 2.25 us
    pallas_call x8 -> x3, Pallas kernels: 44.5 us -> 22.8 us  [call(): pl.pallas_call(kernel, grid=(1,), in_specs=[SMEM] * len(scalars) + specs,...]
    pallas_call x0 -> x6, Pallas kernels: none -> 19.3 us  [the longest x5 17.1 us: near_call(): pl.pallas_call(body, in_specs=[SMEM] * len(scalars) + [VMEM if is_near(op...]
    ppermute x20, waiting for transfers between devices: 43 us -> 35.1 us  [exchanged(): return lax.ppermute(value, ('lon', 'lat'), pairs)]
    ppermute x20, starting transfers between devices: 22.1 us -> 28.7 us  [exchanged(): return lax.ppermute(value, ('lon', 'lat'), pairs)]
    unnamed x24 -> x34, local copies, waits for them, and re-layouts: 2.85 us -> 3.15 us
  transfers between devices with their start and end apart: 26 -> 26, of which waited for: 18 -> 17; matrix products, arithmetic and copies ran while one was open for 2% -> 1% of each run, Pallas kernels for 9% -> 15%
where the time goes in v3:
time: 132 us; the launch traced here: 131 us
  starting transfers between devices  42.9 us (32%)
  Pallas kernels  42.1 us (32%)
  waiting for transfers between devices  39.6 us (30%)
  local copies, waits for them, and re-layouts  3.16 us (2%)
  other arithmetic  2.25 us (2%)
  between operations  1.33 us (1%)
    ppermute x20, waiting for transfers between devices, exchanged(): return lax.ppermute(value, ('lon', 'lat'), pairs)  35.1 us
    ppermute x20, starting transfers between devices, exchanged(): return lax.ppermute(value, ('lon', 'lat'), pairs)  28.7 us
    pallas_call x3, Pallas kernels, call(): pl.pallas_call(kernel, grid=(1,), in_specs=[SMEM] * len(scalars) + specs,...  22.8 us
    pallas_call x5, Pallas kernels, near_call(): pl.pallas_call(body, in_specs=[SMEM] * len(scalars) + [VMEM if is_near(op...  17.1 us
    ppermute x6, starting transfers between devices, shifted(): return lax.ppermute(value, ('lon', 'lat'), pairs)  14.2 us
    ppermute x6, waiting for transfers between devices, shifted(): return lax.ppermute(value, ('lon', 'lat'), pairs)  4.52 us
    unnamed x34, local copies, waits for them, and re-layouts  3.15 us
  transfers between devices with their start and end apart: 26, of which 17 were waited for; matrix products, arithmetic and copies ran while one was open for 1% of the time, Pallas kernels for 15%

profile of v3, /device:TPU:1, one launch (start us, length us, event | category | flops | bytes accessed | tf_op | source)
XLA Modules:
  0.0 131.4 jit_solution(9957255711942605612)
XLA Ops:
  0.6 7.7 %shard_map.197 = (bf16[144,192]{1,0:T(8,128)(2,1)}, bf16[144,192]{1,0:T(8,128)(2,1)}, bf16[144,192]{1,0:T(8,128)(2,1)}, bf16[144,192]{1,0:T(8,128)(2,1)}, bf16[1...) custom-call(s32[1,2]{1,0:T(1,128)} %bitcast.14, ...), custom_call_target="tpu_custom_call" | custom-call | flops 1000000000 | bytes 4000000 | tf_op jit(solution)/shard_map/pallas_call | solution.py:590
  8.3 9.0 %collective-permute-start = (bf16[144,192]{1,0:T(8,128)(2,1)}, bf16[144,192]{1,0:T(8,128)(2,1)S(1)}, u32[]{:S(2)}, u32[]{:S(2)}) collective-permute-start(bf16[144,192]{1,0:T(8,128)(2,1)} %get-tuple-element.69), channel_id=1, source_target_pairs={{16,0},{17,1},{18,2},{19,3},{20,4},{21,5},{22,6},{23,7},{24,8},{25... | collective-permute-start | bytes 165896 | tf_op jit(solution)/shard_map/ppermute | solution.py:689
  18.3 3.2 %collective-permute-start.2 = (bf16[144,192]{1,0:T(8,128)(2,1)}, bf16[144,192]{1,0:T(8,128)(2,1)S(1)}, u32[]{:S(2)}, u32[]{:S(2)}) collective-permute-start(bf16[144,192]{1,0:T(8,128)(2,1)} %get-tuple-element.71), channel_id=1, source_target_pairs={{17,0},{18,1},{19,2},{20,3},{21,4},{22,5},{23,6},{24,7},{25,8},{26... | collective-permute-start | bytes 165896 | tf_op jit(solution)/shard_map/ppermute | solution.py:689
  21.6 3.0 %shard_map.198.bias_ref = bf16[12,144,144]{2,1,0:T(8,128)(2,1)} custom-call(s32[1,2]{1,0:T(1,128)} %bitcast.15, s32[6,4,12]{2,1,0:T(4,128)} %bitcast.24, bf16[2,1,6,2,3312]{4,3,2,1,0:T(2,128)(2,1)} %bitcast.21), custom_call_target="tpu_custom_call" | custom-call | flops 500000000 | bytes 4000000 | tf_op jit(solution)/shard_map/pallas_call | solution.py:590
  25.3 12.1 %shard_map.199 = (bf16[144,192]{1,0:T(8,128)(2,1)}, bf16[144,192]{1,0:T(8,128)(2,1)}, bf16[144,192]{1,0:T(8,128)(2,1)}, bf16[144,192]{1,0:T(8,128)(2,1)}, bf16[1...) custom-call(s32[1]{0:T(128)} %bitcast.upper_ref.refs_0_, ...), custom_call_target="tpu_custom_call" | custom-call | flops 3000000000 | bytes 4000000 | tf_op jit(solution)/shard_map/pallas_call | solution.py:590
  40.4 2.8 %shard_map.200 = (bf16[288,768]{1,0:T(8,128)(2,1)S(1)}, bf16[288,768]{1,0:T(8,128)(2,1)S(1)}, bf16[144,192]{1,0:T(8,128)(2,1)S(1)}, bf16[12,144,144]{2,1,0:T(8,1...) custom-call(bf16[3,288,192]{2,1,0:T(8,128)(2,1)S(1)} %copy-done.1, ...), custom_call_target="tpu_custom_call" | custom-call | flops 300000000 | bytes 4000000 | tf_op jit(solution)/shard_map/pallas_call | solution.py:658
  43.3 3.1 %collective-permute-done.3.refs_1_.refs_0_ = bf16[144,192]{1,0:T(8,128)(2,1)} collective-permute-done((bf16[144,192]{1,0:T(8,128)(2,1)}, bf16[144,192]{1,0:T(8,128)(2,1)}, u32[]{:S(2)}, u32[]{:S(2)}) %collective-permute-start.3) | collective-permute-done | bytes 55328 | tf_op jit(solution)/shard_map/ppermute | solution.py:689
  46.3 1.5 %collective-permute-done.5.refs_3_.refs_2_ = bf16[144,192]{1,0:T(8,128)(2,1)} collective-permute-done((bf16[144,192]{1,0:T(8,128)(2,1)}, bf16[144,192]{1,0:T(8,128)(2,1)}, u32[]{:S(2)}, u32[]{:S(2)}) %collective-permute-start.5) | collective-permute-done | bytes 55328 | tf_op jit(solution)/shard_map/ppermute | solution.py:689
  47.8 7.2 %shard_map.201 = (bf16[1792,128]{1,0:T(8,128)(2,1)S(1)}, bf16[1792,128]{1,0:T(8,128)(2,1)S(1)}, bf16[288,192]{1,0:T(8,128)(2,1)S(1)}, bf16[12,144,144]{2,1,0:T(8,128)(2,1)S(1)}) custom-call(s32[1]{0:T(128)} %bitcast.upper_ref.refs_0_, bf16[144,192]{1,0:T(8,128)(2,1)} %collective-permute-done.3.refs_1_.refs_0_, ...), custom_call_target="tpu_custom_call" | custom-call | flops 2000000000 | bytes 4000000 | tf_op jit(solution)/shard_map/pallas_call | solution.py:658
  56.1 1.1 add_convert_fusion
  58.7 2.4 %shard_map.203.refs_2_ = bf16[320,128]{1,0:T(8,128)(2,1)S(1)} custom-call(s32[1,2]{1,0:T(1,128)S(1)} %bitcast.16, bf16[12,144,144]{2,1,0:T(8,128)(2,1)S(1)} %copy-done.12), custom_call_target="tpu_custom_call" | custom-call | flops 500000000 | bytes 4000000 | tf_op jit(solution)/shard_map/pallas_call | solution.py:658
  61.1 3.5 %collective-permute-done.9 = bf16[896,128]{1,0:T(8,128)(2,1)S(1)} collective-permute-done((bf16[896,128]{1,0:T(8,128)(2,1)S(1)}, bf16[896,128]{1,0:T(8,128)(2,1)S(1)}, u32[]{:S(2)}, u32[]{:S(2)}) %collective-permute-start.9) | collective-permute-done | bytes 229408 | tf_op jit(solution)/shard_map/ppermute | solution.py:835
  65.0 1.5 %collective-permute-start.10 = (bf16[448,128]{1,0:T(8,128)(2,1)S(1)}, bf16[448,128]{1,0:T(8,128)(2,1)S(1)}, u32[]{:S(2)}, u32[]{:S(2)}) collective-permute-start(bf16[448,128]{1,0:T(8,128)(2,1)S(1)} %broadcast_select_fusion.14), channel_id=1, source_target_pairs={{4,0},{5,1},{6,2},{7,3},{0,4},{1,5},{2,6},{3,7},{12,8},{13,9},{14,... | collective-permute-start | bytes 344072 | tf_op jit(solution)/shard_map/ppermute | solution.py:835
  66.5 2.1 %collective-permute-done.11 = bf16[448,128]{1,0:T(8,128)(2,1)S(1)} collective-permute-done((bf16[448,128]{1,0:T(8,128)(2,1)S(1)}, bf16[448,128]{1,0:T(8,128)(2,1)S(1)}, u32[]{:S(2)}, u32[]{:S(2)}) %collective-permute-start.11) | collective-permute-done | bytes 114720 | tf_op jit(solution)/shard_map/ppermute | solution.py:835
  68.8 2.7 %collective-permute-start.12 = (bf16[448,128]{1,0:T(8,128)(2,1)S(1)}, bf16[448,128]{1,0:T(8,128)(2,1)S(1)}, u32[]{:S(2)}, u32[]{:S(2)}) collective-permute-start(bf16[448,128]{1,0:T(8,128)(2,1)S(1)} %broadcast_select_fusion.11), channel_id=1, source_target_pairs={{12,0},{13,1},{14,2},{15,3},{8,4},{9,5},{10,6},{11,7},{4,8},{5,9},... | collective-permute-start | bytes 344072 | tf_op jit(solution)/shard_map/ppermute | solution.py:835
  71.5 2.6 %shard_map.204 = bf16[640,128]{1,0:T(8,128)(2,1)S(1)} custom-call(s32[1,2]{1,0:T(1,128)S(1)} %bitcast.17, bf16[12,144,144]{2,1,0:T(8,128)(2,1)S(1)} %get-tuple-element.109.refs_1_, bf16[320,128]{1,0:T(8,128)(2,1)S(1)} %shard_map.203.refs_2_), custom_call_target="tpu_custom_call" | custom-call | flops 500000000 | bytes 4000000 | tf_op jit(solution)/shard_map/pallas_call | solution.py:658
  74.3 4.5 %collective-permute-done.13 = bf16[768,128]{1,0:T(8,128)(2,1)S(1)} collective-permute-done((bf16[768,128]{1,0:T(8,128)(2,1)S(1)}, bf16[768,128]{1,0:T(8,128)(2,1)S(1)}, u32[]{:S(2)}, u32[]{:S(2)}) %collective-permute-start.13) | collective-permute-done | bytes 196640 | tf_op jit(solution)/shard_map/ppermute | solution.py:835
  79.3 6.4 %collective-permute-done.14 = bf16[608,128]{1,0:T(8,128)(2,1)S(1)} collective-permute-done((bf16[608,128]{1,0:T(8,128)(2,1)S(1)}, bf16[608,128]{1,0:T(8,128)(2,1)S(1)}, u32[]{:S(2)}, u32[]{:S(2)}) %collective-permute-start.14) | collective-permute-done | bytes 155680 | tf_op jit(solution)/shard_map/ppermute | solution.py:835
  86.3 5.8 %collective-permute-done.15 = bf16[608,128]{1,0:T(8,128)(2,1)S(1)} collective-permute-done((bf16[608,128]{1,0:T(8,128)(2,1)S(1)}, bf16[608,128]{1,0:T(8,128)(2,1)S(1)}, u32[]{:S(2)}, u32[]{:S(2)}) %collective-permute-start.15) | collective-permute-done | bytes 155680 | tf_op jit(solution)/shard_map/ppermute | solution.py:835
  92.2 1.8 %collective-permute-start.16 = (bf16[608,128]{1,0:T(8,128)(2,1)S(1)}, bf16[608,128]{1,0:T(8,128)(2,1)S(1)}, u32[]{:S(2)}, u32[]{:S(2)}) collective-permute-start(bf16[608,128]{1,0:T(8,128)(2,1)S(1)} %add_convert_fusion.5), channel_id=1, source_target_pairs={{128,0},{129,1},{130,2},{131,3},{132,4},{133,5},{134,6},{135,7},{1... | collective-permute-start | bytes 466952 | tf_op jit(solution)/shard_map/ppermute | solution.py:835
  94.0 3.8 %collective-permute-done.16 = bf16[608,128]{1,0:T(8,128)(2,1)S(1)} collective-permute-done((bf16[608,128]{1,0:T(8,128)(2,1)S(1)}, bf16[608,128]{1,0:T(8,128)(2,1)S(1)}, u32[]{:S(2)}, u32[]{:S(2)}) %collective-permute-start.16) | collective-permute-done | bytes 155680 | tf_op jit(solution)/shard_map/ppermute | solution.py:835
  99.0 2.0 %collective-permute-start.17 = (bf16[448,128]{1,0:T(8,128)(2,1)S(1)}, bf16[448,128]{1,0:T(8,128)(2,1)S(1)}, u32[]{:S(2)}, u32[]{:S(2)}) collective-permute-start(bf16[448,128]{1,0:T(8,128)(2,1)S(1)} %slice.90), channel_id=1, source_target_pairs={{12,0},{13,1},{14,2},{15,3},{8,4},{9,5},{10,6},{11,7},{4,8},{5,9},... | collective-permute-start | bytes 344072 | tf_op jit(solution)/shard_map/ppermute | solution.py:835
  101.9 1.9 %collective-permute-done.17 = bf16[448,128]{1,0:T(8,128)(2,1)S(1)} collective-permute-done((bf16[448,128]{1,0:T(8,128)(2,1)S(1)}, bf16[448,128]{1,0:T(8,128)(2,1)S(1)}, u32[]{:S(2)}, u32[]{:S(2)}) %collective-permute-start.17) | collective-permute-done | bytes 114720 | tf_op jit(solution)/shard_map/ppermute | solution.py:835
  104.0 1.4 %collective-permute-start.20 = (bf16[448,128]{1,0:T(8,128)(2,1)S(1)}, bf16[448,128]{1,0:T(8,128)(2,1)S(1)}, u32[]{:S(2)}, u32[]{:S(2)}) collective-permute-start(bf16[448,128]{1,0:T(8,128)(2,1)S(1)} %get-tuple-element.115), channel_id=1, source_target_pairs={{2,0},{3,1},{0,2},{1,3},{6,4},{7,5},{4,6},{5,7},{10,8},{11,9},{8,1... | collective-permute-start | bytes 344072 | tf_op jit(solution)/shard_map/ppermute | solution.py:835
  105.4 1.8 %collective-permute-done.21 = bf16[320,128]{1,0:T(8,128)(2,1)S(1)} collective-permute-done((bf16[320,128]{1,0:T(8,128)(2,1)S(1)}, bf16[320,128]{1,0:T(8,128)(2,1)S(1)}, u32[]{:S(2)}, u32[]{:S(2)}) %collective-permute-start.21) | collective-permute-done | bytes 81952 | tf_op jit(solution)/shard_map/ppermute | solution.py:835
  107.8 1.4 %collective-permute-start.22 = (bf16[896,128]{1,0:T(8,128)(2,1)S(1)}, bf16[896,128]{1,0:T(8,128)(2,1)S(1)}, u32[]{:S(2)}, u32[]{:S(2)}) collective-permute-start(bf16[896,128]{1,0:T(8,128)(2,1)S(1)} %get-tuple-element.117), channel_id=1, source_target_pairs={{2,0},{3,1},{0,2},{1,3},{6,4},{7,5},{4,6},{5,7},{10,8},{11,9},{8,1... | collective-permute-start | bytes 688136 | tf_op jit(solution)/shard_map/ppermute | solution.py:835
  109.2 1.4 %collective-permute-start.23 = (bf16[896,128]{1,0:T(8,128)(2,1)S(1)}, bf16[896,128]{1,0:T(8,128)(2,1)S(1)}, u32[]{:S(2)}, u32[]{:S(2)}) collective-permute-start(bf16[896,128]{1,0:T(8,128)(2,1)S(1)} %get-tuple-element.118), channel_id=1, source_target_pairs={{4,0},{5,1},{6,2},{7,3},{0,4},{1,5},{2,6},{3,7},{12,8},{13,9},{14,... | collective-permute-start | bytes 688136 | tf_op jit(solution)/shard_map/ppermute | solution.py:835
  110.6 2.2 %collective-permute-done.22 = bf16[896,128]{1,0:T(8,128)(2,1)S(1)} collective-permute-done((bf16[896,128]{1,0:T(8,128)(2,1)S(1)}, bf16[896,128]{1,0:T(8,128)(2,1)S(1)}, u32[]{:S(2)}, u32[]{:S(2)}) %collective-permute-start.22) | collective-permute-done | bytes 229408 | tf_op jit(solution)/shard_map/ppermute | solution.py:835
  112.9 1.2 collective-permute-done.23
  114.2 12.6 %collective-permute-start.24 = (bf16[1792,128]{1,0:T(8,128)(2,1)S(1)}, bf16[1792,128]{1,0:T(8,128)(2,1)S(1)}, u32[]{:S(2)}, u32[]{:S(2)}) collective-permute-start(bf16[1792,128]{1,0:T(8,128)(2,1)S(1)} %pad_maximum_fusion.first_own), channel_id=1, source_target_pairs={{1,0},{0,1},{3,2},{2,3},{5,4},{4,5},{7,6},{6,7},{9,8},{8,9},{11,10... | collective-permute-start | bytes 1376264 | tf_op jit(solution)/shard_map/ppermute | solution.py:835
  126.9 2.1 %shard_map.202 = (bf16[6,12,4,192]{3,2,1,0:T(4,128)(2,1)}, bf16[6,12,4,192]{3,2,1,0:T(4,128)(2,1)}) custom-call(bf16[144,192]{1,0:T(8,128)(2,1)} %collective-permute-done.3.refs_1_.refs_0_, bf16[144,192]{1,0:T(8,128)(2,1)} %collective-permute-done.4.refs_2_.refs_1_, bf16[144,192]{1,0:T(8,128)(2,1)} %collective-permute-done.5.refs_3_.refs_2_, ...), custom_call_target="tpu_custom_call" | custom-call | flops 100000000 | bytes 4000000 | tf_op jit(solution)/shard_map/pallas_call | solution.py:658
  129.0 2.2 %shard_map.205 = (f32[2,2,192]{2,1,0:T(2,128)}, f32[2,192,576]{2,1,0:T(8,128)}, f32[2,192,192]{2,1,0:T(8,128)}, f32[2,192,768]{2,1,0:T(8,128)}, f32[2,192,768]{2,1,0:T(8,128)}, /*index=5*/f32[2,1,6,2,3312]{4,3,2,1,0:T(2,128)}) custom-call(s32[1]{0:T(128)} %bitcast.upper_ref.refs_0_, bf16[1792,128]{1,0:T(8,128)(2,1)S(1)} %pad_maximum_fusion.first_own, ...), custom_call_target="tpu_custom_call" | custom-call | tf_op jit(solution)/shard_map/pallas_call | solution.py:980
  (100 shorter events, 12.0 us)
Async XLA Ops:
  8.3 16.2 %collective-permute-start = (bf16[144,192]{1,0:T(8,128)(2,1)}, bf16[144,192]{1,0:T(8,128)(2,1)S(1)}, u32[]{:S(2)}, u32[]{:S(2)}) collective-permute-start(bf16[144,192]{1,0:T(8,128)(2,1)} %get-tuple-element.69), channel_id=1, source_target_pairs={{16,0},{17,1},{18,2},{19,3},{20,4},{21,5},{22,6},{23,7},{24,8},{25... | collective-permute-start | bytes 165896 | tf_op jit(solution)/shard_map/ppermute | solution.py:689
  17.4 7.2 %collective-permute-start.1 = (bf16[144,192]{1,0:T(8,128)(2,1)}, bf16[144,192]{1,0:T(8,128)(2,1)S(1)}, u32[]{:S(2)}, u32[]{:S(2)}) collective-permute-start(bf16[144,192]{1,0:T(8,128)(2,1)} %get-tuple-element.70), channel_id=1, source_target_pairs={{1,0},{2,1},{3,2},{4,3},{5,4},{6,5},{7,6},{8,7},{9,8},{10,9},{11,1... | collective-permute-start | bytes 165896 | tf_op jit(solution)/shard_map/ppermute | solution.py:689
  18.3 6.3 %collective-permute-start.2 = (bf16[144,192]{1,0:T(8,128)(2,1)}, bf16[144,192]{1,0:T(8,128)(2,1)S(1)}, u32[]{:S(2)}, u32[]{:S(2)}) collective-permute-start(bf16[144,192]{1,0:T(8,128)(2,1)} %get-tuple-element.71), channel_id=1, source_target_pairs={{17,0},{18,1},{19,2},{20,3},{21,4},{22,5},{23,6},{24,7},{25,8},{26... | collective-permute-start | bytes 165896 | tf_op jit(solution)/shard_map/ppermute | solution.py:689
  25.3 13.2 %copy-start.1 = (bf16[3,288,192]{2,1,0:T(8,128)(2,1)S(1)}, bf16[3,288,192]{2,1,0:T(8,128)(2,1)}, u32[]{:S(2)}) copy-start(bf16[3,288,192]{2,1,0:T(8,128)(2,1)} %get-tuple-element.78.refs_0_.refs_6_) | copy-start | bytes 995332
  25.3 13.2 %copy-start.2 = (bf16[12,144,144]{2,1,0:T(8,128)(2,1)S(1)}, bf16[12,144,144]{2,1,0:T(8,128)(2,1)}, u32[]{:S(2)}) copy-start(bf16[12,144,144]{2,1,0:T(8,128)(2,1)} %get-tuple-element.79.refs_4_) | copy-start | bytes 1492996
  25.3 13.2 %copy-start.3 = (bf16[2,768,192]{1,2,0:T(8,128)(2,1)S(1)}, bf16[2,768,192]{1,2,0:T(8,128)(2,1)}, u32[]{:S(2)}) copy-start(bf16[2,768,192]{1,2,0:T(8,128)(2,1)} %param.22) | copy-start | bytes 1769476
  25.3 13.2 %copy-start.4 = (bf16[2,3,192,144]{3,2,1,0:T(8,128)(2,1)S(1)}, bf16[2,3,192,144]{3,2,1,0:T(8,128)(2,1)}, u32[]{:S(2)}) copy-start(bf16[2,3,192,144]{3,2,1,0:T(8,128)(2,1)} %get-tuple-element.80.refs_5_) | copy-start | bytes 995332
  25.3 13.2 %copy-start.6 = (bf16[288,288]{1,0:T(8,128)(2,1)S(1)}, bf16[288,288]{1,0:T(8,128)(2,1)}, u32[]{:S(2)}) copy-start(bf16[288,288]{1,0:T(8,128)(2,1)} %constant.39.clone.refs_12_.refs_4_) | copy-start | bytes 497668
  37.4 18.6 %collective-permute-start.7 = (bf16[1792,128]{1,0:T(8,128)(2,1)}, bf16[1792,128]{1,0:T(8,128)(2,1)}, u32[]{:S(2)}, u32[]{:S(2)}) collective-permute-start(bf16[1792,128]{1,0:T(8,128)(2,1)} %get-tuple-element.99), channel_id=1, source_target_pairs={{1,0},{0,1},{3,2},{2,3},{5,4},{4,5},{7,6},{6,7},{9,8},{8,9},{11,10... | collective-permute-start | bytes 1376264 | tf_op jit(solution)/shard_map/ppermute | solution.py:835
  37.5 8.9 %collective-permute-start.3 = (bf16[144,192]{1,0:T(8,128)(2,1)}, bf16[144,192]{1,0:T(8,128)(2,1)}, u32[]{:S(2)}, u32[]{:S(2)}) collective-permute-start(bf16[144,192]{1,0:T(8,128)(2,1)} %get-tuple-element.72), channel_id=1, source_target_pairs={{255,0},{240,1},{241,2},{242,3},{243,4},{244,5},{245,6},{246,7},{2... | collective-permute-start | bytes 165896 | tf_op jit(solution)/shard_map/ppermute | solution.py:689
  37.5 8.8 %collective-permute-start.4 = (bf16[144,192]{1,0:T(8,128)(2,1)}, bf16[144,192]{1,0:T(8,128)(2,1)}, u32[]{:S(2)}, u32[]{:S(2)}) collective-permute-start(bf16[144,192]{1,0:T(8,128)(2,1)} %get-tuple-element.73), channel_id=1, source_target_pairs={{15,0},{0,1},{1,2},{2,3},{3,4},{4,5},{5,6},{6,7},{7,8},{8,9},{9,10... | collective-permute-start | bytes 165896 | tf_op jit(solution)/shard_map/ppermute | solution.py:689
  37.8 10.0 %collective-permute-start.5 = (bf16[144,192]{1,0:T(8,128)(2,1)}, bf16[144,192]{1,0:T(8,128)(2,1)}, u32[]{:S(2)}, u32[]{:S(2)}) collective-permute-start(bf16[144,192]{1,0:T(8,128)(2,1)} %get-tuple-element.74), channel_id=1, source_target_pairs={{240,0},{241,1},{242,2},{243,3},{244,4},{245,5},{246,6},{247,7},{2... | collective-permute-start | bytes 165896 | tf_op jit(solution)/shard_map/ppermute | solution.py:689
  55.0 2.5 %collective-permute-start.6 = (bf16[1792,128]{1,0:T(8,128)(2,1)S(1)}, bf16[1792,128]{1,0:T(8,128)(2,1)S(1)}, u32[]{:S(2)}, u32[]{:S(2)}) collective-permute-start(bf16[1792,128]{1,0:T(8,128)(2,1)S(1)} %get-tuple-element.97), channel_id=1, source_target_pairs={{1,0},{0,1},{3,2},{2,3},{5,4},{4,5},{7,6},{6,7},{9,8},{8,9},{11,10... | collective-permute-start | bytes 1376264 | tf_op jit(solution)/shard_map/ppermute | solution.py:835
  57.7 6.9 %collective-permute-start.9 = (bf16[896,128]{1,0:T(8,128)(2,1)S(1)}, bf16[896,128]{1,0:T(8,128)(2,1)S(1)}, u32[]{:S(2)}, u32[]{:S(2)}) collective-permute-start(bf16[896,128]{1,0:T(8,128)(2,1)S(1)} %broadcast_select_fusion.2), channel_id=1, source_target_pairs={{4,0},{5,1},{6,2},{7,3},{0,4},{1,5},{2,6},{3,7},{12,8},{13,9},{14,... | collective-permute-start | bytes 688136 | tf_op jit(solution)/shard_map/ppermute | solution.py:835
  57.8 6.9 %collective-permute-start.8 = (bf16[896,128]{1,0:T(8,128)(2,1)S(1)}, bf16[896,128]{1,0:T(8,128)(2,1)S(1)}, u32[]{:S(2)}, u32[]{:S(2)}) collective-permute-start(bf16[896,128]{1,0:T(8,128)(2,1)S(1)} %broadcast_select_fusion.5), channel_id=1, source_target_pairs={{2,0},{3,1},{0,2},{1,3},{6,4},{7,5},{4,6},{5,7},{10,8},{11,9},{8,1... | collective-permute-start | bytes 688136 | tf_op jit(solution)/shard_map/ppermute | solution.py:835
  64.9 3.7 %collective-permute-start.11 = (bf16[448,128]{1,0:T(8,128)(2,1)S(1)}, bf16[448,128]{1,0:T(8,128)(2,1)S(1)}, u32[]{:S(2)}, u32[]{:S(2)}) collective-permute-start(bf16[448,128]{1,0:T(8,128)(2,1)S(1)} %broadcast_select_fusion.8), channel_id=1, source_target_pairs={{2,0},{3,1},{0,2},{1,3},{6,4},{7,5},{4,6},{5,7},{10,8},{11,9},{8,1... | collective-permute-start | bytes 344072 | tf_op jit(solution)/shard_map/ppermute | solution.py:835
  65.0 3.7 %collective-permute-start.10 = (bf16[448,128]{1,0:T(8,128)(2,1)S(1)}, bf16[448,128]{1,0:T(8,128)(2,1)S(1)}, u32[]{:S(2)}, u32[]{:S(2)}) collective-permute-start(bf16[448,128]{1,0:T(8,128)(2,1)S(1)} %broadcast_select_fusion.14), channel_id=1, source_target_pairs={{4,0},{5,1},{6,2},{7,3},{0,4},{1,5},{2,6},{3,7},{12,8},{13,9},{14,... | collective-permute-start | bytes 344072 | tf_op jit(solution)/shard_map/ppermute | solution.py:835
  68.8 5.3 %collective-permute-start.12 = (bf16[448,128]{1,0:T(8,128)(2,1)S(1)}, bf16[448,128]{1,0:T(8,128)(2,1)S(1)}, u32[]{:S(2)}, u32[]{:S(2)}) collective-permute-start(bf16[448,128]{1,0:T(8,128)(2,1)S(1)} %broadcast_select_fusion.11), channel_id=1, source_target_pairs={{12,0},{13,1},{14,2},{15,3},{8,4},{9,5},{10,6},{11,7},{4,8},{5,9},... | collective-permute-start | bytes 344072 | tf_op jit(solution)/shard_map/ppermute | solution.py:835
  74.2 4.6 %collective-permute-start.13 = (bf16[768,128]{1,0:T(8,128)(2,1)S(1)}, bf16[768,128]{1,0:T(8,128)(2,1)S(1)}, u32[]{:S(2)}, u32[]{:S(2)}) collective-permute-start(bf16[768,128]{1,0:T(8,128)(2,1)S(1)} %pad_maximum_fusion.4), channel_id=1, source_target_pairs={{16,0},{17,1},{18,2},{19,3},{20,4},{21,5},{22,6},{23,7},{24,8},{25... | collective-permute-start | bytes 589832 | tf_op jit(solution)/shard_map/ppermute | solution.py:835
  79.0 6.7 %collective-permute-start.14 = (bf16[608,128]{1,0:T(8,128)(2,1)S(1)}, bf16[608,128]{1,0:T(8,128)(2,1)S(1)}, u32[]{:S(2)}, u32[]{:S(2)}) collective-permute-start(bf16[608,128]{1,0:T(8,128)(2,1)S(1)} %pad_maximum_fusion.6), channel_id=1, source_target_pairs={{32,0},{33,1},{34,2},{35,3},{36,4},{37,5},{38,6},{39,7},{40,8},{41... | collective-permute-start | bytes 466952 | tf_op jit(solution)/shard_map/ppermute | solution.py:835
  85.8 6.4 %collective-permute-start.15 = (bf16[608,128]{1,0:T(8,128)(2,1)S(1)}, bf16[608,128]{1,0:T(8,128)(2,1)S(1)}, u32[]{:S(2)}, u32[]{:S(2)}) collective-permute-start(bf16[608,128]{1,0:T(8,128)(2,1)S(1)} %pad_maximum_fusion.7), channel_id=1, source_target_pairs={{112,0},{113,1},{114,2},{115,3},{116,4},{117,5},{118,6},{119,7},{1... | collective-permute-start | bytes 466952 | tf_op jit(solution)/shard_map/ppermute | solution.py:835
  92.2 5.7 %collective-permute-start.16 = (bf16[608,128]{1,0:T(8,128)(2,1)S(1)}, bf16[608,128]{1,0:T(8,128)(2,1)S(1)}, u32[]{:S(2)}, u32[]{:S(2)}) collective-permute-start(bf16[608,128]{1,0:T(8,128)(2,1)S(1)} %add_convert_fusion.5), channel_id=1, source_target_pairs={{128,0},{129,1},{130,2},{131,3},{132,4},{133,5},{134,6},{135,7},{1... | collective-permute-start | bytes 466952 | tf_op jit(solution)/shard_map/ppermute | solution.py:835
  97.9 3.9 %collective-permute-start.18 = (bf16[160,128]{1,0:T(8,128)(2,1)S(1)}, bf16[160,128]{1,0:T(8,128)(2,1)S(1)}, u32[]{:S(2)}, u32[]{:S(2)}) collective-permute-start(bf16[160,128]{1,0:T(8,128)(2,1)S(1)} %slice.91), channel_id=1, source_target_pairs={{32,0},{33,1},{34,2},{35,3},{36,4},{37,5},{38,6},{39,7},{40,8},{41... | collective-permute-start | bytes 122888 | tf_op jit(solution)/shard_map/ppermute | solution.py:835
  99.0 4.9 %collective-permute-start.17 = (bf16[448,128]{1,0:T(8,128)(2,1)S(1)}, bf16[448,128]{1,0:T(8,128)(2,1)S(1)}, u32[]{:S(2)}, u32[]{:S(2)}) collective-permute-start(bf16[448,128]{1,0:T(8,128)(2,1)S(1)} %slice.90), channel_id=1, source_target_pairs={{12,0},{13,1},{14,2},{15,3},{8,4},{9,5},{10,6},{11,7},{4,8},{5,9},... | collective-permute-start | bytes 344072 | tf_op jit(solution)/shard_map/ppermute | solution.py:835
  103.8 3.4 %collective-permute-start.21 = (bf16[320,128]{1,0:T(8,128)(2,1)S(1)}, bf16[320,128]{1,0:T(8,128)(2,1)S(1)}, u32[]{:S(2)}, u32[]{:S(2)}) collective-permute-start(bf16[320,128]{1,0:T(8,128)(2,1)S(1)} %pad_maximum_fusion.8), channel_id=1, source_target_pairs={{16,0},{17,1},{18,2},{19,3},{20,4},{21,5},{22,6},{23,7},{24,8},{25... | collective-permute-start | bytes 245768 | tf_op jit(solution)/shard_map/ppermute | solution.py:835
  103.9 3.7 %collective-permute-start.19 = (bf16[448,128]{1,0:T(8,128)(2,1)S(1)}, bf16[448,128]{1,0:T(8,128)(2,1)S(1)}, u32[]{:S(2)}, u32[]{:S(2)}) collective-permute-start(bf16[448,128]{1,0:T(8,128)(2,1)S(1)} %get-tuple-element.114), channel_id=1, source_target_pairs={{4,0},{5,1},{6,2},{7,3},{0,4},{1,5},{2,6},{3,7},{12,8},{13,9},{14,... | collective-permute-start | bytes 344072 | tf_op jit(solution)/shard_map/ppermute | solution.py:835
  104.0 3.7 %collective-permute-start.20 = (bf16[448,128]{1,0:T(8,128)(2,1)S(1)}, bf16[448,128]{1,0:T(8,128)(2,1)S(1)}, u32[]{:S(2)}, u32[]{:S(2)}) collective-permute-start(bf16[448,128]{1,0:T(8,128)(2,1)S(1)} %get-tuple-element.115), channel_id=1, source_target_pairs={{2,0},{3,1},{0,2},{1,3},{6,4},{7,5},{4,6},{5,7},{10,8},{11,9},{8,1... | collective-permute-start | bytes 344072 | tf_op jit(solution)/shard_map/ppermute | solution.py:835
  107.8 5.0 %collective-permute-start.22 = (bf16[896,128]{1,0:T(8,128)(2,1)S(1)}, bf16[896,128]{1,0:T(8,128)(2,1)S(1)}, u32[]{:S(2)}, u32[]{:S(2)}) collective-permute-start(bf16[896,128]{1,0:T(8,128)(2,1)S(1)} %get-tuple-element.117), channel_id=1, source_target_pairs={{2,0},{3,1},{0,2},{1,3},{6,4},{7,5},{4,6},{5,7},{10,8},{11,9},{8,1... | collective-permute-start | bytes 688136 | tf_op jit(solution)/shard_map/ppermute | solution.py:835
  109.2 4.9 %collective-permute-start.23 = (bf16[896,128]{1,0:T(8,128)(2,1)S(1)}, bf16[896,128]{1,0:T(8,128)(2,1)S(1)}, u32[]{:S(2)}, u32[]{:S(2)}) collective-permute-start(bf16[896,128]{1,0:T(8,128)(2,1)S(1)} %get-tuple-element.118), channel_id=1, source_target_pairs={{4,0},{5,1},{6,2},{7,3},{0,4},{1,5},{2,6},{3,7},{12,8},{13,9},{14,... | collective-permute-start | bytes 688136 | tf_op jit(solution)/shard_map/ppermute | solution.py:835
  112.8 14.1 %copy-start.9 = (bf16[144,192]{1,0:T(8,128)(2,1)S(1)}, bf16[144,192]{1,0:T(8,128)(2,1)}, u32[]{:S(2)}) copy-start(bf16[144,192]{1,0:T(8,128)(2,1)} %get-tuple-element.77.refs_3_) | copy-start | bytes 165892
  114.2 14.8 %collective-permute-start.24 = (bf16[1792,128]{1,0:T(8,128)(2,1)S(1)}, bf16[1792,128]{1,0:T(8,128)(2,1)S(1)}, u32[]{:S(2)}, u32[]{:S(2)}) collective-permute-start(bf16[1792,128]{1,0:T(8,128)(2,1)S(1)} %pad_maximum_fusion.first_own), channel_id=1, source_target_pairs={{1,0},{0,1},{3,2},{2,3},{5,4},{4,5},{7,6},{6,7},{9,8},{8,9},{11,10... | collective-permute-start | bytes 1376264 | tf_op jit(solution)/shard_map/ppermute | solution.py:835
  126.8 2.2 %collective-permute-start.25 = (bf16[1792,128]{1,0:T(8,128)(2,1)S(1)}, bf16[1792,128]{1,0:T(8,128)(2,1)S(1)}, u32[]{:S(2)}, u32[]{:S(2)}) collective-permute-start(bf16[1792,128]{1,0:T(8,128)(2,1)S(1)} %pad_maximum_fusion.1.second_own), channel_id=1, source_target_pairs={{1,0},{0,1},{3,2},{2,3},{5,4},{4,5},{7,6},{6,7},{9,8},{8,9},{11,10... | collective-permute-start | bytes 1376264 | tf_op jit(solution)/shard_map/ppermute | solution.py:835
  (11 other events, 53.5 us)

commit v4 on v3

--- a/solution.py
+++ b/solution.py
@@ -3,7 +3,6 @@
 
 import jax
 import jax.numpy as jnp
-import numpy as np
 from jax import lax
 from jax.experimental import pallas as pl
 from jax.experimental.pallas import tpu as pltpu
@@ -33,31 +32,6 @@
 BF16 = jnp.bfloat16
 
 
-def quadrant_rows():
-    rows = np.zeros(TOKENS, np.int64)
-    at = 0
-    for lat_half in range(2):
-        for lon_half in range(2):
-            for level in range(4):
-                for row in range(3):
-                    for col in range(6):
-                        rows[at] = (level * 6 + lat_half * 3 + row) * 12 + lon_half * 6 + col
-                        at += 1
-    return rows
-
-
-def rolled_rows():
-    rows = quadrant_rows()
-    level, rest = rows // 72, rows % 72
-    return ((level + 3) % 4) * 72 + rest
-
-
-def one_hot(rows):
-    picked = np.zeros((TOKENS, TOKENS), np.float32)
-    picked[np.arange(TOKENS), rows] = 1.0
-    return picked
-
-
 def mm(left, right):
     return lax.dot_general(left, right, (((1,), (0,)), ((), ())), preferred_element_type=F32)
 
@@ -70,6 +44,39 @@
     return (
         lax.broadcasted_iota(jnp.int32, (size, size), 0) == lax.broadcasted_iota(jnp.int32, (size, size), 1)
     ).astype(F32).astype(BF16)
+
+
+def divided(value, divisor, count):
+    quotient = jnp.zeros_like(value)
+    for number in range(1, count):
+        quotient = quotient + (value >= number * divisor).astype(jnp.int32)
+    return quotient, value - quotient * divisor
+
+
+def lanes_of_tokens():
+    return lax.broadcasted_iota(jnp.int32, (1, TOKENS), 1)
+
+
+def row_of_quad(roll):
+    lat_half, rest = divided(lanes_of_tokens(), 2 * QUAD, 2)
+    lon_half, rest = divided(rest, QUAD, 2)
+    level, rest = divided(rest, 18, 4)
+    row, col = divided(rest, 6, 3)
+    level = (level + 4 - roll) & 3
+    return (level * 6 + lat_half * 3 + row) * 12 + lon_half * 6 + col
+
+
+def quad_of_row(roll):
+    level, rest = divided(lanes_of_tokens(), QUAD, 4)
+    row, col = divided(rest, 12, 6)
+    lat_half, row = divided(row, 3, 2)
+    lon_half, col = divided(col, 6, 2)
+    level = (level + roll) & 3
+    return lat_half * 2 * QUAD + lon_half * QUAD + level * 18 + row * 6 + col
+
+
+def places(rows):
+    return (lax.broadcasted_iota(jnp.int32, (TOKENS, TOKENS), 0) == rows).astype(F32).astype(BF16)
 
 
 def turned(value):
@@ -364,7 +371,6 @@
     up_ref,
     down_ref,
     table_ref,
-    order_ref,
     quad_0,
     quad_1,
     quad_2,
@@ -381,7 +387,7 @@
     gain_one, gain_two, in_weight, out_weight, up_weight, down_weight = block_weights(
         gains_ref, in_ref, out_ref, up_ref, down_ref
     )
-    order = order_ref[...]
+    order = places(quad_of_row(0))
     grad_quads = mm(order, load_grid(grad_ref, rows_ref).astype(BF16))
     flat = load_grid(inputs_ref, rows_ref)
     flat_out[0] = flat.astype(BF16)
@@ -440,8 +446,6 @@
     out_ref,
     up_ref,
     down_ref,
-    ahead_ref,
-    back_ref,
     back_0,
     back_1,
     back_2,
@@ -453,7 +457,7 @@
     packed_ref,
 ):
     quads = [quad[...].astype(F32) for quad in (quad_0, quad_1, quad_2, quad_3)]
-    ahead = ahead_ref[...]
+    ahead = places(row_of_quad(1))
     flat = mm(ahead, jnp.concatenate([quad[:QUAD] for quad in quads], axis=0).astype(BF16))
     grad = mm(ahead, jnp.concatenate([quad[QUAD:] for quad in quads], axis=0).astype(BF16))
     gain_one, gain_two, in_weight, out_weight, up_weight, down_weight = block_weights(
@@ -473,7 +477,7 @@
         first_hat, first_inverse, first_norm, gain_one, gain_two, in_weight, out_weight, up_weight,
         down_weight, scaled_ref, packed_ref,
     )
-    back = back_ref[...]
+    back = places(quad_of_row(1))
     result_quads, grad_quads = mm(back, result), mm(back, grad_in)
     for index, quad in enumerate((back_0, back_1, back_2, back_3)):
         rows = slice(index * QUAD, (index + 1) * QUAD)
@@ -517,7 +521,6 @@
     out_ref,
     up_ref,
     down_ref,
-    natural_ref,
     keep_ref,
     send_ref,
     rows_out,
@@ -525,7 +528,7 @@
     packed_ref,
 ):
     quads = [quad[...].astype(F32) for quad in (quad_0, quad_1, quad_2, quad_3)]
-    grad = mm(natural_ref[...], jnp.concatenate([quad[QUAD:] for quad in quads], axis=0).astype(BF16))
+    grad = mm(places(row_of_quad(0)), jnp.concatenate([quad[QUAD:] for quad in quads], axis=0).astype(BF16))
     gain_one, gain_two, in_weight, out_weight, up_weight, down_weight = block_weights(
         gains_ref, in_ref, out_ref, up_ref, down_ref
     )
@@ -546,9 +549,9 @@
     write_halves(upper_ref, packed_ref, keep_ref, send_ref)
 
 
-def grids_kernel(quad_0, quad_1, quad_2, quad_3, natural_ref, grad_rows_ref, blocks_out, grad_out, rows_ref):
+def grids_kernel(quad_0, quad_1, quad_2, quad_3, grad_rows_ref, blocks_out, grad_out, rows_ref):
     quads = [quad[:QUAD].astype(F32) for quad in (quad_0, quad_1, quad_2, quad_3)]
-    blocks = mm(natural_ref[...], jnp.concatenate(quads, axis=0).astype(BF16))
+    blocks = mm(places(row_of_quad(0)), jnp.concatenate(quads, axis=0).astype(BF16))
     store_grid(blocks, rows_ref, blocks_out)
     store_grid(grad_rows_ref[...].astype(F32), rows_ref, grad_out)
 
@@ -707,10 +710,6 @@
     inputs, grad_out = inputs.transpose(1, 2, 0, 3), grad_out.transpose(1, 2, 0, 3)
     bias_tables = bias_tables.transpose(0, 1, 3, 2, 4)
     bias_level = bias_level.T
-    quadrant = one_hot(quadrant_rows())
-    rolled = one_hot(rolled_rows())
-    half = [jnp.asarray(array, BF16) for array in (quadrant, quadrant.T, rolled, rolled.T)]
-    to_quads, from_quads, rolled_back, rolled_ahead = half
     is_upper = odd(core_step()[1]).reshape(1)
 
     quad_shape = shape_of((2 * QUAD, C), BF16)
@@ -728,7 +727,7 @@
     quads = call(
         first_kernel,
         (bias_level,),
-        (inputs, grad_out, *first_weights, Part(bias_tables, 0), to_quads),
+        (inputs, grad_out, *first_weights, Part(bias_tables, 0)),
         [quad_shape] * 4
         + [
             shape_of(weights_shape, BF16),
@@ -756,7 +755,7 @@
     *back, second_keep, second_send, second_scaled = call(
         second_kernel,
         (is_upper,),
-        (*ahead, bias, *second_weights, rolled_ahead, rolled_back),
+        (*ahead, bias, *second_weights),
         [quad_shape] * 4 + [half_shape, half_shape, shape_of(weights_shape, BF16)],
         [pltpu.VMEM(weights_shape, BF16), packed_scratch],
         3_000_000_000,
@@ -767,7 +766,6 @@
         shifted(back[1], 0, -1),
         back[0],
     ]
-    home[3], stored[2] = tie((home[3], stored[2]))
     active, slope, *first_near = near_call(
         activation_kernel,
         (),
@@ -776,7 +774,7 @@
         [],
         300_000_000,
         (0, 1),
-        (home[3], *stored, *first_weights, from_quads),
+        (home[3], *stored, *first_weights),
     )
     second_got = exchanged(second_send, core_step()[0])
     first_keep, first_send, grad_rows, first_scaled = near_call(
@@ -790,7 +788,7 @@
     blocks_out, grad_inputs = near_call(
         grids_kernel,
         (),
-        (*home, from_quads, grad_rows),
+        (*home, grad_rows),
         [grid_shape, grid_shape],
         [rows_scratch],
         100_000_000,

time: 132 us -> 130 us (0.985)
  Pallas kernels: 42.1 us -> 40.2 us
    pallas_call x5, Pallas kernels: 17.1 us -> 15.4 us  [near_call(): pl.pallas_call(body, in_specs=[SMEM] * len(scalars) + [VMEM if is_near(op...]
    unnamed x34 -> x32, local copies, waits for them, and re-layouts: 3.15 us -> 3.15 us
  transfers between devices with their start and end apart: 26 -> 26, of which waited for: 17 -> 18; matrix products, arithmetic and copies ran while one was open for 1% -> 1% of each run, Pallas kernels for 15% -> 14%
where the time goes in v4:
time: 130 us
  starting transfers between devices  42.7 us (33%)
  waiting for transfers between devices  40.3 us (31%)
  Pallas kernels  40.2 us (31%)
  local copies, waits for them, and re-layouts  3.16 us (2%)
  other arithmetic  2.26 us (2%)
  between operations  1.3 us (1%)
    ppermute x20, waiting for transfers between devices, exchanged(): return lax.ppermute(value, ('lon', 'lat'), pairs)  35.5 us
    ppermute x20, starting transfers between devices, exchanged(): return lax.ppermute(value, ('lon', 'lat'), pairs)  28.5 us
    pallas_call x3, Pallas kernels, call(): pl.pallas_call(kernel, grid=(1,), in_specs=[SMEM] * len(scalars) + specs,...  22.7 us
    pallas_call x5, Pallas kernels, near_call(): pl.pallas_call(body, in_specs=[SMEM] * len(scalars) + [VMEM if is_near(op...  15.4 us
    ppermute x6, starting transfers between devices, shifted(): return lax.ppermute(value, ('lon', 'lat'), pairs)  14.2 us
    ppermute x6, waiting for transfers between devices, shifted(): return lax.ppermute(value, ('lon', 'lat'), pairs)  4.8 us
    unnamed x32, local copies, waits for them, and re-layouts  3.15 us
  transfers between devices with their start and end apart: 26, of which 18 were waited for; matrix products, arithmetic and copies ran while one was open for 1% of the time, Pallas kernels for 14%

profile of v4, /device:TPU:1, one launch (start us, length us, event | category | flops | bytes accessed | tf_op | source)
XLA Modules:
  0.0 129.9 jit_solution(11913150167041518160)
XLA Ops:
  0.6 7.7 %shard_map.161 = (bf16[144,192]{1,0:T(8,128)(2,1)}, bf16[144,192]{1,0:T(8,128)(2,1)}, bf16[144,192]{1,0:T(8,128)(2,1)}, bf16[144,192]{1,0:T(8,128)(2,1)}, bf16[1...) custom-call(s32[1,2]{1,0:T(1,128)} %bitcast.14, ...), custom_call_target="tpu_custom_call" | custom-call | flops 1000000000 | bytes 4000000 | tf_op jit(solution)/shard_map/pallas_call | solution.py:593
  8.3 9.0 %collective-permute-start = (bf16[144,192]{1,0:T(8,128)(2,1)}, bf16[144,192]{1,0:T(8,128)(2,1)S(1)}, u32[]{:S(2)}, u32[]{:S(2)}) collective-permute-start(bf16[144,192]{1,0:T(8,128)(2,1)} %get-tuple-element.66), channel_id=1, source_target_pairs={{16,0},{17,1},{18,2},{19,3},{20,4},{21,5},{22,6},{23,7},{24,8},{25... | collective-permute-start | bytes 165896 | tf_op jit(solution)/shard_map/ppermute | solution.py:692
  18.3 3.2 %collective-permute-start.2 = (bf16[144,192]{1,0:T(8,128)(2,1)}, bf16[144,192]{1,0:T(8,128)(2,1)S(1)}, u32[]{:S(2)}, u32[]{:S(2)}) collective-permute-start(bf16[144,192]{1,0:T(8,128)(2,1)} %get-tuple-element.68), channel_id=1, source_target_pairs={{17,0},{18,1},{19,2},{20,3},{21,4},{22,5},{23,6},{24,7},{25,8},{26... | collective-permute-start | bytes 165896 | tf_op jit(solution)/shard_map/ppermute | solution.py:692
  21.6 3.0 %shard_map.162.bias_ref = bf16[12,144,144]{2,1,0:T(8,128)(2,1)} custom-call(s32[1,2]{1,0:T(1,128)} %bitcast.15, s32[6,4,12]{2,1,0:T(4,128)} %bitcast.24, bf16[2,1,6,2,3312]{4,3,2,1,0:T(2,128)(2,1)} %bitcast.21), custom_call_target="tpu_custom_call" | custom-call | flops 500000000 | bytes 4000000 | tf_op jit(solution)/shard_map/pallas_call | solution.py:593
  25.3 12.0 %shard_map.163 = (bf16[144,192]{1,0:T(8,128)(2,1)}, bf16[144,192]{1,0:T(8,128)(2,1)}, bf16[144,192]{1,0:T(8,128)(2,1)}, bf16[144,192]{1,0:T(8,128)(2,1)}, bf16[1...) custom-call(s32[1]{0:T(128)} %bitcast.upper_ref.refs_0_, ...), custom_call_target="tpu_custom_call" | custom-call | flops 3000000000 | bytes 4000000 | tf_op jit(solution)/shard_map/pallas_call | solution.py:593
  40.3 2.5 %shard_map.164 = (bf16[288,768]{1,0:T(8,128)(2,1)S(1)}, bf16[288,768]{1,0:T(8,128)(2,1)S(1)}, bf16[144,192]{1,0:T(8,128)(2,1)S(1)}, bf16[12,144,144]{2,1,0:T(8,1...) custom-call(bf16[3,288,192]{2,1,0:T(8,128)(2,1)S(1)} %copy-done.1, ...), custom_call_target="tpu_custom_call" | custom-call | flops 300000000 | bytes 4000000 | tf_op jit(solution)/shard_map/pallas_call | solution.py:661
  42.8 3.3 %collective-permute-done.3.refs_1_.refs_0_ = bf16[144,192]{1,0:T(8,128)(2,1)S(1)} collective-permute-done((bf16[144,192]{1,0:T(8,128)(2,1)}, bf16[144,192]{1,0:T(8,128)(2,1)S(1)}, u32[]{:S(2)}, u32[]{:S(2)}) %collective-permute-start.3) | collective-permute-done | bytes 55328 | tf_op jit(solution)/shard_map/ppermute | solution.py:692
  46.1 1.5 %collective-permute-done.5.refs_3_.refs_2_ = bf16[144,192]{1,0:T(8,128)(2,1)S(1)} collective-permute-done((bf16[144,192]{1,0:T(8,128)(2,1)}, bf16[144,192]{1,0:T(8,128)(2,1)S(1)}, u32[]{:S(2)}, u32[]{:S(2)}) %collective-permute-start.5) | collective-permute-done | bytes 55328 | tf_op jit(solution)/shard_map/ppermute | solution.py:692
  47.5 6.2 %shard_map.165 = (bf16[1792,128]{1,0:T(8,128)(2,1)S(1)}, bf16[1792,128]{1,0:T(8,128)(2,1)S(1)}, bf16[288,192]{1,0:T(8,128)(2,1)S(1)}, bf16[12,144,144]{2,1,0:T(8,128)(2,1)S(1)}) custom-call(s32[1]{0:T(128)} %bitcast.upper_ref.refs_0_, bf16[144,192]{1,0:T(8,128)(2,1)S(1)} %collective-permute-done.3.refs_1_.refs_0_, ...), custom_call_target="tpu_custom_call" | custom-call | flops 2000000000 | bytes 4000000 | tf_op jit(solution)/shard_map/pallas_call | solution.py:661
  54.9 1.1 add_convert_fusion
  57.5 2.4 %shard_map.167.refs_2_ = bf16[320,128]{1,0:T(8,128)(2,1)S(1)} custom-call(s32[1,2]{1,0:T(1,128)S(1)} %bitcast.16, bf16[12,144,144]{2,1,0:T(8,128)(2,1)S(1)} %copy-done.11), custom_call_target="tpu_custom_call" | custom-call | flops 500000000 | bytes 4000000 | tf_op jit(solution)/shard_map/pallas_call | solution.py:661
  59.9 3.5 %collective-permute-done.9 = bf16[896,128]{1,0:T(8,128)(2,1)S(1)} collective-permute-done((bf16[896,128]{1,0:T(8,128)(2,1)S(1)}, bf16[896,128]{1,0:T(8,128)(2,1)S(1)}, u32[]{:S(2)}, u32[]{:S(2)}) %collective-permute-start.9) | collective-permute-done | bytes 229408 | tf_op jit(solution)/shard_map/ppermute | solution.py:833
  63.8 1.5 %collective-permute-start.10 = (bf16[448,128]{1,0:T(8,128)(2,1)S(1)}, bf16[448,128]{1,0:T(8,128)(2,1)S(1)}, u32[]{:S(2)}, u32[]{:S(2)}) collective-permute-start(bf16[448,128]{1,0:T(8,128)(2,1)S(1)} %broadcast_select_fusion.14), channel_id=1, source_target_pairs={{4,0},{5,1},{6,2},{7,3},{0,4},{1,5},{2,6},{3,7},{12,8},{13,9},{14,... | collective-permute-start | bytes 344072 | tf_op jit(solution)/shard_map/ppermute | solution.py:833
  65.3 2.1 %collective-permute-done.11 = bf16[448,128]{1,0:T(8,128)(2,1)S(1)} collective-permute-done((bf16[448,128]{1,0:T(8,128)(2,1)S(1)}, bf16[448,128]{1,0:T(8,128)(2,1)S(1)}, u32[]{:S(2)}, u32[]{:S(2)}) %collective-permute-start.11) | collective-permute-done | bytes 114720 | tf_op jit(solution)/shard_map/ppermute | solution.py:833
  67.6 2.7 %collective-permute-start.12 = (bf16[448,128]{1,0:T(8,128)(2,1)S(1)}, bf16[448,128]{1,0:T(8,128)(2,1)S(1)}, u32[]{:S(2)}, u32[]{:S(2)}) collective-permute-start(bf16[448,128]{1,0:T(8,128)(2,1)S(1)} %broadcast_select_fusion.11), channel_id=1, source_target_pairs={{12,0},{13,1},{14,2},{15,3},{8,4},{9,5},{10,6},{11,7},{4,8},{5,9},... | collective-permute-start | bytes 344072 | tf_op jit(solution)/shard_map/ppermute | solution.py:833
  70.3 2.6 %shard_map.168 = bf16[640,128]{1,0:T(8,128)(2,1)S(1)} custom-call(s32[1,2]{1,0:T(1,128)S(1)} %bitcast.17, bf16[12,144,144]{2,1,0:T(8,128)(2,1)S(1)} %get-tuple-element.103.refs_1_, bf16[320,128]{1,0:T(8,128)(2,1)S(1)} %shard_map.167.refs_2_), custom_call_target="tpu_custom_call" | custom-call | flops 500000000 | bytes 4000000 | tf_op jit(solution)/shard_map/pallas_call | solution.py:661
  73.1 4.5 %collective-permute-done.13 = bf16[768,128]{1,0:T(8,128)(2,1)S(1)} collective-permute-done((bf16[768,128]{1,0:T(8,128)(2,1)S(1)}, bf16[768,128]{1,0:T(8,128)(2,1)S(1)}, u32[]{:S(2)}, u32[]{:S(2)}) %collective-permute-start.13) | collective-permute-done | bytes 196640 | tf_op jit(solution)/shard_map/ppermute | solution.py:833
  78.1 6.4 %collective-permute-done.14 = bf16[608,128]{1,0:T(8,128)(2,1)S(1)} collective-permute-done((bf16[608,128]{1,0:T(8,128)(2,1)S(1)}, bf16[608,128]{1,0:T(8,128)(2,1)S(1)}, u32[]{:S(2)}, u32[]{:S(2)}) %collective-permute-start.14) | collective-permute-done | bytes 155680 | tf_op jit(solution)/shard_map/ppermute | solution.py:833
  84.8 6.1 %collective-permute-done.15 = bf16[608,128]{1,0:T(8,128)(2,1)S(1)} collective-permute-done((bf16[608,128]{1,0:T(8,128)(2,1)S(1)}, bf16[608,128]{1,0:T(8,128)(2,1)S(1)}, u32[]{:S(2)}, u32[]{:S(2)}) %collective-permute-start.15) | collective-permute-done | bytes 155680 | tf_op jit(solution)/shard_map/ppermute | solution.py:833
  91.0 1.8 %collective-permute-start.16 = (bf16[608,128]{1,0:T(8,128)(2,1)S(1)}, bf16[608,128]{1,0:T(8,128)(2,1)S(1)}, u32[]{:S(2)}, u32[]{:S(2)}) collective-permute-start(bf16[608,128]{1,0:T(8,128)(2,1)S(1)} %add_convert_fusion.5), channel_id=1, source_target_pairs={{128,0},{129,1},{130,2},{131,3},{132,4},{133,5},{134,6},{135,7},{1... | collective-permute-start | bytes 466952 | tf_op jit(solution)/shard_map/ppermute | solution.py:833
  92.8 3.9 %collective-permute-done.16 = bf16[608,128]{1,0:T(8,128)(2,1)S(1)} collective-permute-done((bf16[608,128]{1,0:T(8,128)(2,1)S(1)}, bf16[608,128]{1,0:T(8,128)(2,1)S(1)}, u32[]{:S(2)}, u32[]{:S(2)}) %collective-permute-start.16) | collective-permute-done | bytes 155680 | tf_op jit(solution)/shard_map/ppermute | solution.py:833
  97.8 1.9 %collective-permute-start.17 = (bf16[448,128]{1,0:T(8,128)(2,1)S(1)}, bf16[448,128]{1,0:T(8,128)(2,1)S(1)}, u32[]{:S(2)}, u32[]{:S(2)}) collective-permute-start(bf16[448,128]{1,0:T(8,128)(2,1)S(1)} %slice.90), channel_id=1, source_target_pairs={{12,0},{13,1},{14,2},{15,3},{8,4},{9,5},{10,6},{11,7},{4,8},{5,9},... | collective-permute-start | bytes 344072 | tf_op jit(solution)/shard_map/ppermute | solution.py:833
  100.8 1.9 %collective-permute-done.17 = bf16[448,128]{1,0:T(8,128)(2,1)S(1)} collective-permute-done((bf16[448,128]{1,0:T(8,128)(2,1)S(1)}, bf16[448,128]{1,0:T(8,128)(2,1)S(1)}, u32[]{:S(2)}, u32[]{:S(2)}) %collective-permute-start.17) | collective-permute-done | bytes 114720 | tf_op jit(solution)/shard_map/ppermute | solution.py:833
  102.9 1.5 %collective-permute-start.20 = (bf16[448,128]{1,0:T(8,128)(2,1)S(1)}, bf16[448,128]{1,0:T(8,128)(2,1)S(1)}, u32[]{:S(2)}, u32[]{:S(2)}) collective-permute-start(bf16[448,128]{1,0:T(8,128)(2,1)S(1)} %get-tuple-element.109), channel_id=1, source_target_pairs={{2,0},{3,1},{0,2},{1,3},{6,4},{7,5},{4,6},{5,7},{10,8},{11,9},{8,1... | collective-permute-start | bytes 344072 | tf_op jit(solution)/shard_map/ppermute | solution.py:833
  104.4 1.7 %collective-permute-done.21 = bf16[320,128]{1,0:T(8,128)(2,1)S(1)} collective-permute-done((bf16[320,128]{1,0:T(8,128)(2,1)S(1)}, bf16[320,128]{1,0:T(8,128)(2,1)S(1)}, u32[]{:S(2)}, u32[]{:S(2)}) %collective-permute-start.21) | collective-permute-done | bytes 81952 | tf_op jit(solution)/shard_map/ppermute | solution.py:833
  106.7 1.6 %collective-permute-start.22 = (bf16[896,128]{1,0:T(8,128)(2,1)S(1)}, bf16[896,128]{1,0:T(8,128)(2,1)S(1)}, u32[]{:S(2)}, u32[]{:S(2)}) collective-permute-start(bf16[896,128]{1,0:T(8,128)(2,1)S(1)} %get-tuple-element.111), channel_id=1, source_target_pairs={{2,0},{3,1},{0,2},{1,3},{6,4},{7,5},{4,6},{5,7},{10,8},{11,9},{8,1... | collective-permute-start | bytes 688136 | tf_op jit(solution)/shard_map/ppermute | solution.py:833
  108.2 1.4 %collective-permute-start.23 = (bf16[896,128]{1,0:T(8,128)(2,1)S(1)}, bf16[896,128]{1,0:T(8,128)(2,1)S(1)}, u32[]{:S(2)}, u32[]{:S(2)}) collective-permute-start(bf16[896,128]{1,0:T(8,128)(2,1)S(1)} %get-tuple-element.112), channel_id=1, source_target_pairs={{4,0},{5,1},{6,2},{7,3},{0,4},{1,5},{2,6},{3,7},{12,8},{13,9},{14,... | collective-permute-start | bytes 688136 | tf_op jit(solution)/shard_map/ppermute | solution.py:833
  109.6 2.0 %collective-permute-done.22 = bf16[896,128]{1,0:T(8,128)(2,1)S(1)} collective-permute-done((bf16[896,128]{1,0:T(8,128)(2,1)S(1)}, bf16[896,128]{1,0:T(8,128)(2,1)S(1)}, u32[]{:S(2)}, u32[]{:S(2)}) %collective-permute-start.22) | collective-permute-done | bytes 229408 | tf_op jit(solution)/shard_map/ppermute | solution.py:833
  111.7 1.4 %collective-permute-done.23 = bf16[896,128]{1,0:T(8,128)(2,1)S(1)} collective-permute-done((bf16[896,128]{1,0:T(8,128)(2,1)S(1)}, bf16[896,128]{1,0:T(8,128)(2,1)S(1)}, u32[]{:S(2)}, u32[]{:S(2)}) %collective-permute-start.23) | collective-permute-done | bytes 229408 | tf_op jit(solution)/shard_map/ppermute | solution.py:833
  113.2 12.3 %collective-permute-start.24 = (bf16[1792,128]{1,0:T(8,128)(2,1)S(1)}, bf16[1792,128]{1,0:T(8,128)(2,1)S(1)}, u32[]{:S(2)}, u32[]{:S(2)}) collective-permute-start(bf16[1792,128]{1,0:T(8,128)(2,1)S(1)} %pad_maximum_fusion.first_own), channel_id=1, source_target_pairs={{1,0},{0,1},{3,2},{2,3},{5,4},{4,5},{7,6},{6,7},{9,8},{8,9},{11,10... | collective-permute-start | bytes 1376264 | tf_op jit(solution)/shard_map/ppermute | solution.py:833
  125.6 1.7 %shard_map.166 = (bf16[6,12,4,192]{3,2,1,0:T(4,128)(2,1)}, bf16[6,12,4,192]{3,2,1,0:T(4,128)(2,1)}) custom-call(bf16[144,192]{1,0:T(8,128)(2,1)S(1)} %collective-permute-done.3.refs_1_.refs_0_, bf16[144,192]{1,0:T(8,128)(2,1)S(1)} %collective-permute-done.4.refs_2_.refs_1_, bf16[144,192]{1,0:T(8,128)(2,1)S(1)} %collective-permute-done.5.refs_3_.refs_2_, ...), custom_call_target="tpu_custom_call" | custom-call | flops 100000000 | bytes 4000000 | tf_op jit(solution)/shard_map/pallas_call | solution.py:661
  127.6 2.1 %shard_map.169 = (f32[2,2,192]{2,1,0:T(2,128)}, f32[2,192,576]{2,1,0:T(8,128)}, f32[2,192,192]{2,1,0:T(8,128)}, f32[2,192,768]{2,1,0:T(8,128)}, f32[2,192,768]{2,1,0:T(8,128)}, /*index=5*/f32[2,1,6,2,3312]{4,3,2,1,0:T(2,128)}) custom-call(s32[1]{0:T(128)} %bitcast.upper_ref.refs_0_, bf16[1792,128]{1,0:T(8,128)(2,1)S(1)} %pad_maximum_fusion.first_own, ...), custom_call_target="tpu_custom_call" | custom-call | tf_op jit(solution)/shard_map/pallas_call | solution.py:978
  (98 shorter events, 12.1 us)
Async XLA Ops:
  8.3 16.2 %collective-permute-start = (bf16[144,192]{1,0:T(8,128)(2,1)}, bf16[144,192]{1,0:T(8,128)(2,1)S(1)}, u32[]{:S(2)}, u32[]{:S(2)}) collective-permute-start(bf16[144,192]{1,0:T(8,128)(2,1)} %get-tuple-element.66), channel_id=1, source_target_pairs={{16,0},{17,1},{18,2},{19,3},{20,4},{21,5},{22,6},{23,7},{24,8},{25... | collective-permute-start | bytes 165896 | tf_op jit(solution)/shard_map/ppermute | solution.py:692
  17.3 7.2 %collective-permute-start.1 = (bf16[144,192]{1,0:T(8,128)(2,1)}, bf16[144,192]{1,0:T(8,128)(2,1)S(1)}, u32[]{:S(2)}, u32[]{:S(2)}) collective-permute-start(bf16[144,192]{1,0:T(8,128)(2,1)} %get-tuple-element.67), channel_id=1, source_target_pairs={{1,0},{2,1},{3,2},{4,3},{5,4},{6,5},{7,6},{8,7},{9,8},{10,9},{11,1... | collective-permute-start | bytes 165896 | tf_op jit(solution)/shard_map/ppermute | solution.py:692
  18.3 6.3 %collective-permute-start.2 = (bf16[144,192]{1,0:T(8,128)(2,1)}, bf16[144,192]{1,0:T(8,128)(2,1)S(1)}, u32[]{:S(2)}, u32[]{:S(2)}) collective-permute-start(bf16[144,192]{1,0:T(8,128)(2,1)} %get-tuple-element.68), channel_id=1, source_target_pairs={{17,0},{18,1},{19,2},{20,3},{21,4},{22,5},{23,6},{24,7},{25,8},{26... | collective-permute-start | bytes 165896 | tf_op jit(solution)/shard_map/ppermute | solution.py:692
  25.2 13.1 %copy-start.1 = (bf16[3,288,192]{2,1,0:T(8,128)(2,1)S(1)}, bf16[3,288,192]{2,1,0:T(8,128)(2,1)}, u32[]{:S(2)}) copy-start(bf16[3,288,192]{2,1,0:T(8,128)(2,1)} %get-tuple-element.73.refs_0_.refs_6_) | copy-start | bytes 995332
  25.2 13.1 %copy-start.2 = (bf16[12,144,144]{2,1,0:T(8,128)(2,1)S(1)}, bf16[12,144,144]{2,1,0:T(8,128)(2,1)}, u32[]{:S(2)}) copy-start(bf16[12,144,144]{2,1,0:T(8,128)(2,1)} %get-tuple-element.74.refs_4_) | copy-start | bytes 1492996
  25.2 13.1 %copy-start.3 = (bf16[2,768,192]{1,2,0:T(8,128)(2,1)S(1)}, bf16[2,768,192]{1,2,0:T(8,128)(2,1)}, u32[]{:S(2)}) copy-start(bf16[2,768,192]{1,2,0:T(8,128)(2,1)} %param.18) | copy-start | bytes 1769476
  25.2 13.1 %copy-start.4 = (bf16[2,3,192,144]{3,2,1,0:T(8,128)(2,1)S(1)}, bf16[2,3,192,144]{3,2,1,0:T(8,128)(2,1)}, u32[]{:S(2)}) copy-start(bf16[2,3,192,144]{3,2,1,0:T(8,128)(2,1)} %get-tuple-element.75.refs_5_) | copy-start | bytes 995332
  25.2 13.1 %copy-start.6 = (bf16[2,192,192]{2,1,0:T(8,128)(2,1)S(1)}, bf16[2,192,192]{2,1,0:T(8,128)(2,1)}, u32[]{:S(2)}) copy-start(bf16[2,192,192]{2,1,0:T(8,128)(2,1)} %refs_9_.1) | copy-start | bytes 442372
  37.3 17.6 %collective-permute-start.7 = (bf16[1792,128]{1,0:T(8,128)(2,1)}, bf16[1792,128]{1,0:T(8,128)(2,1)}, u32[]{:S(2)}, u32[]{:S(2)}) collective-permute-start(bf16[1792,128]{1,0:T(8,128)(2,1)} %get-tuple-element.93), channel_id=1, source_target_pairs={{1,0},{0,1},{3,2},{2,3},{5,4},{4,5},{7,6},{6,7},{9,8},{8,9},{11,10... | collective-permute-start | bytes 1376264 | tf_op jit(solution)/shard_map/ppermute | solution.py:833
  37.3 8.8 %collective-permute-start.3 = (bf16[144,192]{1,0:T(8,128)(2,1)}, bf16[144,192]{1,0:T(8,128)(2,1)S(1)}, u32[]{:S(2)}, u32[]{:S(2)}) collective-permute-start(bf16[144,192]{1,0:T(8,128)(2,1)} %get-tuple-element.69), channel_id=1, source_target_pairs={{255,0},{240,1},{241,2},{242,3},{243,4},{244,5},{245,6},{246,7},{2... | collective-permute-start | bytes 165896 | tf_op jit(solution)/shard_map/ppermute | solution.py:692
  37.4 8.7 %collective-permute-start.4 = (bf16[144,192]{1,0:T(8,128)(2,1)}, bf16[144,192]{1,0:T(8,128)(2,1)S(1)}, u32[]{:S(2)}, u32[]{:S(2)}) collective-permute-start(bf16[144,192]{1,0:T(8,128)(2,1)} %get-tuple-element.70), channel_id=1, source_target_pairs={{15,0},{0,1},{1,2},{2,3},{3,4},{4,5},{5,6},{6,7},{7,8},{8,9},{9,10... | collective-permute-start | bytes 165896 | tf_op jit(solution)/shard_map/ppermute | solution.py:692
  37.6 9.9 %collective-permute-start.5 = (bf16[144,192]{1,0:T(8,128)(2,1)}, bf16[144,192]{1,0:T(8,128)(2,1)S(1)}, u32[]{:S(2)}, u32[]{:S(2)}) collective-permute-start(bf16[144,192]{1,0:T(8,128)(2,1)} %get-tuple-element.71), channel_id=1, source_target_pairs={{240,0},{241,1},{242,2},{243,3},{244,4},{245,5},{246,6},{247,7},{2... | collective-permute-start | bytes 165896 | tf_op jit(solution)/shard_map/ppermute | solution.py:692
  53.8 2.5 %collective-permute-start.6 = (bf16[1792,128]{1,0:T(8,128)(2,1)S(1)}, bf16[1792,128]{1,0:T(8,128)(2,1)S(1)}, u32[]{:S(2)}, u32[]{:S(2)}) collective-permute-start(bf16[1792,128]{1,0:T(8,128)(2,1)S(1)} %get-tuple-element.91), channel_id=1, source_target_pairs={{1,0},{0,1},{3,2},{2,3},{5,4},{4,5},{7,6},{6,7},{9,8},{8,9},{11,10... | collective-permute-start | bytes 1376264 | tf_op jit(solution)/shard_map/ppermute | solution.py:833
  56.5 6.9 %collective-permute-start.9 = (bf16[896,128]{1,0:T(8,128)(2,1)S(1)}, bf16[896,128]{1,0:T(8,128)(2,1)S(1)}, u32[]{:S(2)}, u32[]{:S(2)}) collective-permute-start(bf16[896,128]{1,0:T(8,128)(2,1)S(1)} %broadcast_select_fusion.2), channel_id=1, source_target_pairs={{4,0},{5,1},{6,2},{7,3},{0,4},{1,5},{2,6},{3,7},{12,8},{13,9},{14,... | collective-permute-start | bytes 688136 | tf_op jit(solution)/shard_map/ppermute | solution.py:833
  56.6 6.9 %collective-permute-start.8 = (bf16[896,128]{1,0:T(8,128)(2,1)S(1)}, bf16[896,128]{1,0:T(8,128)(2,1)S(1)}, u32[]{:S(2)}, u32[]{:S(2)}) collective-permute-start(bf16[896,128]{1,0:T(8,128)(2,1)S(1)} %broadcast_select_fusion.5), channel_id=1, source_target_pairs={{2,0},{3,1},{0,2},{1,3},{6,4},{7,5},{4,6},{5,7},{10,8},{11,9},{8,1... | collective-permute-start | bytes 688136 | tf_op jit(solution)/shard_map/ppermute | solution.py:833
  63.6 3.7 %collective-permute-start.11 = (bf16[448,128]{1,0:T(8,128)(2,1)S(1)}, bf16[448,128]{1,0:T(8,128)(2,1)S(1)}, u32[]{:S(2)}, u32[]{:S(2)}) collective-permute-start(bf16[448,128]{1,0:T(8,128)(2,1)S(1)} %broadcast_select_fusion.8), channel_id=1, source_target_pairs={{2,0},{3,1},{0,2},{1,3},{6,4},{7,5},{4,6},{5,7},{10,8},{11,9},{8,1... | collective-permute-start | bytes 344072 | tf_op jit(solution)/shard_map/ppermute | solution.py:833
  63.8 3.7 %collective-permute-start.10 = (bf16[448,128]{1,0:T(8,128)(2,1)S(1)}, bf16[448,128]{1,0:T(8,128)(2,1)S(1)}, u32[]{:S(2)}, u32[]{:S(2)}) collective-permute-start(bf16[448,128]{1,0:T(8,128)(2,1)S(1)} %broadcast_select_fusion.14), channel_id=1, source_target_pairs={{4,0},{5,1},{6,2},{7,3},{0,4},{1,5},{2,6},{3,7},{12,8},{13,9},{14,... | collective-permute-start | bytes 344072 | tf_op jit(solution)/shard_map/ppermute | solution.py:833
  67.6 5.3 %collective-permute-start.12 = (bf16[448,128]{1,0:T(8,128)(2,1)S(1)}, bf16[448,128]{1,0:T(8,128)(2,1)S(1)}, u32[]{:S(2)}, u32[]{:S(2)}) collective-permute-start(bf16[448,128]{1,0:T(8,128)(2,1)S(1)} %broadcast_select_fusion.11), channel_id=1, source_target_pairs={{12,0},{13,1},{14,2},{15,3},{8,4},{9,5},{10,6},{11,7},{4,8},{5,9},... | collective-permute-start | bytes 344072 | tf_op jit(solution)/shard_map/ppermute | solution.py:833
  73.0 4.6 %collective-permute-start.13 = (bf16[768,128]{1,0:T(8,128)(2,1)S(1)}, bf16[768,128]{1,0:T(8,128)(2,1)S(1)}, u32[]{:S(2)}, u32[]{:S(2)}) collective-permute-start(bf16[768,128]{1,0:T(8,128)(2,1)S(1)} %pad_maximum_fusion.4), channel_id=1, source_target_pairs={{16,0},{17,1},{18,2},{19,3},{20,4},{21,5},{22,6},{23,7},{24,8},{25... | collective-permute-start | bytes 589832 | tf_op jit(solution)/shard_map/ppermute | solution.py:833
  77.7 6.7 %collective-permute-start.14 = (bf16[608,128]{1,0:T(8,128)(2,1)S(1)}, bf16[608,128]{1,0:T(8,128)(2,1)S(1)}, u32[]{:S(2)}, u32[]{:S(2)}) collective-permute-start(bf16[608,128]{1,0:T(8,128)(2,1)S(1)} %pad_maximum_fusion.6), channel_id=1, source_target_pairs={{32,0},{33,1},{34,2},{35,3},{36,4},{37,5},{38,6},{39,7},{40,8},{41... | collective-permute-start | bytes 466952 | tf_op jit(solution)/shard_map/ppermute | solution.py:833
  84.5 6.4 %collective-permute-start.15 = (bf16[608,128]{1,0:T(8,128)(2,1)S(1)}, bf16[608,128]{1,0:T(8,128)(2,1)S(1)}, u32[]{:S(2)}, u32[]{:S(2)}) collective-permute-start(bf16[608,128]{1,0:T(8,128)(2,1)S(1)} %pad_maximum_fusion.7), channel_id=1, source_target_pairs={{112,0},{113,1},{114,2},{115,3},{116,4},{117,5},{118,6},{119,7},{1... | collective-permute-start | bytes 466952 | tf_op jit(solution)/shard_map/ppermute | solution.py:833
  91.0 5.7 %collective-permute-start.16 = (bf16[608,128]{1,0:T(8,128)(2,1)S(1)}, bf16[608,128]{1,0:T(8,128)(2,1)S(1)}, u32[]{:S(2)}, u32[]{:S(2)}) collective-permute-start(bf16[608,128]{1,0:T(8,128)(2,1)S(1)} %add_convert_fusion.5), channel_id=1, source_target_pairs={{128,0},{129,1},{130,2},{131,3},{132,4},{133,5},{134,6},{135,7},{1... | collective-permute-start | bytes 466952 | tf_op jit(solution)/shard_map/ppermute | solution.py:833
  96.7 4.0 %collective-permute-start.18 = (bf16[160,128]{1,0:T(8,128)(2,1)S(1)}, bf16[160,128]{1,0:T(8,128)(2,1)S(1)}, u32[]{:S(2)}, u32[]{:S(2)}) collective-permute-start(bf16[160,128]{1,0:T(8,128)(2,1)S(1)} %slice.91), channel_id=1, source_target_pairs={{32,0},{33,1},{34,2},{35,3},{36,4},{37,5},{38,6},{39,7},{40,8},{41... | collective-permute-start | bytes 122888 | tf_op jit(solution)/shard_map/ppermute | solution.py:833
  97.8 4.9 %collective-permute-start.17 = (bf16[448,128]{1,0:T(8,128)(2,1)S(1)}, bf16[448,128]{1,0:T(8,128)(2,1)S(1)}, u32[]{:S(2)}, u32[]{:S(2)}) collective-permute-start(bf16[448,128]{1,0:T(8,128)(2,1)S(1)} %slice.90), channel_id=1, source_target_pairs={{12,0},{13,1},{14,2},{15,3},{8,4},{9,5},{10,6},{11,7},{4,8},{5,9},... | collective-permute-start | bytes 344072 | tf_op jit(solution)/shard_map/ppermute | solution.py:833
  102.7 3.4 %collective-permute-start.21 = (bf16[320,128]{1,0:T(8,128)(2,1)S(1)}, bf16[320,128]{1,0:T(8,128)(2,1)S(1)}, u32[]{:S(2)}, u32[]{:S(2)}) collective-permute-start(bf16[320,128]{1,0:T(8,128)(2,1)S(1)} %pad_maximum_fusion.8), channel_id=1, source_target_pairs={{16,0},{17,1},{18,2},{19,3},{20,4},{21,5},{22,6},{23,7},{24,8},{25... | collective-permute-start | bytes 245768 | tf_op jit(solution)/shard_map/ppermute | solution.py:833
  102.8 3.7 %collective-permute-start.19 = (bf16[448,128]{1,0:T(8,128)(2,1)S(1)}, bf16[448,128]{1,0:T(8,128)(2,1)S(1)}, u32[]{:S(2)}, u32[]{:S(2)}) collective-permute-start(bf16[448,128]{1,0:T(8,128)(2,1)S(1)} %get-tuple-element.108), channel_id=1, source_target_pairs={{4,0},{5,1},{6,2},{7,3},{0,4},{1,5},{2,6},{3,7},{12,8},{13,9},{14,... | collective-permute-start | bytes 344072 | tf_op jit(solution)/shard_map/ppermute | solution.py:833
  102.9 3.7 %collective-permute-start.20 = (bf16[448,128]{1,0:T(8,128)(2,1)S(1)}, bf16[448,128]{1,0:T(8,128)(2,1)S(1)}, u32[]{:S(2)}, u32[]{:S(2)}) collective-permute-start(bf16[448,128]{1,0:T(8,128)(2,1)S(1)} %get-tuple-element.109), channel_id=1, source_target_pairs={{2,0},{3,1},{0,2},{1,3},{6,4},{7,5},{4,6},{5,7},{10,8},{11,9},{8,1... | collective-permute-start | bytes 344072 | tf_op jit(solution)/shard_map/ppermute | solution.py:833
  106.7 5.0 %collective-permute-start.22 = (bf16[896,128]{1,0:T(8,128)(2,1)S(1)}, bf16[896,128]{1,0:T(8,128)(2,1)S(1)}, u32[]{:S(2)}, u32[]{:S(2)}) collective-permute-start(bf16[896,128]{1,0:T(8,128)(2,1)S(1)} %get-tuple-element.111), channel_id=1, source_target_pairs={{2,0},{3,1},{0,2},{1,3},{6,4},{7,5},{4,6},{5,7},{10,8},{11,9},{8,1... | collective-permute-start | bytes 688136 | tf_op jit(solution)/shard_map/ppermute | solution.py:833
  108.2 4.9 %collective-permute-start.23 = (bf16[896,128]{1,0:T(8,128)(2,1)S(1)}, bf16[896,128]{1,0:T(8,128)(2,1)S(1)}, u32[]{:S(2)}, u32[]{:S(2)}) collective-permute-start(bf16[896,128]{1,0:T(8,128)(2,1)S(1)} %get-tuple-element.112), channel_id=1, source_target_pairs={{4,0},{5,1},{6,2},{7,3},{0,4},{1,5},{2,6},{3,7},{12,8},{13,9},{14,... | collective-permute-start | bytes 688136 | tf_op jit(solution)/shard_map/ppermute | solution.py:833
  111.7 13.9 %copy-start.8 = (bf16[144,192]{1,0:T(8,128)(2,1)S(1)}, bf16[144,192]{1,0:T(8,128)(2,1)}, u32[]{:S(2)}) copy-start(bf16[144,192]{1,0:T(8,128)(2,1)} %get-tuple-element.72.refs_3_) | copy-start | bytes 165892
  113.2 14.1 %collective-permute-start.24 = (bf16[1792,128]{1,0:T(8,128)(2,1)S(1)}, bf16[1792,128]{1,0:T(8,128)(2,1)S(1)}, u32[]{:S(2)}, u32[]{:S(2)}) collective-permute-start(bf16[1792,128]{1,0:T(8,128)(2,1)S(1)} %pad_maximum_fusion.first_own), channel_id=1, source_target_pairs={{1,0},{0,1},{3,2},{2,3},{5,4},{4,5},{7,6},{6,7},{9,8},{8,9},{11,10... | collective-permute-start | bytes 1376264 | tf_op jit(solution)/shard_map/ppermute | solution.py:833
  125.5 2.1 %collective-permute-start.25 = (bf16[1792,128]{1,0:T(8,128)(2,1)S(1)}, bf16[1792,128]{1,0:T(8,128)(2,1)S(1)}, u32[]{:S(2)}, u32[]{:S(2)}) collective-permute-start(bf16[1792,128]{1,0:T(8,128)(2,1)S(1)} %pad_maximum_fusion.1.second_own), channel_id=1, source_target_pairs={{1,0},{0,1},{3,2},{2,3},{5,4},{4,5},{7,6},{6,7},{9,8},{8,9},{11,10... | collective-permute-start | bytes 1376264 | tf_op jit(solution)/shard_map/ppermute | solution.py:833
  (10 other events, 39.2 us)

commit v5 on v4

--- a/solution.py
+++ b/solution.py
@@ -498,7 +498,7 @@
     tables_out[TABLE_ROWS:] = second_tables_ref[...]
 
 
-def activation_kernel(flat_ref, gains_ref, up_ref, active_out, slope_out):
+def activation_kernel(_, flat_ref, gains_ref, up_ref, active_out, slope_out):
     _, _, _, expanded = feed_forward(flat_ref[1].astype(F32), gains_ref[1:2], up_ref[...])
     active, slope = gelu_parts(expanded)
     active_out[...] = active
@@ -530,7 +530,7 @@
     quads = [quad[...].astype(F32) for quad in (quad_0, quad_1, quad_2, quad_3)]
     grad = mm(places(row_of_quad(0)), jnp.concatenate([quad[QUAD:] for quad in quads], axis=0).astype(BF16))
     gain_one, gain_two, in_weight, out_weight, up_weight, down_weight = block_weights(
-        gains_ref, in_ref, out_ref, up_ref, down_ref
+        gains_ref, in_ref.at[0], out_ref, up_ref, down_ref
     )
     first_hat, first_inverse = norm_stats(flat_ref[0].astype(F32))
     first_norm = (first_hat * gain_one).astype(BF16)
@@ -766,21 +766,22 @@
         shifted(back[1], 0, -1),
         back[0],
     ]
+    home[3], after_second = tie((home[3], is_upper))
     active, slope, *first_near = near_call(
         activation_kernel,
-        (),
+        (after_second,),
         (stored[2], first_weights[0], first_weights[3]),
         [shape_of((TOKENS, FFN), BF16), shape_of((TOKENS, FFN), BF16)],
         [],
         300_000_000,
         (0, 1),
-        (home[3], *stored, *first_weights),
+        (*stored, first_weights[0], *first_weights[2:]),
     )
     second_got = exchanged(second_send, core_step()[0])
     first_keep, first_send, grad_rows, first_scaled = near_call(
         third_kernel,
         (is_upper,),
-        tuple(map(Near, (*home[:3], *first_near[:4], active, slope, *first_near[4:]))),
+        tuple(map(Near, (*home, *first_near[:3], active, slope, first_near[3], in_weight, *first_near[4:]))),
         [half_shape, half_shape, shape_of((TOKENS, C), BF16), shape_of(weights_shape, BF16)],
         [packed_scratch],
         2_000_000_000,
@@ -893,12 +894,14 @@
     for mask in (z_high, y_high):
         joined = added(joined, exchanged(joined, mask))
     joined, tables = tie((joined[:rows], joined[rows:]))
-    joined, tables = double(joined, *x_high), double(tables, *z_mid)
-    first, second, tables = tie((joined[:rows], joined[rows:], tables))
-    first, second, tables = double(first, *x_low), double(second, *y_low), double(tables, *z_low)
+    tables = double(tables, *z_mid)
+    joined = double(joined, *x_high)
+    first, second = tie((joined[:rows], joined[rows:]))
+    first, second = double(first, *x_low), double(second, *y_low)
     first, second, tables = tie((first, second, tables))
     first, second = double(first, *y_low), double(second, *x_low)
-    first, second = tie((first, second))
+    tables = double(tables, *z_low)
+    first, second, tables = tie((first, second, tables))
     return first, exchanged(first, core), second, exchanged(second, core), tables
 
 

time: 130 us -> 130 us (level)
  waiting for transfers between devices: 40.3 us -> 43.6 us
  local copies, waits for them, and re-layouts: 3.16 us -> 1.26 us
  starting transfers between devices: 42.7 us -> 41.4 us
    ppermute x6, waiting for transfers between devices: 4.8 us -> 7.22 us  [shifted(): return lax.ppermute(value, ('lon', 'lat'), pairs)]
    unnamed x32, local copies, waits for them, and re-layouts: 3.15 us -> 1.25 us
where the time goes in v5:
time: 130 us
  waiting for transfers between devices  43.6 us (34%)
  starting transfers between devices  41.4 us (32%)
  Pallas kernels  39.7 us (31%)
  other arithmetic  2.29 us (2%)
  between operations  1.31 us (1%)
    ppermute x20, waiting for transfers between devices, exchanged(): return lax.ppermute(value, ('lon', 'lat'), pairs)  36.4 us
    ppermute x20, starting transfers between devices, exchanged(): return lax.ppermute(value, ('lon', 'lat'), pairs)  27.2 us
    pallas_call x3, Pallas kernels, call(): pl.pallas_call(kernel, grid=(1,), in_specs=[SMEM] * len(scalars) + specs,...  22.7 us
    pallas_call x5, Pallas kernels, near_call(): pl.pallas_call(body, in_specs=[SMEM] * len(scalars) + [VMEM if is_near(op...  14.8 us
    ppermute x6, starting transfers between devices, shifted(): return lax.ppermute(value, ('lon', 'lat'), pairs)  14.2 us
    ppermute x6, waiting for transfers between devices, shifted(): return lax.ppermute(value, ('lon', 'lat'), pairs)  7.22 us
  transfers between devices with their start and end apart: 26, of which 18 were waited for; matrix products, arithmetic and copies ran while one was open for 1% of the time, Pallas kernels for 14%

profile of v5, /device:TPU:1, one launch (start us, length us, event | category | flops | bytes accessed | tf_op | source)
XLA Modules:
  0.0 129.6 jit_solution(3059690761589607493)
XLA Ops:
  0.6 7.7 %shard_map.161 = (bf16[144,192]{1,0:T(8,128)(2,1)}, bf16[144,192]{1,0:T(8,128)(2,1)}, bf16[144,192]{1,0:T(8,128)(2,1)}, bf16[144,192]{1,0:T(8,128)(2,1)}, bf16[1...) custom-call(s32[1,2]{1,0:T(1,128)} %bitcast.14, ...), custom_call_target="tpu_custom_call" | custom-call | flops 1000000000 | bytes 4000000 | tf_op jit(solution)/shard_map/pallas_call | solution.py:593
  8.3 9.0 %collective-permute-start = (bf16[144,192]{1,0:T(8,128)(2,1)}, bf16[144,192]{1,0:T(8,128)(2,1)S(1)}, u32[]{:S(2)}, u32[]{:S(2)}) collective-permute-start(bf16[144,192]{1,0:T(8,128)(2,1)} %get-tuple-element.66), channel_id=1, source_target_pairs={{16,0},{17,1},{18,2},{19,3},{20,4},{21,5},{22,6},{23,7},{24,8},{25... | collective-permute-start | bytes 165896 | tf_op jit(solution)/shard_map/ppermute | solution.py:692
  18.3 3.2 %collective-permute-start.2 = (bf16[144,192]{1,0:T(8,128)(2,1)}, bf16[144,192]{1,0:T(8,128)(2,1)S(1)}, u32[]{:S(2)}, u32[]{:S(2)}) collective-permute-start(bf16[144,192]{1,0:T(8,128)(2,1)} %get-tuple-element.68), channel_id=1, source_target_pairs={{17,0},{18,1},{19,2},{20,3},{21,4},{22,5},{23,6},{24,7},{25,8},{26... | collective-permute-start | bytes 165896 | tf_op jit(solution)/shard_map/ppermute | solution.py:692
  21.6 3.0 %shard_map.162.bias_ref = bf16[12,144,144]{2,1,0:T(8,128)(2,1)} custom-call(s32[1,2]{1,0:T(1,128)} %bitcast.15, s32[6,4,12]{2,1,0:T(4,128)} %bitcast.24, bf16[2,1,6,2,3312]{4,3,2,1,0:T(2,128)(2,1)} %bitcast.21), custom_call_target="tpu_custom_call" | custom-call | flops 500000000 | bytes 4000000 | tf_op jit(solution)/shard_map/pallas_call | solution.py:593
  25.3 12.0 %shard_map.163 = (bf16[144,192]{1,0:T(8,128)(2,1)}, bf16[144,192]{1,0:T(8,128)(2,1)}, bf16[144,192]{1,0:T(8,128)(2,1)}, bf16[144,192]{1,0:T(8,128)(2,1)}, bf16[1...) custom-call(s32[1]{0:T(128)} %bitcast.upper_ref.refs_0_, ...), custom_call_target="tpu_custom_call" | custom-call | flops 3000000000 | bytes 4000000 | tf_op jit(solution)/shard_map/pallas_call | solution.py:593
  38.4 2.0 %shard_map.164 = (bf16[288,768]{1,0:T(8,128)(2,1)S(1)}, bf16[288,768]{1,0:T(8,128)(2,1)S(1)}, bf16[12,144,144]{2,1,0:T(8,128)(2,1)S(1)}, bf16[2,3,192,144]{3,2,1...) custom-call(s32[1]{0:T(128)} %bitcast.upper_ref.refs_0_, ...), custom_call_target="tpu_custom_call" | custom-call | flops 300000000 | bytes 4000000 | tf_op jit(solution)/shard_map/pallas_call | solution.py:661
  40.3 5.7 %collective-permute-done.3.refs_1_.refs_0_ = bf16[144,192]{1,0:T(8,128)(2,1)S(1)} collective-permute-done((bf16[144,192]{1,0:T(8,128)(2,1)}, bf16[144,192]{1,0:T(8,128)(2,1)S(1)}, u32[]{:S(2)}, u32[]{:S(2)}) %collective-permute-start.3) | collective-permute-done | bytes 55328 | tf_op jit(solution)/shard_map/ppermute | solution.py:692
  46.1 1.5 %collective-permute-done.5.refs_3_.refs_2_ = bf16[144,192]{1,0:T(8,128)(2,1)S(1)} collective-permute-done((bf16[144,192]{1,0:T(8,128)(2,1)}, bf16[144,192]{1,0:T(8,128)(2,1)S(1)}, u32[]{:S(2)}, u32[]{:S(2)}) %collective-permute-start.5) | collective-permute-done | bytes 55328 | tf_op jit(solution)/shard_map/ppermute | solution.py:692
  47.5 6.2 %shard_map.165 = (bf16[1792,128]{1,0:T(8,128)(2,1)S(1)}, bf16[1792,128]{1,0:T(8,128)(2,1)S(1)}, bf16[288,192]{1,0:T(8,128)(2,1)S(1)}, bf16[12,144,144]{2,1,0:T(8,128)(2,1)S(1)}) custom-call(s32[1]{0:T(128)} %bitcast.upper_ref.refs_0_, bf16[144,192]{1,0:T(8,128)(2,1)S(1)} %collective-permute-done.3.refs_1_.refs_0_, ...), custom_call_target="tpu_custom_call" | custom-call | flops 2000000000 | bytes 4000000 | tf_op jit(solution)/shard_map/pallas_call | solution.py:661
  53.8 1.1 collective-permute-start.6
  54.9 1.1 add_convert_fusion
  57.5 2.4 %shard_map.167.refs_2_ = bf16[320,128]{1,0:T(8,128)(2,1)S(1)} custom-call(s32[1,2]{1,0:T(1,128)S(1)} %bitcast.16, bf16[12,144,144]{2,1,0:T(8,128)(2,1)S(1)} %copy-done.9), custom_call_target="tpu_custom_call" | custom-call | flops 500000000 | bytes 4000000 | tf_op jit(solution)/shard_map/pallas_call | solution.py:661
  59.9 3.5 %collective-permute-done.9 = bf16[896,128]{1,0:T(8,128)(2,1)S(1)} collective-permute-done((bf16[896,128]{1,0:T(8,128)(2,1)S(1)}, bf16[896,128]{1,0:T(8,128)(2,1)S(1)}, u32[]{:S(2)}, u32[]{:S(2)}) %collective-permute-start.9) | collective-permute-done | bytes 229408 | tf_op jit(solution)/shard_map/ppermute | solution.py:834
  63.8 1.5 %collective-permute-start.10 = (bf16[448,128]{1,0:T(8,128)(2,1)S(1)}, bf16[448,128]{1,0:T(8,128)(2,1)S(1)}, u32[]{:S(2)}, u32[]{:S(2)}) collective-permute-start(bf16[448,128]{1,0:T(8,128)(2,1)S(1)} %broadcast_select_fusion.14), channel_id=1, source_target_pairs={{4,0},{5,1},{6,2},{7,3},{0,4},{1,5},{2,6},{3,7},{12,8},{13,9},{14,... | collective-permute-start | bytes 344072 | tf_op jit(solution)/shard_map/ppermute | solution.py:834
  65.3 2.1 %collective-permute-done.11 = bf16[448,128]{1,0:T(8,128)(2,1)S(1)} collective-permute-done((bf16[448,128]{1,0:T(8,128)(2,1)S(1)}, bf16[448,128]{1,0:T(8,128)(2,1)S(1)}, u32[]{:S(2)}, u32[]{:S(2)}) %collective-permute-start.11) | collective-permute-done | bytes 114720 | tf_op jit(solution)/shard_map/ppermute | solution.py:834
  67.6 2.7 %collective-permute-start.12 = (bf16[448,128]{1,0:T(8,128)(2,1)S(1)}, bf16[448,128]{1,0:T(8,128)(2,1)S(1)}, u32[]{:S(2)}, u32[]{:S(2)}) collective-permute-start(bf16[448,128]{1,0:T(8,128)(2,1)S(1)} %broadcast_select_fusion.11), channel_id=1, source_target_pairs={{12,0},{13,1},{14,2},{15,3},{8,4},{9,5},{10,6},{11,7},{4,8},{5,9},... | collective-permute-start | bytes 344072 | tf_op jit(solution)/shard_map/ppermute | solution.py:834
  70.3 2.6 %shard_map.168 = bf16[640,128]{1,0:T(8,128)(2,1)S(1)} custom-call(s32[1,2]{1,0:T(1,128)S(1)} %bitcast.17, bf16[12,144,144]{2,1,0:T(8,128)(2,1)S(1)} %get-tuple-element.103.refs_1_, bf16[320,128]{1,0:T(8,128)(2,1)S(1)} %shard_map.167.refs_2_), custom_call_target="tpu_custom_call" | custom-call | flops 500000000 | bytes 4000000 | tf_op jit(solution)/shard_map/pallas_call | solution.py:661
  73.1 4.5 %collective-permute-done.13 = bf16[768,128]{1,0:T(8,128)(2,1)S(1)} collective-permute-done((bf16[768,128]{1,0:T(8,128)(2,1)S(1)}, bf16[768,128]{1,0:T(8,128)(2,1)S(1)}, u32[]{:S(2)}, u32[]{:S(2)}) %collective-permute-start.13) | collective-permute-done | bytes 196640 | tf_op jit(solution)/shard_map/ppermute | solution.py:834
  77.8 6.4 %collective-permute-done.14 = bf16[608,128]{1,0:T(8,128)(2,1)S(1)} collective-permute-done((bf16[608,128]{1,0:T(8,128)(2,1)S(1)}, bf16[608,128]{1,0:T(8,128)(2,1)S(1)}, u32[]{:S(2)}, u32[]{:S(2)}) %collective-permute-start.14) | collective-permute-done | bytes 155680 | tf_op jit(solution)/shard_map/ppermute | solution.py:834
  84.6 6.3 %collective-permute-done.15 = bf16[608,128]{1,0:T(8,128)(2,1)S(1)} collective-permute-done((bf16[608,128]{1,0:T(8,128)(2,1)S(1)}, bf16[608,128]{1,0:T(8,128)(2,1)S(1)}, u32[]{:S(2)}, u32[]{:S(2)}) %collective-permute-start.15) | collective-permute-done | bytes 155680 | tf_op jit(solution)/shard_map/ppermute | solution.py:834
  91.0 2.3 %collective-permute-start.16 = (bf16[608,128]{1,0:T(8,128)(2,1)S(1)}, bf16[608,128]{1,0:T(8,128)(2,1)S(1)}, u32[]{:S(2)}, u32[]{:S(2)}) collective-permute-start(bf16[608,128]{1,0:T(8,128)(2,1)S(1)} %add_convert_fusion.5), channel_id=1, source_target_pairs={{128,0},{129,1},{130,2},{131,3},{132,4},{133,5},{134,6},{135,7},{1... | collective-permute-start | bytes 466952 | tf_op jit(solution)/shard_map/ppermute | solution.py:834
  93.3 3.4 %collective-permute-done.16 = bf16[608,128]{1,0:T(8,128)(2,1)S(1)} collective-permute-done((bf16[608,128]{1,0:T(8,128)(2,1)S(1)}, bf16[608,128]{1,0:T(8,128)(2,1)S(1)}, u32[]{:S(2)}, u32[]{:S(2)}) %collective-permute-start.16) | collective-permute-done | bytes 155680 | tf_op jit(solution)/shard_map/ppermute | solution.py:834
  96.7 2.3 %collective-permute-start.17 = (bf16[448,128]{1,0:T(8,128)(2,1)S(1)}, bf16[448,128]{1,0:T(8,128)(2,1)S(1)}, u32[]{:S(2)}, u32[]{:S(2)}) collective-permute-start(bf16[448,128]{1,0:T(8,128)(2,1)S(1)} %slice.90), channel_id=1, source_target_pairs={{12,0},{13,1},{14,2},{15,3},{8,4},{9,5},{10,6},{11,7},{4,8},{5,9},... | collective-permute-start | bytes 344072 | tf_op jit(solution)/shard_map/ppermute | solution.py:834
  99.8 1.9 %collective-permute-done.17 = bf16[448,128]{1,0:T(8,128)(2,1)S(1)} collective-permute-done((bf16[448,128]{1,0:T(8,128)(2,1)S(1)}, bf16[448,128]{1,0:T(8,128)(2,1)S(1)}, u32[]{:S(2)}, u32[]{:S(2)}) %collective-permute-start.17) | collective-permute-done | bytes 114720 | tf_op jit(solution)/shard_map/ppermute | solution.py:834
  103.5 1.9 %collective-permute-done.18 = bf16[448,128]{1,0:T(8,128)(2,1)S(1)} collective-permute-done((bf16[448,128]{1,0:T(8,128)(2,1)S(1)}, bf16[448,128]{1,0:T(8,128)(2,1)S(1)}, u32[]{:S(2)}, u32[]{:S(2)}) %collective-permute-start.18) | collective-permute-done | bytes 114720 | tf_op jit(solution)/shard_map/ppermute | solution.py:834
  105.4 1.2 collective-permute-done.19
  107.4 1.4 %collective-permute-start.22 = (bf16[896,128]{1,0:T(8,128)(2,1)S(1)}, bf16[896,128]{1,0:T(8,128)(2,1)S(1)}, u32[]{:S(2)}, u32[]{:S(2)}) collective-permute-start(bf16[896,128]{1,0:T(8,128)(2,1)S(1)} %get-tuple-element.111), channel_id=1, source_target_pairs={{4,0},{5,1},{6,2},{7,3},{0,4},{1,5},{2,6},{3,7},{12,8},{13,9},{14,... | collective-permute-start | bytes 688136 | tf_op jit(solution)/shard_map/ppermute | solution.py:834
  108.9 1.5 %collective-permute-done.23 = bf16[320,128]{1,0:T(8,128)(2,1)S(1)} collective-permute-done((bf16[320,128]{1,0:T(8,128)(2,1)S(1)}, bf16[320,128]{1,0:T(8,128)(2,1)S(1)}, u32[]{:S(2)}, u32[]{:S(2)}) %collective-permute-start.23) | collective-permute-done | bytes 81952 | tf_op jit(solution)/shard_map/ppermute | solution.py:834
  110.4 1.3 %collective-permute-done.21 = bf16[896,128]{1,0:T(8,128)(2,1)S(1)} collective-permute-done((bf16[896,128]{1,0:T(8,128)(2,1)S(1)}, bf16[896,128]{1,0:T(8,128)(2,1)S(1)}, u32[]{:S(2)}, u32[]{:S(2)}) %collective-permute-start.21) | collective-permute-done | bytes 229408 | tf_op jit(solution)/shard_map/ppermute | solution.py:834
  112.7 12.4 %collective-permute-start.24 = (bf16[1792,128]{1,0:T(8,128)(2,1)S(1)}, bf16[1792,128]{1,0:T(8,128)(2,1)S(1)}, u32[]{:S(2)}, u32[]{:S(2)}) collective-permute-start(bf16[1792,128]{1,0:T(8,128)(2,1)S(1)} %pad_maximum_fusion.first_own), channel_id=1, source_target_pairs={{1,0},{0,1},{3,2},{2,3},{5,4},{4,5},{7,6},{6,7},{9,8},{8,9},{11,10... | collective-permute-start | bytes 1376264 | tf_op jit(solution)/shard_map/ppermute | solution.py:834
  125.2 1.7 %shard_map.166 = (bf16[6,12,4,192]{3,2,1,0:T(4,128)(2,1)}, bf16[6,12,4,192]{3,2,1,0:T(4,128)(2,1)}) custom-call(bf16[144,192]{1,0:T(8,128)(2,1)S(1)} %collective-permute-done.3.refs_1_.refs_0_, bf16[144,192]{1,0:T(8,128)(2,1)S(1)} %collective-permute-done.4.refs_2_.refs_1_, bf16[144,192]{1,0:T(8,128)(2,1)S(1)} %collective-permute-done.5.refs_3_.refs_2_, ...), custom_call_target="tpu_custom_call" | custom-call | flops 100000000 | bytes 4000000 | tf_op jit(solution)/shard_map/pallas_call | solution.py:661
  127.2 2.1 %shard_map.169 = (f32[2,2,192]{2,1,0:T(2,128)}, f32[2,192,576]{2,1,0:T(8,128)}, f32[2,192,192]{2,1,0:T(8,128)}, f32[2,192,768]{2,1,0:T(8,128)}, f32[2,192,768]{2,1,0:T(8,128)}, /*index=5*/f32[2,1,6,2,3312]{4,3,2,1,0:T(2,128)}) custom-call(s32[1]{0:T(128)} %bitcast.upper_ref.refs_0_, bf16[1792,128]{1,0:T(8,128)(2,1)S(1)} %pad_maximum_fusion.first_own, ...), custom_call_target="tpu_custom_call" | custom-call | tf_op jit(solution)/shard_map/pallas_call | solution.py:981
  (98 shorter events, 10.3 us)
Async XLA Ops:
  8.3 16.2 %collective-permute-start = (bf16[144,192]{1,0:T(8,128)(2,1)}, bf16[144,192]{1,0:T(8,128)(2,1)S(1)}, u32[]{:S(2)}, u32[]{:S(2)}) collective-permute-start(bf16[144,192]{1,0:T(8,128)(2,1)} %get-tuple-element.66), channel_id=1, source_target_pairs={{16,0},{17,1},{18,2},{19,3},{20,4},{21,5},{22,6},{23,7},{24,8},{25... | collective-permute-start | bytes 165896 | tf_op jit(solution)/shard_map/ppermute | solution.py:692
  17.3 7.2 %collective-permute-start.1 = (bf16[144,192]{1,0:T(8,128)(2,1)}, bf16[144,192]{1,0:T(8,128)(2,1)S(1)}, u32[]{:S(2)}, u32[]{:S(2)}) collective-permute-start(bf16[144,192]{1,0:T(8,128)(2,1)} %get-tuple-element.67), channel_id=1, source_target_pairs={{1,0},{2,1},{3,2},{4,3},{5,4},{6,5},{7,6},{8,7},{9,8},{10,9},{11,1... | collective-permute-start | bytes 165896 | tf_op jit(solution)/shard_map/ppermute | solution.py:692
  18.3 6.3 %collective-permute-start.2 = (bf16[144,192]{1,0:T(8,128)(2,1)}, bf16[144,192]{1,0:T(8,128)(2,1)S(1)}, u32[]{:S(2)}, u32[]{:S(2)}) collective-permute-start(bf16[144,192]{1,0:T(8,128)(2,1)} %get-tuple-element.68), channel_id=1, source_target_pairs={{17,0},{18,1},{19,2},{20,3},{21,4},{22,5},{23,6},{24,7},{25,8},{26... | collective-permute-start | bytes 165896 | tf_op jit(solution)/shard_map/ppermute | solution.py:692
  25.2 13.1 %copy-start.1 = (bf16[3,288,192]{2,1,0:T(8,128)(2,1)S(1)}, bf16[3,288,192]{2,1,0:T(8,128)(2,1)}, u32[]{:S(2)}) copy-start(bf16[3,288,192]{2,1,0:T(8,128)(2,1)} %get-tuple-element.75.refs_1_.refs_6_) | copy-start | bytes 995332
  25.2 13.1 %copy-start.2 = (bf16[12,144,144]{2,1,0:T(8,128)(2,1)S(1)}, bf16[12,144,144]{2,1,0:T(8,128)(2,1)}, u32[]{:S(2)}) copy-start(bf16[12,144,144]{2,1,0:T(8,128)(2,1)} %get-tuple-element.76.refs_4_) | copy-start | bytes 1492996
  25.2 13.1 %copy-start.3 = (bf16[2,768,192]{1,2,0:T(8,128)(2,1)S(1)}, bf16[2,768,192]{1,2,0:T(8,128)(2,1)}, u32[]{:S(2)}) copy-start(bf16[2,768,192]{1,2,0:T(8,128)(2,1)} %param.18) | copy-start | bytes 1769476
  25.2 13.1 %copy-start.4 = (bf16[2,3,192,144]{3,2,1,0:T(8,128)(2,1)S(1)}, bf16[2,3,192,144]{3,2,1,0:T(8,128)(2,1)}, u32[]{:S(2)}) copy-start(bf16[2,3,192,144]{3,2,1,0:T(8,128)(2,1)} %get-tuple-element.77.refs_5_) | copy-start | bytes 995332
  25.2 13.1 %copy-start.5 = (bf16[2,192,192]{2,1,0:T(8,128)(2,1)S(1)}, bf16[2,192,192]{2,1,0:T(8,128)(2,1)}, u32[]{:S(2)}) copy-start(bf16[2,192,192]{2,1,0:T(8,128)(2,1)} %refs_8_.1) | copy-start | bytes 442372
  37.3 17.6 %collective-permute-start.7 = (bf16[1792,128]{1,0:T(8,128)(2,1)}, bf16[1792,128]{1,0:T(8,128)(2,1)}, u32[]{:S(2)}, u32[]{:S(2)}) collective-permute-start(bf16[1792,128]{1,0:T(8,128)(2,1)} %get-tuple-element.93), channel_id=1, source_target_pairs={{1,0},{0,1},{3,2},{2,3},{5,4},{4,5},{7,6},{6,7},{9,8},{8,9},{11,10... | collective-permute-start | bytes 1376264 | tf_op jit(solution)/shard_map/ppermute | solution.py:834
  37.3 8.8 %collective-permute-start.3 = (bf16[144,192]{1,0:T(8,128)(2,1)}, bf16[144,192]{1,0:T(8,128)(2,1)S(1)}, u32[]{:S(2)}, u32[]{:S(2)}) collective-permute-start(bf16[144,192]{1,0:T(8,128)(2,1)} %get-tuple-element.69), channel_id=1, source_target_pairs={{255,0},{240,1},{241,2},{242,3},{243,4},{244,5},{245,6},{246,7},{2... | collective-permute-start | bytes 165896 | tf_op jit(solution)/shard_map/ppermute | solution.py:692
  37.4 8.7 %collective-permute-start.4 = (bf16[144,192]{1,0:T(8,128)(2,1)}, bf16[144,192]{1,0:T(8,128)(2,1)S(1)}, u32[]{:S(2)}, u32[]{:S(2)}) collective-permute-start(bf16[144,192]{1,0:T(8,128)(2,1)} %get-tuple-element.70), channel_id=1, source_target_pairs={{15,0},{0,1},{1,2},{2,3},{3,4},{4,5},{5,6},{6,7},{7,8},{8,9},{9,10... | collective-permute-start | bytes 165896 | tf_op jit(solution)/shard_map/ppermute | solution.py:692
  37.6 9.9 %collective-permute-start.5 = (bf16[144,192]{1,0:T(8,128)(2,1)}, bf16[144,192]{1,0:T(8,128)(2,1)S(1)}, u32[]{:S(2)}, u32[]{:S(2)}) collective-permute-start(bf16[144,192]{1,0:T(8,128)(2,1)} %get-tuple-element.71), channel_id=1, source_target_pairs={{240,0},{241,1},{242,2},{243,3},{244,4},{245,5},{246,6},{247,7},{2... | collective-permute-start | bytes 165896 | tf_op jit(solution)/shard_map/ppermute | solution.py:692
  53.8 2.5 %collective-permute-start.6 = (bf16[1792,128]{1,0:T(8,128)(2,1)S(1)}, bf16[1792,128]{1,0:T(8,128)(2,1)S(1)}, u32[]{:S(2)}, u32[]{:S(2)}) collective-permute-start(bf16[1792,128]{1,0:T(8,128)(2,1)S(1)} %get-tuple-element.91), channel_id=1, source_target_pairs={{1,0},{0,1},{3,2},{2,3},{5,4},{4,5},{7,6},{6,7},{9,8},{8,9},{11,10... | collective-permute-start | bytes 1376264 | tf_op jit(solution)/shard_map/ppermute | solution.py:834
  56.5 6.9 %collective-permute-start.9 = (bf16[896,128]{1,0:T(8,128)(2,1)S(1)}, bf16[896,128]{1,0:T(8,128)(2,1)S(1)}, u32[]{:S(2)}, u32[]{:S(2)}) collective-permute-start(bf16[896,128]{1,0:T(8,128)(2,1)S(1)} %broadcast_select_fusion.2), channel_id=1, source_target_pairs={{4,0},{5,1},{6,2},{7,3},{0,4},{1,5},{2,6},{3,7},{12,8},{13,9},{14,... | collective-permute-start | bytes 688136 | tf_op jit(solution)/shard_map/ppermute | solution.py:834
  56.6 6.9 %collective-permute-start.8 = (bf16[896,128]{1,0:T(8,128)(2,1)S(1)}, bf16[896,128]{1,0:T(8,128)(2,1)S(1)}, u32[]{:S(2)}, u32[]{:S(2)}) collective-permute-start(bf16[896,128]{1,0:T(8,128)(2,1)S(1)} %broadcast_select_fusion.5), channel_id=1, source_target_pairs={{2,0},{3,1},{0,2},{1,3},{6,4},{7,5},{4,6},{5,7},{10,8},{11,9},{8,1... | collective-permute-start | bytes 688136 | tf_op jit(solution)/shard_map/ppermute | solution.py:834
  63.6 3.7 %collective-permute-start.11 = (bf16[448,128]{1,0:T(8,128)(2,1)S(1)}, bf16[448,128]{1,0:T(8,128)(2,1)S(1)}, u32[]{:S(2)}, u32[]{:S(2)}) collective-permute-start(bf16[448,128]{1,0:T(8,128)(2,1)S(1)} %broadcast_select_fusion.8), channel_id=1, source_target_pairs={{2,0},{3,1},{0,2},{1,3},{6,4},{7,5},{4,6},{5,7},{10,8},{11,9},{8,1... | collective-permute-start | bytes 344072 | tf_op jit(solution)/shard_map/ppermute | solution.py:834
  63.8 3.7 %collective-permute-start.10 = (bf16[448,128]{1,0:T(8,128)(2,1)S(1)}, bf16[448,128]{1,0:T(8,128)(2,1)S(1)}, u32[]{:S(2)}, u32[]{:S(2)}) collective-permute-start(bf16[448,128]{1,0:T(8,128)(2,1)S(1)} %broadcast_select_fusion.14), channel_id=1, source_target_pairs={{4,0},{5,1},{6,2},{7,3},{0,4},{1,5},{2,6},{3,7},{12,8},{13,9},{14,... | collective-permute-start | bytes 344072 | tf_op jit(solution)/shard_map/ppermute | solution.py:834
  67.6 5.3 %collective-permute-start.12 = (bf16[448,128]{1,0:T(8,128)(2,1)S(1)}, bf16[448,128]{1,0:T(8,128)(2,1)S(1)}, u32[]{:S(2)}, u32[]{:S(2)}) collective-permute-start(bf16[448,128]{1,0:T(8,128)(2,1)S(1)} %broadcast_select_fusion.11), channel_id=1, source_target_pairs={{12,0},{13,1},{14,2},{15,3},{8,4},{9,5},{10,6},{11,7},{4,8},{5,9},... | collective-permute-start | bytes 344072 | tf_op jit(solution)/shard_map/ppermute | solution.py:834
  73.0 4.6 %collective-permute-start.13 = (bf16[768,128]{1,0:T(8,128)(2,1)S(1)}, bf16[768,128]{1,0:T(8,128)(2,1)S(1)}, u32[]{:S(2)}, u32[]{:S(2)}) collective-permute-start(bf16[768,128]{1,0:T(8,128)(2,1)S(1)} %pad_maximum_fusion.4), channel_id=1, source_target_pairs={{16,0},{17,1},{18,2},{19,3},{20,4},{21,5},{22,6},{23,7},{24,8},{25... | collective-permute-start | bytes 589832 | tf_op jit(solution)/shard_map/ppermute | solution.py:834
  77.7 6.5 %collective-permute-start.14 = (bf16[608,128]{1,0:T(8,128)(2,1)S(1)}, bf16[608,128]{1,0:T(8,128)(2,1)S(1)}, u32[]{:S(2)}, u32[]{:S(2)}) collective-permute-start(bf16[608,128]{1,0:T(8,128)(2,1)S(1)} %pad_maximum_fusion.6), channel_id=1, source_target_pairs={{32,0},{33,1},{34,2},{35,3},{36,4},{37,5},{38,6},{39,7},{40,8},{41... | collective-permute-start | bytes 466952 | tf_op jit(solution)/shard_map/ppermute | solution.py:834
  84.3 6.6 %collective-permute-start.15 = (bf16[608,128]{1,0:T(8,128)(2,1)S(1)}, bf16[608,128]{1,0:T(8,128)(2,1)S(1)}, u32[]{:S(2)}, u32[]{:S(2)}) collective-permute-start(bf16[608,128]{1,0:T(8,128)(2,1)S(1)} %pad_maximum_fusion.7), channel_id=1, source_target_pairs={{112,0},{113,1},{114,2},{115,3},{116,4},{117,5},{118,6},{119,7},{1... | collective-permute-start | bytes 466952 | tf_op jit(solution)/shard_map/ppermute | solution.py:834
  91.0 5.7 %collective-permute-start.16 = (bf16[608,128]{1,0:T(8,128)(2,1)S(1)}, bf16[608,128]{1,0:T(8,128)(2,1)S(1)}, u32[]{:S(2)}, u32[]{:S(2)}) collective-permute-start(bf16[608,128]{1,0:T(8,128)(2,1)S(1)} %add_convert_fusion.5), channel_id=1, source_target_pairs={{128,0},{129,1},{130,2},{131,3},{132,4},{133,5},{134,6},{135,7},{1... | collective-permute-start | bytes 466952 | tf_op jit(solution)/shard_map/ppermute | solution.py:834
  96.7 4.9 %collective-permute-start.17 = (bf16[448,128]{1,0:T(8,128)(2,1)S(1)}, bf16[448,128]{1,0:T(8,128)(2,1)S(1)}, u32[]{:S(2)}, u32[]{:S(2)}) collective-permute-start(bf16[448,128]{1,0:T(8,128)(2,1)S(1)} %slice.90), channel_id=1, source_target_pairs={{12,0},{13,1},{14,2},{15,3},{8,4},{9,5},{10,6},{11,7},{4,8},{5,9},... | collective-permute-start | bytes 344072 | tf_op jit(solution)/shard_map/ppermute | solution.py:834
  99.0 3.8 %collective-permute-start.20 = (bf16[160,128]{1,0:T(8,128)(2,1)S(1)}, bf16[160,128]{1,0:T(8,128)(2,1)S(1)}, u32[]{:S(2)}, u32[]{:S(2)}) collective-permute-start(bf16[160,128]{1,0:T(8,128)(2,1)S(1)} %slice.91), channel_id=1, source_target_pairs={{32,0},{33,1},{34,2},{35,3},{36,4},{37,5},{38,6},{39,7},{40,8},{41... | collective-permute-start | bytes 122888 | tf_op jit(solution)/shard_map/ppermute | solution.py:834
  101.7 3.7 %collective-permute-start.18 = (bf16[448,128]{1,0:T(8,128)(2,1)S(1)}, bf16[448,128]{1,0:T(8,128)(2,1)S(1)}, u32[]{:S(2)}, u32[]{:S(2)}) collective-permute-start(bf16[448,128]{1,0:T(8,128)(2,1)S(1)} %get-tuple-element.107), channel_id=1, source_target_pairs={{4,0},{5,1},{6,2},{7,3},{0,4},{1,5},{2,6},{3,7},{12,8},{13,9},{14,... | collective-permute-start | bytes 344072 | tf_op jit(solution)/shard_map/ppermute | solution.py:834
  102.9 3.7 %collective-permute-start.19 = (bf16[448,128]{1,0:T(8,128)(2,1)S(1)}, bf16[448,128]{1,0:T(8,128)(2,1)S(1)}, u32[]{:S(2)}, u32[]{:S(2)}) collective-permute-start(bf16[448,128]{1,0:T(8,128)(2,1)S(1)} %get-tuple-element.108), channel_id=1, source_target_pairs={{2,0},{3,1},{0,2},{1,3},{6,4},{7,5},{4,6},{5,7},{10,8},{11,9},{8,1... | collective-permute-start | bytes 344072 | tf_op jit(solution)/shard_map/ppermute | solution.py:834
  106.7 3.7 %collective-permute-start.23 = (bf16[320,128]{1,0:T(8,128)(2,1)S(1)}, bf16[320,128]{1,0:T(8,128)(2,1)S(1)}, u32[]{:S(2)}, u32[]{:S(2)}) collective-permute-start(bf16[320,128]{1,0:T(8,128)(2,1)S(1)} %pad_maximum_fusion.8), channel_id=1, source_target_pairs={{16,0},{17,1},{18,2},{19,3},{20,4},{21,5},{22,6},{23,7},{24,8},{25... | collective-permute-start | bytes 245768 | tf_op jit(solution)/shard_map/ppermute | solution.py:834
  106.8 5.0 %collective-permute-start.21 = (bf16[896,128]{1,0:T(8,128)(2,1)S(1)}, bf16[896,128]{1,0:T(8,128)(2,1)S(1)}, u32[]{:S(2)}, u32[]{:S(2)}) collective-permute-start(bf16[896,128]{1,0:T(8,128)(2,1)S(1)} %get-tuple-element.110), channel_id=1, source_target_pairs={{2,0},{3,1},{0,2},{1,3},{6,4},{7,5},{4,6},{5,7},{10,8},{11,9},{8,1... | collective-permute-start | bytes 688136 | tf_op jit(solution)/shard_map/ppermute | solution.py:834
  107.4 5.2 %collective-permute-start.22 = (bf16[896,128]{1,0:T(8,128)(2,1)S(1)}, bf16[896,128]{1,0:T(8,128)(2,1)S(1)}, u32[]{:S(2)}, u32[]{:S(2)}) collective-permute-start(bf16[896,128]{1,0:T(8,128)(2,1)S(1)} %get-tuple-element.111), channel_id=1, source_target_pairs={{4,0},{5,1},{6,2},{7,3},{0,4},{1,5},{2,6},{3,7},{12,8},{13,9},{14,... | collective-permute-start | bytes 688136 | tf_op jit(solution)/shard_map/ppermute | solution.py:834
  111.8 13.4 %copy-start.11 = (bf16[144,192]{1,0:T(8,128)(2,1)S(1)}, bf16[144,192]{1,0:T(8,128)(2,1)}, u32[]{:S(2)}) copy-start(bf16[144,192]{1,0:T(8,128)(2,1)} %get-tuple-element.73.refs_4_.refs_3_) | copy-start | bytes 165892
  112.7 14.2 %collective-permute-start.24 = (bf16[1792,128]{1,0:T(8,128)(2,1)S(1)}, bf16[1792,128]{1,0:T(8,128)(2,1)S(1)}, u32[]{:S(2)}, u32[]{:S(2)}) collective-permute-start(bf16[1792,128]{1,0:T(8,128)(2,1)S(1)} %pad_maximum_fusion.first_own), channel_id=1, source_target_pairs={{1,0},{0,1},{3,2},{2,3},{5,4},{4,5},{7,6},{6,7},{9,8},{8,9},{11,10... | collective-permute-start | bytes 1376264 | tf_op jit(solution)/shard_map/ppermute | solution.py:834
  125.1 2.1 %collective-permute-start.25 = (bf16[1792,128]{1,0:T(8,128)(2,1)S(1)}, bf16[1792,128]{1,0:T(8,128)(2,1)S(1)}, u32[]{:S(2)}, u32[]{:S(2)}) collective-permute-start(bf16[1792,128]{1,0:T(8,128)(2,1)S(1)} %pad_maximum_fusion.1.second_own), channel_id=1, source_target_pairs={{1,0},{0,1},{3,2},{2,3},{5,4},{4,5},{7,6},{6,7},{9,8},{8,9},{11,10... | collective-permute-start | bytes 1376264 | tf_op jit(solution)/shard_map/ppermute | solution.py:834
  (10 other events, 55.6 us)

commit v6 on v5

--- a/solution.py
+++ b/solution.py
@@ -880,9 +880,8 @@
     z_low, z_mid, z_high = ((0, 1), (0, 5)), ((0, 2), (0, 6)), (0, 7)
 
     first, second = halve(first, *y_low), halve(second, *x_low)
-    first, second, second_tables = tie((first, second, second_tables))
+    first, second_tables = tie((first, second_tables))
     first, second = halve(first, *x_low), halve(second, *y_low)
-    first, second = tie((first, second))
     rows = first.shape[0]
     joined = halve(jnp.concatenate([first, second], axis=0), *x_high)
     joined, tables = tie((joined, tables))
@@ -898,7 +897,7 @@
     joined = double(joined, *x_high)
     first, second = tie((joined[:rows], joined[rows:]))
     first, second = double(first, *x_low), double(second, *y_low)
-    first, second, tables = tie((first, second, tables))
+    first, tables = tie((first, tables))
     first, second = double(first, *y_low), double(second, *x_low)
     tables = double(tables, *z_low)
     first, second, tables = tie((first, second, tables))

time: 130 us -> 129 us (level)
  starting transfers between devices: 41.4 us -> 39.7 us
    ppermute x20, starting transfers between devices: 27.2 us -> 25.5 us  [exchanged(): return lax.ppermute(value, ('lon', 'lat'), pairs)]
  transfers between devices with their start and end apart: 26 -> 26, of which waited for: 18 -> 17; matrix products, arithmetic and copies ran while one was open for 1% -> 1% of each run, Pallas kernels for 14% -> 14%
where the time goes in v6:
time: 129 us
  waiting for transfers between devices  44.8 us (35%)
  Pallas kernels  39.7 us (31%)
  starting transfers between devices  39.7 us (31%)
  other arithmetic  2.3 us (2%)
  between operations  1.32 us (1%)
    ppermute x20, waiting for transfers between devices, exchanged(): return lax.ppermute(value, ('lon', 'lat'), pairs)  37.6 us
    ppermute x20, starting transfers between devices, exchanged(): return lax.ppermute(value, ('lon', 'lat'), pairs)  25.5 us
    pallas_call x3, Pallas kernels, call(): pl.pallas_call(kernel, grid=(1,), in_specs=[SMEM] * len(scalars) + specs,...  22.7 us
    pallas_call x5, Pallas kernels, near_call(): pl.pallas_call(body, in_specs=[SMEM] * len(scalars) + [VMEM if is_near(op...  14.8 us
    ppermute x6, starting transfers between devices, shifted(): return lax.ppermute(value, ('lon', 'lat'), pairs)  14.2 us
    ppermute x6, waiting for transfers between devices, shifted(): return lax.ppermute(value, ('lon', 'lat'), pairs)  7.2 us
  transfers between devices with their start and end apart: 26, of which 17 were waited for; matrix products, arithmetic and copies ran while one was open for 1% of the time, Pallas kernels for 14%

profile of v6, /device:TPU:1, one launch (start us, length us, event | category | flops | bytes accessed | tf_op | source)
XLA Modules:
  0.0 129.1 jit_solution(16863129058436645356)
XLA Ops:
  0.6 7.7 %shard_map.161 = (bf16[144,192]{1,0:T(8,128)(2,1)}, bf16[144,192]{1,0:T(8,128)(2,1)}, bf16[144,192]{1,0:T(8,128)(2,1)}, bf16[144,192]{1,0:T(8,128)(2,1)}, bf16[1...) custom-call(s32[1,2]{1,0:T(1,128)} %bitcast.14, ...), custom_call_target="tpu_custom_call" | custom-call | flops 1000000000 | bytes 4000000 | tf_op jit(solution)/shard_map/pallas_call | solution.py:593
  8.3 9.0 %collective-permute-start = (bf16[144,192]{1,0:T(8,128)(2,1)}, bf16[144,192]{1,0:T(8,128)(2,1)S(1)}, u32[]{:S(2)}, u32[]{:S(2)}) collective-permute-start(bf16[144,192]{1,0:T(8,128)(2,1)} %get-tuple-element.62), channel_id=1, source_target_pairs={{16,0},{17,1},{18,2},{19,3},{20,4},{21,5},{22,6},{23,7},{24,8},{25... | collective-permute-start | bytes 165896 | tf_op jit(solution)/shard_map/ppermute | solution.py:692
  18.3 3.2 %collective-permute-start.2 = (bf16[144,192]{1,0:T(8,128)(2,1)}, bf16[144,192]{1,0:T(8,128)(2,1)S(1)}, u32[]{:S(2)}, u32[]{:S(2)}) collective-permute-start(bf16[144,192]{1,0:T(8,128)(2,1)} %get-tuple-element.64), channel_id=1, source_target_pairs={{17,0},{18,1},{19,2},{20,3},{21,4},{22,5},{23,6},{24,7},{25,8},{26... | collective-permute-start | bytes 165896 | tf_op jit(solution)/shard_map/ppermute | solution.py:692
  21.6 3.0 %shard_map.162.bias_ref = bf16[12,144,144]{2,1,0:T(8,128)(2,1)} custom-call(s32[1,2]{1,0:T(1,128)} %bitcast.15, s32[6,4,12]{2,1,0:T(4,128)} %bitcast.24, bf16[2,1,6,2,3312]{4,3,2,1,0:T(2,128)(2,1)} %bitcast.21), custom_call_target="tpu_custom_call" | custom-call | flops 500000000 | bytes 4000000 | tf_op jit(solution)/shard_map/pallas_call | solution.py:593
  25.3 12.0 %shard_map.163 = (bf16[144,192]{1,0:T(8,128)(2,1)}, bf16[144,192]{1,0:T(8,128)(2,1)}, bf16[144,192]{1,0:T(8,128)(2,1)}, bf16[144,192]{1,0:T(8,128)(2,1)}, bf16[1...) custom-call(s32[1]{0:T(128)} %bitcast.upper_ref.refs_0_, ...), custom_call_target="tpu_custom_call" | custom-call | flops 3000000000 | bytes 4000000 | tf_op jit(solution)/shard_map/pallas_call | solution.py:593
  38.4 2.0 %shard_map.164 = (bf16[288,768]{1,0:T(8,128)(2,1)S(1)}, bf16[288,768]{1,0:T(8,128)(2,1)S(1)}, bf16[12,144,144]{2,1,0:T(8,128)(2,1)S(1)}, bf16[2,3,192,144]{3,2,1...) custom-call(s32[1]{0:T(128)} %bitcast.upper_ref.refs_0_, ...), custom_call_target="tpu_custom_call" | custom-call | flops 300000000 | bytes 4000000 | tf_op jit(solution)/shard_map/pallas_call | solution.py:661
  40.3 5.7 %collective-permute-done.3.refs_1_.refs_0_ = bf16[144,192]{1,0:T(8,128)(2,1)S(1)} collective-permute-done((bf16[144,192]{1,0:T(8,128)(2,1)}, bf16[144,192]{1,0:T(8,128)(2,1)S(1)}, u32[]{:S(2)}, u32[]{:S(2)}) %collective-permute-start.3) | collective-permute-done | bytes 55328 | tf_op jit(solution)/shard_map/ppermute | solution.py:692
  46.1 1.5 %collective-permute-done.5.refs_3_.refs_2_ = bf16[144,192]{1,0:T(8,128)(2,1)S(1)} collective-permute-done((bf16[144,192]{1,0:T(8,128)(2,1)}, bf16[144,192]{1,0:T(8,128)(2,1)S(1)}, u32[]{:S(2)}, u32[]{:S(2)}) %collective-permute-start.5) | collective-permute-done | bytes 55328 | tf_op jit(solution)/shard_map/ppermute | solution.py:692
  47.5 6.2 %shard_map.165 = (bf16[1792,128]{1,0:T(8,128)(2,1)S(1)}, bf16[1792,128]{1,0:T(8,128)(2,1)S(1)}, bf16[288,192]{1,0:T(8,128)(2,1)S(1)}, bf16[12,144,144]{2,1,0:T(8,128)(2,1)S(1)}) custom-call(s32[1]{0:T(128)} %bitcast.upper_ref.refs_0_, bf16[144,192]{1,0:T(8,128)(2,1)S(1)} %collective-permute-done.3.refs_1_.refs_0_, ...), custom_call_target="tpu_custom_call" | custom-call | flops 2000000000 | bytes 4000000 | tf_op jit(solution)/shard_map/pallas_call | solution.py:661
  53.8 1.1 collective-permute-start.6
  54.9 1.1 add_convert_fusion
  57.5 2.4 %shard_map.167.refs_2_ = bf16[320,128]{1,0:T(8,128)(2,1)S(1)} custom-call(s32[1,2]{1,0:T(1,128)S(1)} %bitcast.16, bf16[12,144,144]{2,1,0:T(8,128)(2,1)S(1)} %copy-done.9), custom_call_target="tpu_custom_call" | custom-call | flops 500000000 | bytes 4000000 | tf_op jit(solution)/shard_map/pallas_call | solution.py:661
  59.9 3.5 %collective-permute-done.10 = bf16[896,128]{1,0:T(8,128)(2,1)S(1)} collective-permute-done((bf16[896,128]{1,0:T(8,128)(2,1)S(1)}, bf16[896,128]{1,0:T(8,128)(2,1)S(1)}, u32[]{:S(2)}, u32[]{:S(2)}) %collective-permute-start.10) | collective-permute-done | bytes 229408 | tf_op jit(solution)/shard_map/ppermute | solution.py:834
  63.7 1.1 collective-permute-start.9
  64.8 2.4 %collective-permute-done.11 = bf16[448,128]{1,0:T(8,128)(2,1)S(1)} collective-permute-done((bf16[448,128]{1,0:T(8,128)(2,1)S(1)}, bf16[448,128]{1,0:T(8,128)(2,1)S(1)}, u32[]{:S(2)}, u32[]{:S(2)}) %collective-permute-start.11) | collective-permute-done | bytes 114720 | tf_op jit(solution)/shard_map/ppermute | solution.py:834
  67.6 2.3 %collective-permute-start.12 = (bf16[448,128]{1,0:T(8,128)(2,1)S(1)}, bf16[448,128]{1,0:T(8,128)(2,1)S(1)}, u32[]{:S(2)}, u32[]{:S(2)}) collective-permute-start(bf16[448,128]{1,0:T(8,128)(2,1)S(1)} %get-tuple-element.114), channel_id=1, source_target_pairs={{12,0},{13,1},{14,2},{15,3},{8,4},{9,5},{10,6},{11,7},{4,8},{5,9},... | collective-permute-start | bytes 344072 | tf_op jit(solution)/shard_map/ppermute | solution.py:834
  69.9 2.6 %shard_map.168 = bf16[640,128]{1,0:T(8,128)(2,1)S(1)} custom-call(s32[1,2]{1,0:T(1,128)S(1)} %bitcast.17, bf16[12,144,144]{2,1,0:T(8,128)(2,1)S(1)} %get-tuple-element.96.refs_1_, bf16[320,128]{1,0:T(8,128)(2,1)S(1)} %shard_map.167.refs_2_), custom_call_target="tpu_custom_call" | custom-call | flops 500000000 | bytes 4000000 | tf_op jit(solution)/shard_map/pallas_call | solution.py:661
  72.7 4.5 %collective-permute-done.13 = bf16[768,128]{1,0:T(8,128)(2,1)S(1)} collective-permute-done((bf16[768,128]{1,0:T(8,128)(2,1)S(1)}, bf16[768,128]{1,0:T(8,128)(2,1)S(1)}, u32[]{:S(2)}, u32[]{:S(2)}) %collective-permute-start.13) | collective-permute-done | bytes 196640 | tf_op jit(solution)/shard_map/ppermute | solution.py:834
  77.4 6.4 %collective-permute-done.14 = bf16[608,128]{1,0:T(8,128)(2,1)S(1)} collective-permute-done((bf16[608,128]{1,0:T(8,128)(2,1)S(1)}, bf16[608,128]{1,0:T(8,128)(2,1)S(1)}, u32[]{:S(2)}, u32[]{:S(2)}) %collective-permute-start.14) | collective-permute-done | bytes 155680 | tf_op jit(solution)/shard_map/ppermute | solution.py:834
  84.3 6.3 %collective-permute-done.15 = bf16[608,128]{1,0:T(8,128)(2,1)S(1)} collective-permute-done((bf16[608,128]{1,0:T(8,128)(2,1)S(1)}, bf16[608,128]{1,0:T(8,128)(2,1)S(1)}, u32[]{:S(2)}, u32[]{:S(2)}) %collective-permute-start.15) | collective-permute-done | bytes 155680 | tf_op jit(solution)/shard_map/ppermute | solution.py:834
  90.6 2.4 %collective-permute-start.16 = (bf16[608,128]{1,0:T(8,128)(2,1)S(1)}, bf16[608,128]{1,0:T(8,128)(2,1)S(1)}, u32[]{:S(2)}, u32[]{:S(2)}) collective-permute-start(bf16[608,128]{1,0:T(8,128)(2,1)S(1)} %add_convert_fusion.5), channel_id=1, source_target_pairs={{128,0},{129,1},{130,2},{131,3},{132,4},{133,5},{134,6},{135,7},{1... | collective-permute-start | bytes 466952 | tf_op jit(solution)/shard_map/ppermute | solution.py:834
  93.0 3.3 %collective-permute-done.16 = bf16[608,128]{1,0:T(8,128)(2,1)S(1)} collective-permute-done((bf16[608,128]{1,0:T(8,128)(2,1)S(1)}, bf16[608,128]{1,0:T(8,128)(2,1)S(1)}, u32[]{:S(2)}, u32[]{:S(2)}) %collective-permute-start.16) | collective-permute-done | bytes 155680 | tf_op jit(solution)/shard_map/ppermute | solution.py:834
  96.3 2.3 %collective-permute-start.17 = (bf16[448,128]{1,0:T(8,128)(2,1)S(1)}, bf16[448,128]{1,0:T(8,128)(2,1)S(1)}, u32[]{:S(2)}, u32[]{:S(2)}) collective-permute-start(bf16[448,128]{1,0:T(8,128)(2,1)S(1)} %slice.92), channel_id=1, source_target_pairs={{12,0},{13,1},{14,2},{15,3},{8,4},{9,5},{10,6},{11,7},{4,8},{5,9},... | collective-permute-start | bytes 344072 | tf_op jit(solution)/shard_map/ppermute | solution.py:834
  99.7 1.6 %collective-permute-done.17 = bf16[448,128]{1,0:T(8,128)(2,1)S(1)} collective-permute-done((bf16[448,128]{1,0:T(8,128)(2,1)S(1)}, bf16[448,128]{1,0:T(8,128)(2,1)S(1)}, u32[]{:S(2)}, u32[]{:S(2)}) %collective-permute-start.17) | collective-permute-done | bytes 114720 | tf_op jit(solution)/shard_map/ppermute | solution.py:834
  101.4 1.7 %collective-permute-done.19 = bf16[160,128]{1,0:T(8,128)(2,1)S(1)} collective-permute-done((bf16[160,128]{1,0:T(8,128)(2,1)S(1)}, bf16[160,128]{1,0:T(8,128)(2,1)S(1)}, u32[]{:S(2)}, u32[]{:S(2)}) %collective-permute-start.19) | collective-permute-done | bytes 40992 | tf_op jit(solution)/shard_map/ppermute | solution.py:834
  103.3 1.8 %collective-permute-done.18 = bf16[448,128]{1,0:T(8,128)(2,1)S(1)} collective-permute-done((bf16[448,128]{1,0:T(8,128)(2,1)S(1)}, bf16[448,128]{1,0:T(8,128)(2,1)S(1)}, u32[]{:S(2)}, u32[]{:S(2)}) %collective-permute-start.18) | collective-permute-done | bytes 114720 | tf_op jit(solution)/shard_map/ppermute | solution.py:834
  105.3 1.6 %collective-permute-done.21 = bf16[448,128]{1,0:T(8,128)(2,1)S(1)} collective-permute-done((bf16[448,128]{1,0:T(8,128)(2,1)S(1)}, bf16[448,128]{1,0:T(8,128)(2,1)S(1)}, u32[]{:S(2)}, u32[]{:S(2)}) %collective-permute-start.21) | collective-permute-done | bytes 114720 | tf_op jit(solution)/shard_map/ppermute | solution.py:834
  107.0 1.3 %collective-permute-start.20 = (bf16[896,128]{1,0:T(8,128)(2,1)S(1)}, bf16[896,128]{1,0:T(8,128)(2,1)S(1)}, u32[]{:S(2)}, u32[]{:S(2)}) collective-permute-start(bf16[896,128]{1,0:T(8,128)(2,1)S(1)} %pad_maximum_fusion.2), channel_id=1, source_target_pairs={{2,0},{3,1},{0,2},{1,3},{6,4},{7,5},{4,6},{5,7},{10,8},{11,9},{8,1... | collective-permute-start | bytes 688136 | tf_op jit(solution)/shard_map/ppermute | solution.py:834
  108.5 3.7 %collective-permute-done.22 = bf16[896,128]{1,0:T(8,128)(2,1)S(1)} collective-permute-done((bf16[896,128]{1,0:T(8,128)(2,1)S(1)}, bf16[896,128]{1,0:T(8,128)(2,1)S(1)}, u32[]{:S(2)}, u32[]{:S(2)}) %collective-permute-start.22) | collective-permute-done | bytes 229408 | tf_op jit(solution)/shard_map/ppermute | solution.py:834
  112.4 12.3 %collective-permute-start.24 = (bf16[1792,128]{1,0:T(8,128)(2,1)S(1)}, bf16[1792,128]{1,0:T(8,128)(2,1)S(1)}, u32[]{:S(2)}, u32[]{:S(2)}) collective-permute-start(bf16[1792,128]{1,0:T(8,128)(2,1)S(1)} %get-tuple-element.105.first_own), channel_id=1, source_target_pairs={{1,0},{0,1},{3,2},{2,3},{5,4},{4,5},{7,6},{6,7},{9,8},{8,9},{11,10... | collective-permute-start | bytes 1376264 | tf_op jit(solution)/shard_map/ppermute | solution.py:834
  124.8 1.7 %shard_map.166 = (bf16[6,12,4,192]{3,2,1,0:T(4,128)(2,1)}, bf16[6,12,4,192]{3,2,1,0:T(4,128)(2,1)}) custom-call(bf16[144,192]{1,0:T(8,128)(2,1)S(1)} %collective-permute-done.3.refs_1_.refs_0_, bf16[144,192]{1,0:T(8,128)(2,1)S(1)} %collective-permute-done.4.refs_2_.refs_1_, bf16[144,192]{1,0:T(8,128)(2,1)S(1)} %collective-permute-done.5.refs_3_.refs_2_, ...), custom_call_target="tpu_custom_call" | custom-call | flops 100000000 | bytes 4000000 | tf_op jit(solution)/shard_map/pallas_call | solution.py:661
  126.8 2.1 %shard_map.169 = (f32[2,2,192]{2,1,0:T(2,128)}, f32[2,192,576]{2,1,0:T(8,128)}, f32[2,192,192]{2,1,0:T(8,128)}, f32[2,192,768]{2,1,0:T(8,128)}, f32[2,192,768]{2,1,0:T(8,128)}, /*index=5*/f32[2,1,6,2,3312]{4,3,2,1,0:T(2,128)}) custom-call(s32[1]{0:T(128)} %bitcast.upper_ref.refs_0_, bf16[1792,128]{1,0:T(8,128)(2,1)S(1)} %get-tuple-element.105.first_own, ...), custom_call_target="tpu_custom_call" | custom-call | tf_op jit(solution)/shard_map/pallas_call | solution.py:980
  (96 shorter events, 8.0 us)
Async XLA Ops:
  8.3 16.2 %collective-permute-start = (bf16[144,192]{1,0:T(8,128)(2,1)}, bf16[144,192]{1,0:T(8,128)(2,1)S(1)}, u32[]{:S(2)}, u32[]{:S(2)}) collective-permute-start(bf16[144,192]{1,0:T(8,128)(2,1)} %get-tuple-element.62), channel_id=1, source_target_pairs={{16,0},{17,1},{18,2},{19,3},{20,4},{21,5},{22,6},{23,7},{24,8},{25... | collective-permute-start | bytes 165896 | tf_op jit(solution)/shard_map/ppermute | solution.py:692
  17.3 7.2 %collective-permute-start.1 = (bf16[144,192]{1,0:T(8,128)(2,1)}, bf16[144,192]{1,0:T(8,128)(2,1)S(1)}, u32[]{:S(2)}, u32[]{:S(2)}) collective-permute-start(bf16[144,192]{1,0:T(8,128)(2,1)} %get-tuple-element.63), channel_id=1, source_target_pairs={{1,0},{2,1},{3,2},{4,3},{5,4},{6,5},{7,6},{8,7},{9,8},{10,9},{11,1... | collective-permute-start | bytes 165896 | tf_op jit(solution)/shard_map/ppermute | solution.py:692
  18.3 6.3 %collective-permute-start.2 = (bf16[144,192]{1,0:T(8,128)(2,1)}, bf16[144,192]{1,0:T(8,128)(2,1)S(1)}, u32[]{:S(2)}, u32[]{:S(2)}) collective-permute-start(bf16[144,192]{1,0:T(8,128)(2,1)} %get-tuple-element.64), channel_id=1, source_target_pairs={{17,0},{18,1},{19,2},{20,3},{21,4},{22,5},{23,6},{24,7},{25,8},{26... | collective-permute-start | bytes 165896 | tf_op jit(solution)/shard_map/ppermute | solution.py:692
  25.2 13.1 %copy-start = (bf16[2,192,768]{2,1,0:T(8,128)(2,1)S(1)}, bf16[2,192,768]{2,1,0:T(8,128)(2,1)}, u32[]{:S(2)}) copy-start(bf16[2,192,768]{2,1,0:T(8,128)(2,1)} %refs_9_.1) | copy-start | bytes 1769476
  25.2 13.1 %copy-start.1 = (bf16[3,288,192]{2,1,0:T(8,128)(2,1)S(1)}, bf16[3,288,192]{2,1,0:T(8,128)(2,1)}, u32[]{:S(2)}) copy-start(bf16[3,288,192]{2,1,0:T(8,128)(2,1)} %get-tuple-element.71.refs_1_.refs_6_) | copy-start | bytes 995332
  25.2 13.1 %copy-start.2 = (bf16[12,144,144]{2,1,0:T(8,128)(2,1)S(1)}, bf16[12,144,144]{2,1,0:T(8,128)(2,1)}, u32[]{:S(2)}) copy-start(bf16[12,144,144]{2,1,0:T(8,128)(2,1)} %get-tuple-element.72.refs_4_) | copy-start | bytes 1492996
  25.2 13.1 %copy-start.3 = (bf16[2,768,192]{1,2,0:T(8,128)(2,1)S(1)}, bf16[2,768,192]{1,2,0:T(8,128)(2,1)}, u32[]{:S(2)}) copy-start(bf16[2,768,192]{1,2,0:T(8,128)(2,1)} %param.18) | copy-start | bytes 1769476
  25.2 13.1 %copy-start.4 = (bf16[2,3,192,144]{3,2,1,0:T(8,128)(2,1)S(1)}, bf16[2,3,192,144]{3,2,1,0:T(8,128)(2,1)}, u32[]{:S(2)}) copy-start(bf16[2,3,192,144]{3,2,1,0:T(8,128)(2,1)} %get-tuple-element.73.refs_5_) | copy-start | bytes 995332
  25.3 13.1 %copy-start.5 = (bf16[2,192,192]{2,1,0:T(8,128)(2,1)S(1)}, bf16[2,192,192]{2,1,0:T(8,128)(2,1)}, u32[]{:S(2)}) copy-start(bf16[2,192,192]{2,1,0:T(8,128)(2,1)} %refs_8_.1) | copy-start | bytes 442372
  37.3 17.6 %collective-permute-start.7 = (bf16[1792,128]{1,0:T(8,128)(2,1)}, bf16[1792,128]{1,0:T(8,128)(2,1)}, u32[]{:S(2)}, u32[]{:S(2)}) collective-permute-start(bf16[1792,128]{1,0:T(8,128)(2,1)} %get-tuple-element.89), channel_id=1, source_target_pairs={{1,0},{0,1},{3,2},{2,3},{5,4},{4,5},{7,6},{6,7},{9,8},{8,9},{11,10... | collective-permute-start | bytes 1376264 | tf_op jit(solution)/shard_map/ppermute | solution.py:834
  37.3 8.8 %collective-permute-start.3 = (bf16[144,192]{1,0:T(8,128)(2,1)}, bf16[144,192]{1,0:T(8,128)(2,1)S(1)}, u32[]{:S(2)}, u32[]{:S(2)}) collective-permute-start(bf16[144,192]{1,0:T(8,128)(2,1)} %get-tuple-element.65), channel_id=1, source_target_pairs={{255,0},{240,1},{241,2},{242,3},{243,4},{244,5},{245,6},{246,7},{2... | collective-permute-start | bytes 165896 | tf_op jit(solution)/shard_map/ppermute | solution.py:692
  37.4 8.7 %collective-permute-start.4 = (bf16[144,192]{1,0:T(8,128)(2,1)}, bf16[144,192]{1,0:T(8,128)(2,1)S(1)}, u32[]{:S(2)}, u32[]{:S(2)}) collective-permute-start(bf16[144,192]{1,0:T(8,128)(2,1)} %get-tuple-element.66), channel_id=1, source_target_pairs={{15,0},{0,1},{1,2},{2,3},{3,4},{4,5},{5,6},{6,7},{7,8},{8,9},{9,10... | collective-permute-start | bytes 165896 | tf_op jit(solution)/shard_map/ppermute | solution.py:692
  37.6 9.9 %collective-permute-start.5 = (bf16[144,192]{1,0:T(8,128)(2,1)}, bf16[144,192]{1,0:T(8,128)(2,1)S(1)}, u32[]{:S(2)}, u32[]{:S(2)}) collective-permute-start(bf16[144,192]{1,0:T(8,128)(2,1)} %get-tuple-element.67), channel_id=1, source_target_pairs={{240,0},{241,1},{242,2},{243,3},{244,4},{245,5},{246,6},{247,7},{2... | collective-permute-start | bytes 165896 | tf_op jit(solution)/shard_map/ppermute | solution.py:692
  53.8 2.5 %collective-permute-start.6 = (bf16[1792,128]{1,0:T(8,128)(2,1)S(1)}, bf16[1792,128]{1,0:T(8,128)(2,1)S(1)}, u32[]{:S(2)}, u32[]{:S(2)}) collective-permute-start(bf16[1792,128]{1,0:T(8,128)(2,1)S(1)} %get-tuple-element.87), channel_id=1, source_target_pairs={{1,0},{0,1},{3,2},{2,3},{5,4},{4,5},{7,6},{6,7},{9,8},{8,9},{11,10... | collective-permute-start | bytes 1376264 | tf_op jit(solution)/shard_map/ppermute | solution.py:834
  56.5 6.9 %collective-permute-start.10 = (bf16[896,128]{1,0:T(8,128)(2,1)S(1)}, bf16[896,128]{1,0:T(8,128)(2,1)S(1)}, u32[]{:S(2)}, u32[]{:S(2)}) collective-permute-start(bf16[896,128]{1,0:T(8,128)(2,1)S(1)} %broadcast_select_fusion.5), channel_id=1, source_target_pairs={{2,0},{3,1},{0,2},{1,3},{6,4},{7,5},{4,6},{5,7},{10,8},{11,9},{8,1... | collective-permute-start | bytes 688136 | tf_op jit(solution)/shard_map/ppermute | solution.py:834
  56.6 7.0 %collective-permute-start.8 = (bf16[896,128]{1,0:T(8,128)(2,1)S(1)}, bf16[896,128]{1,0:T(8,128)(2,1)S(1)}, u32[]{:S(2)}, u32[]{:S(2)}) collective-permute-start(bf16[896,128]{1,0:T(8,128)(2,1)S(1)} %broadcast_select_fusion.2), channel_id=1, source_target_pairs={{4,0},{5,1},{6,2},{7,3},{0,4},{1,5},{2,6},{3,7},{12,8},{13,9},{14,... | collective-permute-start | bytes 688136 | tf_op jit(solution)/shard_map/ppermute | solution.py:834
  63.5 3.7 %collective-permute-start.11 = (bf16[448,128]{1,0:T(8,128)(2,1)S(1)}, bf16[448,128]{1,0:T(8,128)(2,1)S(1)}, u32[]{:S(2)}, u32[]{:S(2)}) collective-permute-start(bf16[448,128]{1,0:T(8,128)(2,1)S(1)} %broadcast_select_fusion.14), channel_id=1, source_target_pairs={{4,0},{5,1},{6,2},{7,3},{0,4},{1,5},{2,6},{3,7},{12,8},{13,9},{14,... | collective-permute-start | bytes 344072 | tf_op jit(solution)/shard_map/ppermute | solution.py:834
  63.7 3.7 %collective-permute-start.9 = (bf16[448,128]{1,0:T(8,128)(2,1)S(1)}, bf16[448,128]{1,0:T(8,128)(2,1)S(1)}, u32[]{:S(2)}, u32[]{:S(2)}) collective-permute-start(bf16[448,128]{1,0:T(8,128)(2,1)S(1)} %broadcast_select_fusion.8), channel_id=1, source_target_pairs={{2,0},{3,1},{0,2},{1,3},{6,4},{7,5},{4,6},{5,7},{10,8},{11,9},{8,1... | collective-permute-start | bytes 344072 | tf_op jit(solution)/shard_map/ppermute | solution.py:834
  67.6 4.9 %collective-permute-start.12 = (bf16[448,128]{1,0:T(8,128)(2,1)S(1)}, bf16[448,128]{1,0:T(8,128)(2,1)S(1)}, u32[]{:S(2)}, u32[]{:S(2)}) collective-permute-start(bf16[448,128]{1,0:T(8,128)(2,1)S(1)} %get-tuple-element.114), channel_id=1, source_target_pairs={{12,0},{13,1},{14,2},{15,3},{8,4},{9,5},{10,6},{11,7},{4,8},{5,9},... | collective-permute-start | bytes 344072 | tf_op jit(solution)/shard_map/ppermute | solution.py:834
  72.6 4.6 %collective-permute-start.13 = (bf16[768,128]{1,0:T(8,128)(2,1)S(1)}, bf16[768,128]{1,0:T(8,128)(2,1)S(1)}, u32[]{:S(2)}, u32[]{:S(2)}) collective-permute-start(bf16[768,128]{1,0:T(8,128)(2,1)S(1)} %pad_maximum_fusion.4), channel_id=1, source_target_pairs={{16,0},{17,1},{18,2},{19,3},{20,4},{21,5},{22,6},{23,7},{24,8},{25... | collective-permute-start | bytes 589832 | tf_op jit(solution)/shard_map/ppermute | solution.py:834
  77.3 6.5 %collective-permute-start.14 = (bf16[608,128]{1,0:T(8,128)(2,1)S(1)}, bf16[608,128]{1,0:T(8,128)(2,1)S(1)}, u32[]{:S(2)}, u32[]{:S(2)}) collective-permute-start(bf16[608,128]{1,0:T(8,128)(2,1)S(1)} %pad_maximum_fusion.6), channel_id=1, source_target_pairs={{32,0},{33,1},{34,2},{35,3},{36,4},{37,5},{38,6},{39,7},{40,8},{41... | collective-permute-start | bytes 466952 | tf_op jit(solution)/shard_map/ppermute | solution.py:834
  83.9 6.6 %collective-permute-start.15 = (bf16[608,128]{1,0:T(8,128)(2,1)S(1)}, bf16[608,128]{1,0:T(8,128)(2,1)S(1)}, u32[]{:S(2)}, u32[]{:S(2)}) collective-permute-start(bf16[608,128]{1,0:T(8,128)(2,1)S(1)} %pad_maximum_fusion.7), channel_id=1, source_target_pairs={{112,0},{113,1},{114,2},{115,3},{116,4},{117,5},{118,6},{119,7},{1... | collective-permute-start | bytes 466952 | tf_op jit(solution)/shard_map/ppermute | solution.py:834
  90.6 5.7 %collective-permute-start.16 = (bf16[608,128]{1,0:T(8,128)(2,1)S(1)}, bf16[608,128]{1,0:T(8,128)(2,1)S(1)}, u32[]{:S(2)}, u32[]{:S(2)}) collective-permute-start(bf16[608,128]{1,0:T(8,128)(2,1)S(1)} %add_convert_fusion.5), channel_id=1, source_target_pairs={{128,0},{129,1},{130,2},{131,3},{132,4},{133,5},{134,6},{135,7},{1... | collective-permute-start | bytes 466952 | tf_op jit(solution)/shard_map/ppermute | solution.py:834
  96.3 4.9 %collective-permute-start.17 = (bf16[448,128]{1,0:T(8,128)(2,1)S(1)}, bf16[448,128]{1,0:T(8,128)(2,1)S(1)}, u32[]{:S(2)}, u32[]{:S(2)}) collective-permute-start(bf16[448,128]{1,0:T(8,128)(2,1)S(1)} %slice.92), channel_id=1, source_target_pairs={{12,0},{13,1},{14,2},{15,3},{8,4},{9,5},{10,6},{11,7},{4,8},{5,9},... | collective-permute-start | bytes 344072 | tf_op jit(solution)/shard_map/ppermute | solution.py:834
  98.6 4.5 %collective-permute-start.19 = (bf16[160,128]{1,0:T(8,128)(2,1)S(1)}, bf16[160,128]{1,0:T(8,128)(2,1)S(1)}, u32[]{:S(2)}, u32[]{:S(2)}) collective-permute-start(bf16[160,128]{1,0:T(8,128)(2,1)S(1)} %slice.93), channel_id=1, source_target_pairs={{32,0},{33,1},{34,2},{35,3},{36,4},{37,5},{38,6},{39,7},{40,8},{41... | collective-permute-start | bytes 122888 | tf_op jit(solution)/shard_map/ppermute | solution.py:834
  101.3 3.7 %collective-permute-start.18 = (bf16[448,128]{1,0:T(8,128)(2,1)S(1)}, bf16[448,128]{1,0:T(8,128)(2,1)S(1)}, u32[]{:S(2)}, u32[]{:S(2)}) collective-permute-start(bf16[448,128]{1,0:T(8,128)(2,1)S(1)} %get-tuple-element.100), channel_id=1, source_target_pairs={{4,0},{5,1},{6,2},{7,3},{0,4},{1,5},{2,6},{3,7},{12,8},{13,9},{14,... | collective-permute-start | bytes 344072 | tf_op jit(solution)/shard_map/ppermute | solution.py:834
  103.2 3.7 %collective-permute-start.21 = (bf16[448,128]{1,0:T(8,128)(2,1)S(1)}, bf16[448,128]{1,0:T(8,128)(2,1)S(1)}, u32[]{:S(2)}, u32[]{:S(2)}) collective-permute-start(bf16[448,128]{1,0:T(8,128)(2,1)S(1)} %get-tuple-element.103), channel_id=1, source_target_pairs={{2,0},{3,1},{0,2},{1,3},{6,4},{7,5},{4,6},{5,7},{10,8},{11,9},{8,1... | collective-permute-start | bytes 344072 | tf_op jit(solution)/shard_map/ppermute | solution.py:834
  105.1 3.4 %collective-permute-start.23 = (bf16[320,128]{1,0:T(8,128)(2,1)S(1)}, bf16[320,128]{1,0:T(8,128)(2,1)S(1)}, u32[]{:S(2)}, u32[]{:S(2)}) collective-permute-start(bf16[320,128]{1,0:T(8,128)(2,1)S(1)} %pad_maximum_fusion.8), channel_id=1, source_target_pairs={{16,0},{17,1},{18,2},{19,3},{20,4},{21,5},{22,6},{23,7},{24,8},{25... | collective-permute-start | bytes 245768 | tf_op jit(solution)/shard_map/ppermute | solution.py:834
  106.9 5.3 %collective-permute-start.22 = (bf16[896,128]{1,0:T(8,128)(2,1)S(1)}, bf16[896,128]{1,0:T(8,128)(2,1)S(1)}, u32[]{:S(2)}, u32[]{:S(2)}) collective-permute-start(bf16[896,128]{1,0:T(8,128)(2,1)S(1)} %pad_maximum_fusion.3), channel_id=1, source_target_pairs={{4,0},{5,1},{6,2},{7,3},{0,4},{1,5},{2,6},{3,7},{12,8},{13,9},{14,... | collective-permute-start | bytes 688136 | tf_op jit(solution)/shard_map/ppermute | solution.py:834
  107.0 5.3 %collective-permute-start.20 = (bf16[896,128]{1,0:T(8,128)(2,1)S(1)}, bf16[896,128]{1,0:T(8,128)(2,1)S(1)}, u32[]{:S(2)}, u32[]{:S(2)}) collective-permute-start(bf16[896,128]{1,0:T(8,128)(2,1)S(1)} %pad_maximum_fusion.2), channel_id=1, source_target_pairs={{2,0},{3,1},{0,2},{1,3},{6,4},{7,5},{4,6},{5,7},{10,8},{11,9},{8,1... | collective-permute-start | bytes 688136 | tf_op jit(solution)/shard_map/ppermute | solution.py:834
  112.4 14.1 %collective-permute-start.24 = (bf16[1792,128]{1,0:T(8,128)(2,1)S(1)}, bf16[1792,128]{1,0:T(8,128)(2,1)S(1)}, u32[]{:S(2)}, u32[]{:S(2)}) collective-permute-start(bf16[1792,128]{1,0:T(8,128)(2,1)S(1)} %get-tuple-element.105.first_own), channel_id=1, source_target_pairs={{1,0},{0,1},{3,2},{2,3},{5,4},{4,5},{7,6},{6,7},{9,8},{8,9},{11,10... | collective-permute-start | bytes 1376264 | tf_op jit(solution)/shard_map/ppermute | solution.py:834
  124.7 2.1 %collective-permute-start.25 = (bf16[1792,128]{1,0:T(8,128)(2,1)S(1)}, bf16[1792,128]{1,0:T(8,128)(2,1)S(1)}, u32[]{:S(2)}, u32[]{:S(2)}) collective-permute-start(bf16[1792,128]{1,0:T(8,128)(2,1)S(1)} %get-tuple-element.106.second_own), channel_id=1, source_target_pairs={{1,0},{0,1},{3,2},{2,3},{5,4},{4,5},{7,6},{6,7},{9,8},{8,9},{11,10... | collective-permute-start | bytes 1376264 | tf_op jit(solution)/shard_map/ppermute | solution.py:834
  (10 other events, 55.0 us)

commit v7 on v6

--- a/solution.py
+++ b/solution.py
@@ -20,7 +20,7 @@
 QUAD = 72
 RELPOS = 3312
 SPAN = 2 * WIN_LON - 1
-ROWS = 3584
+ROWS = 3520
 GAIN_ROWS = 3456
 TABLE_ROWS = 320
 

time: 129 us -> 129 us (level)
  waiting for transfers between devices: 44.8 us -> 42.1 us
  starting transfers between devices: 39.7 us -> 42.1 us
    ppermute x20, waiting for transfers between devices: 37.6 us -> 34.9 us  [exchanged(): return lax.ppermute(value, ('lon', 'lat'), pairs)]
    ppermute x20, starting transfers between devices: 25.5 us -> 27.9 us  [exchanged(): return lax.ppermute(value, ('lon', 'lat'), pairs)]
where the time goes in v7:
time: 129 us
  starting transfers between devices  42.1 us (33%)
  waiting for transfers between devices  42.1 us (33%)
  Pallas kernels  39.6 us (31%)
  other arithmetic  2.43 us (2%)
  between operations  1.31 us (1%)
    ppermute x20, waiting for transfers between devices, exchanged(): return lax.ppermute(value, ('lon', 'lat'), pairs)  34.9 us
    ppermute x20, starting transfers between devices, exchanged(): return lax.ppermute(value, ('lon', 'lat'), pairs)  27.9 us
    pallas_call x3, Pallas kernels, call(): pl.pallas_call(kernel, grid=(1,), in_specs=[SMEM] * len(scalars) + specs,...  22.7 us
    pallas_call x5, Pallas kernels, near_call(): pl.pallas_call(body, in_specs=[SMEM] * len(scalars) + [VMEM if is_near(op...  14.8 us
    ppermute x6, starting transfers between devices, shifted(): return lax.ppermute(value, ('lon', 'lat'), pairs)  14.2 us
    ppermute x6, waiting for transfers between devices, shifted(): return lax.ppermute(value, ('lon', 'lat'), pairs)  7.23 us
  transfers between devices with their start and end apart: 26, of which 17 were waited for; matrix products, arithmetic and copies ran while one was open for 1% of the time, Pallas kernels for 14%

profile of v7, /device:TPU:1, one launch (start us, length us, event | category | flops | bytes accessed | tf_op | source)
XLA Modules:
  0.0 128.8 jit_solution(2704203838603169105)
XLA Ops:
  0.6 7.7 %shard_map.161 = (bf16[144,192]{1,0:T(8,128)(2,1)}, bf16[144,192]{1,0:T(8,128)(2,1)}, bf16[144,192]{1,0:T(8,128)(2,1)}, bf16[144,192]{1,0:T(8,128)(2,1)}, bf16[1...) custom-call(s32[1,2]{1,0:T(1,128)} %bitcast.14, ...), custom_call_target="tpu_custom_call" | custom-call | flops 1000000000 | bytes 4000000 | tf_op jit(solution)/shard_map/pallas_call | solution.py:593
  8.3 9.0 %collective-permute-start = (bf16[144,192]{1,0:T(8,128)(2,1)}, bf16[144,192]{1,0:T(8,128)(2,1)S(1)}, u32[]{:S(2)}, u32[]{:S(2)}) collective-permute-start(bf16[144,192]{1,0:T(8,128)(2,1)} %get-tuple-element.62), channel_id=1, source_target_pairs={{16,0},{17,1},{18,2},{19,3},{20,4},{21,5},{22,6},{23,7},{24,8},{25... | collective-permute-start | bytes 165896 | tf_op jit(solution)/shard_map/ppermute | solution.py:692
  18.3 3.2 %collective-permute-start.2 = (bf16[144,192]{1,0:T(8,128)(2,1)}, bf16[144,192]{1,0:T(8,128)(2,1)S(1)}, u32[]{:S(2)}, u32[]{:S(2)}) collective-permute-start(bf16[144,192]{1,0:T(8,128)(2,1)} %get-tuple-element.64), channel_id=1, source_target_pairs={{17,0},{18,1},{19,2},{20,3},{21,4},{22,5},{23,6},{24,7},{25,8},{26... | collective-permute-start | bytes 165896 | tf_op jit(solution)/shard_map/ppermute | solution.py:692
  21.6 3.0 %shard_map.162.bias_ref = bf16[12,144,144]{2,1,0:T(8,128)(2,1)} custom-call(s32[1,2]{1,0:T(1,128)} %bitcast.15, s32[6,4,12]{2,1,0:T(4,128)} %bitcast.24, bf16[2,1,6,2,3312]{4,3,2,1,0:T(2,128)(2,1)} %bitcast.21), custom_call_target="tpu_custom_call" | custom-call | flops 500000000 | bytes 4000000 | tf_op jit(solution)/shard_map/pallas_call | solution.py:593
  25.3 12.0 %shard_map.163 = (bf16[144,192]{1,0:T(8,128)(2,1)}, bf16[144,192]{1,0:T(8,128)(2,1)}, bf16[144,192]{1,0:T(8,128)(2,1)}, bf16[144,192]{1,0:T(8,128)(2,1)}, bf16[1...) custom-call(s32[1]{0:T(128)} %bitcast.upper_ref.refs_0_, ...), custom_call_target="tpu_custom_call" | custom-call | flops 3000000000 | bytes 4000000 | tf_op jit(solution)/shard_map/pallas_call | solution.py:593
  38.3 2.0 %shard_map.164 = (bf16[288,768]{1,0:T(8,128)(2,1)S(1)}, bf16[288,768]{1,0:T(8,128)(2,1)S(1)}, bf16[12,144,144]{2,1,0:T(8,128)(2,1)S(1)}, bf16[2,3,192,144]{3,2,1...) custom-call(s32[1]{0:T(128)} %bitcast.upper_ref.refs_0_, ...), custom_call_target="tpu_custom_call" | custom-call | flops 300000000 | bytes 4000000 | tf_op jit(solution)/shard_map/pallas_call | solution.py:661
  40.3 5.7 %collective-permute-done.3.refs_1_.refs_0_ = bf16[144,192]{1,0:T(8,128)(2,1)S(1)} collective-permute-done((bf16[144,192]{1,0:T(8,128)(2,1)}, bf16[144,192]{1,0:T(8,128)(2,1)S(1)}, u32[]{:S(2)}, u32[]{:S(2)}) %collective-permute-start.3) | collective-permute-done | bytes 55328 | tf_op jit(solution)/shard_map/ppermute | solution.py:692
  46.1 1.5 %collective-permute-done.5.refs_3_.refs_2_ = bf16[144,192]{1,0:T(8,128)(2,1)S(1)} collective-permute-done((bf16[144,192]{1,0:T(8,128)(2,1)}, bf16[144,192]{1,0:T(8,128)(2,1)S(1)}, u32[]{:S(2)}, u32[]{:S(2)}) %collective-permute-start.5) | collective-permute-done | bytes 55328 | tf_op jit(solution)/shard_map/ppermute | solution.py:692
  47.5 6.2 %shard_map.165 = (bf16[1760,128]{1,0:T(8,128)(2,1)S(1)}, bf16[1760,128]{1,0:T(8,128)(2,1)S(1)}, bf16[288,192]{1,0:T(8,128)(2,1)S(1)}, bf16[12,144,144]{2,1,0:T(8,128)(2,1)S(1)}) custom-call(s32[1]{0:T(128)} %bitcast.upper_ref.refs_0_, bf16[144,192]{1,0:T(8,128)(2,1)S(1)} %collective-permute-done.3.refs_1_.refs_0_, ...), custom_call_target="tpu_custom_call" | custom-call | flops 2000000000 | bytes 4000000 | tf_op jit(solution)/shard_map/pallas_call | solution.py:661
  54.8 1.1 add_convert_fusion
  57.5 2.4 %shard_map.167.refs_2_ = bf16[320,128]{1,0:T(8,128)(2,1)S(1)} custom-call(s32[1,2]{1,0:T(1,128)S(1)} %bitcast.16, bf16[12,144,144]{2,1,0:T(8,128)(2,1)S(1)} %copy-done.9), custom_call_target="tpu_custom_call" | custom-call | flops 500000000 | bytes 4000000 | tf_op jit(solution)/shard_map/pallas_call | solution.py:661
  59.8 3.4 %collective-permute-done.10 = bf16[880,128]{1,0:T(8,128)(2,1)S(1)} collective-permute-done((bf16[880,128]{1,0:T(8,128)(2,1)S(1)}, bf16[880,128]{1,0:T(8,128)(2,1)S(1)}, u32[]{:S(2)}, u32[]{:S(2)}) %collective-permute-start.10) | collective-permute-done | bytes 225312 | tf_op jit(solution)/shard_map/ppermute | solution.py:834
  63.6 1.1 collective-permute-start.9
  64.7 2.4 %collective-permute-done.11 = bf16[440,128]{1,0:T(8,128)(2,1)S(1)} collective-permute-done((bf16[440,128]{1,0:T(8,128)(2,1)S(1)}, bf16[440,128]{1,0:T(8,128)(2,1)S(1)}, u32[]{:S(2)}, u32[]{:S(2)}) %collective-permute-start.11) | collective-permute-done | bytes 112672 | tf_op jit(solution)/shard_map/ppermute | solution.py:834
  67.5 2.3 %collective-permute-start.12 = (bf16[440,128]{1,0:T(8,128)(2,1)S(1)}, bf16[440,128]{1,0:T(8,128)(2,1)S(1)}, u32[]{:S(2)}, u32[]{:S(2)}) collective-permute-start(bf16[440,128]{1,0:T(8,128)(2,1)S(1)} %get-tuple-element.114), channel_id=1, source_target_pairs={{12,0},{13,1},{14,2},{15,3},{8,4},{9,5},{10,6},{11,7},{4,8},{5,9},... | collective-permute-start | bytes 337928 | tf_op jit(solution)/shard_map/ppermute | solution.py:834
  69.7 2.6 %shard_map.168 = bf16[640,128]{1,0:T(8,128)(2,1)S(1)} custom-call(s32[1,2]{1,0:T(1,128)S(1)} %bitcast.17, bf16[12,144,144]{2,1,0:T(8,128)(2,1)S(1)} %get-tuple-element.96.refs_1_, bf16[320,128]{1,0:T(8,128)(2,1)S(1)} %shard_map.167.refs_2_), custom_call_target="tpu_custom_call" | custom-call | flops 500000000 | bytes 4000000 | tf_op jit(solution)/shard_map/pallas_call | solution.py:661
  72.6 4.5 %collective-permute-done.13 = bf16[760,128]{1,0:T(8,128)(2,1)S(1)} collective-permute-done((bf16[760,128]{1,0:T(8,128)(2,1)S(1)}, bf16[760,128]{1,0:T(8,128)(2,1)S(1)}, u32[]{:S(2)}, u32[]{:S(2)}) %collective-permute-start.13) | collective-permute-done | bytes 194592 | tf_op jit(solution)/shard_map/ppermute | solution.py:834
  77.3 6.3 %collective-permute-done.14 = bf16[600,128]{1,0:T(8,128)(2,1)S(1)} collective-permute-done((bf16[600,128]{1,0:T(8,128)(2,1)S(1)}, bf16[600,128]{1,0:T(8,128)(2,1)S(1)}, u32[]{:S(2)}, u32[]{:S(2)}) %collective-permute-start.14) | collective-permute-done | bytes 153632 | tf_op jit(solution)/shard_map/ppermute | solution.py:834
  84.0 6.3 %collective-permute-done.15 = bf16[600,128]{1,0:T(8,128)(2,1)S(1)} collective-permute-done((bf16[600,128]{1,0:T(8,128)(2,1)S(1)}, bf16[600,128]{1,0:T(8,128)(2,1)S(1)}, u32[]{:S(2)}, u32[]{:S(2)}) %collective-permute-start.15) | collective-permute-done | bytes 153632 | tf_op jit(solution)/shard_map/ppermute | solution.py:834
  90.3 2.4 %collective-permute-start.16 = (bf16[600,128]{1,0:T(8,128)(2,1)S(1)}, bf16[600,128]{1,0:T(8,128)(2,1)S(1)}, u32[]{:S(2)}, u32[]{:S(2)}) collective-permute-start(bf16[600,128]{1,0:T(8,128)(2,1)S(1)} %add_convert_fusion.5), channel_id=1, source_target_pairs={{128,0},{129,1},{130,2},{131,3},{132,4},{133,5},{134,6},{135,7},{1... | collective-permute-start | bytes 460808 | tf_op jit(solution)/shard_map/ppermute | solution.py:834
  92.7 3.3 %collective-permute-done.16 = bf16[600,128]{1,0:T(8,128)(2,1)S(1)} collective-permute-done((bf16[600,128]{1,0:T(8,128)(2,1)S(1)}, bf16[600,128]{1,0:T(8,128)(2,1)S(1)}, u32[]{:S(2)}, u32[]{:S(2)}) %collective-permute-start.16) | collective-permute-done | bytes 153632 | tf_op jit(solution)/shard_map/ppermute | solution.py:834
  97.0 2.4 %collective-permute-start.17 = (bf16[440,128]{1,0:T(8,128)(2,1)S(1)}, bf16[440,128]{1,0:T(8,128)(2,1)S(1)}, u32[]{:S(2)}, u32[]{:S(2)}) collective-permute-start(bf16[440,128]{1,0:T(8,128)(2,1)S(1)} %slice.92), channel_id=1, source_target_pairs={{12,0},{13,1},{14,2},{15,3},{8,4},{9,5},{10,6},{11,7},{4,8},{5,9},... | collective-permute-start | bytes 337928 | tf_op jit(solution)/shard_map/ppermute | solution.py:834
  100.2 1.5 %collective-permute-done.17 = bf16[440,128]{1,0:T(8,128)(2,1)S(1)} collective-permute-done((bf16[440,128]{1,0:T(8,128)(2,1)S(1)}, bf16[440,128]{1,0:T(8,128)(2,1)S(1)}, u32[]{:S(2)}, u32[]{:S(2)}) %collective-permute-start.17) | collective-permute-done | bytes 112672 | tf_op jit(solution)/shard_map/ppermute | solution.py:834
  101.9 1.4 %collective-permute-start.21 = (bf16[440,128]{1,0:T(8,128)(2,1)S(1)}, bf16[440,128]{1,0:T(8,128)(2,1)S(1)}, u32[]{:S(2)}, u32[]{:S(2)}) collective-permute-start(bf16[440,128]{1,0:T(8,128)(2,1)S(1)} %get-tuple-element.103), channel_id=1, source_target_pairs={{2,0},{3,1},{0,2},{1,3},{6,4},{7,5},{4,6},{5,7},{10,8},{11,9},{8,1... | collective-permute-start | bytes 337928 | tf_op jit(solution)/shard_map/ppermute | solution.py:834
  103.4 2.2 %collective-permute-done.18 = bf16[440,128]{1,0:T(8,128)(2,1)S(1)} collective-permute-done((bf16[440,128]{1,0:T(8,128)(2,1)S(1)}, bf16[440,128]{1,0:T(8,128)(2,1)S(1)}, u32[]{:S(2)}, u32[]{:S(2)}) %collective-permute-start.18) | collective-permute-done | bytes 112672 | tf_op jit(solution)/shard_map/ppermute | solution.py:834
  105.8 1.4 %collective-permute-start.22 = (bf16[880,128]{1,0:T(8,128)(2,1)S(1)}, bf16[880,128]{1,0:T(8,128)(2,1)S(1)}, u32[]{:S(2)}, u32[]{:S(2)}) collective-permute-start(bf16[880,128]{1,0:T(8,128)(2,1)S(1)} %pad_maximum_fusion.3), channel_id=1, source_target_pairs={{4,0},{5,1},{6,2},{7,3},{0,4},{1,5},{2,6},{3,7},{12,8},{13,9},{14,... | collective-permute-start | bytes 675848 | tf_op jit(solution)/shard_map/ppermute | solution.py:834
  107.2 1.3 %collective-permute-start.20 = (bf16[880,128]{1,0:T(8,128)(2,1)S(1)}, bf16[880,128]{1,0:T(8,128)(2,1)S(1)}, u32[]{:S(2)}, u32[]{:S(2)}) collective-permute-start(bf16[880,128]{1,0:T(8,128)(2,1)S(1)} %pad_maximum_fusion.2), channel_id=1, source_target_pairs={{2,0},{3,1},{0,2},{1,3},{6,4},{7,5},{4,6},{5,7},{10,8},{11,9},{8,1... | collective-permute-start | bytes 675848 | tf_op jit(solution)/shard_map/ppermute | solution.py:834
  108.5 1.2 collective-permute-done.23
  110.8 1.2 collective-permute-done.20
  112.1 12.3 %collective-permute-start.24 = (bf16[1760,128]{1,0:T(8,128)(2,1)S(1)}, bf16[1760,128]{1,0:T(8,128)(2,1)S(1)}, u32[]{:S(2)}, u32[]{:S(2)}) collective-permute-start(bf16[1760,128]{1,0:T(8,128)(2,1)S(1)} %get-tuple-element.105.first_own), channel_id=1, source_target_pairs={{1,0},{0,1},{3,2},{2,3},{5,4},{4,5},{7,6},{6,7},{9,8},{8,9},{11,10... | collective-permute-start | bytes 1351688 | tf_op jit(solution)/shard_map/ppermute | solution.py:834
  124.5 1.7 %shard_map.166 = (bf16[6,12,4,192]{3,2,1,0:T(4,128)(2,1)}, bf16[6,12,4,192]{3,2,1,0:T(4,128)(2,1)}) custom-call(bf16[144,192]{1,0:T(8,128)(2,1)S(1)} %collective-permute-done.3.refs_1_.refs_0_, bf16[144,192]{1,0:T(8,128)(2,1)S(1)} %collective-permute-done.4.refs_2_.refs_1_, bf16[144,192]{1,0:T(8,128)(2,1)S(1)} %collective-permute-done.5.refs_3_.refs_2_, ...), custom_call_target="tpu_custom_call" | custom-call | flops 100000000 | bytes 4000000 | tf_op jit(solution)/shard_map/pallas_call | solution.py:661
  126.5 2.1 %shard_map.169 = (f32[2,2,192]{2,1,0:T(2,128)}, f32[2,192,576]{2,1,0:T(8,128)}, f32[2,192,192]{2,1,0:T(8,128)}, f32[2,192,768]{2,1,0:T(8,128)}, f32[2,192,768]{2,1,0:T(8,128)}, /*index=5*/f32[2,1,6,2,3312]{4,3,2,1,0:T(2,128)}) custom-call(s32[1]{0:T(128)} %bitcast.upper_ref.refs_0_, bf16[1760,128]{1,0:T(8,128)(2,1)S(1)} %get-tuple-element.105.first_own, ...), custom_call_target="tpu_custom_call" | custom-call | tf_op jit(solution)/shard_map/pallas_call | solution.py:980
  (96 shorter events, 10.5 us)
Async XLA Ops:
  8.3 16.2 %collective-permute-start = (bf16[144,192]{1,0:T(8,128)(2,1)}, bf16[144,192]{1,0:T(8,128)(2,1)S(1)}, u32[]{:S(2)}, u32[]{:S(2)}) collective-permute-start(bf16[144,192]{1,0:T(8,128)(2,1)} %get-tuple-element.62), channel_id=1, source_target_pairs={{16,0},{17,1},{18,2},{19,3},{20,4},{21,5},{22,6},{23,7},{24,8},{25... | collective-permute-start | bytes 165896 | tf_op jit(solution)/shard_map/ppermute | solution.py:692
  17.3 7.2 %collective-permute-start.1 = (bf16[144,192]{1,0:T(8,128)(2,1)}, bf16[144,192]{1,0:T(8,128)(2,1)S(1)}, u32[]{:S(2)}, u32[]{:S(2)}) collective-permute-start(bf16[144,192]{1,0:T(8,128)(2,1)} %get-tuple-element.63), channel_id=1, source_target_pairs={{1,0},{2,1},{3,2},{4,3},{5,4},{6,5},{7,6},{8,7},{9,8},{10,9},{11,1... | collective-permute-start | bytes 165896 | tf_op jit(solution)/shard_map/ppermute | solution.py:692
  18.3 6.3 %collective-permute-start.2 = (bf16[144,192]{1,0:T(8,128)(2,1)}, bf16[144,192]{1,0:T(8,128)(2,1)S(1)}, u32[]{:S(2)}, u32[]{:S(2)}) collective-permute-start(bf16[144,192]{1,0:T(8,128)(2,1)} %get-tuple-element.64), channel_id=1, source_target_pairs={{17,0},{18,1},{19,2},{20,3},{21,4},{22,5},{23,6},{24,7},{25,8},{26... | collective-permute-start | bytes 165896 | tf_op jit(solution)/shard_map/ppermute | solution.py:692
  25.2 13.1 %copy-start.1 = (bf16[3,288,192]{2,1,0:T(8,128)(2,1)S(1)}, bf16[3,288,192]{2,1,0:T(8,128)(2,1)}, u32[]{:S(2)}) copy-start(bf16[3,288,192]{2,1,0:T(8,128)(2,1)} %get-tuple-element.71.refs_1_.refs_6_) | copy-start | bytes 995332
  25.2 13.1 %copy-start.2 = (bf16[12,144,144]{2,1,0:T(8,128)(2,1)S(1)}, bf16[12,144,144]{2,1,0:T(8,128)(2,1)}, u32[]{:S(2)}) copy-start(bf16[12,144,144]{2,1,0:T(8,128)(2,1)} %get-tuple-element.72.refs_4_) | copy-start | bytes 1492996
  25.2 13.1 %copy-start.3 = (bf16[2,768,192]{1,2,0:T(8,128)(2,1)S(1)}, bf16[2,768,192]{1,2,0:T(8,128)(2,1)}, u32[]{:S(2)}) copy-start(bf16[2,768,192]{1,2,0:T(8,128)(2,1)} %param.18) | copy-start | bytes 1769476
  25.2 13.1 %copy-start.4 = (bf16[2,3,192,144]{3,2,1,0:T(8,128)(2,1)S(1)}, bf16[2,3,192,144]{3,2,1,0:T(8,128)(2,1)}, u32[]{:S(2)}) copy-start(bf16[2,3,192,144]{3,2,1,0:T(8,128)(2,1)} %get-tuple-element.73.refs_5_) | copy-start | bytes 995332
  25.2 13.1 %copy-start.5 = (bf16[2,192,192]{2,1,0:T(8,128)(2,1)S(1)}, bf16[2,192,192]{2,1,0:T(8,128)(2,1)}, u32[]{:S(2)}) copy-start(bf16[2,192,192]{2,1,0:T(8,128)(2,1)} %refs_8_.1) | copy-start | bytes 442372
  37.3 17.6 %collective-permute-start.7 = (bf16[1760,128]{1,0:T(8,128)(2,1)}, bf16[1760,128]{1,0:T(8,128)(2,1)}, u32[]{:S(2)}, u32[]{:S(2)}) collective-permute-start(bf16[1760,128]{1,0:T(8,128)(2,1)} %get-tuple-element.89), channel_id=1, source_target_pairs={{1,0},{0,1},{3,2},{2,3},{5,4},{4,5},{7,6},{6,7},{9,8},{8,9},{11,10... | collective-permute-start | bytes 1351688 | tf_op jit(solution)/shard_map/ppermute | solution.py:834
  37.3 8.8 %collective-permute-start.3 = (bf16[144,192]{1,0:T(8,128)(2,1)}, bf16[144,192]{1,0:T(8,128)(2,1)S(1)}, u32[]{:S(2)}, u32[]{:S(2)}) collective-permute-start(bf16[144,192]{1,0:T(8,128)(2,1)} %get-tuple-element.65), channel_id=1, source_target_pairs={{255,0},{240,1},{241,2},{242,3},{243,4},{244,5},{245,6},{246,7},{2... | collective-permute-start | bytes 165896 | tf_op jit(solution)/shard_map/ppermute | solution.py:692
  37.4 8.7 %collective-permute-start.4 = (bf16[144,192]{1,0:T(8,128)(2,1)}, bf16[144,192]{1,0:T(8,128)(2,1)S(1)}, u32[]{:S(2)}, u32[]{:S(2)}) collective-permute-start(bf16[144,192]{1,0:T(8,128)(2,1)} %get-tuple-element.66), channel_id=1, source_target_pairs={{15,0},{0,1},{1,2},{2,3},{3,4},{4,5},{5,6},{6,7},{7,8},{8,9},{9,10... | collective-permute-start | bytes 165896 | tf_op jit(solution)/shard_map/ppermute | solution.py:692
  37.6 9.9 %collective-permute-start.5 = (bf16[144,192]{1,0:T(8,128)(2,1)}, bf16[144,192]{1,0:T(8,128)(2,1)S(1)}, u32[]{:S(2)}, u32[]{:S(2)}) collective-permute-start(bf16[144,192]{1,0:T(8,128)(2,1)} %get-tuple-element.67), channel_id=1, source_target_pairs={{240,0},{241,1},{242,2},{243,3},{244,4},{245,5},{246,6},{247,7},{2... | collective-permute-start | bytes 165896 | tf_op jit(solution)/shard_map/ppermute | solution.py:692
  53.8 2.5 %collective-permute-start.6 = (bf16[1760,128]{1,0:T(8,128)(2,1)S(1)}, bf16[1760,128]{1,0:T(8,128)(2,1)S(1)}, u32[]{:S(2)}, u32[]{:S(2)}) collective-permute-start(bf16[1760,128]{1,0:T(8,128)(2,1)S(1)} %get-tuple-element.87), channel_id=1, source_target_pairs={{1,0},{0,1},{3,2},{2,3},{5,4},{4,5},{7,6},{6,7},{9,8},{8,9},{11,10... | collective-permute-start | bytes 1351688 | tf_op jit(solution)/shard_map/ppermute | solution.py:834
  56.4 6.8 %collective-permute-start.10 = (bf16[880,128]{1,0:T(8,128)(2,1)S(1)}, bf16[880,128]{1,0:T(8,128)(2,1)S(1)}, u32[]{:S(2)}, u32[]{:S(2)}) collective-permute-start(bf16[880,128]{1,0:T(8,128)(2,1)S(1)} %broadcast_select_fusion.5), channel_id=1, source_target_pairs={{2,0},{3,1},{0,2},{1,3},{6,4},{7,5},{4,6},{5,7},{10,8},{11,9},{8,1... | collective-permute-start | bytes 675848 | tf_op jit(solution)/shard_map/ppermute | solution.py:834
  56.6 6.9 %collective-permute-start.8 = (bf16[880,128]{1,0:T(8,128)(2,1)S(1)}, bf16[880,128]{1,0:T(8,128)(2,1)S(1)}, u32[]{:S(2)}, u32[]{:S(2)}) collective-permute-start(bf16[880,128]{1,0:T(8,128)(2,1)S(1)} %broadcast_select_fusion.2), channel_id=1, source_target_pairs={{4,0},{5,1},{6,2},{7,3},{0,4},{1,5},{2,6},{3,7},{12,8},{13,9},{14,... | collective-permute-start | bytes 675848 | tf_op jit(solution)/shard_map/ppermute | solution.py:834
  63.4 3.7 %collective-permute-start.11 = (bf16[440,128]{1,0:T(8,128)(2,1)S(1)}, bf16[440,128]{1,0:T(8,128)(2,1)S(1)}, u32[]{:S(2)}, u32[]{:S(2)}) collective-permute-start(bf16[440,128]{1,0:T(8,128)(2,1)S(1)} %broadcast_select_fusion.14), channel_id=1, source_target_pairs={{4,0},{5,1},{6,2},{7,3},{0,4},{1,5},{2,6},{3,7},{12,8},{13,9},{14,... | collective-permute-start | bytes 337928 | tf_op jit(solution)/shard_map/ppermute | solution.py:834
  63.6 3.7 %collective-permute-start.9 = (bf16[440,128]{1,0:T(8,128)(2,1)S(1)}, bf16[440,128]{1,0:T(8,128)(2,1)S(1)}, u32[]{:S(2)}, u32[]{:S(2)}) collective-permute-start(bf16[440,128]{1,0:T(8,128)(2,1)S(1)} %broadcast_select_fusion.8), channel_id=1, source_target_pairs={{2,0},{3,1},{0,2},{1,3},{6,4},{7,5},{4,6},{5,7},{10,8},{11,9},{8,1... | collective-permute-start | bytes 337928 | tf_op jit(solution)/shard_map/ppermute | solution.py:834
  67.5 4.9 %collective-permute-start.12 = (bf16[440,128]{1,0:T(8,128)(2,1)S(1)}, bf16[440,128]{1,0:T(8,128)(2,1)S(1)}, u32[]{:S(2)}, u32[]{:S(2)}) collective-permute-start(bf16[440,128]{1,0:T(8,128)(2,1)S(1)} %get-tuple-element.114), channel_id=1, source_target_pairs={{12,0},{13,1},{14,2},{15,3},{8,4},{9,5},{10,6},{11,7},{4,8},{5,9},... | collective-permute-start | bytes 337928 | tf_op jit(solution)/shard_map/ppermute | solution.py:834
  72.5 4.6 %collective-permute-start.13 = (bf16[760,128]{1,0:T(8,128)(2,1)S(1)}, bf16[760,128]{1,0:T(8,128)(2,1)S(1)}, u32[]{:S(2)}, u32[]{:S(2)}) collective-permute-start(bf16[760,128]{1,0:T(8,128)(2,1)S(1)} %pad_maximum_fusion.4), channel_id=1, source_target_pairs={{16,0},{17,1},{18,2},{19,3},{20,4},{21,5},{22,6},{23,7},{24,8},{25... | collective-permute-start | bytes 583688 | tf_op jit(solution)/shard_map/ppermute | solution.py:834
  77.2 6.4 %collective-permute-start.14 = (bf16[600,128]{1,0:T(8,128)(2,1)S(1)}, bf16[600,128]{1,0:T(8,128)(2,1)S(1)}, u32[]{:S(2)}, u32[]{:S(2)}) collective-permute-start(bf16[600,128]{1,0:T(8,128)(2,1)S(1)} %pad_maximum_fusion.6), channel_id=1, source_target_pairs={{32,0},{33,1},{34,2},{35,3},{36,4},{37,5},{38,6},{39,7},{40,8},{41... | collective-permute-start | bytes 460808 | tf_op jit(solution)/shard_map/ppermute | solution.py:834
  83.7 6.6 %collective-permute-start.15 = (bf16[600,128]{1,0:T(8,128)(2,1)S(1)}, bf16[600,128]{1,0:T(8,128)(2,1)S(1)}, u32[]{:S(2)}, u32[]{:S(2)}) collective-permute-start(bf16[600,128]{1,0:T(8,128)(2,1)S(1)} %pad_maximum_fusion.7), channel_id=1, source_target_pairs={{112,0},{113,1},{114,2},{115,3},{116,4},{117,5},{118,6},{119,7},{1... | collective-permute-start | bytes 460808 | tf_op jit(solution)/shard_map/ppermute | solution.py:834
  90.3 5.7 %collective-permute-start.16 = (bf16[600,128]{1,0:T(8,128)(2,1)S(1)}, bf16[600,128]{1,0:T(8,128)(2,1)S(1)}, u32[]{:S(2)}, u32[]{:S(2)}) collective-permute-start(bf16[600,128]{1,0:T(8,128)(2,1)S(1)} %add_convert_fusion.5), channel_id=1, source_target_pairs={{128,0},{129,1},{130,2},{131,3},{132,4},{133,5},{134,6},{135,7},{1... | collective-permute-start | bytes 460808 | tf_op jit(solution)/shard_map/ppermute | solution.py:834
  96.1 4.1 %collective-permute-start.19 = (bf16[160,128]{1,0:T(8,128)(2,1)S(1)}, bf16[160,128]{1,0:T(8,128)(2,1)S(1)}, u32[]{:S(2)}, u32[]{:S(2)}) collective-permute-start(bf16[160,128]{1,0:T(8,128)(2,1)S(1)} %slice.93), channel_id=1, source_target_pairs={{32,0},{33,1},{34,2},{35,3},{36,4},{37,5},{38,6},{39,7},{40,8},{41... | collective-permute-start | bytes 122888 | tf_op jit(solution)/shard_map/ppermute | solution.py:834
  97.0 4.8 %collective-permute-start.17 = (bf16[440,128]{1,0:T(8,128)(2,1)S(1)}, bf16[440,128]{1,0:T(8,128)(2,1)S(1)}, u32[]{:S(2)}, u32[]{:S(2)}) collective-permute-start(bf16[440,128]{1,0:T(8,128)(2,1)S(1)} %slice.92), channel_id=1, source_target_pairs={{12,0},{13,1},{14,2},{15,3},{8,4},{9,5},{10,6},{11,7},{4,8},{5,9},... | collective-permute-start | bytes 337928 | tf_op jit(solution)/shard_map/ppermute | solution.py:834
  101.8 3.7 %collective-permute-start.18 = (bf16[440,128]{1,0:T(8,128)(2,1)S(1)}, bf16[440,128]{1,0:T(8,128)(2,1)S(1)}, u32[]{:S(2)}, u32[]{:S(2)}) collective-permute-start(bf16[440,128]{1,0:T(8,128)(2,1)S(1)} %get-tuple-element.100), channel_id=1, source_target_pairs={{4,0},{5,1},{6,2},{7,3},{0,4},{1,5},{2,6},{3,7},{12,8},{13,9},{14,... | collective-permute-start | bytes 337928 | tf_op jit(solution)/shard_map/ppermute | solution.py:834
  101.9 3.8 %collective-permute-start.21 = (bf16[440,128]{1,0:T(8,128)(2,1)S(1)}, bf16[440,128]{1,0:T(8,128)(2,1)S(1)}, u32[]{:S(2)}, u32[]{:S(2)}) collective-permute-start(bf16[440,128]{1,0:T(8,128)(2,1)S(1)} %get-tuple-element.103), channel_id=1, source_target_pairs={{2,0},{3,1},{0,2},{1,3},{6,4},{7,5},{4,6},{5,7},{10,8},{11,9},{8,1... | collective-permute-start | bytes 337928 | tf_op jit(solution)/shard_map/ppermute | solution.py:834
  105.6 4.1 %collective-permute-start.23 = (bf16[320,128]{1,0:T(8,128)(2,1)S(1)}, bf16[320,128]{1,0:T(8,128)(2,1)S(1)}, u32[]{:S(2)}, u32[]{:S(2)}) collective-permute-start(bf16[320,128]{1,0:T(8,128)(2,1)S(1)} %pad_maximum_fusion.8), channel_id=1, source_target_pairs={{16,0},{17,1},{18,2},{19,3},{20,4},{21,5},{22,6},{23,7},{24,8},{25... | collective-permute-start | bytes 245768 | tf_op jit(solution)/shard_map/ppermute | solution.py:834
  105.8 4.9 %collective-permute-start.22 = (bf16[880,128]{1,0:T(8,128)(2,1)S(1)}, bf16[880,128]{1,0:T(8,128)(2,1)S(1)}, u32[]{:S(2)}, u32[]{:S(2)}) collective-permute-start(bf16[880,128]{1,0:T(8,128)(2,1)S(1)} %pad_maximum_fusion.3), channel_id=1, source_target_pairs={{4,0},{5,1},{6,2},{7,3},{0,4},{1,5},{2,6},{3,7},{12,8},{13,9},{14,... | collective-permute-start | bytes 675848 | tf_op jit(solution)/shard_map/ppermute | solution.py:834
  107.2 4.8 %collective-permute-start.20 = (bf16[880,128]{1,0:T(8,128)(2,1)S(1)}, bf16[880,128]{1,0:T(8,128)(2,1)S(1)}, u32[]{:S(2)}, u32[]{:S(2)}) collective-permute-start(bf16[880,128]{1,0:T(8,128)(2,1)S(1)} %pad_maximum_fusion.2), channel_id=1, source_target_pairs={{2,0},{3,1},{0,2},{1,3},{6,4},{7,5},{4,6},{5,7},{10,8},{11,9},{8,1... | collective-permute-start | bytes 675848 | tf_op jit(solution)/shard_map/ppermute | solution.py:834
  110.8 13.7 %copy-start.11 = (bf16[144,192]{1,0:T(8,128)(2,1)S(1)}, bf16[144,192]{1,0:T(8,128)(2,1)}, u32[]{:S(2)}) copy-start(bf16[144,192]{1,0:T(8,128)(2,1)} %get-tuple-element.69.refs_4_.refs_3_) | copy-start | bytes 165892
  112.1 14.1 %collective-permute-start.24 = (bf16[1760,128]{1,0:T(8,128)(2,1)S(1)}, bf16[1760,128]{1,0:T(8,128)(2,1)S(1)}, u32[]{:S(2)}, u32[]{:S(2)}) collective-permute-start(bf16[1760,128]{1,0:T(8,128)(2,1)S(1)} %get-tuple-element.105.first_own), channel_id=1, source_target_pairs={{1,0},{0,1},{3,2},{2,3},{5,4},{4,5},{7,6},{6,7},{9,8},{8,9},{11,10... | collective-permute-start | bytes 1351688 | tf_op jit(solution)/shard_map/ppermute | solution.py:834
  124.4 2.1 %collective-permute-start.25 = (bf16[1760,128]{1,0:T(8,128)(2,1)S(1)}, bf16[1760,128]{1,0:T(8,128)(2,1)S(1)}, u32[]{:S(2)}, u32[]{:S(2)}) collective-permute-start(bf16[1760,128]{1,0:T(8,128)(2,1)S(1)} %get-tuple-element.106.second_own), channel_id=1, source_target_pairs={{1,0},{0,1},{3,2},{2,3},{5,4},{4,5},{7,6},{6,7},{9,8},{8,9},{11,10... | collective-permute-start | bytes 1351688 | tf_op jit(solution)/shard_map/ppermute | solution.py:834
  (10 other events, 55.6 us)
